TPU v7x, 256 devices: a whole 4x4x8 slice. The times are simulated.
256 devices in a mesh: orb: 16 (over y_lo, z), slab: 16 (over y_hi, x, core).
Axes of the slice: x: 4, y: 4 (y_hi: 2, y_lo: 2; y = y_hi * 2 + y_lo), z: 8, core: 2. Of those that a mesh axis runs over, the one named last changes fastest.
Arguments:
- psi_re: float32 [16, 128, 256, 256], P('orb', 'slab'), may hold values from -6 to 6
- psi_im: float32 [16, 128, 256, 256], P('orb', 'slab'), may hold values from -6 to 6
- v_local: float32 [128, 256, 256], P('slab'), may hold values from -5 to 1
- n_ground: float32 [128, 256, 256], P('slab', 'orb'), may hold values from 1 to 10
Outputs:
- psi_re_out: float32 [16, 128, 256, 256], P('orb', 'slab')
- psi_im_out: float32 [16, 128, 256, 256], P('orb', 'slab')
All inputs are finite; a program needn't handle non-finite values.
Results may differ from a plain program's by a relative error of at most 0.0001.
Values sent between devices are 32-bit elements; how exact they have to be, the bound alone decides.
No kernel may reach another device: no remote copies, remote signals or barrier semaphores. Data moves between devices by JAX's collectives and lax.ppermute only.
A program may use at most 128 MiB of HBM per device.

v0:
```python
import math

import jax
import jax.numpy as jnp
from jax import lax
from jax.sharding import PartitionSpec as P

SPACING = 0.5
TIME_STEP = 0.02
HIGHEST = lax.Precision.HIGHEST


def with_halo(cells, sides, width):
    for axis, dim in sides:
        count = lax.axis_size(axis)
        head = lax.slice_in_dim(cells, 0, width, axis=dim)
        tail = lax.slice_in_dim(cells, cells.shape[dim] - width, cells.shape[dim], axis=dim)
        cells = jnp.concatenate(
            [
                lax.ppermute(tail, axis, [(i, (i + 1) % count) for i in range(count)]),
                cells,
                lax.ppermute(head, axis, [((i + 1) % count, i) for i in range(count)]),
            ],
            axis=dim,
        )
    return cells


def tables(length):
    positions = jnp.arange(length, dtype=jnp.int32)
    phase_index = positions[:, None] * positions[None, :] % length
    angles = phase_index.astype(jnp.float32) * (2.0 * math.pi / length)
    return (jnp.cos(angles), jnp.sin(angles))


def wave_sq(freq_index, length):
    signed = jnp.where(freq_index * 2 <= length, freq_index, freq_index - length)
    wave_number = signed.astype(jnp.float32) * (2.0 * math.pi / (length * SPACING))
    return wave_number * wave_number


def greens_block(z_index, y_index, x_index, z_len, y_len, x_len):
    wave_total = (
        wave_sq(z_index, z_len)[:, None, None]
        + wave_sq(y_index, y_len)[None, :, None]
        + wave_sq(x_index, x_len)[None, None, :]
    )
    anchor = (
        (z_index[:, None, None] == 0)
        & (y_index[None, :, None] == 0)
        & (x_index[None, None, :] == 0)
    )
    safe = jnp.where(anchor, jnp.float32(1.0), wave_total)
    return jnp.where(anchor, jnp.float32(0.0), 4.0 * math.pi / safe)


def mix(form, left, right):
    return jnp.einsum(form, left, right, precision=HIGHEST)


def across_orb(fields):
    return (
        lax.all_to_all(fields[0], "orb", split_axis=0, concat_axis=2, tiled=True),
        lax.all_to_all(fields[1], "orb", split_axis=0, concat_axis=2, tiled=True),
    )


def across_slab(fields):
    return (
        lax.all_to_all(fields[0], "slab", split_axis=0, concat_axis=2, tiled=True),
        lax.all_to_all(fields[1], "slab", split_axis=0, concat_axis=2, tiled=True),
    )


def widen_once(values):
    return with_halo(values, (("slab", 2),), 1)


def kinetic_plus(widened, potential):
    centre = widened[:, :, 1:-1]
    laplace = (
        jnp.roll(centre, 1, 4)
        + jnp.roll(centre, -1, 4)
        + (jnp.roll(centre, 1, 3) + jnp.roll(centre, -1, 3))
        + (widened[:, :, 2:] + widened[:, :, :-2])
        - 6.0 * centre
    )
    return -0.5 / (SPACING * SPACING) * laplace + potential * centre


def hartree_block(density, x_tabs, y_tabs, z_tabs, greens, norm_scale):
    x_cosine, x_sine = x_tabs
    y_cosine, y_sine = y_tabs
    z_cosine, z_sine = z_tabs
    x_real = mix("kx,zyx->kzy", x_cosine, density)
    x_imag = -mix("kx,zyx->kzy", x_sine, density)
    x_real, x_imag = across_orb((x_real, x_imag))
    y_real = mix("qy,kzy->qkz", y_cosine, x_real) + mix("qy,kzy->qkz", y_sine, x_imag)
    y_imag = mix("qy,kzy->qkz", y_cosine, x_imag) - mix("qy,kzy->qkz", y_sine, x_real)
    y_real, y_imag = across_slab((y_real, y_imag))
    z_real = mix("wz,qkz->wqk", z_cosine, y_real) + mix("wz,qkz->wqk", z_sine, y_imag)
    z_imag = mix("wz,qkz->wqk", z_cosine, y_imag) - mix("wz,qkz->wqk", z_sine, y_real)
    f_real = z_real * greens
    f_imag = z_imag * greens
    b_real = mix("zw,wqk->zkq", z_cosine, f_real) - mix("zw,wqk->zkq", z_sine, f_imag)
    b_imag = mix("zw,wqk->zkq", z_cosine, f_imag) + mix("zw,wqk->zkq", z_sine, f_real)
    b_real, b_imag = across_slab((b_real, b_imag))
    c_real = mix("yq,zkq->yzk", y_cosine, b_real) - mix("yq,zkq->yzk", y_sine, b_imag)
    c_imag = mix("yq,zkq->yzk", y_cosine, b_imag) + mix("yq,zkq->yzk", y_sine, b_real)
    c_real, c_imag = across_orb((c_real, c_imag))
    result = mix("yzk,kx->zyx", c_real, x_cosine) - mix("yzk,kx->zyx", c_imag, x_sine)
    return result * norm_scale


def on_device(psi_re, psi_im, v_local, n_ground):
    orbital_count = psi_re.shape[0]
    total_orbs = orbital_count * lax.axis_size("orb")
    planes, grid_rows, grid_cols = v_local.shape
    grid_depth = planes * lax.axis_size("slab")
    kx_part = grid_cols // lax.axis_size("orb")
    ky_part = grid_rows // lax.axis_size("slab")
    x_tabs = tables(grid_cols)
    y_tabs = tables(grid_rows)
    z_tabs = tables(grid_depth)
    z_index = jnp.arange(grid_depth, dtype=jnp.int32)
    y_index = lax.axis_index("slab") * ky_part + jnp.arange(ky_part, dtype=jnp.int32)
    x_index = lax.axis_index("orb") * kx_part + jnp.arange(kx_part, dtype=jnp.int32)
    greens = greens_block(z_index, y_index, x_index, grid_depth, grid_rows, grid_cols)
    norm_scale = 1.0 / (grid_cols * grid_rows * grid_depth)
    half_sq = 0.5 * TIME_STEP * TIME_STEP
    orbitals_now = jnp.stack([psi_re, psi_im])
    partial_value = (
        2.0
        / total_orbs
        * jnp.sum(orbitals_now[0] * orbitals_now[0] + orbitals_now[1] * orbitals_now[1], axis=0)
    )
    density = lax.psum_scatter(partial_value, "orb", scatter_dimension=1, tiled=True) - n_ground
    hartree = hartree_block(density, x_tabs, y_tabs, z_tabs, greens, norm_scale)
    full_hartree = lax.all_gather(hartree, "orb", axis=1, tiled=True)
    potential = v_local + full_hartree
    first_apply = kinetic_plus(widen_once(orbitals_now), potential)
    second_apply = kinetic_plus(widen_once(first_apply), potential)
    new_re = orbitals_now[0] + TIME_STEP * first_apply[1] - half_sq * second_apply[0]
    new_im = orbitals_now[1] - TIME_STEP * first_apply[0] - half_sq * second_apply[1]
    orbitals_now = jnp.stack([new_re, new_im])
    return (orbitals_now[0], orbitals_now[1])


def solution(mesh):
    placed = (
        P("orb", "slab", None, None),
        P("orb", "slab", None, None),
        P("slab", None, None),
        P("slab", "orb", None),
    )
    return jax.shard_map(
        on_device,
        mesh=mesh,
        in_specs=placed,
        out_specs=(P("orb", "slab", None, None), P("orb", "slab", None, None)),
        check_vma=False,
    )
```

profile of v0, /device:TPU:8, one launch (start us, length us, event | category | flops | bytes accessed | tf_op | source)
XLA Modules:
  0.0 341.8 jit_solution(7285895814618386743)
XLA Ops:
  7.2 3.8 %multiply_bitcast_fusion = f32[8,256,256]{2,1,0:T(8,128)} fusion(f32[1,8,256,256]{3,2,1,0:T(8,128)} %param.5, f32[1,8,256,256]{3,2,1,0:T(8,128)} %param.4), kind=kLoop, calls=%fused_computation.61 | loop fusion | flops 2097152 | bytes 6291456 | tf_op jit(solution)/shard_map/mul | solution.py:133
  11.3 76.1 %reduce-scatter.2.cloned.1.call-done = f32[8,16,256]{2,1,0:T(8,128)} async-done(((f32[8,256,256]{2,1,0:T(8,128)}), f32[8,16,256]{2,1,0:T(8,128)}) %reduce-scatter.2.cloned.1.call-update) | async-done | bytes 131088 | tf_op jit(solution)/shard_map/reduce_scatter | solution.py:137
  87.5 2.3 fusion.63
  91.2 4.9 %all-to-all-start = ((f32[16,1,2048]{2,1,0:T(1,128)}), f32[16,1,2048]{2,1,0:T(1,128)S(1)}, u32[]{:S(2)}, u32[]{:S(2)}) async-start(f32[16,1,2048]{2,1,0:T(1,128)} %reshape.469), calls=%async_computation.1 | async-start | bytes 262144 | tf_op jit(solution)/shard_map/all_to_all | solution.py:63
  96.1 2.3 convolution_negate_fusion
  99.9 4.2 %all-to-all-done = f32[16,1,2048]{2,1,0:T(1,128)S(1)} async-done(((f32[16,1,2048]{2,1,0:T(1,128)}), f32[16,1,2048]{2,1,0:T(1,128)S(1)}, u32[]{:S(2)}, u32[]{:S(2)}) %all-to-all-start) | async-done | bytes 131104 | tf_op jit(solution)/shard_map/all_to_all | solution.py:63
  104.0 5.3 %all-to-all-start.1 = ((f32[16,1,2048]{2,1,0:T(1,128)}), f32[16,1,2048]{2,1,0:T(1,128)S(1)}, u32[]{:S(2)}, u32[]{:S(2)}) async-start(f32[16,1,2048]{2,1,0:T(1,128)} %reshape.471), calls=%async_computation.2 | async-start | bytes 262144 | tf_op jit(solution)/shard_map/all_to_all | solution.py:64
  112.2 1.4 fusion.61
  113.6 3.1 all-to-all-done.1
  120.5 1.4 convolution_subtract_fusion.2
  123.3 6.6 %all-to-all-start.3 = ((f32[16,1,2048]{2,1,0:T(1,128)}), f32[16,1,2048]{2,1,0:T(1,128)S(1)}, u32[]{:S(2)}, u32[]{:S(2)}) async-start(f32[16,1,2048]{2,1,0:T(1,128)} %reshape.475), calls=%async_computation.4 | async-start | bytes 262144 | tf_op jit(solution)/shard_map/all_to_all | solution.py:71
  129.9 1.4 convolution_add_fusion.1
  132.8 5.1 %all-to-all-done.3 = f32[16,1,2048]{2,1,0:T(1,128)S(1)} async-done(((f32[16,1,2048]{2,1,0:T(1,128)}), f32[16,1,2048]{2,1,0:T(1,128)S(1)}, u32[]{:S(2)}, u32[]{:S(2)}) %all-to-all-start.3) | async-done | bytes 131104 | tf_op jit(solution)/shard_map/all_to_all | solution.py:71
  137.9 3.7 %all-to-all-start.2 = ((f32[16,1,2048]{2,1,0:T(1,128)}), f32[16,1,2048]{2,1,0:T(1,128)S(1)}, u32[]{:S(2)}, u32[]{:S(2)}) async-start(f32[16,1,2048]{2,1,0:T(1,128)} %reshape.473), calls=%async_computation.3 | async-start | bytes 262144 | tf_op jit(solution)/shard_map/all_to_all | solution.py:70
  142.9 1.8 fusion.35
  144.7 4.9 %all-to-all-done.2 = f32[16,1,2048]{2,1,0:T(1,128)S(1)} async-done(((f32[16,1,2048]{2,1,0:T(1,128)}), f32[16,1,2048]{2,1,0:T(1,128)S(1)}, u32[]{:S(2)}, u32[]{:S(2)}) %all-to-all-start.2) | async-done | bytes 131104 | tf_op jit(solution)/shard_map/all_to_all | solution.py:70
  150.8 1.8 fusion.33
  152.7 1.8 fusion.31
  154.5 1.8 fusion.30
  159.4 3.5 %all-to-all-start.5 = ((f32[16,1,2048]{2,1,0:T(1,128)}), f32[16,1,2048]{2,1,0:T(1,128)S(1)}, u32[]{:S(2)}, u32[]{:S(2)}) async-start(f32[16,1,2048]{2,1,0:T(1,128)} %reshape.479), calls=%async_computation.6 | async-start | bytes 262144 | tf_op jit(solution)/shard_map/all_to_all | solution.py:71
  165.0 5.8 %all-to-all-done.5 = f32[16,1,2048]{2,1,0:T(1,128)S(1)} async-done(((f32[16,1,2048]{2,1,0:T(1,128)}), f32[16,1,2048]{2,1,0:T(1,128)S(1)}, u32[]{:S(2)}, u32[]{:S(2)}) %all-to-all-start.5) | async-done | bytes 131104 | tf_op jit(solution)/shard_map/all_to_all | solution.py:71
  170.8 3.7 %all-to-all-start.4 = ((f32[16,1,2048]{2,1,0:T(1,128)}), f32[16,1,2048]{2,1,0:T(1,128)S(1)}, u32[]{:S(2)}, u32[]{:S(2)}) async-start(f32[16,1,2048]{2,1,0:T(1,128)} %reshape.477), calls=%async_computation.5 | async-start | bytes 262144 | tf_op jit(solution)/shard_map/all_to_all | solution.py:70
  176.8 5.7 %all-to-all-done.4 = f32[16,1,2048]{2,1,0:T(1,128)S(1)} async-done(((f32[16,1,2048]{2,1,0:T(1,128)}), f32[16,1,2048]{2,1,0:T(1,128)S(1)}, u32[]{:S(2)}, u32[]{:S(2)}) %all-to-all-start.4) | async-done | bytes 131104 | tf_op jit(solution)/shard_map/all_to_all | solution.py:70
  184.7 1.4 fusion.57
  186.1 1.4 convolution_subtract_fusion.1
  188.9 5.1 %all-to-all-start.6 = ((f32[16,1,2048]{2,1,0:T(1,128)}), f32[16,1,2048]{2,1,0:T(1,128)S(1)}, u32[]{:S(2)}, u32[]{:S(2)}) async-start(f32[16,1,2048]{2,1,0:T(1,128)} %reshape.481), calls=%async_computation.7 | async-start | bytes 262144 | tf_op jit(solution)/shard_map/all_to_all | solution.py:63
  194.0 1.4 fusion.53
  195.4 1.4 convolution_add_fusion
  198.2 3.7 %all-to-all-done.6 = f32[16,1,2048]{2,1,0:T(1,128)S(1)} async-done(((f32[16,1,2048]{2,1,0:T(1,128)}), f32[16,1,2048]{2,1,0:T(1,128)S(1)}, u32[]{:S(2)}, u32[]{:S(2)}) %all-to-all-start.6) | async-done | bytes 131104 | tf_op jit(solution)/shard_map/all_to_all | solution.py:63
  202.0 4.5 %all-to-all-start.7 = ((f32[16,1,2048]{2,1,0:T(1,128)}), f32[16,1,2048]{2,1,0:T(1,128)S(1)}, u32[]{:S(2)}, u32[]{:S(2)}) async-start(f32[16,1,2048]{2,1,0:T(1,128)} %reshape.483), calls=%async_computation.8 | async-start | bytes 262144 | tf_op jit(solution)/shard_map/all_to_all | solution.py:64
  210.5 3.5 %all-to-all-done.7 = f32[16,1,2048]{2,1,0:T(1,128)S(1)} async-done(((f32[16,1,2048]{2,1,0:T(1,128)}), f32[16,1,2048]{2,1,0:T(1,128)S(1)}, u32[]{:S(2)}, u32[]{:S(2)}) %all-to-all-start.7) | async-done | bytes 131104 | tf_op jit(solution)/shard_map/all_to_all | solution.py:64
  215.3 1.6 copy.76
  216.9 1.6 all_to_all.135
  218.5 1.9 fusion.27
  220.5 2.3 fusion.42
  223.4 3.7 %fusion.3 = (f32[2,1,8,255,256]{4,3,2,1,0:T(8,128)}, f32[2,1,8,255,256]{4,3,2,1,0:T(8,128)}) fusion(f32[1,1,8,256,256]{4,3,2,1,0:T(8,128)S(1)} %bitcast.156, f32[1,1,8,256,256]{4,3,2,1,0:T(8,128)S(1)} %bitcast.162), kind=kLoop, calls=%fused_computation.24 | loop fusion | flops 2088960 | bytes 12550144 | tf_op jit(solution)/shard_map/stack | solution.py:131
  227.1 2.7 fusion.17
  229.9 4.2 %fusion.1 = (f32[2,1,8,256,255]{4,3,2,1,0:T(8,128)}, f32[2,1,8,256,255]{4,3,2,1,0:T(8,128)}) fusion(f32[1,1,8,256,256]{4,3,2,1,0:T(8,128)S(1)} %bitcast.158, f32[1,1,8,256,256]{4,3,2,1,0:T(8,128)S(1)} %bitcast.164), kind=kLoop, calls=%fused_computation.22 | loop fusion | flops 2088960 | bytes 12550144 | tf_op jit(solution)/shard_map/stack | solution.py:131
  234.0 53.1 %all-gather.2.cloned.1.call-done = f32[8,256,256]{2,1,0:T(8,128)} async-done(((f32[8,16,256]{2,1,0:T(8,128)}), f32[8,256,256]{2,1,0:T(8,128)}) %all-gather.2.cloned.1.call-update) | async-done | bytes 2097168 | tf_op jit(solution)/shard_map/all_gather | solution.py:139
  287.2 2.6 add.255
  290.0 9.2 %fusion.13 = f32[2,1,8,256,256]{4,3,2,1,0:T(8,128)S(1)} fusion(f32[2,1,1,256,256]{4,3,2,1,0:T(8,128)S(1)} %collective-permute-done.1, f32[1,1,8,256,256]{4,3,2,1,0:T(8,128)S(1)} %bitcast.165, f32[1,1,8,256,256]{4,3,2,1,0:T(8,128)S(1)} %bitcast.159, f32[2,1,1,256,256]{4,3,2,1,0:T(8,128)S(1)} %collective-permute-done, ...), kind=kLoop, calls=%fused_computation.37 | loop fusion | flops 19922944 | bytes 28311552 | tf_op jit(solution)/shard_map/add | solution.py:88
  299.3 2.7 fusion.201
  302.1 4.8 %fusion.200 = (f32[2,1,8,256,255]{4,3,2,1,0:T(8,128)}, f32[2,1,8,256,255]{4,3,2,1,0:T(8,128)}) fusion(f32[2,1,8,256,256]{4,3,2,1,0:T(8,128)S(1)} %fusion.13), kind=kLoop, calls=%fused_computation.250 | loop fusion | bytes 16711680 | tf_op jit(solution)/shard_map/jit(_roll_static)/slice | solution.py:83
  307.4 4.1 %fusion.198 = (f32[2,1,8,255,256]{4,3,2,1,0:T(8,128)}, f32[2,1,8,255,256]{4,3,2,1,0:T(8,128)}) fusion(f32[2,1,8,256,256]{4,3,2,1,0:T(8,128)S(1)} %fusion.13), kind=kLoop, calls=%fused_computation.248 | loop fusion | bytes 16711680 | tf_op jit(solution)/shard_map/jit(_roll_static)/slice | solution.py:84
  311.4 2.1 collective-permute-done.2
  313.6 5.5 %collective-permute-done.3 = f32[2,1,1,256,256]{4,3,2,1,0:T(8,128)S(1)} collective-permute-done((f32[2,1,1,256,256]{4,3,2,1,0:T(8,128)S(1)}, f32[2,1,1,256,256]{4,3,2,1,0:T(8,128)S(1)}, u32[]{:S(2)}, u32[]{:S(2)}) %collective-permute-start.3) | collective-permute-done | bytes 524320 | tf_op jit(solution)/shard_map/ppermute | solution.py:20
  319.1 10.6 %fusion.8 = f32[2,1,8,256,256]{4,3,2,1,0:T(8,128)} fusion(f32[2,1,8,256,256]{4,3,2,1,0:T(8,128)S(1)} %fusion.13, f32[2,1,1,256,256]{4,3,2,1,0:T(8,128)S(1)} %collective-permute-done.3, f32[2,1,1,256,256]{4,3,2,1,0:T(8,128)S(1)} %collective-permute-done.2, f32[2,1,8,256,255]{4,3,2,1,0:T(8,128)} %get-tuple-element.9, ...), kind=kLoop, calls=%fused_computation.30 | loop fusion | flops 16777216 | bytes 28311552 | tf_op jit(solution)/shard_map/add | solution.py:88
  329.7 5.1 %fusion.19 = (f32[1,8,256,256]{3,2,1,0:T(8,128)}, f32[1,8,256,256]{3,2,1,0:T(8,128)}) fusion(f32[2,1,8,256,256]{4,3,2,1,0:T(8,128)} %fusion.8, f32[1,8,256,256]{3,2,1,0:T(8,128)S(1)} %copy-done.2, f32[2,1,8,256,256]{4,3,2,1,0:T(8,128)S(1)} %fusion.13, f32[1,8,256,256]{3,2,1,0:T(8,128)S(1)} %copy-done), kind=kLoop, calls=%fused_computation.51 | loop fusion | flops 4194304 | bytes 16777216 | tf_op jit(solution)/shard_map/sub | solution.py:144
  (78 shorter events, 34.6 us)
Async XLA Ops:
  7.2 80.3 %copy-start.3 = (f32[8,16,256]{2,1,0:T(8,128)S(1)}, f32[8,16,256]{2,1,0:T(8,128)}, u32[]{:S(2)}) copy-start(f32[8,16,256]{2,1,0:T(8,128)} %param.7) | copy-start | bytes 393220
  7.2 80.3 %reduce-scatter.2.cloned.1.call-start = ((), (), s32[]{:S(2)}) async-start(), calls=%async_computation.9 | async-start | bytes 2228224 | tf_op jit(solution)/shard_map/reduce_scatter | solution.py:137
  91.2 12.8 %all-to-all-start = ((f32[16,1,2048]{2,1,0:T(1,128)}), f32[16,1,2048]{2,1,0:T(1,128)S(1)}, u32[]{:S(2)}, u32[]{:S(2)}) async-start(f32[16,1,2048]{2,1,0:T(1,128)} %reshape.469), calls=%async_computation.1 | async-start | bytes 262144 | tf_op jit(solution)/shard_map/all_to_all | solution.py:63
  104.0 12.7 %all-to-all-start.1 = ((f32[16,1,2048]{2,1,0:T(1,128)}), f32[16,1,2048]{2,1,0:T(1,128)S(1)}, u32[]{:S(2)}, u32[]{:S(2)}) async-start(f32[16,1,2048]{2,1,0:T(1,128)} %reshape.471), calls=%async_computation.2 | async-start | bytes 262144 | tf_op jit(solution)/shard_map/all_to_all | solution.py:64
  123.3 14.6 %all-to-all-start.3 = ((f32[16,1,2048]{2,1,0:T(1,128)}), f32[16,1,2048]{2,1,0:T(1,128)S(1)}, u32[]{:S(2)}, u32[]{:S(2)}) async-start(f32[16,1,2048]{2,1,0:T(1,128)} %reshape.475), calls=%async_computation.4 | async-start | bytes 262144 | tf_op jit(solution)/shard_map/all_to_all | solution.py:71
  137.9 11.7 %all-to-all-start.2 = ((f32[16,1,2048]{2,1,0:T(1,128)}), f32[16,1,2048]{2,1,0:T(1,128)S(1)}, u32[]{:S(2)}, u32[]{:S(2)}) async-start(f32[16,1,2048]{2,1,0:T(1,128)} %reshape.473), calls=%async_computation.3 | async-start | bytes 262144 | tf_op jit(solution)/shard_map/all_to_all | solution.py:70
  159.4 11.4 %all-to-all-start.5 = ((f32[16,1,2048]{2,1,0:T(1,128)}), f32[16,1,2048]{2,1,0:T(1,128)S(1)}, u32[]{:S(2)}, u32[]{:S(2)}) async-start(f32[16,1,2048]{2,1,0:T(1,128)} %reshape.479), calls=%async_computation.6 | async-start | bytes 262144 | tf_op jit(solution)/shard_map/all_to_all | solution.py:71
  170.8 11.7 %all-to-all-start.4 = ((f32[16,1,2048]{2,1,0:T(1,128)}), f32[16,1,2048]{2,1,0:T(1,128)S(1)}, u32[]{:S(2)}, u32[]{:S(2)}) async-start(f32[16,1,2048]{2,1,0:T(1,128)} %reshape.477), calls=%async_computation.5 | async-start | bytes 262144 | tf_op jit(solution)/shard_map/all_to_all | solution.py:70
  188.9 13.0 %all-to-all-start.6 = ((f32[16,1,2048]{2,1,0:T(1,128)}), f32[16,1,2048]{2,1,0:T(1,128)S(1)}, u32[]{:S(2)}, u32[]{:S(2)}) async-start(f32[16,1,2048]{2,1,0:T(1,128)} %reshape.481), calls=%async_computation.7 | async-start | bytes 262144 | tf_op jit(solution)/shard_map/all_to_all | solution.py:63
  202.0 12.0 %all-to-all-start.7 = ((f32[16,1,2048]{2,1,0:T(1,128)}), f32[16,1,2048]{2,1,0:T(1,128)S(1)}, u32[]{:S(2)}, u32[]{:S(2)}) async-start(f32[16,1,2048]{2,1,0:T(1,128)} %reshape.483), calls=%async_computation.8 | async-start | bytes 262144 | tf_op jit(solution)/shard_map/all_to_all | solution.py:64
  206.4 80.7 %all-gather.2.cloned.1.call-start = ((), (), s32[]{:S(2)}) async-start(), calls=%async_computation.10 | async-start | bytes 2228224 | tf_op jit(solution)/shard_map/all_gather | solution.py:139
  208.8 11.7 %copy-start = (f32[1,8,256,256]{3,2,1,0:T(8,128)S(1)}, f32[1,8,256,256]{3,2,1,0:T(8,128)}, u32[]{:S(2)}) copy-start(f32[1,8,256,256]{3,2,1,0:T(8,128)} %param.4) | copy-start | bytes 6291460
  220.5 2.9 copy-start.1
  222.7 67.1 %collective-permute-start = (f32[2,1,1,256,256]{4,3,2,1,0:T(8,128)}, f32[2,1,1,256,256]{4,3,2,1,0:T(8,128)S(1)}, u32[]{:S(2)}, u32[]{:S(2)}) collective-permute-start(f32[2,1,1,256,256]{4,3,2,1,0:T(8,128)} %get-tuple-element.22), channel_id=1, source_target_pairs={{1,0},{2,1},{3,2},{4,3},{5,4},{6,5},{7,6},{8,7},{9,8},{10,9},{11,1... | collective-permute-start | bytes 1572872 | tf_op jit(solution)/shard_map/ppermute | solution.py:22
  222.7 67.1 %collective-permute-start.1 = (f32[2,1,1,256,256]{4,3,2,1,0:T(8,128)}, f32[2,1,1,256,256]{4,3,2,1,0:T(8,128)S(1)}, u32[]{:S(2)}, u32[]{:S(2)}) collective-permute-start(f32[2,1,1,256,256]{4,3,2,1,0:T(8,128)} %get-tuple-element.23), channel_id=1, source_target_pairs={{0,1},{1,2},{2,3},{3,4},{4,5},{5,6},{6,7},{7,8},{8,9},{9,10},{10,1... | collective-permute-start | bytes 1572872 | tf_op jit(solution)/shard_map/ppermute | solution.py:20
  287.1 2.9 copy-start.2
  306.9 6.7 %collective-permute-start.2 = (f32[2,1,1,256,256]{4,3,2,1,0:T(8,128)S(1)}, f32[2,1,1,256,256]{4,3,2,1,0:T(8,128)S(1)}, u32[]{:S(2)}, u32[]{:S(2)}) collective-permute-start(f32[2,1,1,256,256]{4,3,2,1,0:T(8,128)S(1)} %get-tuple-element.12), channel_id=1, source_target_pairs={{1,0},{2,1},{3,2},{4,3},{5,4},{6,5},{7,6},{8,7},{9,8},{10,9},{11,1... | collective-permute-start | bytes 1572872 | tf_op jit(solution)/shard_map/ppermute | solution.py:22
  306.9 12.2 %collective-permute-start.3 = (f32[2,1,1,256,256]{4,3,2,1,0:T(8,128)S(1)}, f32[2,1,1,256,256]{4,3,2,1,0:T(8,128)S(1)}, u32[]{:S(2)}, u32[]{:S(2)}) collective-permute-start(f32[2,1,1,256,256]{4,3,2,1,0:T(8,128)S(1)} %get-tuple-element.13), channel_id=1, source_target_pairs={{0,1},{1,2},{2,3},{3,4},{4,5},{5,6},{6,7},{7,8},{8,9},{9,10},{10,1... | collective-permute-start | bytes 1572872 | tf_op jit(solution)/shard_map/ppermute | solution.py:20
Sparse Core Ops, SparseCore 0:
  11.2 76.1 reduce-scatter.1
  220.6 66.5 all-gather.1
where the time goes:
time: 347 us; the launch traced here: 342 us
  waiting for transfers between devices  173 us (50%)
  other arithmetic  51.9 us (15%)
  starting transfers between devices  38.9 us (11%)
  local copies, waits for them, and re-layouts  35.3 us (10%)
  matrix products  28 us (8%)
  between operations  14.7 us (4%)
    reduce_scatter x1, waiting for transfers between devices, on_device(): lax.psum_scatter(partial_value, 'orb', scatter_dimension=1, tiled=True)  76.1 us
    all_gather x1, waiting for transfers between devices, on_device(): full_hartree = lax.all_gather(hartree, 'orb', axis=1, tiled=True)  53.1 us
    dot_general x20, matrix products, mix(): return jnp.einsum(form, left, right, precision=HIGHEST)  28 us
    add x2, other arithmetic, kinetic_plus(): return -0.5 / (SPACING * SPACING) * laplace + potential * centre  19.8 us
    another operation x5, other arithmetic, on_device(): orbitals_now = jnp.stack([psi_re, psi_im])  12.9 us
    unnamed x24, local copies, waits for them, and re-layouts  11.4 us
    all_to_all x2, waiting for transfers between devices, across_slab(): lax.all_to_all(fields[1], 'slab', split_axis=0, concat_axis=2, tiled=True)  11 us
    all_to_all x2, waiting for transfers between devices, across_slab(): lax.all_to_all(fields[0], 'slab', split_axis=0, concat_axis=2, tiled=True)  10.6 us
  transfers between devices with their start and end apart: 14, of which 12 were waited for; matrix products, arithmetic and copies ran while one was open for 13% of the time, Pallas kernels for 0%

commit v1 on v0

v1 whole, which is shorter than its diff:
```python
import functools
import math

import jax
import jax.numpy as jnp
import numpy as np
from jax import lax
from jax.experimental import pallas as pl
from jax.experimental.pallas import tpu as pltpu
from jax.sharding import PartitionSpec as P

SPACING = 0.5
TIME_STEP = 0.02
HALF_SQ = 0.5 * TIME_STEP * TIME_STEP
KINETIC = -0.5 / (SPACING * SPACING)
HIGHEST = lax.Precision.HIGHEST
Z_RING = 8
STRIP = 32
MIB = 1 << 20


def cas_table(length):
    index = np.arange(length)
    angles = (index[:, None] * index[None, :] % length) * (2.0 * math.pi / length)
    return jnp.asarray((np.cos(angles) + np.sin(angles)).astype(np.float32))


def dot(left, right):
    return jnp.dot(left, right, precision=HIGHEST, preferred_element_type=jnp.float32)


def fill_rows(rows_ref, table_ref, offsets, width):
    place = lax.axis_index("orb")
    z = lax.rem(place, Z_RING)
    y = place // Z_RING
    half = width // 2
    for block, offset in enumerate(offsets):
        owner = lax.rem(z + offset, Z_RING)
        for part in range(2):
            side = y if part == 0 else 1 - y
            start = pl.multiple_of(owner * width + side * half, half)
            rows_ref[block * width + part * half : block * width + (part + 1) * half, :] = table_ref[
                pl.ds(start, half), :
            ]


def density_kernel(scale, psi_re, psi_im, ground, table, *rest):
    outs, (rows, rho) = rest[:-2], rest[-2:]
    width = rows.shape[0] // Z_RING
    ground_rows = ground.shape[1]

    @pl.when(pl.program_id(0) == 0)
    def _():
        fill_rows(rows, table, range(Z_RING), width)

    re, im = psi_re[0, 0], psi_im[0, 0]
    rho[...] = scale * (re * re + im * im)
    start = pl.multiple_of(lax.axis_index("orb") * ground_rows, ground_rows)
    own = pl.ds(start, ground_rows)
    rho[own, :] = rho[own, :] - ground[0]
    image = dot(rows[...], rho[...])
    at = 0
    for out in outs:
        out[0] = image[at : at + out.shape[1]]
        at += out.shape[1]


def density_pieces(psi_re, psi_im, n_ground, table, total_orbs):
    _, planes, ny, nx = psi_re.shape
    width = ny // Z_RING
    heights = [width] * 4 + [width // 2] * 2 + [width] * 3
    return pl.pallas_call(
        functools.partial(density_kernel, 2.0 / total_orbs),
        grid=(planes,),
        in_specs=[
            pl.BlockSpec((1, 1, ny, nx), lambda i: (0, i, 0, 0)),
            pl.BlockSpec((1, 1, ny, nx), lambda i: (0, i, 0, 0)),
            pl.BlockSpec((1,) + n_ground.shape[1:], lambda i: (i, 0, 0)),
            pl.BlockSpec((ny, ny), lambda i: (0, 0)),
        ],
        out_specs=[pl.BlockSpec((1, h, nx), lambda i: (i, 0, 0)) for h in heights],
        out_shape=[jax.ShapeDtypeStruct((planes, h, nx), jnp.float32) for h in heights],
        scratch_shapes=[pltpu.VMEM((ny, ny), jnp.float32), pltpu.VMEM((ny, nx), jnp.float32)],
        compiler_params=pltpu.CompilerParams(vmem_limit_bytes=16 * MIB),
        cost_estimate=pl.CostEstimate(flops=12 * planes * ny * ny * nx, bytes_accessed=6 * MIB, transcendentals=0),
        name="density_y",
    )(psi_re, psi_im, n_ground, table)


def wave_sq(freq_index, length):
    signed = jnp.where(freq_index * 2 <= length, freq_index, freq_index - length)
    wave_number = signed.astype(jnp.float32) * (2.0 * math.pi / (length * SPACING))
    return wave_number * wave_number


def solve_kernel(y_len, field, x_table, z_table, out, work):
    nz, nx = field.shape
    planes = out.shape[1] - 2
    place = lax.axis_index("orb")
    width = y_len // Z_RING
    ky = lax.rem(place, Z_RING) * width + (place // Z_RING) * (width // 2) + lax.axis_index("slab")
    z_index = lax.broadcasted_iota(jnp.int32, (nz, nx), 0)
    x_index = lax.broadcasted_iota(jnp.int32, (nz, nx), 1)
    y_index = jnp.full((nz, nx), ky, jnp.int32)
    total = wave_sq(z_index, nz) + wave_sq(y_index, y_len) + wave_sq(x_index, nx)
    anchor = (z_index == 0) & (y_index == 0) & (x_index == 0)
    safe = jnp.where(anchor, jnp.float32(1.0), total)
    greens = jnp.where(anchor, jnp.float32(0.0), (4.0 * math.pi) / safe) * (1.0 / (nz * y_len * nx))
    spectrum = dot(z_table[...], dot(field[...], x_table[...]))
    work[...] = dot(dot(z_table[...], spectrum * greens), x_table[...])
    slabs = out.shape[0]
    for slab in range(slabs):
        first = slab * planes
        out[slab, 0:planes] = work[first : first + planes]
        below = (first - 1) % nz
        above = (first + planes) % nz
        out[slab, planes : planes + 1] = work[below : below + 1]
        out[slab, planes + 1 : planes + 2] = work[above : above + 1]


def solve(field, x_table, z_table, y_len, planes):
    nz, nx = field.shape
    return pl.pallas_call(
        functools.partial(solve_kernel, y_len),
        out_shape=jax.ShapeDtypeStruct((nz // planes, planes + 2, nx), jnp.float32),
        scratch_shapes=[pltpu.VMEM((nz, nx), jnp.float32)],
        compiler_params=pltpu.CompilerParams(vmem_limit_bytes=8 * MIB),
        name="solve_xz",
    )(field, x_table, z_table)


def in_plane(ref, slot, start, rows):
    mid = ref[slot, pl.ds(start, STRIP), :]
    before = ref[slot, pl.ds(pl.multiple_of(lax.rem(start + rows - 8, rows), 8), 8), :]
    after = ref[slot, pl.ds(pl.multiple_of(lax.rem(start + STRIP, rows), 8), 8), :]
    tall = jnp.concatenate([before, mid, after], axis=0)
    height = tall.shape[0]
    columns = mid.shape[1]
    up = pltpu.roll(tall, 1, 0)[8 : 8 + STRIP]
    down = pltpu.roll(tall, height - 1, 0)[8 : 8 + STRIP]
    left = pltpu.roll(mid, 1, 1)
    right = pltpu.roll(mid, columns - 1, 1)
    return mid, (up + down) + (left + right)


def kinetic(ref, below, slot, above, start, rows):
    mid, ring = in_plane(ref, slot, start, rows)
    strip = pl.ds(start, STRIP)
    total = ring + (ref[below, strip, :] + ref[above, strip, :])
    return mid, KINETIC * (total - 6.0 * mid)


def kinetic_kernel(
    planes, psi_re, psi_im, lo_re, lo_im, hi_re, hi_im, t1_re, t1_im, base_re, base_im, field_re, field_im, once_re, once_im
):
    step = pl.program_id(0)
    rows = field_re.shape[1]
    s0, s1, s2 = lax.rem(step + 1, 3), lax.rem(step + 2, 3), lax.rem(step, 3)

    @pl.when(step < 2)
    def _():
        field_re[s2] = lo_re[0]
        field_im[s2] = lo_im[0]

    @pl.when((step >= 2) & (step < planes + 2))
    def _():
        field_re[s2] = psi_re[0, 0]
        field_im[s2] = psi_im[0, 0]

    @pl.when(step >= planes + 2)
    def _():
        field_re[s2] = hi_re[0]
        field_im[s2] = hi_im[0]

    @pl.when(step >= 2)
    def _():
        @pl.loop(0, rows // STRIP)
        def _(index):
            start = pl.multiple_of(index * STRIP, STRIP)
            for field, once in ((field_re, once_re), (field_im, once_im)):
                _, value = kinetic(field, s0, s1, s2, start, rows)
                once[s1, pl.ds(start, STRIP), :] = value

    @pl.when((step >= 3) & (step < planes + 3))
    def _():
        t1_re[0] = once_re[s1]
        t1_im[0] = once_im[s1]

    @pl.when(step >= 4)
    def _():
        @pl.loop(0, rows // STRIP)
        def _(index):
            start = pl.multiple_of(index * STRIP, STRIP)
            strip = pl.ds(start, STRIP)
            first_re, second_re = kinetic(once_re, s2, s0, s1, start, rows)
            first_im, second_im = kinetic(once_im, s2, s0, s1, start, rows)
            base_re[0, strip, :] = field_re[s0, strip, :] + TIME_STEP * first_im - HALF_SQ * second_re
            base_im[0, strip, :] = field_im[s0, strip, :] - TIME_STEP * first_re - HALF_SQ * second_im


def kinetic_parts(psi_re, psi_im, low, high):
    _, planes, ny, nx = psi_re.shape

    def clip(value, top):
        return jnp.clip(value, 0, top)

    plane = (1, ny, nx)
    own = pl.BlockSpec((1, 1, ny, nx), lambda i: (0, clip(i - 2, planes - 1), 0, 0))
    out = jax.ShapeDtypeStruct((planes, ny, nx), jnp.float32)
    return pl.pallas_call(
        functools.partial(kinetic_kernel, planes),
        grid=(planes + 4,),
        in_specs=[
            own,
            own,
            pl.BlockSpec(plane, lambda i: (clip(i, 1), 0, 0)),
            pl.BlockSpec(plane, lambda i: (2 + clip(i, 1), 0, 0)),
            pl.BlockSpec(plane, lambda i: (clip(i - planes - 2, 1), 0, 0)),
            pl.BlockSpec(plane, lambda i: (2 + clip(i - planes - 2, 1), 0, 0)),
        ],
        out_specs=[
            pl.BlockSpec(plane, lambda i: (clip(i - 3, planes - 1), 0, 0)),
            pl.BlockSpec(plane, lambda i: (clip(i - 3, planes - 1), 0, 0)),
            pl.BlockSpec(plane, lambda i: (clip(i - 4, planes - 1), 0, 0)),
            pl.BlockSpec(plane, lambda i: (clip(i - 4, planes - 1), 0, 0)),
        ],
        out_shape=[out] * 4,
        scratch_shapes=[pltpu.VMEM((3, ny, nx), jnp.float32)] * 4,
        compiler_params=pltpu.CompilerParams(vmem_limit_bytes=24 * MIB),
        cost_estimate=pl.CostEstimate(flops=100 * planes * ny * nx, bytes_accessed=14 * MIB, transcendentals=0),
        name="kinetic_parts",
    )(psi_re, psi_im, low, low, high, high)


def update_kernel(planes, blocks, *refs):
    pieces = refs[:blocks]
    (table, v_own, v_lo, v_hi, psi_re, psi_im, lo_re, lo_im, hi_re, hi_im) = refs[blocks : blocks + 10]
    (t1_re, t1_im, base_re, base_im, out_re, out_im, rows, columns, pot, w_re, w_im) = refs[blocks + 10 :]
    step = pl.program_id(0)
    ny = rows.shape[0]
    width = ny // Z_RING
    s0, s1, s2 = lax.rem(step + 1, 3), lax.rem(step + 2, 3), lax.rem(step, 3)

    @pl.when(step == 0)
    def _():
        fill_rows(rows, table, (0, 7, 6, 5, 4, 3, 2, 1), width)
        columns[...] = rows[...].T

    hat = jnp.concatenate([piece[0] for piece in pieces], axis=0)
    hartree = dot(columns[...], hat)

    def place(local, re, im):
        total = local + hartree
        pot[s2] = total
        w_re[s2] = total * re
        w_im[s2] = total * im

    @pl.when(step == 0)
    def _():
        place(v_lo[0], lo_re[0], lo_im[0])

    @pl.when((step >= 1) & (step <= planes))
    def _():
        place(v_own[0], psi_re[0, 0], psi_im[0, 0])

    @pl.when(step == planes + 1)
    def _():
        place(v_hi[0], hi_re[0], hi_im[0])

    @pl.when(step >= 2)
    def _():
        @pl.loop(0, ny // STRIP)
        def _(index):
            start = pl.multiple_of(index * STRIP, STRIP)
            strip = pl.ds(start, STRIP)
            local = pot[s1, strip, :]
            mid_re, kin_re = kinetic(w_re, s0, s1, s2, start, ny)
            mid_im, kin_im = kinetic(w_im, s0, s1, s2, start, ny)
            second_re = kin_re + local * (t1_re[0, strip, :] + mid_re)
            second_im = kin_im + local * (t1_im[0, strip, :] + mid_im)
            out_re[0, 0, strip, :] = base_re[0, strip, :] + TIME_STEP * mid_im - HALF_SQ * second_re
            out_im[0, 0, strip, :] = base_im[0, strip, :] - TIME_STEP * mid_re - HALF_SQ * second_im


def update(pieces, table, v_local, psi_re, psi_im, low, high, parts):
    _, planes, ny, nx = psi_re.shape

    def clip(value):
        return jnp.clip(value, 0, planes - 1)

    def hat_plane(i):
        return jnp.where(i == 0, planes, jnp.where(i == planes + 1, planes + 1, i - 1))

    plane = (1, ny, nx)
    own = pl.BlockSpec((1, 1, ny, nx), lambda i: (0, clip(i - 1), 0, 0))
    late = pl.BlockSpec(plane, lambda i: (clip(i - 2), 0, 0))
    out = pl.BlockSpec((1, 1, ny, nx), lambda i: (0, clip(i - 2), 0, 0))

    def fixed(which):
        return pl.BlockSpec(plane, lambda i: (which, 0, 0))

    return pl.pallas_call(
        functools.partial(update_kernel, planes, len(pieces)),
        grid=(planes + 2,),
        in_specs=[pl.BlockSpec((1,) + piece.shape[1:], lambda i: (hat_plane(i), 0, 0)) for piece in pieces]
        + [
            pl.BlockSpec((ny, ny), lambda i: (0, 0)),
            pl.BlockSpec(plane, lambda i: (clip(i - 1), 0, 0)),
            fixed(4),
            fixed(4),
            own,
            own,
            fixed(1),
            fixed(3),
            fixed(0),
            fixed(2),
            late,
            late,
            late,
            late,
        ],
        out_specs=[out, out],
        out_shape=[jax.ShapeDtypeStruct(psi_re.shape, jnp.float32)] * 2,
        scratch_shapes=[pltpu.VMEM((ny, ny), jnp.float32)] * 2 + [pltpu.VMEM((3, ny, nx), jnp.float32)] * 3,
        compiler_params=pltpu.CompilerParams(vmem_limit_bytes=24 * MIB),
        cost_estimate=pl.CostEstimate(flops=12 * (planes + 2) * ny * ny * nx, bytes_accessed=22 * MIB, transcendentals=0),
        name="update",
    )(*pieces, table, v_local, low, high, psi_re, psi_im, low, low, high, high, *parts)


def ring_pairs(shift):
    return [(y * Z_RING + z, y * Z_RING + (z + shift) % Z_RING) for y in range(2) for z in range(Z_RING)]


def forward(value):
    return lax.ppermute(value, "orb", ring_pairs(1))


def backward(value):
    return lax.ppermute(value, "orb", ring_pairs(-1))


def swap(value):
    return lax.ppermute(value, "orb", [(i, (i + Z_RING) % (2 * Z_RING)) for i in range(2 * Z_RING)])


def sum_over_orb(pieces):
    s0, s1, s2, s3, s4_first, s4_second, s5, s6, s7 = pieces
    half = s4_first.shape[1]
    got_up, got_down = forward(s4_first), backward(s4_second)
    up = jnp.concatenate([s3[:, :half] + got_up, s3[:, half:]], axis=1)
    down = jnp.concatenate([s5[:, :half], s5[:, half:] + got_down], axis=1)
    up, down = forward(up), backward(down)
    up, down = forward(up + s2), backward(down + s6)
    up, down = forward(up + s1), backward(down + s7)
    total = up + down + s0
    return total[:, :half] + swap(total[:, half:])


def gather_over_orb(block):
    half = block.shape[1]
    both = jnp.concatenate([block, swap(block)], axis=1)
    up1, down1 = forward(both), backward(both)
    up2, down2 = forward(up1), backward(down1)
    up3, down3 = forward(up2), backward(down2)
    up4, down4 = forward(up3[:, :half]), backward(down3[:, half:])
    return [both, up1, up2, up3, up4, down4, down3, down2, down1]


def on_device(psi_re, psi_im, v_local, n_ground):
    total_orbs = psi_re.shape[0] * lax.axis_size("orb")
    slabs = lax.axis_size("slab")
    planes, ny, nx = v_local.shape
    nz = planes * slabs
    y_table, x_table, z_table = cas_table(ny), cas_table(nx), cas_table(nz)

    pieces = density_pieces(psi_re, psi_im, n_ground, y_table, total_orbs)

    def edge(first, v_plane):
        return jnp.concatenate(
            [psi_re[0, first : first + 2], psi_im[0, first : first + 2], v_local[v_plane : v_plane + 1]], axis=0
        )

    low = lax.ppermute(edge(planes - 2, planes - 1), "slab", [(i, (i + 1) % slabs) for i in range(slabs)])
    high = lax.ppermute(edge(0, 0), "slab", [((i + 1) % slabs, i) for i in range(slabs)])
    parts = kinetic_parts(psi_re, psi_im, low, high)

    rows = sum_over_orb(pieces)
    pencils = lax.all_to_all(jnp.transpose(rows, (1, 0, 2)), "slab", split_axis=0, concat_axis=0, tiled=True)
    solved = solve(pencils.reshape(nz, nx), x_table, z_table, ny, planes)
    back = lax.all_to_all(solved, "slab", split_axis=0, concat_axis=0, tiled=True)
    hats = gather_over_orb(jnp.transpose(back, (1, 0, 2)))
    new_re, new_im = update(hats, y_table, v_local, psi_re, psi_im, low, high, parts)
    return new_re, new_im


def solution(mesh):
    placed = (
        P("orb", "slab", None, None),
        P("orb", "slab", None, None),
        P("slab", None, None),
        P("slab", "orb", None),
    )
    return jax.shard_map(
        on_device,
        mesh=mesh,
        in_specs=placed,
        out_specs=(P("orb", "slab", None, None), P("orb", "slab", None, None)),
        check_vma=False,
    )
```

time: 347 us -> 163 us (0.47); the launches traced: 342 us -> 162 us
  waiting for transfers between devices: 173 us -> 69.9 us
  other arithmetic: 51.9 us -> 3.01 us
  Pallas kernels: 0 us -> 35.9 us
  matrix products: 28 us -> 0 us
  local copies, waits for them, and re-layouts: 35.3 us -> 11.2 us
  between operations: 14.7 us -> 0.92 us
    reduce_scatter x1 -> x0, waiting for transfers between devices: 76.1 us -> none  [on_device(): lax.psum_scatter(partial_value, 'orb', scatter_dimension=1, tiled=True)]
    all_gather x1 -> x0, waiting for transfers between devices: 53.1 us -> none  [on_device(): full_hartree = lax.all_gather(hartree, 'orb', axis=1, tiled=True)]
    ppermute x4 -> x20, waiting for transfers between devices: 7.65 us -> 58.2 us  [the longest x8 34.8 us: backward(): return lax.ppermute(value, 'orb', ring_pairs(-1))]
    pallas_call x0 -> x4, Pallas kernels: none -> 35.9 us  [the longest x1 17 us: kinetic_parts(): pl.pallas_call(functools.partial(kinetic_kernel, planes), grid=(planes +...]
    ppermute x4 -> x20, starting transfers between devices: 1.17 us -> 30.9 us  [the longest x8 25.8 us: backward(): return lax.ppermute(value, 'orb', ring_pairs(-1))]
    dot_general x20 -> x0, matrix products: 28 us -> none  [mix(): return jnp.einsum(form, left, right, precision=HIGHEST)]
    all_to_all x8 -> x2, starting transfers between devices: 37.2 us -> 10.3 us  [the longest x1 6.14 us: on_device(): lax.all_to_all(jnp.transpose(rows, (1, 0, 2)), 'slab', split_axis=0, conc...]
    all_to_all x8 -> x2, waiting for transfers between devices: 36 us -> 11.7 us  [the longest x1 6.15 us: on_device(): lax.all_to_all(solved, 'slab', split_axis=0, concat_axis=0, tiled=True)]
  transfers between devices with their start and end apart: 14 -> 22, of which waited for: 12 -> 12; matrix products, arithmetic and copies ran while one was open for 13% -> 5% of each run, Pallas kernels for 0% -> 10%
where the time goes in v1:
time: 163 us; the launch traced here: 162 us
  waiting for transfers between devices  69.9 us (43%)
  starting transfers between devices  41.3 us (25%)
  Pallas kernels  35.9 us (22%)
  local copies, waits for them, and re-layouts  11.2 us (7%)
  other arithmetic  3.01 us (2%)
    ppermute x8, waiting for transfers between devices, backward(): return lax.ppermute(value, 'orb', ring_pairs(-1))  34.8 us
    ppermute x8, starting transfers between devices, backward(): return lax.ppermute(value, 'orb', ring_pairs(-1))  25.8 us
    ppermute x2, waiting for transfers between devices, swap(): lax.ppermute(value, 'orb', [(i, (i + Z_RING) % (2 * Z_RING)) for i in ran...  19.5 us
    pallas_call x1, Pallas kernels, kinetic_parts(): pl.pallas_call(functools.partial(kinetic_kernel, planes), grid=(planes +...  17 us
    pallas_call x1, Pallas kernels, update(): pl.pallas_call(functools.partial(update_kernel, planes, len(pieces)), gri...  13.3 us
    all_to_all x1, waiting for transfers between devices, on_device(): lax.all_to_all(solved, 'slab', split_axis=0, concat_axis=0, tiled=True)  6.15 us
    all_to_all x1, starting transfers between devices, on_device(): lax.all_to_all(jnp.transpose(rows, (1, 0, 2)), 'slab', split_axis=0, conc...  6.14 us
    all_to_all x1, waiting for transfers between devices, on_device(): lax.all_to_all(jnp.transpose(rows, (1, 0, 2)), 'slab', split_axis=0, conc...  5.51 us
  transfers between devices with their start and end apart: 22, of which 12 were waited for; matrix products, arithmetic and copies ran while one was open for 5% of the time, Pallas kernels for 10%

profile of v1, /device:TPU:8, one launch (start us, length us, event | category | flops | bytes accessed | tf_op | source)
XLA Modules:
  0.0 162.2 jit_solution(9232253735669706507)
XLA Ops:
  0.6 1.6 copy-done
  2.2 1.6 copy-done.2
  3.8 0.9 copy-done.5
  4.8 0.9 copy-done.9
  5.7 3.7 %density_y.1 = (f32[8,32,256]{2,1,0:T(8,128)S(1)}, f32[8,32,256]{2,1,0:T(8,128)S(1)}, f32[8,32,256]{2,1,0:T(8,128)S(1)}, f32[8,32,256]{2,1,0:T(8,128)S(1)}, f32[...) custom-call(f32[1,8,256,256]{3,2,1,0:T(8,128)S(1)} %copy-done, ...), custom_call_target="tpu_custom_call" | custom-call | flops 1610612736 | bytes 6291456 | tf_op jit(solution)/shard_map/density_y/pallas_call | solution.py:72
  9.4 5.9 %collective-permute-start.4 = (f32[8,16,256]{2,1,0:T(8,128)S(1)}, f32[8,16,256]{2,1,0:T(8,128)S(1)}, u32[]{:S(2)}, u32[]{:S(2)}) collective-permute-start(f32[8,16,256]{2,1,0:T(8,128)S(1)} %get-tuple-element.20), channel_id=1, source_target_pairs={{0,112},{16,0},{32,16},{48,32},{64,48},{80,64},{96,80},{112,96},{1... | collective-permute-start | bytes 393224 | tf_op jit(solution)/shard_map/ppermute | solution.py:340
  15.3 2.8 %collective-permute-done.4 = f32[8,16,256]{2,1,0:T(8,128)S(1)} collective-permute-done((f32[8,16,256]{2,1,0:T(8,128)S(1)}, f32[8,16,256]{2,1,0:T(8,128)S(1)}, u32[]{:S(2)}, u32[]{:S(2)}) %collective-permute-start.4) | collective-permute-done | bytes 131104 | tf_op jit(solution)/shard_map/ppermute | solution.py:340
  18.1 3.8 %collective-permute-start.5 = (f32[8,32,256]{2,1,0:T(8,128)S(1)}, f32[8,32,256]{2,1,0:T(8,128)S(1)}, u32[]{:S(2)}, u32[]{:S(2)}) collective-permute-start(f32[8,32,256]{2,1,0:T(8,128)S(1)} %pad_maximum_fusion.4), channel_id=1, source_target_pairs={{0,112},{16,0},{32,16},{48,32},{64,48},{80,64},{96,80},{112,96},{1... | collective-permute-start | bytes 786440 | tf_op jit(solution)/shard_map/ppermute | solution.py:340
  22.0 0.1 collective-permute-start.1
  22.1 4.5 %collective-permute-done.5 = f32[8,32,256]{2,1,0:T(8,128)S(1)} collective-permute-done((f32[8,32,256]{2,1,0:T(8,128)S(1)}, f32[8,32,256]{2,1,0:T(8,128)S(1)}, u32[]{:S(2)}, u32[]{:S(2)}) %collective-permute-start.5) | collective-permute-done | bytes 262176 | tf_op jit(solution)/shard_map/ppermute | solution.py:340
  26.6 3.8 %collective-permute-start.6 = (f32[8,32,256]{2,1,0:T(8,128)S(1)}, f32[8,32,256]{2,1,0:T(8,128)S(1)}, u32[]{:S(2)}, u32[]{:S(2)}) collective-permute-start(f32[8,32,256]{2,1,0:T(8,128)S(1)} %add.31), channel_id=1, source_target_pairs={{0,112},{16,0},{32,16},{48,32},{64,48},{80,64},{96,80},{112,96},{1... | collective-permute-start | bytes 786440 | tf_op jit(solution)/shard_map/ppermute | solution.py:340
  30.4 0.1 collective-permute-start.2
  30.5 3.8 %collective-permute-done.6 = f32[8,32,256]{2,1,0:T(8,128)S(1)} collective-permute-done((f32[8,32,256]{2,1,0:T(8,128)S(1)}, f32[8,32,256]{2,1,0:T(8,128)S(1)}, u32[]{:S(2)}, u32[]{:S(2)}) %collective-permute-start.6) | collective-permute-done | bytes 262176 | tf_op jit(solution)/shard_map/ppermute | solution.py:340
  34.3 3.8 %collective-permute-start.7 = (f32[8,32,256]{2,1,0:T(8,128)S(1)}, f32[8,32,256]{2,1,0:T(8,128)S(1)}, u32[]{:S(2)}, u32[]{:S(2)}) collective-permute-start(f32[8,32,256]{2,1,0:T(8,128)S(1)} %add.32), channel_id=1, source_target_pairs={{0,112},{16,0},{32,16},{48,32},{64,48},{80,64},{96,80},{112,96},{1... | collective-permute-start | bytes 786440 | tf_op jit(solution)/shard_map/ppermute | solution.py:340
  38.1 0.0 collective-permute-done.2
  38.2 0.1 collective-permute-start.3
  38.2 3.7 %collective-permute-done.7 = f32[8,32,256]{2,1,0:T(8,128)S(1)} collective-permute-done((f32[8,32,256]{2,1,0:T(8,128)S(1)}, f32[8,32,256]{2,1,0:T(8,128)S(1)}, u32[]{:S(2)}, u32[]{:S(2)}) %collective-permute-start.7) | collective-permute-done | bytes 262176 | tf_op jit(solution)/shard_map/ppermute | solution.py:340
  42.0 3.8 %collective-permute-done.3 = f32[8,32,256]{2,1,0:T(8,128)S(1)} collective-permute-done((f32[8,32,256]{2,1,0:T(8,128)S(1)}, f32[8,32,256]{2,1,0:T(8,128)S(1)}, u32[]{:S(2)}, u32[]{:S(2)}) %collective-permute-start.3) | collective-permute-done | bytes 262176 | tf_op jit(solution)/shard_map/ppermute | solution.py:336
  45.8 0.1 add_add_fusion
  45.9 0.5 collective-permute-start.8
  46.4 4.5 %collective-permute-done.8 = f32[8,16,256]{2,1,0:T(8,128)S(1)} collective-permute-done((f32[8,16,256]{2,1,0:T(8,128)S(1)}, f32[8,16,256]{2,1,0:T(8,128)S(1)}, u32[]{:S(2)}, u32[]{:S(2)}) %collective-permute-start.8) | collective-permute-done | bytes 131104 | tf_op jit(solution)/shard_map/ppermute | solution.py:344
  51.0 0.7 copy.11
  51.7 6.1 %all-to-all-start = ((f32[16,8,256]{2,1,0:T(8,128)}), f32[16,8,256]{2,1,0:T(8,128)S(1)}, u32[]{:S(2)}, u32[]{:S(2)}) async-start(f32[16,8,256]{2,1,0:T(8,128)} %copy.11), calls=%async_computation | async-start | bytes 262144 | tf_op jit(solution)/shard_map/all_to_all | solution.py:389
  57.9 2.4 %slice_bitcast_fusion = (f32[2,256,256]{2,1,0:T(8,128)}, f32[2,256,256]{2,1,0:T(8,128)S(1)}, f32[2,256,256]{2,1,0:T(8,128)}, f32[2,256,256]{2,1,0:T(8,128)}) fusion(f32[1,8,256,256]{3,2,1,0:T(8,128)} %refs_14_.1, f32[1,8,256,256]{3,2,1,0:T(8,128)S(1)} %copy-done.1), kind=kLoop, calls=%fused_computation.2 | loop fusion | bytes 4194304 | tf_op jit(solution)/shard_map/squeeze | solution.py:381
  60.3 5.5 %all-to-all-done = f32[16,8,256]{2,1,0:T(8,128)S(1)} async-done(((f32[16,8,256]{2,1,0:T(8,128)}), f32[16,8,256]{2,1,0:T(8,128)S(1)}, u32[]{:S(2)}, u32[]{:S(2)}) %all-to-all-start) | async-done | bytes 131104 | tf_op jit(solution)/shard_map/all_to_all | solution.py:389
  65.8 2.0 %solve_xz.1 = f32[16,10,256]{2,1,0:T(8,128)} custom-call(f32[128,256]{1,0:T(8,128)S(1)} %bitcast.14, f32[256,256]{1,0:T(8,128)S(1)} %copy-done.6, f32[128,128]{1,0:T(8,128)S(1)} %copy-done.8), custom_call_target="tpu_custom_call" | custom-call | tf_op jit(solution)/shard_map/solve_xz/pallas_call | solution.py:123
  67.8 4.2 %all-to-all-start.1 = ((f32[16,10,256]{2,1,0:T(8,128)}), f32[16,10,256]{2,1,0:T(8,128)}, u32[]{:S(2)}, u32[]{:S(2)}) async-start(f32[16,10,256]{2,1,0:T(8,128)} %solve_xz.1), calls=%async_computation.1 | async-start | bytes 524288 | tf_op jit(solution)/shard_map/all_to_all | solution.py:391
  72.0 1.8 %fusion.1 = (f32[1,256,256]{2,1,0:T(8,128)}, f32[1,256,256]{2,1,0:T(8,128)S(1)}) fusion(f32[8,256,256]{2,1,0:T(8,128)} %refs_10_.1), kind=kLoop, calls=%fused_computation.15 | loop fusion | bytes 1048576 | tf_op jit(solution)/shard_map/slice | solution.py:381
  73.9 1.2 pad_maximum_fusion
  75.0 0.2 collective-permute-start.18
  75.3 6.1 %all-to-all-done.1 = f32[16,10,256]{2,1,0:T(8,128)} async-done(((f32[16,10,256]{2,1,0:T(8,128)}), f32[16,10,256]{2,1,0:T(8,128)}, u32[]{:S(2)}, u32[]{:S(2)}) %all-to-all-start.1) | async-done | bytes 163872 | tf_op jit(solution)/shard_map/all_to_all | solution.py:391
  81.4 1.0 copy.14
  82.5 1.4 collective-permute-start.9
  83.9 1.5 pad_maximum_fusion.1
  85.4 0.1 collective-permute-start.19
  85.5 15.0 %collective-permute-done.9 = f32[10,16,256]{2,1,0:T(8,128)S(1)} collective-permute-done((f32[10,16,256]{2,1,0:T(8,128)S(1)}, f32[10,16,256]{2,1,0:T(8,128)S(1)}, u32[]{:S(2)}, u32[]{:S(2)}) %collective-permute-start.9) | collective-permute-done | bytes 163872 | tf_op jit(solution)/shard_map/ppermute | solution.py:344
  100.5 0.3 collective-permute-start.14
  100.8 2.0 %collective-permute-start.10 = (f32[10,32,256]{2,1,0:T(8,128)S(1)}, f32[10,32,256]{2,1,0:T(8,128)S(1)}, u32[]{:S(2)}, u32[]{:S(2)}) collective-permute-start(f32[10,32,256]{2,1,0:T(8,128)S(1)} %pad_maximum_fusion.2.refs_0_), channel_id=1, source_target_pairs={{0,16},{16,32},{32,48},{48,64},{64,80},{80,96},{96,112},{112,0},{1... | collective-permute-start | bytes 983048 | tf_op jit(solution)/shard_map/ppermute | solution.py:336
  102.8 7.6 %collective-permute-done.14.refs_8_ = f32[10,32,256]{2,1,0:T(8,128)S(1)} collective-permute-done((f32[10,32,256]{2,1,0:T(8,128)S(1)}, f32[10,32,256]{2,1,0:T(8,128)S(1)}, u32[]{:S(2)}, u32[]{:S(2)}) %collective-permute-start.14) | collective-permute-done | bytes 327712 | tf_op jit(solution)/shard_map/ppermute | solution.py:340
  110.4 1.5 collective-permute-start.15
  111.9 0.5 collective-permute-start.11
  112.5 6.8 %collective-permute-done.15.refs_7_ = f32[10,32,256]{2,1,0:T(8,128)S(1)} collective-permute-done((f32[10,32,256]{2,1,0:T(8,128)S(1)}, f32[10,32,256]{2,1,0:T(8,128)S(1)}, u32[]{:S(2)}, u32[]{:S(2)}) %collective-permute-start.15) | collective-permute-done | bytes 327712 | tf_op jit(solution)/shard_map/ppermute | solution.py:340
  119.2 3.0 %collective-permute-start.16 = (f32[10,32,256]{2,1,0:T(8,128)S(1)}, f32[10,32,256]{2,1,0:T(8,128)S(1)}, u32[]{:S(2)}, u32[]{:S(2)}) collective-permute-start(f32[10,32,256]{2,1,0:T(8,128)S(1)} %collective-permute-done.15.refs_7_), channel_id=1, source_target_pairs={{0,112},{16,0},{32,16},{48,32},{64,48},{80,64},{96,80},{112,96},{1... | collective-permute-start | bytes 983048 | tf_op jit(solution)/shard_map/ppermute | solution.py:340
  122.2 5.7 %collective-permute-done.16.refs_6_ = f32[10,32,256]{2,1,0:T(8,128)S(1)} collective-permute-done((f32[10,32,256]{2,1,0:T(8,128)S(1)}, f32[10,32,256]{2,1,0:T(8,128)S(1)}, u32[]{:S(2)}, u32[]{:S(2)}) %collective-permute-start.16) | collective-permute-done | bytes 327712 | tf_op jit(solution)/shard_map/ppermute | solution.py:340
  128.0 3.8 %collective-permute-start.17 = (f32[10,16,256]{2,1,0:T(8,128)S(1)}, f32[10,16,256]{2,1,0:T(8,128)S(1)}, u32[]{:S(2)}, u32[]{:S(2)}) collective-permute-start(f32[10,16,256]{2,1,0:T(8,128)S(1)} %slice.59), channel_id=1, source_target_pairs={{0,112},{16,0},{32,16},{48,32},{64,48},{80,64},{96,80},{112,96},{1... | collective-permute-start | bytes 491528 | tf_op jit(solution)/shard_map/ppermute | solution.py:340
  131.8 0.1 collective-permute-start.13
  131.9 17.0 %kinetic_parts.1 = (f32[8,256,256]{2,1,0:T(8,128)S(1)}, f32[8,256,256]{2,1,0:T(8,128)S(1)}, f32[8,256,256]{2,1,0:T(8,128)S(1)}, f32[8,256,256]{2,1,0:T(8,128)S(1)}) custom-call(f32[1,8,256,256]{3,2,1,0:T(8,128)S(1)} %copy-done.1, f32[1,8,256,256]{3,2,1,0:T(8,128)S(1)} %copy-done.3, ...), custom_call_target="tpu_custom_call" | custom-call | flops 52428800 | bytes 14680064 | tf_op jit(solution)/shard_map/kinetic_parts/pallas_call | solution.py:210
  148.9 13.3 %update.1 = (f32[1,8,256,256]{3,2,1,0:T(8,128)}, f32[1,8,256,256]{3,2,1,0:T(8,128)}) custom-call(f32[10,32,256]{2,1,0:T(8,128)S(1)} %pad_maximum_fusion.2.refs_0_, f32[10,32,256]{2,1,0:T(8,128)S(1)} %collective-permute-done.10.refs_1_, f32[10,32,256]{2,1,0:T(8,128)S(1)} %collective-permute-done.11.refs_2_, ...), custom_call_target="tpu_custom_call" | custom-call | flops 2013265920 | bytes 23068672 | tf_op jit(solution)/shard_map/update/pallas_call | solution.py:302
  (42 shorter events, 0.4 us)
Async XLA Ops:
  0.6 1.6 copy-start
  2.2 1.6 copy-start.2
  3.8 0.9 copy-start.5
  4.8 0.9 copy-start.9
  9.4 8.7 %collective-permute-start.4 = (f32[8,16,256]{2,1,0:T(8,128)S(1)}, f32[8,16,256]{2,1,0:T(8,128)S(1)}, u32[]{:S(2)}, u32[]{:S(2)}) collective-permute-start(f32[8,16,256]{2,1,0:T(8,128)S(1)} %get-tuple-element.20), channel_id=1, source_target_pairs={{0,112},{16,0},{32,16},{48,32},{64,48},{80,64},{96,80},{112,96},{1... | collective-permute-start | bytes 393224 | tf_op jit(solution)/shard_map/ppermute | solution.py:340
  15.3 6.6 %collective-permute-start = (f32[8,16,256]{2,1,0:T(8,128)S(1)}, f32[8,16,256]{2,1,0:T(8,128)S(1)}, u32[]{:S(2)}, u32[]{:S(2)}) collective-permute-start(f32[8,16,256]{2,1,0:T(8,128)S(1)} %get-tuple-element.16), channel_id=1, source_target_pairs={{0,16},{16,32},{32,48},{48,64},{64,80},{80,96},{96,112},{112,0},{1... | collective-permute-start | bytes 393224 | tf_op jit(solution)/shard_map/ppermute | solution.py:336
  18.1 8.5 %collective-permute-start.5 = (f32[8,32,256]{2,1,0:T(8,128)S(1)}, f32[8,32,256]{2,1,0:T(8,128)S(1)}, u32[]{:S(2)}, u32[]{:S(2)}) collective-permute-start(f32[8,32,256]{2,1,0:T(8,128)S(1)} %pad_maximum_fusion.4), channel_id=1, source_target_pairs={{0,112},{16,0},{32,16},{48,32},{64,48},{80,64},{96,80},{112,96},{1... | collective-permute-start | bytes 786440 | tf_op jit(solution)/shard_map/ppermute | solution.py:340
  22.0 8.4 %collective-permute-start.1 = (f32[8,32,256]{2,1,0:T(8,128)S(1)}, f32[8,32,256]{2,1,0:T(8,128)S(1)}, u32[]{:S(2)}, u32[]{:S(2)}) collective-permute-start(f32[8,32,256]{2,1,0:T(8,128)S(1)} %pad_maximum_fusion.3), channel_id=1, source_target_pairs={{0,16},{16,32},{32,48},{48,64},{64,80},{80,96},{96,112},{112,0},{1... | collective-permute-start | bytes 786440 | tf_op jit(solution)/shard_map/ppermute | solution.py:336
  26.6 7.7 %collective-permute-start.6 = (f32[8,32,256]{2,1,0:T(8,128)S(1)}, f32[8,32,256]{2,1,0:T(8,128)S(1)}, u32[]{:S(2)}, u32[]{:S(2)}) collective-permute-start(f32[8,32,256]{2,1,0:T(8,128)S(1)} %add.31), channel_id=1, source_target_pairs={{0,112},{16,0},{32,16},{48,32},{64,48},{80,64},{96,80},{112,96},{1... | collective-permute-start | bytes 786440 | tf_op jit(solution)/shard_map/ppermute | solution.py:340
  30.4 7.7 %collective-permute-start.2 = (f32[8,32,256]{2,1,0:T(8,128)S(1)}, f32[8,32,256]{2,1,0:T(8,128)S(1)}, u32[]{:S(2)}, u32[]{:S(2)}) collective-permute-start(f32[8,32,256]{2,1,0:T(8,128)S(1)} %add.28), channel_id=1, source_target_pairs={{0,16},{16,32},{32,48},{48,64},{64,80},{80,96},{96,112},{112,0},{1... | collective-permute-start | bytes 786440 | tf_op jit(solution)/shard_map/ppermute | solution.py:336
  34.3 7.7 %collective-permute-start.7 = (f32[8,32,256]{2,1,0:T(8,128)S(1)}, f32[8,32,256]{2,1,0:T(8,128)S(1)}, u32[]{:S(2)}, u32[]{:S(2)}) collective-permute-start(f32[8,32,256]{2,1,0:T(8,128)S(1)} %add.32), channel_id=1, source_target_pairs={{0,112},{16,0},{32,16},{48,32},{64,48},{80,64},{96,80},{112,96},{1... | collective-permute-start | bytes 786440 | tf_op jit(solution)/shard_map/ppermute | solution.py:340
  38.1 19.7 %copy-start.1 = (f32[1,8,256,256]{3,2,1,0:T(8,128)S(1)}, f32[1,8,256,256]{3,2,1,0:T(8,128)}, u32[]{:S(2)}) copy-start(f32[1,8,256,256]{3,2,1,0:T(8,128)} %refs_13_.1) | copy-start | bytes 6291460
  38.2 7.7 %collective-permute-start.3 = (f32[8,32,256]{2,1,0:T(8,128)S(1)}, f32[8,32,256]{2,1,0:T(8,128)S(1)}, u32[]{:S(2)}, u32[]{:S(2)}) collective-permute-start(f32[8,32,256]{2,1,0:T(8,128)S(1)} %add.29), channel_id=1, source_target_pairs={{0,16},{16,32},{32,48},{48,64},{64,80},{80,96},{96,112},{112,0},{1... | collective-permute-start | bytes 786440 | tf_op jit(solution)/shard_map/ppermute | solution.py:336
  45.9 5.1 %collective-permute-start.8 = (f32[8,16,256]{2,1,0:T(8,128)S(1)}, f32[8,16,256]{2,1,0:T(8,128)S(1)}, u32[]{:S(2)}, u32[]{:S(2)}) collective-permute-start(f32[8,16,256]{2,1,0:T(8,128)S(1)} %slice.57), channel_id=1, source_target_pairs={{0,128},{16,144},{32,160},{48,176},{64,192},{80,208},{96,224},{112... | collective-permute-start | bytes 393224 | tf_op jit(solution)/shard_map/ppermute | solution.py:344
  51.7 14.1 %all-to-all-start = ((f32[16,8,256]{2,1,0:T(8,128)}), f32[16,8,256]{2,1,0:T(8,128)S(1)}, u32[]{:S(2)}, u32[]{:S(2)}) async-start(f32[16,8,256]{2,1,0:T(8,128)} %copy.11), calls=%async_computation | async-start | bytes 262144 | tf_op jit(solution)/shard_map/all_to_all | solution.py:389
  57.9 8.0 %copy-start.6 = (f32[256,256]{1,0:T(8,128)S(1)}, f32[256,256]{1,0:T(8,128)}, u32[]{:S(2)}) copy-start(f32[256,256]{1,0:T(8,128)} %constant.4.clone.table.x_table.refs_9_) | copy-start | bytes 786436
  57.9 7.9 %copy-start.8 = (f32[128,128]{1,0:T(8,128)S(1)}, f32[128,128]{1,0:T(8,128)}, u32[]{:S(2)}) copy-start(f32[128,128]{1,0:T(8,128)} %constant.5.clone.z_table) | copy-start | bytes 196612
  67.8 13.6 %all-to-all-start.1 = ((f32[16,10,256]{2,1,0:T(8,128)}), f32[16,10,256]{2,1,0:T(8,128)}, u32[]{:S(2)}, u32[]{:S(2)}) async-start(f32[16,10,256]{2,1,0:T(8,128)} %solve_xz.1), calls=%async_computation.1 | async-start | bytes 524288 | tf_op jit(solution)/shard_map/all_to_all | solution.py:391
  72.0 1.9 %copy-start.10 = (f32[2,256,256]{2,1,0:T(8,128)S(1)}, f32[2,256,256]{2,1,0:T(8,128)}, u32[]{:S(2)}) copy-start(f32[2,256,256]{2,1,0:T(8,128)} %get-tuple-element.38) | copy-start | bytes 1572868
  75.0 56.8 %collective-permute-start.18 = (f32[5,256,256]{2,1,0:T(8,128)}, f32[5,256,256]{2,1,0:T(8,128)S(1)}, u32[]{:S(2)}, u32[]{:S(2)}) collective-permute-start(f32[5,256,256]{2,1,0:T(8,128)} %pad_maximum_fusion), channel_id=1, source_target_pairs={{0,1},{1,2},{2,3},{3,4},{4,5},{5,6},{6,7},{7,8},{8,9},{9,10},{10,1... | collective-permute-start | bytes 3932168 | tf_op jit(solution)/shard_map/ppermute | solution.py:384
  82.5 18.0 %collective-permute-start.9 = (f32[10,16,256]{2,1,0:T(8,128)S(1)}, f32[10,16,256]{2,1,0:T(8,128)S(1)}, u32[]{:S(2)}, u32[]{:S(2)}) collective-permute-start(f32[10,16,256]{2,1,0:T(8,128)S(1)} %bitcast.15), channel_id=1, source_target_pairs={{0,128},{16,144},{32,160},{48,176},{64,192},{80,208},{96,224},{112... | collective-permute-start | bytes 491528 | tf_op jit(solution)/shard_map/ppermute | solution.py:344
  83.9 48.0 %copy-start.3 = (f32[1,8,256,256]{3,2,1,0:T(8,128)S(1)}, f32[1,8,256,256]{3,2,1,0:T(8,128)}, u32[]{:S(2)}) copy-start(f32[1,8,256,256]{3,2,1,0:T(8,128)} %refs_14_.1) | copy-start | bytes 6291460
  85.4 46.5 %collective-permute-start.19 = (f32[5,256,256]{2,1,0:T(8,128)S(1)}, f32[5,256,256]{2,1,0:T(8,128)S(1)}, u32[]{:S(2)}, u32[]{:S(2)}) collective-permute-start(f32[5,256,256]{2,1,0:T(8,128)S(1)} %pad_maximum_fusion.1), channel_id=1, source_target_pairs={{1,0},{2,1},{3,2},{4,3},{5,4},{6,5},{7,6},{8,7},{9,8},{10,9},{11,1... | collective-permute-start | bytes 3932168 | tf_op jit(solution)/shard_map/ppermute | solution.py:385
  100.5 9.9 %collective-permute-start.14 = (f32[10,32,256]{2,1,0:T(8,128)S(1)}, f32[10,32,256]{2,1,0:T(8,128)S(1)}, u32[]{:S(2)}, u32[]{:S(2)}) collective-permute-start(f32[10,32,256]{2,1,0:T(8,128)S(1)} %pad_maximum_fusion.2.refs_0_), channel_id=1, source_target_pairs={{0,112},{16,0},{32,16},{48,32},{64,48},{80,64},{96,80},{112,96},{1... | collective-permute-start | bytes 983048 | tf_op jit(solution)/shard_map/ppermute | solution.py:340
  100.8 11.1 %collective-permute-start.10 = (f32[10,32,256]{2,1,0:T(8,128)S(1)}, f32[10,32,256]{2,1,0:T(8,128)S(1)}, u32[]{:S(2)}, u32[]{:S(2)}) collective-permute-start(f32[10,32,256]{2,1,0:T(8,128)S(1)} %pad_maximum_fusion.2.refs_0_), channel_id=1, source_target_pairs={{0,16},{16,32},{32,48},{48,64},{64,80},{80,96},{96,112},{112,0},{1... | collective-permute-start | bytes 983048 | tf_op jit(solution)/shard_map/ppermute | solution.py:336
  110.4 8.8 %collective-permute-start.15 = (f32[10,32,256]{2,1,0:T(8,128)S(1)}, f32[10,32,256]{2,1,0:T(8,128)S(1)}, u32[]{:S(2)}, u32[]{:S(2)}) collective-permute-start(f32[10,32,256]{2,1,0:T(8,128)S(1)} %collective-permute-done.14.refs_8_), channel_id=1, source_target_pairs={{0,112},{16,0},{32,16},{48,32},{64,48},{80,64},{96,80},{112,96},{1... | collective-permute-start | bytes 983048 | tf_op jit(solution)/shard_map/ppermute | solution.py:340
  111.9 10.3 %collective-permute-start.11 = (f32[10,32,256]{2,1,0:T(8,128)S(1)}, f32[10,32,256]{2,1,0:T(8,128)S(1)}, u32[]{:S(2)}, u32[]{:S(2)}) collective-permute-start(f32[10,32,256]{2,1,0:T(8,128)S(1)} %collective-permute-done.10.refs_1_), channel_id=1, source_target_pairs={{0,16},{16,32},{32,48},{48,64},{64,80},{80,96},{96,112},{112,0},{1... | collective-permute-start | bytes 983048 | tf_op jit(solution)/shard_map/ppermute | solution.py:336
  119.2 8.7 %collective-permute-start.16 = (f32[10,32,256]{2,1,0:T(8,128)S(1)}, f32[10,32,256]{2,1,0:T(8,128)S(1)}, u32[]{:S(2)}, u32[]{:S(2)}) collective-permute-start(f32[10,32,256]{2,1,0:T(8,128)S(1)} %collective-permute-done.15.refs_7_), channel_id=1, source_target_pairs={{0,112},{16,0},{32,16},{48,32},{64,48},{80,64},{96,80},{112,96},{1... | collective-permute-start | bytes 983048 | tf_op jit(solution)/shard_map/ppermute | solution.py:340
  122.2 9.5 %collective-permute-start.12 = (f32[10,32,256]{2,1,0:T(8,128)S(1)}, f32[10,32,256]{2,1,0:T(8,128)S(1)}, u32[]{:S(2)}, u32[]{:S(2)}) collective-permute-start(f32[10,32,256]{2,1,0:T(8,128)S(1)} %collective-permute-done.11.refs_2_), channel_id=1, source_target_pairs={{0,16},{16,32},{32,48},{48,64},{64,80},{80,96},{96,112},{112,0},{1... | collective-permute-start | bytes 983048 | tf_op jit(solution)/shard_map/ppermute | solution.py:336
  128.0 20.9 %collective-permute-start.17 = (f32[10,16,256]{2,1,0:T(8,128)S(1)}, f32[10,16,256]{2,1,0:T(8,128)S(1)}, u32[]{:S(2)}, u32[]{:S(2)}) collective-permute-start(f32[10,16,256]{2,1,0:T(8,128)S(1)} %slice.59), channel_id=1, source_target_pairs={{0,112},{16,0},{32,16},{48,32},{64,48},{80,64},{96,80},{112,96},{1... | collective-permute-start | bytes 491528 | tf_op jit(solution)/shard_map/ppermute | solution.py:340
  131.7 17.1 %copy-start.7 = (f32[256,256]{1,0:T(8,128)S(1)}, f32[256,256]{1,0:T(8,128)}, u32[]{:S(2)}) copy-start(f32[256,256]{1,0:T(8,128)} %constant.4.clone.table.x_table.refs_9_) | copy-start | bytes 786436
  131.8 17.1 %collective-permute-start.13 = (f32[10,16,256]{2,1,0:T(8,128)S(1)}, f32[10,16,256]{2,1,0:T(8,128)S(1)}, u32[]{:S(2)}, u32[]{:S(2)}) collective-permute-start(f32[10,16,256]{2,1,0:T(8,128)S(1)} %slice.58), channel_id=1, source_target_pairs={{0,16},{16,32},{32,48},{48,64},{64,80},{80,96},{96,112},{112,0},{1... | collective-permute-start | bytes 491528 | tf_op jit(solution)/shard_map/ppermute | solution.py:336
  131.9 17.0 %copy-start.4 = (f32[8,256,256]{2,1,0:T(8,128)S(1)}, f32[8,256,256]{2,1,0:T(8,128)}, u32[]{:S(2)}) copy-start(f32[8,256,256]{2,1,0:T(8,128)} %refs_10_.1) | copy-start | bytes 6291460

commit v2 on v0

v2 whole, which is shorter than its diff:
```python
import functools
import math

import jax
import jax.numpy as jnp
import numpy as np
from jax import lax
from jax.experimental import pallas as pl
from jax.experimental.pallas import tpu as pltpu
from jax.sharding import Mesh
from jax.sharding import PartitionSpec as P

SPACING = 0.5
TIME_STEP = 0.02
HALF_SQ = 0.5 * TIME_STEP * TIME_STEP
KINETIC = -0.5 / (SPACING * SPACING)
HIGHEST = lax.Precision.HIGHEST
SIDES = 2
STRIP = 32
MIB = 1 << 20
VMEM = pl.BlockSpec(memory_space=pltpu.VMEM)
ANY = pl.BlockSpec(memory_space=pl.ANY)


def cas_table(length):
    index = np.arange(length)
    angles = (index[:, None] * index[None, :] % length) * (2.0 * math.pi / length)
    return jnp.asarray((np.cos(angles) + np.sin(angles)).astype(np.float32))


def dot(left, right):
    return jnp.dot(left, right, precision=HIGHEST, preferred_element_type=jnp.float32)


def shaped(*shape):
    return jax.ShapeDtypeStruct(shape, jnp.float32)


def plane_scratch(*lead, ny, nx):
    return pltpu.VMEM(lead + (ny, nx), jnp.float32)


def cost(planes, weight):
    return pl.CostEstimate(flops=planes * weight, bytes_accessed=planes * MIB // 2, transcendentals=0)


def fill_rows(rows, table):
    ring = lax.axis_size("z")
    width = rows.shape[0] // ring
    z = lax.axis_index("z")
    for offset in range(ring):
        start = pl.multiple_of(lax.rem(z + offset, ring) * width, width)
        rows[offset * width : (offset + 1) * width, :] = table[pl.ds(start, width), :]


def density_kernel(scale, psi_re, psi_im, v_local, ground, y_table, *refs):
    pieces, (near_re, near_im, to_prev, to_next) = refs[:9], refs[9:13]
    table, own_ground, rows, rho, plane_sem, edge_sem, small_sem = refs[13:]
    planes, ny, nx = near_re.shape
    copies = []
    small = [
        pltpu.make_async_copy(y_table, table, small_sem.at[0]),
        pltpu.make_async_copy(ground, own_ground, small_sem.at[1]),
    ]
    for copy in small:
        copy.start()
    for z in range(planes):
        pair = [
            pltpu.make_async_copy(psi_re.at[0, z], near_re.at[z], plane_sem.at[0, z]),
            pltpu.make_async_copy(psi_im.at[0, z], near_im.at[z], plane_sem.at[1, z]),
        ]
        for copy in pair:
            copy.start()
        copies.append(pair)
    edges = []
    for which, (target, first, v_plane) in enumerate(((to_prev, 0, 0), (to_next, planes - 2, planes - 1))):
        edges += [
            pltpu.make_async_copy(psi_re.at[0, pl.ds(first, 2)], target.at[pl.ds(0, 2)], edge_sem.at[which, 0]),
            pltpu.make_async_copy(psi_im.at[0, pl.ds(first, 2)], target.at[pl.ds(2, 2)], edge_sem.at[which, 1]),
            pltpu.make_async_copy(v_local.at[pl.ds(v_plane, 1)], target.at[pl.ds(4, 1)], edge_sem.at[which, 2]),
        ]
    for copy in edges:
        copy.start()
    for copy in small:
        copy.wait()
    fill_rows(rows, table)
    ground_rows = own_ground.shape[1]
    place = lax.axis_index("y") * lax.axis_size("z") + lax.axis_index("z")
    own = pl.ds(pl.multiple_of(place * ground_rows, ground_rows), ground_rows)
    for z in range(planes):
        for copy in copies[z]:
            copy.wait()
        re, im = near_re[z], near_im[z]
        rho[...] = scale * (re * re + im * im)
        rho[own, :] = rho[own, :] - own_ground[z]
        image = dot(rows[...], rho[...])
        at = 0
        for piece in pieces:
            piece[:, z, :] = image[at : at + piece.shape[0]]
            at += piece.shape[0]
    for copy in edges:
        copy.wait()


def density(psi_re, psi_im, v_local, n_ground, y_table, total_orbs):
    planes, ny, nx = v_local.shape
    width = ny // lax.axis_size("z")
    heights = [width] * 4 + [width // 2] * 2 + [width] * 3
    outs = [shaped(h, planes, nx) for h in heights] + [shaped(planes, ny, nx)] * 2 + [shaped(5, ny, nx)] * 2
    far = [pltpu.with_memory_space_constraint(a, pltpu.HBM) for a in (psi_re, psi_im, v_local, n_ground, y_table)]
    result = pl.pallas_call(
        functools.partial(density_kernel, 2.0 / total_orbs),
        in_specs=[ANY] * 5,
        out_specs=[VMEM] * len(outs),
        out_shape=outs,
        scratch_shapes=[
            pltpu.VMEM((ny, ny), jnp.float32),
            pltpu.VMEM(n_ground.shape, jnp.float32),
            pltpu.VMEM((ny, ny), jnp.float32),
            pltpu.VMEM((ny, nx), jnp.float32),
            pltpu.SemaphoreType.DMA((2, planes)),
            pltpu.SemaphoreType.DMA((2, 3)),
            pltpu.SemaphoreType.DMA((2,)),
        ],
        compiler_params=pltpu.CompilerParams(vmem_limit_bytes=24 * MIB),
        name="density_y",
    )(*far)
    return result[:9], result[9], result[10], result[11], result[12]


def wave_sq(freq_index, length):
    signed = jnp.where(freq_index * 2 <= length, freq_index, freq_index - length)
    wave_number = signed.astype(jnp.float32) * (2.0 * math.pi / (length * SPACING))
    return wave_number * wave_number


def solve_kernel(y_len, field, x_table, z_table, out):
    nz, nx = z_table.shape[0], x_table.shape[0]
    half = out.shape[0] // SIDES
    width = y_len // lax.axis_size("z")
    ky = lax.axis_index("z") * width + lax.axis_index("y") * lax.axis_size("slab") + lax.axis_index("slab")
    z_index = lax.broadcasted_iota(jnp.int32, (nz, nx), 0)
    x_index = lax.broadcasted_iota(jnp.int32, (nz, nx), 1)
    y_index = jnp.full((nz, nx), ky, jnp.int32)
    total = wave_sq(z_index, nz) + wave_sq(y_index, y_len) + wave_sq(x_index, nx)
    anchor = (z_index == 0) & (y_index == 0) & (x_index == 0)
    safe = jnp.where(anchor, jnp.float32(1.0), total)
    greens = jnp.where(anchor, jnp.float32(0.0), (4.0 * math.pi) / safe) * (1.0 / (nz * y_len * nx))
    rho = field[0:nz] + field[nz : 2 * nz]
    spectrum = dot(z_table[...], dot(rho, x_table[...]))
    solved = dot(dot(z_table[...], spectrum * greens), x_table[...])
    solved = solved.reshape((half,) + out.shape[1:])
    out[0:half] = solved
    out[half:] = solved


def solve(field, x_table, z_table, y_len, planes):
    rows, nx = field.shape
    return pl.pallas_call(
        functools.partial(solve_kernel, y_len),
        in_specs=[VMEM] * 3,
        out_specs=VMEM,
        out_shape=shaped(rows // planes, planes, nx),
        compiler_params=pltpu.CompilerParams(vmem_limit_bytes=8 * MIB),
        name="solve_xz",
    )(field, x_table, z_table)


def strip_of(plane, start, rows):
    ref, lead = plane
    return ref[lead + (pl.ds(start, rows), slice(None))]


def kinetic(below, plane, above, start):
    ny = plane[0].shape[-2]
    mid = strip_of(plane, start, STRIP)
    before = strip_of(plane, pl.multiple_of(lax.rem(start + ny - 8, ny), 8), 8)
    after = strip_of(plane, pl.multiple_of(lax.rem(start + STRIP, ny), 8), 8)
    tall = jnp.concatenate([before, mid, after], axis=0)
    up = pltpu.roll(tall, 1, 0)[8 : 8 + STRIP]
    down = pltpu.roll(tall, tall.shape[0] - 1, 0)[8 : 8 + STRIP]
    left = pltpu.roll(mid, 1, 1)
    right = pltpu.roll(mid, mid.shape[1] - 1, 1)
    along = strip_of(below, start, STRIP) + strip_of(above, start, STRIP)
    return mid, KINETIC * ((up + down) + (left + right) + along - 6.0 * mid)


def each_strip(ny, body):
    @pl.loop(0, ny // STRIP)
    def _(index):
        body(pl.multiple_of(index * STRIP, STRIP))


def psi_plane(fields, low, high, planes, part, z):
    if z < 0:
        return (low, (2 * part + z + 2,))
    if z >= planes:
        return (high, (2 * part + z - planes,))
    return (fields[part], (z,))


def once_kernel(planes, wanted, with_edges, *refs):
    refs = list(refs)
    fields = [refs.pop(0), refs.pop(0)]
    low, high = (refs.pop(0), refs.pop(0)) if with_edges else (None, None)
    out = refs.pop(0)
    ny = out.shape[-2]
    at = functools.partial(psi_plane, fields, low, high, planes)
    for slot, z in enumerate(wanted):

        def body(start):
            for part in range(2):
                _, value = kinetic(at(part, z - 1), at(part, z), at(part, z + 1), start)
                out[part, slot, pl.ds(start, STRIP), :] = value

        each_strip(ny, body)


def once(near, edges, wanted, name):
    planes, ny, nx = near[0].shape
    return pl.pallas_call(
        functools.partial(once_kernel, planes, wanted, bool(edges)),
        in_specs=[VMEM] * (2 + len(edges)),
        out_specs=VMEM,
        out_shape=shaped(2, len(wanted), ny, nx),
        compiler_params=pltpu.CompilerParams(vmem_limit_bytes=16 * MIB),
        cost_estimate=cost(len(wanted), 100 * ny * nx),
        name=name,
    )(*near, *edges)


def once_plane(groups, refs, part, z):
    for ref, group in zip(refs, groups):
        if z in group:
            return (ref, (part, group.index(z)))


def base_kernel(groups, wanted, re, im, *refs):
    onces, out = refs[:-1], refs[-1]
    ny = out.shape[-2]
    at = functools.partial(once_plane, groups, onces)
    for slot, z in enumerate(wanted):

        def body(start):
            strip = pl.ds(start, STRIP)
            first_re, second_re = kinetic(at(0, z - 1), at(0, z), at(0, z + 1), start)
            first_im, second_im = kinetic(at(1, z - 1), at(1, z), at(1, z + 1), start)
            out[0, slot, strip, :] = re[z, strip, :] + TIME_STEP * first_im - HALF_SQ * second_re
            out[1, slot, strip, :] = im[z, strip, :] - TIME_STEP * first_re - HALF_SQ * second_im

        each_strip(ny, body)


def base(near, onces, groups, wanted, name):
    planes, ny, nx = near[0].shape
    return pl.pallas_call(
        functools.partial(base_kernel, groups, wanted),
        in_specs=[VMEM] * (2 + len(onces)),
        out_specs=VMEM,
        out_shape=shaped(2, len(wanted), ny, nx),
        compiler_params=pltpu.CompilerParams(vmem_limit_bytes=16 * MIB),
        cost_estimate=cost(len(wanted), 100 * ny * nx),
        name=name,
    )(*near, *onces)


def columns_kernel(table, out, rows):
    fill_rows(rows, table)
    out[...] = rows[...].T


def ring_columns(y_table):
    return pl.pallas_call(
        columns_kernel,
        in_specs=[VMEM],
        out_specs=VMEM,
        out_shape=shaped(*y_table.shape),
        scratch_shapes=[pltpu.VMEM(y_table.shape, jnp.float32)],
        name="ring_columns",
    )(y_table)


def potential_plane(v_local, columns, hats, z):
    hat = jnp.concatenate([h[:, z, :] for h in hats], axis=0)
    return v_local[z] + dot(columns[...], hat)


def outer_kernel(v_local, columns, *refs):
    hats, (first, last) = refs[:-2], refs[-2:]
    first[0] = potential_plane(v_local, columns, hats, 0)
    last[0] = potential_plane(v_local, columns, hats, v_local.shape[0] - 1)


def outer_potential(v_local, columns, hats):
    planes, ny, nx = v_local.shape
    return pl.pallas_call(
        outer_kernel,
        in_specs=[VMEM] * (2 + len(hats)),
        out_specs=[VMEM] * 2,
        out_shape=[shaped(1, ny, nx)] * 2,
        compiler_params=pltpu.CompilerParams(vmem_limit_bytes=16 * MIB),
        name="outer_potential",
    )(v_local, columns, *hats)


def update_strip(at_w, at_once, at_base, local, stage, slot, z, start):
    strip = pl.ds(start, STRIP)
    here = strip_of(local, start, STRIP)
    mid_re, kin_re = kinetic(at_w(0, z - 1), at_w(0, z), at_w(0, z + 1), start)
    mid_im, kin_im = kinetic(at_w(1, z - 1), at_w(1, z), at_w(1, z + 1), start)
    second_re = kin_re + here * (strip_of(at_once(0, z), start, STRIP) + mid_re)
    second_im = kin_im + here * (strip_of(at_once(1, z), start, STRIP) + mid_im)
    stage[0, slot, strip, :] = strip_of(at_base(0, z), start, STRIP) + TIME_STEP * mid_im - HALF_SQ * second_re
    stage[1, slot, strip, :] = strip_of(at_base(1, z), start, STRIP) - TIME_STEP * mid_re - HALF_SQ * second_im


def inner_kernel(once_groups, base_groups, hat_count, *refs):
    refs = list(refs)
    v_local, columns, v_first, v_last, re, im = [refs.pop(0) for _ in range(6)]
    hats = [refs.pop(0) for _ in range(hat_count)]
    onces = [refs.pop(0) for _ in once_groups]
    bases = [refs.pop(0) for _ in base_groups]
    out_re, out_im, v_kept, pot, work, stage, sem = refs
    planes, ny, _ = re.shape
    fields = (re, im)

    def at_w(part, z):
        return (work, (part, z))

    copies = []
    for z in range(planes):
        if z == 0:
            here = v_first[0]
        elif z == planes - 1:
            here = v_last[0]
        else:
            here = potential_plane(v_local, columns, hats, z)
            pot[z] = here
        for part in range(2):
            work[part, z] = here * fields[part][z]
        if z >= 2:
            done = z - 1
            each_strip(
                ny,
                lambda start: update_strip(
                    at_w,
                    functools.partial(once_plane, once_groups, onces),
                    functools.partial(once_plane, base_groups, bases),
                    (pot, (done,)),
                    stage,
                    done - 1,
                    done,
                    start,
                ),
            )
            for part, out in enumerate((out_re, out_im)):
                copy = pltpu.make_async_copy(stage.at[part, done - 1], out.at[0, done], sem.at[part, done - 1])
                copy.start()
                copies.append(copy)
    v_kept[0] = pot[1]
    v_kept[1] = pot[planes - 2]
    for copy in copies:
        copy.wait()


def inner_update(v_local, columns, v_first, v_last, near, hats, onces, once_groups, bases, base_groups):
    planes, ny, nx = v_local.shape
    operands = [v_local, columns, v_first, v_last, *near, *hats, *onces, *bases]
    full = shaped(1, planes, ny, nx)
    return pl.pallas_call(
        functools.partial(inner_kernel, once_groups, base_groups, len(hats)),
        in_specs=[VMEM] * len(operands),
        out_specs=[ANY, ANY, VMEM],
        out_shape=[full, full, shaped(2, ny, nx)],
        scratch_shapes=[
            plane_scratch(planes, ny=ny, nx=nx),
            plane_scratch(2, planes, ny=ny, nx=nx),
            plane_scratch(2, planes - 2, ny=ny, nx=nx),
            pltpu.SemaphoreType.DMA((2, planes - 2)),
        ],
        compiler_params=pltpu.CompilerParams(vmem_limit_bytes=44 * MIB),
        cost_estimate=cost(planes, 400 * ny * nx),
        name="inner_update",
    )(*operands)


def outer_kernel_update(once_groups, base_groups, *refs):
    refs = list(refs)
    v_first, v_last, v_before, v_after, v_kept, re, im, low, high = [refs.pop(0) for _ in range(9)]
    onces = [refs.pop(0) for _ in once_groups]
    bases = [refs.pop(0) for _ in base_groups]
    _, _, out_re, out_im, work, stage, sem = refs
    planes, ny, _ = re.shape
    at_psi = functools.partial(psi_plane, (re, im), low, high, planes)
    locals_of = {
        -1: (v_before, (0,)),
        0: (v_first, (0,)),
        1: (v_kept, (0,)),
        planes - 2: (v_kept, (1,)),
        planes - 1: (v_last, (0,)),
        planes: (v_after, (0,)),
    }
    order = list(locals_of)

    def at_w(part, z):
        return (work, (part, order.index(z)))

    copies = []
    for slot, z in enumerate((0, planes - 1)):
        for near in (z - 1, z, z + 1):
            ref, lead = locals_of[near]
            here = ref[lead]
            for part in range(2):
                source, where = at_psi(part, near)
                work[part, order.index(near)] = here * source[where]
        each_strip(
            ny,
            lambda start: update_strip(
                at_w,
                functools.partial(once_plane, once_groups, onces),
                functools.partial(once_plane, base_groups, bases),
                locals_of[z],
                stage,
                slot,
                z,
                start,
            ),
        )
        for part, out in enumerate((out_re, out_im)):
            copy = pltpu.make_async_copy(stage.at[part, slot], out.at[0, z], sem.at[part, slot])
            copy.start()
            copies.append(copy)
    for copy in copies:
        copy.wait()


def outer_update(new_re, new_im, v_planes, near, edges, onces, once_groups, bases, base_groups):
    planes, ny, nx = near[0].shape
    operands = [*v_planes, *near, *edges, *onces, *bases]
    return pl.pallas_call(
        functools.partial(outer_kernel_update, once_groups, base_groups),
        in_specs=[VMEM] * len(operands) + [ANY, ANY],
        out_specs=[ANY, ANY],
        out_shape=[shaped(*new_re.shape)] * 2,
        input_output_aliases={len(operands): 0, len(operands) + 1: 1},
        scratch_shapes=[
            plane_scratch(2, 6, ny=ny, nx=nx),
            plane_scratch(2, 2, ny=ny, nx=nx),
            pltpu.SemaphoreType.DMA((2, 2)),
        ],
        compiler_params=pltpu.CompilerParams(vmem_limit_bytes=32 * MIB),
        name="outer_update",
    )(*operands, new_re, new_im)


def ring(axis, shift):
    count = lax.axis_size(axis)
    return [(i, (i + shift) % count) for i in range(count)]


def forward(value, axis="z"):
    return lax.ppermute(value, axis, ring(axis, 1))


def backward(value, axis="z"):
    return lax.ppermute(value, axis, ring(axis, -1))


def slab_shift(value, shift):
    return lax.ppermute(value, "slab", ring("slab", shift))


def sum_over_ring(pieces):
    s0, s1, s2, s3, s4_first, s4_second, s5, s6, s7 = pieces
    half = s4_first.shape[0]
    got_up, got_down = forward(s4_first), backward(s4_second)
    up = jnp.concatenate([s3[:half] + got_up, s3[half:]], axis=0)
    down = jnp.concatenate([s5[:half], s5[half:] + got_down], axis=0)
    up, down = forward(up), backward(down)
    up, down = forward(up + s2), backward(down + s6)
    up, down = forward(up + s1), backward(down + s7)
    return up + down + s0


def gather_over_ring(block):
    half = block.shape[0] // 2
    up1, down1 = forward(block), backward(block)
    up2, down2 = forward(up1), backward(down1)
    up3, down3 = forward(up2), backward(down2)
    up4, down4 = forward(up3[:half]), backward(down3[half:])
    return [block, down1, down2, down3, up4, down4, up3, up2, up1]


def across(value):
    return lax.all_to_all(value, ("y", "slab"), split_axis=0, concat_axis=0, tiled=True)


def on_device(psi_re, psi_im, v_local, n_ground):
    total_orbs = psi_re.shape[0] * lax.axis_size("y") * lax.axis_size("z")
    planes, ny, nx = v_local.shape
    nz = planes * lax.axis_size("slab")
    y_table, x_table, z_table = cas_table(ny), cas_table(nx), cas_table(nz)

    pieces, near_re, near_im, to_prev, to_next = density(psi_re, psi_im, v_local, n_ground, y_table, total_orbs)
    near = (near_re, near_im)
    low, high = slab_shift(to_next, 1), slab_shift(to_prev, -1)
    edges = (low, high)

    middle = planes // 2
    once_groups = [list(range(1, middle)), list(range(middle, planes - 1)), [-1, 0, planes - 1, planes]]
    base_groups = [list(range(middle)), list(range(middle, planes))]
    onces = [
        once(near, (), once_groups[0], "once_a"),
        once(near, (), once_groups[1], "once_b"),
        once(near, edges, once_groups[2], "once_c"),
    ]
    bases = [base(near, onces, once_groups, group, name) for group, name in zip(base_groups, ("base_a", "base_b"))]
    columns = ring_columns(y_table)

    share = sum_over_ring(pieces)
    pencils = across(share).reshape(SIDES * nz, nx)
    hats = gather_over_ring(across(solve(pencils, x_table, z_table, ny, planes)))

    v_first, v_last = outer_potential(v_local, columns, hats)
    v_before, v_after = slab_shift(v_last, 1), slab_shift(v_first, -1)
    new_re, new_im, v_kept = inner_update(
        v_local, columns, v_first, v_last, near, hats, onces, once_groups, bases, base_groups
    )
    v_planes = (v_first, v_last, v_before, v_after, v_kept)
    return tuple(outer_update(new_re, new_im, v_planes, near, edges, onces, once_groups, bases, base_groups))


def solution(mesh):
    orbs, slabs = mesh.devices.shape
    mesh = Mesh(mesh.devices.reshape(SIDES, orbs // SIDES, slabs), ("y", "z", "slab"))
    orb = ("y", "z")
    placed = (
        P(orb, "slab", None, None),
        P(orb, "slab", None, None),
        P("slab", None, None),
        P("slab", orb, None),
    )
    return jax.shard_map(
        on_device,
        mesh=mesh,
        in_specs=placed,
        out_specs=(P(orb, "slab", None, None), P(orb, "slab", None, None)),
        check_vma=False,
    )
```

time: 347 us -> 169 us (0.49)
  waiting for transfers between devices: 173 us -> 38.5 us
  other arithmetic: 51.9 us -> 0.27 us
  Pallas kernels: 0 us -> 49 us
  matrix products: 28 us -> 0 us
  local copies, waits for them, and re-layouts: 35.3 us -> 19.5 us
  blocking collectives: 0 us -> 14.9 us
  between operations: 14.7 us -> 1.24 us
  starting transfers between devices: 38.9 us -> 42.4 us
    reduce_scatter x1 -> x0, waiting for transfers between devices: 76.1 us -> none  [on_device(): lax.psum_scatter(partial_value, 'orb', scatter_dimension=1, tiled=True)]
    all_gather x1 -> x0, waiting for transfers between devices: 53.1 us -> none  [on_device(): full_hartree = lax.all_gather(hartree, 'orb', axis=1, tiled=True)]
    pallas_call x0 -> x11, Pallas kernels: none -> 49 us  [the longest x1 13.9 us: inner_update(): pl.pallas_call(functools.partial(inner_kernel, once_groups, base_groups,...]
    ppermute x4 -> x20, starting transfers between devices: 1.17 us -> 36.4 us  [the longest x8 30.1 us: backward(): return lax.ppermute(value, axis, ring(axis, -1))]
    all_to_all x8 -> x1, waiting for transfers between devices: 36 us -> 2.39 us  [across(): lax.all_to_all(value, ('y', 'slab'), split_axis=0, concat_axis=0, tiled=T...]
    all_to_all x8 -> x1, starting transfers between devices: 37.2 us -> 6.03 us  [across(): lax.all_to_all(value, ('y', 'slab'), split_axis=0, concat_axis=0, tiled=T...]
    ppermute x4 -> x20, waiting for transfers between devices: 7.65 us -> 36.1 us  [the longest x8 20.3 us: forward(): return lax.ppermute(value, axis, ring(axis, 1))]
    dot_general x20 -> x0, matrix products: 28 us -> none  [mix(): return jnp.einsum(form, left, right, precision=HIGHEST)]
  transfers between devices with their start and end apart: 14 -> 21, of which waited for: 12 -> 10; matrix products, arithmetic and copies ran while one was open for 13% -> 1% of each run, Pallas kernels for 0% -> 21%
where the time goes in v2:
time: 169 us; the launch traced here: 166 us
  Pallas kernels  49 us (29%)
  starting transfers between devices  42.4 us (25%)
  waiting for transfers between devices  38.5 us (23%)
  local copies, waits for them, and re-layouts  19.5 us (12%)
  blocking collectives  14.9 us (9%)
    ppermute x8, starting transfers between devices, backward(): return lax.ppermute(value, axis, ring(axis, -1))  30.1 us
    ppermute x8, waiting for transfers between devices, forward(): return lax.ppermute(value, axis, ring(axis, 1))  20.3 us
    unnamed x74, local copies, waits for them, and re-layouts  18.2 us
    ppermute x8, waiting for transfers between devices, backward(): return lax.ppermute(value, axis, ring(axis, -1))  15.9 us
    all_to_all x1, blocking collectives, across(): lax.all_to_all(value, ('y', 'slab'), split_axis=0, concat_axis=0, tiled=T...  14.9 us
    pallas_call x1, Pallas kernels, inner_update(): pl.pallas_call(functools.partial(inner_kernel, once_groups, base_groups,...  13.9 us
    pallas_call x3, Pallas kernels, once(): pl.pallas_call(functools.partial(once_kernel, planes, wanted, bool(edges)...  9.9 us
    pallas_call x1, Pallas kernels, density(): pl.pallas_call(functools.partial(density_kernel, 2.0 / total_orbs), in_sp...  8.4 us
  transfers between devices with their start and end apart: 21, of which 10 were waited for; matrix products, arithmetic and copies ran while one was open for 1% of the time, Pallas kernels for 21%

profile of v2, /device:TPU:8, one launch (start us, length us, event | category | flops | bytes accessed | tf_op | source)
XLA Modules:
  0.0 165.8 jit_solution(1704565774598356429)
XLA Ops:
  0.6 8.4 %density_y.1 = (f32[32,8,256]{2,1,0:T(8,128)S(1)}, f32[32,8,256]{2,1,0:T(8,128)S(1)}, f32[32,8,256]{2,1,0:T(8,128)S(1)}, f32[32,8,256]{2,1,0:T(8,128)S(1)}, f32[...) custom-call(f32[1,8,256,256]{3,2,1,0:T(8,128)} %psi_re.1, ...), custom_call_target="tpu_custom_call" | custom-call | tf_op jit(solution)/shard_map/density_y/pallas_call | solution.py:111
  9.0 1.0 copy-done.35
  10.1 1.1 copy-done.36
  11.2 5.9 %collective-permute-start.4 = (f32[16,8,256]{2,1,0:T(8,128)S(1)}, f32[16,8,256]{2,1,0:T(8,128)S(1)}, u32[]{:S(2)}, u32[]{:S(2)}) collective-permute-start(f32[16,8,256]{2,1,0:T(8,128)S(1)} %get-tuple-element.25), channel_id=1, source_target_pairs={{0,112},{16,0},{32,16},{48,32},{64,48},{80,64},{96,80},{112,96},{1... | collective-permute-start | bytes 393224 | tf_op jit(solution)/shard_map/ppermute | solution.py:466
  17.0 2.8 %collective-permute-done.4 = f32[16,8,256]{2,1,0:T(8,128)S(1)} collective-permute-done((f32[16,8,256]{2,1,0:T(8,128)S(1)}, f32[16,8,256]{2,1,0:T(8,128)S(1)}, u32[]{:S(2)}, u32[]{:S(2)}) %collective-permute-start.4) | collective-permute-done | bytes 131104 | tf_op jit(solution)/shard_map/ppermute | solution.py:466
  19.9 3.8 %collective-permute-start.5 = (f32[32,8,256]{2,1,0:T(8,128)S(1)}, f32[32,8,256]{2,1,0:T(8,128)S(1)}, u32[]{:S(2)}, u32[]{:S(2)}) collective-permute-start(f32[32,8,256]{2,1,0:T(8,128)S(1)} %pad_maximum_fusion.1), channel_id=1, source_target_pairs={{0,112},{16,0},{32,16},{48,32},{64,48},{80,64},{96,80},{112,96},{1... | collective-permute-start | bytes 786440 | tf_op jit(solution)/shard_map/ppermute | solution.py:466
  23.8 4.5 %collective-permute-done.5 = f32[32,8,256]{2,1,0:T(8,128)S(1)} collective-permute-done((f32[32,8,256]{2,1,0:T(8,128)S(1)}, f32[32,8,256]{2,1,0:T(8,128)S(1)}, u32[]{:S(2)}, u32[]{:S(2)}) %collective-permute-start.5) | collective-permute-done | bytes 262176 | tf_op jit(solution)/shard_map/ppermute | solution.py:466
  28.4 3.8 %collective-permute-start.6 = (f32[32,8,256]{2,1,0:T(8,128)S(1)}, f32[32,8,256]{2,1,0:T(8,128)S(1)}, u32[]{:S(2)}, u32[]{:S(2)}) collective-permute-start(f32[32,8,256]{2,1,0:T(8,128)S(1)} %add.28), channel_id=1, source_target_pairs={{0,112},{16,0},{32,16},{48,32},{64,48},{80,64},{96,80},{112,96},{1... | collective-permute-start | bytes 786440 | tf_op jit(solution)/shard_map/ppermute | solution.py:466
  32.3 3.8 %collective-permute-done.6 = f32[32,8,256]{2,1,0:T(8,128)S(1)} collective-permute-done((f32[32,8,256]{2,1,0:T(8,128)S(1)}, f32[32,8,256]{2,1,0:T(8,128)S(1)}, u32[]{:S(2)}, u32[]{:S(2)}) %collective-permute-start.6) | collective-permute-done | bytes 262176 | tf_op jit(solution)/shard_map/ppermute | solution.py:466
  36.1 3.8 %collective-permute-start.7 = (f32[32,8,256]{2,1,0:T(8,128)S(1)}, f32[32,8,256]{2,1,0:T(8,128)S(1)}, u32[]{:S(2)}, u32[]{:S(2)}) collective-permute-start(f32[32,8,256]{2,1,0:T(8,128)S(1)} %add.29), channel_id=1, source_target_pairs={{0,112},{16,0},{32,16},{48,32},{64,48},{80,64},{96,80},{112,96},{1... | collective-permute-start | bytes 786440 | tf_op jit(solution)/shard_map/ppermute | solution.py:466
  40.0 3.8 %collective-permute-done.7 = f32[32,8,256]{2,1,0:T(8,128)S(1)} collective-permute-done((f32[32,8,256]{2,1,0:T(8,128)S(1)}, f32[32,8,256]{2,1,0:T(8,128)S(1)}, u32[]{:S(2)}, u32[]{:S(2)}) %collective-permute-start.7) | collective-permute-done | bytes 262176 | tf_op jit(solution)/shard_map/ppermute | solution.py:466
  43.7 3.8 %collective-permute-done.3 = f32[32,8,256]{2,1,0:T(8,128)S(1)} collective-permute-done((f32[32,8,256]{2,1,0:T(8,128)S(1)}, f32[32,8,256]{2,1,0:T(8,128)S(1)}, u32[]{:S(2)}, u32[]{:S(2)}) %collective-permute-start.3) | collective-permute-done | bytes 262176 | tf_op jit(solution)/shard_map/ppermute | solution.py:462
  47.6 14.9 %all_to_all.10 = f32[32,8,256]{2,1,0:T(8,128)S(1)} all-to-all(f32[32,8,256]{2,1,0:T(8,128)S(1)} %add_add_fusion), channel_id=1, replica_groups=mesh['y'=2,'z'=8,'slab'=16] {'y','slab'}, dimensions={0} | all-to-all | bytes 524288 | tf_op jit(solution)/shard_map/all_to_all | solution.py:495
  62.5 2.0 %solve_xz.1 = f32[32,8,256]{2,1,0:T(8,128)} custom-call(f32[256,256]{1,0:T(8,128)S(1)} %bitcast.1, f32[256,256]{1,0:T(8,128)S(1)} %copy-done.15, f32[128,128]{1,0:T(8,128)S(1)} %copy-done.34), custom_call_target="tpu_custom_call" | custom-call | tf_op jit(solution)/shard_map/solve_xz/pallas_call | solution.py:159
  64.5 6.0 %all-to-all-start.1 = ((f32[32,8,256]{2,1,0:T(8,128)}), f32[32,8,256]{2,1,0:T(8,128)}, u32[]{:S(2)}, u32[]{:S(2)}) async-start(f32[32,8,256]{2,1,0:T(8,128)} %solve_xz.1), calls=%async_computation.1 | async-start | bytes 524288 | tf_op jit(solution)/shard_map/all_to_all | solution.py:495
  70.8 5.2 %collective-permute-start.19 = (f32[5,256,256]{2,1,0:T(8,128)}, f32[5,256,256]{2,1,0:T(8,128)}, u32[]{:S(2)}, u32[]{:S(2)}) collective-permute-start(f32[5,256,256]{2,1,0:T(8,128)} %copy-done.35), channel_id=1, source_target_pairs={{0,15},{1,0},{2,1},{3,2},{4,3},{5,4},{6,5},{7,6},{8,7},{9,8},{10,9... | collective-permute-start | bytes 3932168 | tf_op jit(solution)/shard_map/ppermute | solution.py:470
  76.0 2.4 %all-to-all-done.1.refs_0_.refs_6_ = f32[32,8,256]{2,1,0:T(8,128)} async-done(((f32[32,8,256]{2,1,0:T(8,128)}), f32[32,8,256]{2,1,0:T(8,128)}, u32[]{:S(2)}, u32[]{:S(2)}) %all-to-all-start.1) | async-done | bytes 262176 | tf_op jit(solution)/shard_map/all_to_all | solution.py:495
  78.4 3.2 %collective-permute-start.8 = (f32[32,8,256]{2,1,0:T(8,128)}, f32[32,8,256]{2,1,0:T(8,128)S(1)}, u32[]{:S(2)}, u32[]{:S(2)}) collective-permute-start(f32[32,8,256]{2,1,0:T(8,128)} %all-to-all-done.1.refs_0_.refs_6_), channel_id=1, source_target_pairs={{0,112},{16,0},{32,16},{48,32},{64,48},{80,64},{96,80},{112,96},{1... | collective-permute-start | bytes 786440 | tf_op jit(solution)/shard_map/ppermute | solution.py:466
  81.6 7.2 %collective-permute-done.11.refs_8_.refs_14_ = f32[32,8,256]{2,1,0:T(8,128)S(1)} collective-permute-done((f32[32,8,256]{2,1,0:T(8,128)}, f32[32,8,256]{2,1,0:T(8,128)S(1)}, u32[]{:S(2)}, u32[]{:S(2)}) %collective-permute-start.11) | collective-permute-done | bytes 262176 | tf_op jit(solution)/shard_map/ppermute | solution.py:462
  89.5 3.2 %collective-permute-start.9 = (f32[32,8,256]{2,1,0:T(8,128)S(1)}, f32[32,8,256]{2,1,0:T(8,128)S(1)}, u32[]{:S(2)}, u32[]{:S(2)}) collective-permute-start(f32[32,8,256]{2,1,0:T(8,128)S(1)} %collective-permute-done.8.refs_1_.refs_7_), channel_id=1, source_target_pairs={{0,112},{16,0},{32,16},{48,32},{64,48},{80,64},{96,80},{112,96},{1... | collective-permute-start | bytes 786440 | tf_op jit(solution)/shard_map/ppermute | solution.py:466
  92.7 0.7 copy-done.25
  93.5 4.7 %collective-permute-done.12.refs_7_.refs_13_ = f32[32,8,256]{2,1,0:T(8,128)S(1)} collective-permute-done((f32[32,8,256]{2,1,0:T(8,128)S(1)}, f32[32,8,256]{2,1,0:T(8,128)S(1)}, u32[]{:S(2)}, u32[]{:S(2)}) %collective-permute-start.12) | collective-permute-done | bytes 262176 | tf_op jit(solution)/shard_map/ppermute | solution.py:462
  98.2 0.7 copy-done.28
  98.9 3.2 %collective-permute-start.10 = (f32[32,8,256]{2,1,0:T(8,128)S(1)}, f32[32,8,256]{2,1,0:T(8,128)S(1)}, u32[]{:S(2)}, u32[]{:S(2)}) collective-permute-start(f32[32,8,256]{2,1,0:T(8,128)S(1)} %collective-permute-done.9.refs_2_.refs_8_), channel_id=1, source_target_pairs={{0,112},{16,0},{32,16},{48,32},{64,48},{80,64},{96,80},{112,96},{1... | collective-permute-start | bytes 786440 | tf_op jit(solution)/shard_map/ppermute | solution.py:466
  102.1 4.6 %collective-permute-done.13.refs_6_.refs_12_ = f32[32,8,256]{2,1,0:T(8,128)S(1)} collective-permute-done((f32[32,8,256]{2,1,0:T(8,128)S(1)}, f32[32,8,256]{2,1,0:T(8,128)S(1)}, u32[]{:S(2)}, u32[]{:S(2)}) %collective-permute-start.13) | collective-permute-done | bytes 262176 | tf_op jit(solution)/shard_map/ppermute | solution.py:462
  108.7 0.7 copy-done.19
  109.4 3.2 %collective-permute-start.15 = (f32[16,8,256]{2,1,0:T(8,128)}, f32[16,8,256]{2,1,0:T(8,128)}, u32[]{:S(2)}, u32[]{:S(2)}) collective-permute-start(f32[16,8,256]{2,1,0:T(8,128)} %slice.25), channel_id=1, source_target_pairs={{0,112},{16,0},{32,16},{48,32},{64,48},{80,64},{96,80},{112,96},{1... | collective-permute-start | bytes 393224 | tf_op jit(solution)/shard_map/ppermute | solution.py:466
  112.6 1.8 %ring_columns.1.columns.refs_1_ = f32[256,256]{1,0:T(8,128)} custom-call(f32[256,256]{1,0:T(8,128)} %constant.4.clone.table.y_table.x_table), custom_call_target="tpu_custom_call" | custom-call | tf_op jit(solution)/shard_map/ring_columns/pallas_call | solution.py:273
  114.4 1.0 collective-permute-done.15.refs_5_.refs_11_
  115.5 1.6 copy-done.7
  117.0 0.9 copy-done.13
  118.0 0.9 copy-done.17
  118.9 0.9 copy-done.20
  119.9 0.9 copy-done.23
  120.8 0.9 copy-done.26
  121.8 0.9 copy-done.29
  122.8 0.9 copy-done.32
  123.7 1.8 %outer_potential.1 = (f32[1,256,256]{2,1,0:T(8,128)S(1)}, f32[1,256,256]{2,1,0:T(8,128)S(1)}) custom-call(f32[8,256,256]{2,1,0:T(8,128)S(1)} %copy-done.7, f32[256,256]{1,0:T(8,128)S(1)} %copy-done.13, f32[32,8,256]{2,1,0:T(8,128)} %all-to-all-done.1.refs_0_.refs_6_, f32[32,8,256]{2,1,0:T(8,128)S(1)} %copy-done.26, f32[32,8,256]{2,1,0:T(8,128)S(1)} %copy-done.32, ...), custom_call_target="tpu_custom_call" | custom-call | tf_op jit(solution)/shard_map/outer_potential/pallas_call | solution.py:296
  126.0 2.6 %once_b.1.refs_1_.refs_16_.refs_10_ = f32[2,3,256,256]{3,2,1,0:T(8,128)S(1)} custom-call(f32[8,256,256]{2,1,0:T(8,128)S(1)} %get-tuple-element.31.refs_0_.re.refs_4_.refs_5_, f32[8,256,256]{2,1,0:T(8,128)S(1)} %copy-done.3), custom_call_target="tpu_custom_call" | custom-call | flops 19660800 | bytes 1572864 | tf_op jit(solution)/shard_map/once_b/pallas_call | solution.py:221
  128.6 2.6 %once_a.1.refs_0_.refs_15_.refs_9_ = f32[2,3,256,256]{3,2,1,0:T(8,128)S(1)} custom-call(f32[8,256,256]{2,1,0:T(8,128)S(1)} %get-tuple-element.31.refs_0_.re.refs_4_.refs_5_, f32[8,256,256]{2,1,0:T(8,128)S(1)} %copy-done.3), custom_call_target="tpu_custom_call" | custom-call | flops 19660800 | bytes 1572864 | tf_op jit(solution)/shard_map/once_a/pallas_call | solution.py:221
  131.2 4.8 %once_c.1.refs_2_.refs_17_.refs_11_ = f32[2,4,256,256]{3,2,1,0:T(8,128)S(1)} custom-call(f32[8,256,256]{2,1,0:T(8,128)S(1)} %get-tuple-element.31.refs_0_.re.refs_4_.refs_5_, f32[8,256,256]{2,1,0:T(8,128)S(1)} %copy-done.3, f32[5,256,256]{2,1,0:T(8,128)S(1)} %collective-permute-done.18.refs_2_.refs_7_, f32[5,256,256]{2,1,0:T(8,128)} %collective-permute-done.19.refs_3_.refs_8_), custom_call_target="tpu_custom_call" | custom-call | flops 26214400 | bytes 2097152 | tf_op jit(solution)/shard_map/once_c/pallas_call | solution.py:221
  136.0 3.5 %base_b.1.refs_19_.refs_13_ = f32[2,4,256,256]{3,2,1,0:T(8,128)S(1)} custom-call(f32[8,256,256]{2,1,0:T(8,128)S(1)} %get-tuple-element.31.refs_0_.re.refs_4_.refs_5_, f32[8,256,256]{2,1,0:T(8,128)S(1)} %copy-done.3, f32[2,3,256,256]{3,2,1,0:T(8,128)S(1)} %once_a.1.refs_0_.refs_15_.refs_9_, f32[2,3,256,256]{3,2,1,0:T(8,128)S(1)} %once_b.1.refs_1_.refs_16_.refs_10_, ...), custom_call_target="tpu_custom_call" | custom-call | flops 26214400 | bytes 2097152 | tf_op jit(solution)/shard_map/base_b/pallas_call | solution.py:256
  139.6 1.3 copy-done.9
  140.9 3.5 %base_a.1.refs_18_.refs_12_ = f32[2,4,256,256]{3,2,1,0:T(8,128)S(1)} custom-call(f32[8,256,256]{2,1,0:T(8,128)S(1)} %get-tuple-element.31.refs_0_.re.refs_4_.refs_5_, f32[8,256,256]{2,1,0:T(8,128)S(1)} %copy-done.3, f32[2,3,256,256]{3,2,1,0:T(8,128)S(1)} %once_a.1.refs_0_.refs_15_.refs_9_, f32[2,3,256,256]{3,2,1,0:T(8,128)S(1)} %once_b.1.refs_1_.refs_16_.refs_10_, ...), custom_call_target="tpu_custom_call" | custom-call | flops 26214400 | bytes 2097152 | tf_op jit(solution)/shard_map/base_a/pallas_call | solution.py:256
  144.4 1.4 copy-done.11
  145.9 13.9 %inner_update.1 = (f32[1,8,256,256]{3,2,1,0:T(8,128)}, f32[1,8,256,256]{3,2,1,0:T(8,128)}, f32[2,256,256]{2,1,0:T(8,128)S(1)}) custom-call(f32[8,256,256]{2,1,0:T(8,128)S(1)} %copy-done.8, f32[256,256]{1,0:T(8,128)S(1)} %copy-done.14, f32[1,256,256]{2,1,0:T(8,128)S(1)} %get-tuple-element.29.refs_2_.refs_0_, ...), custom_call_target="tpu_custom_call" | custom-call | flops 209715200 | bytes 4194304 | tf_op jit(solution)/shard_map/inner_update/pallas_call | solution.py:370
  159.9 1.6 copy-done.12
  161.5 4.2 %outer_update.1 = (f32[1,8,256,256]{3,2,1,0:T(8,128)}, f32[1,8,256,256]{3,2,1,0:T(8,128)}) custom-call(f32[1,256,256]{2,1,0:T(8,128)S(1)} %get-tuple-element.29.refs_2_.refs_0_, f32[1,256,256]{2,1,0:T(8,128)S(1)} %get-tuple-element.30.refs_3_.refs_1_, ...), custom_call_target="tpu_custom_call", output_to_operand_aliasing={{0}: (14, {}), {1}: (15, {})} | custom-call | tf_op jit(solution)/shard_map/outer_update/pallas_call | solution.py:440
  (91 shorter events, 4.2 us)
Async XLA Ops:
  9.0 1.1 copy-start.35
  10.1 1.1 copy-start.36
  11.2 24.9 %copy-start.2 = (f32[8,256,256]{2,1,0:T(8,128)}, f32[8,256,256]{2,1,0:T(8,128)S(1)}, u32[]{:S(2)}) copy-start(f32[8,256,256]{2,1,0:T(8,128)S(1)} %get-tuple-element.32.refs_1_.im.refs_5_.refs_6_) | copy-start | bytes 6291460
  11.2 128.4 %copy-start = (f32[8,256,256]{2,1,0:T(8,128)}, f32[8,256,256]{2,1,0:T(8,128)S(1)}, u32[]{:S(2)}) copy-start(f32[8,256,256]{2,1,0:T(8,128)S(1)} %get-tuple-element.31.refs_0_.re.refs_4_.refs_5_) | copy-start | bytes 6291460
  11.2 8.6 %collective-permute-start.4 = (f32[16,8,256]{2,1,0:T(8,128)S(1)}, f32[16,8,256]{2,1,0:T(8,128)S(1)}, u32[]{:S(2)}, u32[]{:S(2)}) collective-permute-start(f32[16,8,256]{2,1,0:T(8,128)S(1)} %get-tuple-element.25), channel_id=1, source_target_pairs={{0,112},{16,0},{32,16},{48,32},{64,48},{80,64},{96,80},{112,96},{1... | collective-permute-start | bytes 393224 | tf_op jit(solution)/shard_map/ppermute | solution.py:466
  17.0 6.6 %collective-permute-start = (f32[16,8,256]{2,1,0:T(8,128)S(1)}, f32[16,8,256]{2,1,0:T(8,128)S(1)}, u32[]{:S(2)}, u32[]{:S(2)}) collective-permute-start(f32[16,8,256]{2,1,0:T(8,128)S(1)} %get-tuple-element.21), channel_id=1, source_target_pairs={{0,16},{16,32},{32,48},{48,64},{64,80},{80,96},{96,112},{112,0},{1... | collective-permute-start | bytes 393224 | tf_op jit(solution)/shard_map/ppermute | solution.py:462
  19.9 8.5 %collective-permute-start.5 = (f32[32,8,256]{2,1,0:T(8,128)S(1)}, f32[32,8,256]{2,1,0:T(8,128)S(1)}, u32[]{:S(2)}, u32[]{:S(2)}) collective-permute-start(f32[32,8,256]{2,1,0:T(8,128)S(1)} %pad_maximum_fusion.1), channel_id=1, source_target_pairs={{0,112},{16,0},{32,16},{48,32},{64,48},{80,64},{96,80},{112,96},{1... | collective-permute-start | bytes 786440 | tf_op jit(solution)/shard_map/ppermute | solution.py:466
  23.7 8.5 %collective-permute-start.1 = (f32[32,8,256]{2,1,0:T(8,128)S(1)}, f32[32,8,256]{2,1,0:T(8,128)S(1)}, u32[]{:S(2)}, u32[]{:S(2)}) collective-permute-start(f32[32,8,256]{2,1,0:T(8,128)S(1)} %pad_maximum_fusion), channel_id=1, source_target_pairs={{0,16},{16,32},{32,48},{48,64},{64,80},{80,96},{96,112},{112,0},{1... | collective-permute-start | bytes 786440 | tf_op jit(solution)/shard_map/ppermute | solution.py:462
  28.4 34.1 %copy-start.15 = (f32[256,256]{1,0:T(8,128)S(1)}, f32[256,256]{1,0:T(8,128)}, u32[]{:S(2)}) copy-start(f32[256,256]{1,0:T(8,128)} %constant.4.clone.table.y_table.x_table) | copy-start | bytes 786436
  28.4 34.1 %copy-start.34 = (f32[128,128]{1,0:T(8,128)S(1)}, f32[128,128]{1,0:T(8,128)}, u32[]{:S(2)}) copy-start(f32[128,128]{1,0:T(8,128)} %constant.5.clone.z_table) | copy-start | bytes 196612
  28.4 7.7 %collective-permute-start.6 = (f32[32,8,256]{2,1,0:T(8,128)S(1)}, f32[32,8,256]{2,1,0:T(8,128)S(1)}, u32[]{:S(2)}, u32[]{:S(2)}) collective-permute-start(f32[32,8,256]{2,1,0:T(8,128)S(1)} %add.28), channel_id=1, source_target_pairs={{0,112},{16,0},{32,16},{48,32},{64,48},{80,64},{96,80},{112,96},{1... | collective-permute-start | bytes 786440 | tf_op jit(solution)/shard_map/ppermute | solution.py:466
  32.2 7.7 %collective-permute-start.2 = (f32[32,8,256]{2,1,0:T(8,128)S(1)}, f32[32,8,256]{2,1,0:T(8,128)S(1)}, u32[]{:S(2)}, u32[]{:S(2)}) collective-permute-start(f32[32,8,256]{2,1,0:T(8,128)S(1)} %add.25), channel_id=1, source_target_pairs={{0,16},{16,32},{32,48},{48,64},{64,80},{80,96},{96,112},{112,0},{1... | collective-permute-start | bytes 786440 | tf_op jit(solution)/shard_map/ppermute | solution.py:462
  36.1 7.7 %collective-permute-start.7 = (f32[32,8,256]{2,1,0:T(8,128)S(1)}, f32[32,8,256]{2,1,0:T(8,128)S(1)}, u32[]{:S(2)}, u32[]{:S(2)}) collective-permute-start(f32[32,8,256]{2,1,0:T(8,128)S(1)} %add.29), channel_id=1, source_target_pairs={{0,112},{16,0},{32,16},{48,32},{64,48},{80,64},{96,80},{112,96},{1... | collective-permute-start | bytes 786440 | tf_op jit(solution)/shard_map/ppermute | solution.py:466
  39.9 7.7 %collective-permute-start.3 = (f32[32,8,256]{2,1,0:T(8,128)S(1)}, f32[32,8,256]{2,1,0:T(8,128)S(1)}, u32[]{:S(2)}, u32[]{:S(2)}) collective-permute-start(f32[32,8,256]{2,1,0:T(8,128)S(1)} %add.26), channel_id=1, source_target_pairs={{0,16},{16,32},{32,48},{48,64},{64,80},{80,96},{96,112},{112,0},{1... | collective-permute-start | bytes 786440 | tf_op jit(solution)/shard_map/ppermute | solution.py:462
  64.5 13.9 %all-to-all-start.1 = ((f32[32,8,256]{2,1,0:T(8,128)}), f32[32,8,256]{2,1,0:T(8,128)}, u32[]{:S(2)}, u32[]{:S(2)}) async-start(f32[32,8,256]{2,1,0:T(8,128)} %solve_xz.1), calls=%async_computation.1 | async-start | bytes 524288 | tf_op jit(solution)/shard_map/all_to_all | solution.py:495
  70.5 60.7 %collective-permute-start.18 = (f32[5,256,256]{2,1,0:T(8,128)}, f32[5,256,256]{2,1,0:T(8,128)S(1)}, u32[]{:S(2)}, u32[]{:S(2)}) collective-permute-start(f32[5,256,256]{2,1,0:T(8,128)} %copy-done.36), channel_id=1, source_target_pairs={{0,1},{1,2},{2,3},{3,4},{4,5},{5,6},{6,7},{7,8},{8,9},{9,10},{10,1... | collective-permute-start | bytes 3932168 | tf_op jit(solution)/shard_map/ppermute | solution.py:470
  70.8 60.4 %collective-permute-start.19 = (f32[5,256,256]{2,1,0:T(8,128)}, f32[5,256,256]{2,1,0:T(8,128)}, u32[]{:S(2)}, u32[]{:S(2)}) collective-permute-start(f32[5,256,256]{2,1,0:T(8,128)} %copy-done.35), channel_id=1, source_target_pairs={{0,15},{1,0},{2,1},{3,2},{4,3},{5,4},{6,5},{7,6},{8,7},{9,8},{10,9... | collective-permute-start | bytes 3932168 | tf_op jit(solution)/shard_map/ppermute | solution.py:470
  78.4 10.4 %collective-permute-start.11 = (f32[32,8,256]{2,1,0:T(8,128)}, f32[32,8,256]{2,1,0:T(8,128)S(1)}, u32[]{:S(2)}, u32[]{:S(2)}) collective-permute-start(f32[32,8,256]{2,1,0:T(8,128)} %all-to-all-done.1.refs_0_.refs_6_), channel_id=1, source_target_pairs={{0,16},{16,32},{32,48},{48,64},{64,80},{80,96},{96,112},{112,0},{1... | collective-permute-start | bytes 786440 | tf_op jit(solution)/shard_map/ppermute | solution.py:462
  78.4 11.1 %collective-permute-start.8 = (f32[32,8,256]{2,1,0:T(8,128)}, f32[32,8,256]{2,1,0:T(8,128)S(1)}, u32[]{:S(2)}, u32[]{:S(2)}) collective-permute-start(f32[32,8,256]{2,1,0:T(8,128)} %all-to-all-done.1.refs_0_.refs_6_), channel_id=1, source_target_pairs={{0,112},{16,0},{32,16},{48,32},{64,48},{80,64},{96,80},{112,96},{1... | collective-permute-start | bytes 786440 | tf_op jit(solution)/shard_map/ppermute | solution.py:466
  88.8 9.4 %collective-permute-start.12 = (f32[32,8,256]{2,1,0:T(8,128)S(1)}, f32[32,8,256]{2,1,0:T(8,128)S(1)}, u32[]{:S(2)}, u32[]{:S(2)}) collective-permute-start(f32[32,8,256]{2,1,0:T(8,128)S(1)} %collective-permute-done.11.refs_8_.refs_14_), channel_id=1, source_target_pairs={{0,16},{16,32},{32,48},{48,64},{64,80},{80,96},{96,112},{112,0},{1... | collective-permute-start | bytes 786440 | tf_op jit(solution)/shard_map/ppermute | solution.py:462
  89.5 9.4 %collective-permute-start.9 = (f32[32,8,256]{2,1,0:T(8,128)S(1)}, f32[32,8,256]{2,1,0:T(8,128)S(1)}, u32[]{:S(2)}, u32[]{:S(2)}) collective-permute-start(f32[32,8,256]{2,1,0:T(8,128)S(1)} %collective-permute-done.8.refs_1_.refs_7_), channel_id=1, source_target_pairs={{0,112},{16,0},{32,16},{48,32},{64,48},{80,64},{96,80},{112,96},{1... | collective-permute-start | bytes 786440 | tf_op jit(solution)/shard_map/ppermute | solution.py:466
  98.2 8.5 %collective-permute-start.13 = (f32[32,8,256]{2,1,0:T(8,128)S(1)}, f32[32,8,256]{2,1,0:T(8,128)S(1)}, u32[]{:S(2)}, u32[]{:S(2)}) collective-permute-start(f32[32,8,256]{2,1,0:T(8,128)S(1)} %collective-permute-done.12.refs_7_.refs_13_), channel_id=1, source_target_pairs={{0,16},{16,32},{32,48},{48,64},{64,80},{80,96},{96,112},{112,0},{1... | collective-permute-start | bytes 786440 | tf_op jit(solution)/shard_map/ppermute | solution.py:462
  98.9 9.8 %copy-start.31 = (f32[32,8,256]{2,1,0:T(8,128)}, f32[32,8,256]{2,1,0:T(8,128)S(1)}, u32[]{:S(2)}) copy-start(f32[32,8,256]{2,1,0:T(8,128)S(1)} %collective-permute-done.9.refs_2_.refs_8_) | copy-start | bytes 786436
  98.9 9.1 %collective-permute-start.10 = (f32[32,8,256]{2,1,0:T(8,128)S(1)}, f32[32,8,256]{2,1,0:T(8,128)S(1)}, u32[]{:S(2)}, u32[]{:S(2)}) collective-permute-start(f32[32,8,256]{2,1,0:T(8,128)S(1)} %collective-permute-done.9.refs_2_.refs_8_), channel_id=1, source_target_pairs={{0,112},{16,0},{32,16},{48,32},{64,48},{80,64},{96,80},{112,96},{1... | collective-permute-start | bytes 786440 | tf_op jit(solution)/shard_map/ppermute | solution.py:466
  108.0 6.4 %collective-permute-start.14 = (f32[16,8,256]{2,1,0:T(8,128)}, f32[16,8,256]{2,1,0:T(8,128)S(1)}, u32[]{:S(2)}, u32[]{:S(2)}) collective-permute-start(f32[16,8,256]{2,1,0:T(8,128)} %slice.24), channel_id=1, source_target_pairs={{0,16},{16,32},{32,48},{48,64},{64,80},{80,96},{96,112},{112,0},{1... | collective-permute-start | bytes 393224 | tf_op jit(solution)/shard_map/ppermute | solution.py:462
  109.4 6.1 %collective-permute-start.15 = (f32[16,8,256]{2,1,0:T(8,128)}, f32[16,8,256]{2,1,0:T(8,128)}, u32[]{:S(2)}, u32[]{:S(2)}) collective-permute-start(f32[16,8,256]{2,1,0:T(8,128)} %slice.25), channel_id=1, source_target_pairs={{0,112},{16,0},{32,16},{48,32},{64,48},{80,64},{96,80},{112,96},{1... | collective-permute-start | bytes 393224 | tf_op jit(solution)/shard_map/ppermute | solution.py:466
  114.4 11.6 %copy-start.3 = (f32[8,256,256]{2,1,0:T(8,128)S(1)}, f32[8,256,256]{2,1,0:T(8,128)}, u32[]{:S(2)}) copy-start(f32[8,256,256]{2,1,0:T(8,128)} %copy-done.2) | copy-start | bytes 6291460
  115.5 1.6 copy-start.7
  117.0 0.9 copy-start.13
  118.0 0.9 copy-start.17
  125.5 34.4 %collective-permute-start.17 = (f32[1,256,256]{2,1,0:T(8,128)S(1)}, f32[1,256,256]{2,1,0:T(8,128)S(1)}, u32[]{:S(2)}, u32[]{:S(2)}) collective-permute-start(f32[1,256,256]{2,1,0:T(8,128)S(1)} %get-tuple-element.29.refs_2_.refs_0_), channel_id=1, source_target_pairs={{0,15},{1,0},{2,1},{3,2},{4,3},{5,4},{6,5},{7,6},{8,7},{9,8},{10,9... | collective-permute-start | bytes 786440 | tf_op jit(solution)/shard_map/ppermute | solution.py:470
  125.5 34.3 %collective-permute-start.16 = (f32[1,256,256]{2,1,0:T(8,128)S(1)}, f32[1,256,256]{2,1,0:T(8,128)S(1)}, u32[]{:S(2)}, u32[]{:S(2)}) collective-permute-start(f32[1,256,256]{2,1,0:T(8,128)S(1)} %get-tuple-element.30.refs_3_.refs_1_), channel_id=1, source_target_pairs={{0,1},{1,2},{2,3},{3,4},{4,5},{5,6},{6,7},{7,8},{8,9},{9,10},{10,1... | collective-permute-start | bytes 786440 | tf_op jit(solution)/shard_map/ppermute | solution.py:470
  136.0 3.5 %copy-start.5 = (f32[2,4,256,256]{3,2,1,0:T(8,128)}, f32[2,4,256,256]{3,2,1,0:T(8,128)S(1)}, u32[]{:S(2)}) copy-start(f32[2,4,256,256]{3,2,1,0:T(8,128)S(1)} %once_c.1.refs_2_.refs_17_.refs_11_) | copy-start | bytes 6291460
  139.5 1.3 copy-start.9
  140.9 5.0 %copy-start.8 = (f32[8,256,256]{2,1,0:T(8,128)S(1)}, f32[8,256,256]{2,1,0:T(8,128)}, u32[]{:S(2)}) copy-start(f32[8,256,256]{2,1,0:T(8,128)} %refs_0_.1) | copy-start | bytes 6291460
  140.9 5.0 %copy-start.14 = (f32[256,256]{1,0:T(8,128)S(1)}, f32[256,256]{1,0:T(8,128)}, u32[]{:S(2)}) copy-start(f32[256,256]{1,0:T(8,128)} %ring_columns.1.columns.refs_1_) | copy-start | bytes 786436
  140.9 5.0 %copy-start.18 = (f32[32,8,256]{2,1,0:T(8,128)S(1)}, f32[32,8,256]{2,1,0:T(8,128)}, u32[]{:S(2)}) copy-start(f32[32,8,256]{2,1,0:T(8,128)} %copy-done.16) | copy-start | bytes 786436
  140.9 5.0 %copy-start.21 = (f32[32,8,256]{2,1,0:T(8,128)S(1)}, f32[32,8,256]{2,1,0:T(8,128)}, u32[]{:S(2)}) copy-start(f32[32,8,256]{2,1,0:T(8,128)} %copy-done.19) | copy-start | bytes 786436
  140.9 5.0 %copy-start.24 = (f32[32,8,256]{2,1,0:T(8,128)S(1)}, f32[32,8,256]{2,1,0:T(8,128)}, u32[]{:S(2)}) copy-start(f32[32,8,256]{2,1,0:T(8,128)} %copy-done.22) | copy-start | bytes 786436
  140.9 5.0 %copy-start.27 = (f32[32,8,256]{2,1,0:T(8,128)S(1)}, f32[32,8,256]{2,1,0:T(8,128)}, u32[]{:S(2)}) copy-start(f32[32,8,256]{2,1,0:T(8,128)} %copy-done.25) | copy-start | bytes 786436
  140.9 5.0 %copy-start.30 = (f32[32,8,256]{2,1,0:T(8,128)S(1)}, f32[32,8,256]{2,1,0:T(8,128)}, u32[]{:S(2)}) copy-start(f32[32,8,256]{2,1,0:T(8,128)} %copy-done.28) | copy-start | bytes 786436
  140.9 5.0 %copy-start.33 = (f32[32,8,256]{2,1,0:T(8,128)S(1)}, f32[32,8,256]{2,1,0:T(8,128)}, u32[]{:S(2)}) copy-start(f32[32,8,256]{2,1,0:T(8,128)} %copy-done.31) | copy-start | bytes 786436
  144.4 1.4 copy-start.11
  145.9 14.0 %copy-start.1 = (f32[8,256,256]{2,1,0:T(8,128)S(1)}, f32[8,256,256]{2,1,0:T(8,128)}, u32[]{:S(2)}) copy-start(f32[8,256,256]{2,1,0:T(8,128)} %copy-done) | copy-start | bytes 6291460
  145.9 14.0 %copy-start.4 = (f32[8,256,256]{2,1,0:T(8,128)S(1)}, f32[8,256,256]{2,1,0:T(8,128)}, u32[]{:S(2)}) copy-start(f32[8,256,256]{2,1,0:T(8,128)} %copy-done.2) | copy-start | bytes 6291460
  145.9 14.0 %copy-start.6 = (f32[2,4,256,256]{3,2,1,0:T(8,128)S(1)}, f32[2,4,256,256]{3,2,1,0:T(8,128)}, u32[]{:S(2)}) copy-start(f32[2,4,256,256]{3,2,1,0:T(8,128)} %copy-done.5) | copy-start | bytes 6291460
  145.9 14.0 %copy-start.10 = (f32[2,4,256,256]{3,2,1,0:T(8,128)S(1)}, f32[2,4,256,256]{3,2,1,0:T(8,128)}, u32[]{:S(2)}) copy-start(f32[2,4,256,256]{3,2,1,0:T(8,128)} %copy-done.9) | copy-start | bytes 6291460
  159.9 1.6 copy-start.12
  (10 other events, 8.3 us)

commit v3 on v2

--- a/solution.py
+++ b/solution.py
@@ -16,7 +16,6 @@
 KINETIC = -0.5 / (SPACING * SPACING)
 HIGHEST = lax.Precision.HIGHEST
 SIDES = 2
-STRIP = 32
 MIB = 1 << 20
 VMEM = pl.BlockSpec(memory_space=pltpu.VMEM)
 ANY = pl.BlockSpec(memory_space=pl.ANY)
@@ -122,7 +121,7 @@
             pltpu.SemaphoreType.DMA((2, 3)),
             pltpu.SemaphoreType.DMA((2,)),
         ],
-        compiler_params=pltpu.CompilerParams(vmem_limit_bytes=24 * MIB),
+        compiler_params=pltpu.CompilerParams(vmem_limit_bytes=6 * MIB),
         name="density_y",
     )(*far)
     return result[:9], result[9], result[10], result[11], result[12]
@@ -166,29 +165,29 @@
     )(field, x_table, z_table)
 
 
-def strip_of(plane, start, rows):
+def whole(plane):
     ref, lead = plane
-    return ref[lead + (pl.ds(start, rows), slice(None))]
-
-
-def kinetic(below, plane, above, start):
-    ny = plane[0].shape[-2]
-    mid = strip_of(plane, start, STRIP)
-    before = strip_of(plane, pl.multiple_of(lax.rem(start + ny - 8, ny), 8), 8)
-    after = strip_of(plane, pl.multiple_of(lax.rem(start + STRIP, ny), 8), 8)
-    tall = jnp.concatenate([before, mid, after], axis=0)
-    up = pltpu.roll(tall, 1, 0)[8 : 8 + STRIP]
-    down = pltpu.roll(tall, tall.shape[0] - 1, 0)[8 : 8 + STRIP]
-    left = pltpu.roll(mid, 1, 1)
-    right = pltpu.roll(mid, mid.shape[1] - 1, 1)
-    along = strip_of(below, start, STRIP) + strip_of(above, start, STRIP)
-    return mid, KINETIC * ((up + down) + (left + right) + along - 6.0 * mid)
-
-
-def each_strip(ny, body):
-    @pl.loop(0, ny // STRIP)
-    def _(index):
-        body(pl.multiple_of(index * STRIP, STRIP))
+    return ref[lead]
+
+
+def neighbour_matrix(length):
+    matrix = np.zeros((length, length), np.float32)
+    index = np.arange(length)
+    matrix[index, (index + 1) % length] = KINETIC
+    matrix[index, (index - 1) % length] = KINETIC
+    return jnp.asarray(matrix, jnp.bfloat16)
+
+
+def kinetic(below, plane, above, sides):
+    mid = whole(plane)
+    high = mid.astype(jnp.bfloat16)
+    rest = (mid - high.astype(jnp.float32)).astype(jnp.bfloat16)
+    matrix = sides[...]
+    along_x = jnp.dot(high, matrix, preferred_element_type=jnp.float32)
+    along_x = along_x + jnp.dot(rest, matrix, preferred_element_type=jnp.float32)
+    along_y = pltpu.roll(mid, 1, 0) + pltpu.roll(mid, mid.shape[0] - 1, 0)
+    along_z = whole(below) + whole(above)
+    return mid, along_x + (KINETIC * (along_y + along_z) - (6.0 * KINETIC) * mid)
 
 
 def psi_plane(fields, low, high, planes, part, z):
@@ -199,34 +198,29 @@
     return (fields[part], (z,))
 
 
-def once_kernel(planes, wanted, with_edges, *refs):
+def once_kernel(planes, wanted, with_edges, sides, *refs):
     refs = list(refs)
     fields = [refs.pop(0), refs.pop(0)]
     low, high = (refs.pop(0), refs.pop(0)) if with_edges else (None, None)
     out = refs.pop(0)
-    ny = out.shape[-2]
     at = functools.partial(psi_plane, fields, low, high, planes)
     for slot, z in enumerate(wanted):
-
-        def body(start):
-            for part in range(2):
-                _, value = kinetic(at(part, z - 1), at(part, z), at(part, z + 1), start)
-                out[part, slot, pl.ds(start, STRIP), :] = value
-
-        each_strip(ny, body)
-
-
-def once(near, edges, wanted, name):
+        for part in range(2):
+            _, value = kinetic(at(part, z - 1), at(part, z), at(part, z + 1), sides)
+            out[part, slot] = value
+
+
+def once(sides, near, edges, wanted, name):
     planes, ny, nx = near[0].shape
     return pl.pallas_call(
         functools.partial(once_kernel, planes, wanted, bool(edges)),
-        in_specs=[VMEM] * (2 + len(edges)),
+        in_specs=[VMEM] * (3 + len(edges)),
         out_specs=VMEM,
         out_shape=shaped(2, len(wanted), ny, nx),
-        compiler_params=pltpu.CompilerParams(vmem_limit_bytes=16 * MIB),
+        compiler_params=pltpu.CompilerParams(vmem_limit_bytes=6 * MIB),
         cost_estimate=cost(len(wanted), 100 * ny * nx),
         name=name,
-    )(*near, *edges)
+    )(sides, *near, *edges)
 
 
 def once_plane(groups, refs, part, z):
@@ -235,33 +229,27 @@
             return (ref, (part, group.index(z)))
 
 
-def base_kernel(groups, wanted, re, im, *refs):
+def base_kernel(groups, wanted, sides, re, im, *refs):
     onces, out = refs[:-1], refs[-1]
-    ny = out.shape[-2]
     at = functools.partial(once_plane, groups, onces)
     for slot, z in enumerate(wanted):
-
-        def body(start):
-            strip = pl.ds(start, STRIP)
-            first_re, second_re = kinetic(at(0, z - 1), at(0, z), at(0, z + 1), start)
-            first_im, second_im = kinetic(at(1, z - 1), at(1, z), at(1, z + 1), start)
-            out[0, slot, strip, :] = re[z, strip, :] + TIME_STEP * first_im - HALF_SQ * second_re
-            out[1, slot, strip, :] = im[z, strip, :] - TIME_STEP * first_re - HALF_SQ * second_im
-
-        each_strip(ny, body)
-
-
-def base(near, onces, groups, wanted, name):
+        first_re, second_re = kinetic(at(0, z - 1), at(0, z), at(0, z + 1), sides)
+        first_im, second_im = kinetic(at(1, z - 1), at(1, z), at(1, z + 1), sides)
+        out[0, slot] = re[z] + TIME_STEP * first_im - HALF_SQ * second_re
+        out[1, slot] = im[z] - TIME_STEP * first_re - HALF_SQ * second_im
+
+
+def base(sides, near, onces, groups, wanted, name):
     planes, ny, nx = near[0].shape
     return pl.pallas_call(
         functools.partial(base_kernel, groups, wanted),
-        in_specs=[VMEM] * (2 + len(onces)),
+        in_specs=[VMEM] * (3 + len(onces)),
         out_specs=VMEM,
         out_shape=shaped(2, len(wanted), ny, nx),
-        compiler_params=pltpu.CompilerParams(vmem_limit_bytes=16 * MIB),
+        compiler_params=pltpu.CompilerParams(vmem_limit_bytes=6 * MIB),
         cost_estimate=cost(len(wanted), 100 * ny * nx),
         name=name,
-    )(*near, *onces)
+    )(sides, *near, *onces)
 
 
 def columns_kernel(table, out, rows):
@@ -298,25 +286,24 @@
         in_specs=[VMEM] * (2 + len(hats)),
         out_specs=[VMEM] * 2,
         out_shape=[shaped(1, ny, nx)] * 2,
-        compiler_params=pltpu.CompilerParams(vmem_limit_bytes=16 * MIB),
+        compiler_params=pltpu.CompilerParams(vmem_limit_bytes=6 * MIB),
         name="outer_potential",
     )(v_local, columns, *hats)
 
 
-def update_strip(at_w, at_once, at_base, local, stage, slot, z, start):
-    strip = pl.ds(start, STRIP)
-    here = strip_of(local, start, STRIP)
-    mid_re, kin_re = kinetic(at_w(0, z - 1), at_w(0, z), at_w(0, z + 1), start)
-    mid_im, kin_im = kinetic(at_w(1, z - 1), at_w(1, z), at_w(1, z + 1), start)
-    second_re = kin_re + here * (strip_of(at_once(0, z), start, STRIP) + mid_re)
-    second_im = kin_im + here * (strip_of(at_once(1, z), start, STRIP) + mid_im)
-    stage[0, slot, strip, :] = strip_of(at_base(0, z), start, STRIP) + TIME_STEP * mid_im - HALF_SQ * second_re
-    stage[1, slot, strip, :] = strip_of(at_base(1, z), start, STRIP) - TIME_STEP * mid_re - HALF_SQ * second_im
+def update_plane(at_w, at_once, at_base, local, sides, stage, slot, z):
+    here = whole(local)
+    mid_re, kin_re = kinetic(at_w(0, z - 1), at_w(0, z), at_w(0, z + 1), sides)
+    mid_im, kin_im = kinetic(at_w(1, z - 1), at_w(1, z), at_w(1, z + 1), sides)
+    second_re = kin_re + here * (whole(at_once(0, z)) + mid_re)
+    second_im = kin_im + here * (whole(at_once(1, z)) + mid_im)
+    stage[0, slot] = whole(at_base(0, z)) + TIME_STEP * mid_im - HALF_SQ * second_re
+    stage[1, slot] = whole(at_base(1, z)) - TIME_STEP * mid_re - HALF_SQ * second_im
 
 
 def inner_kernel(once_groups, base_groups, hat_count, *refs):
     refs = list(refs)
-    v_local, columns, v_first, v_last, re, im = [refs.pop(0) for _ in range(6)]
+    sides, v_local, columns, v_first, v_last, re, im = [refs.pop(0) for _ in range(7)]
     hats = [refs.pop(0) for _ in range(hat_count)]
     onces = [refs.pop(0) for _ in once_groups]
     bases = [refs.pop(0) for _ in base_groups]
@@ -340,18 +327,15 @@
             work[part, z] = here * fields[part][z]
         if z >= 2:
             done = z - 1
-            each_strip(
-                ny,
-                lambda start: update_strip(
-                    at_w,
-                    functools.partial(once_plane, once_groups, onces),
-                    functools.partial(once_plane, base_groups, bases),
-                    (pot, (done,)),
-                    stage,
-                    done - 1,
-                    done,
-                    start,
-                ),
+            update_plane(
+                at_w,
+                functools.partial(once_plane, once_groups, onces),
+                functools.partial(once_plane, base_groups, bases),
+                (pot, (done,)),
+                sides,
+                stage,
+                done - 1,
+                done,
             )
             for part, out in enumerate((out_re, out_im)):
                 copy = pltpu.make_async_copy(stage.at[part, done - 1], out.at[0, done], sem.at[part, done - 1])
@@ -363,9 +347,9 @@
         copy.wait()
 
 
-def inner_update(v_local, columns, v_first, v_last, near, hats, onces, once_groups, bases, base_groups):
+def inner_update(sides, v_local, columns, v_first, v_last, near, hats, onces, once_groups, bases, base_groups):
     planes, ny, nx = v_local.shape
-    operands = [v_local, columns, v_first, v_last, *near, *hats, *onces, *bases]
+    operands = [sides, v_local, columns, v_first, v_last, *near, *hats, *onces, *bases]
     full = shaped(1, planes, ny, nx)
     return pl.pallas_call(
         functools.partial(inner_kernel, once_groups, base_groups, len(hats)),
@@ -378,7 +362,7 @@
             plane_scratch(2, planes - 2, ny=ny, nx=nx),
             pltpu.SemaphoreType.DMA((2, planes - 2)),
         ],
-        compiler_params=pltpu.CompilerParams(vmem_limit_bytes=44 * MIB),
+        compiler_params=pltpu.CompilerParams(vmem_limit_bytes=14 * MIB),
         cost_estimate=cost(planes, 400 * ny * nx),
         name="inner_update",
     )(*operands)
@@ -386,11 +370,11 @@
 
 def outer_kernel_update(once_groups, base_groups, *refs):
     refs = list(refs)
-    v_first, v_last, v_before, v_after, v_kept, re, im, low, high = [refs.pop(0) for _ in range(9)]
+    sides, v_first, v_last, v_before, v_after, v_kept, re, im, low, high = [refs.pop(0) for _ in range(10)]
     onces = [refs.pop(0) for _ in once_groups]
     bases = [refs.pop(0) for _ in base_groups]
     _, _, out_re, out_im, work, stage, sem = refs
-    planes, ny, _ = re.shape
+    planes = re.shape[0]
     at_psi = functools.partial(psi_plane, (re, im), low, high, planes)
     locals_of = {
         -1: (v_before, (0,)),
@@ -413,18 +397,15 @@
             for part in range(2):
                 source, where = at_psi(part, near)
                 work[part, order.index(near)] = here * source[where]
-        each_strip(
-            ny,
-            lambda start: update_strip(
-                at_w,
-                functools.partial(once_plane, once_groups, onces),
-                functools.partial(once_plane, base_groups, bases),
-                locals_of[z],
-                stage,
-                slot,
-                z,
-                start,
-            ),
+        update_plane(
+            at_w,
+            functools.partial(once_plane, once_groups, onces),
+            functools.partial(once_plane, base_groups, bases),
+            locals_of[z],
+            sides,
+            stage,
+            slot,
+            z,
         )
         for part, out in enumerate((out_re, out_im)):
             copy = pltpu.make_async_copy(stage.at[part, slot], out.at[0, z], sem.at[part, slot])
@@ -434,9 +415,9 @@
         copy.wait()
 
 
-def outer_update(new_re, new_im, v_planes, near, edges, onces, once_groups, bases, base_groups):
+def outer_update(sides, new_re, new_im, v_planes, near, edges, onces, once_groups, bases, base_groups):
     planes, ny, nx = near[0].shape
-    operands = [*v_planes, *near, *edges, *onces, *bases]
+    operands = [sides, *v_planes, *near, *edges, *onces, *bases]
     return pl.pallas_call(
         functools.partial(outer_kernel_update, once_groups, base_groups),
         in_specs=[VMEM] * len(operands) + [ANY, ANY],
@@ -448,7 +429,7 @@
             plane_scratch(2, 2, ny=ny, nx=nx),
             pltpu.SemaphoreType.DMA((2, 2)),
         ],
-        compiler_params=pltpu.CompilerParams(vmem_limit_bytes=32 * MIB),
+        compiler_params=pltpu.CompilerParams(vmem_limit_bytes=8 * MIB),
         name="outer_update",
     )(*operands, new_re, new_im)
 
@@ -470,15 +451,23 @@
     return lax.ppermute(value, "slab", ring("slab", shift))
 
 
-def sum_over_ring(pieces):
+def after(value, *others):
+    return lax.optimization_barrier((value,) + others)[0]
+
+
+def sum_over_ring(pieces, beside):
     s0, s1, s2, s3, s4_first, s4_second, s5, s6, s7 = pieces
     half = s4_first.shape[0]
     got_up, got_down = forward(s4_first), backward(s4_second)
+    got_up = after(got_up, *beside[0])
     up = jnp.concatenate([s3[:half] + got_up, s3[half:]], axis=0)
     down = jnp.concatenate([s5[:half], s5[half:] + got_down], axis=0)
     up, down = forward(up), backward(down)
+    up = after(up, *beside[1])
     up, down = forward(up + s2), backward(down + s6)
+    up = after(up, *beside[2])
     up, down = forward(up + s1), backward(down + s7)
+    up = after(up, *beside[3])
     return up + down + s0
 
 
@@ -509,25 +498,29 @@
     middle = planes // 2
     once_groups = [list(range(1, middle)), list(range(middle, planes - 1)), [-1, 0, planes - 1, planes]]
     base_groups = [list(range(middle)), list(range(middle, planes))]
+    sides = neighbour_matrix(nx)
     onces = [
-        once(near, (), once_groups[0], "once_a"),
-        once(near, (), once_groups[1], "once_b"),
-        once(near, edges, once_groups[2], "once_c"),
+        once(sides, near, (), once_groups[0], "once_a"),
+        once(sides, near, (), once_groups[1], "once_b"),
+        once(sides, near, edges, once_groups[2], "once_c"),
     ]
-    bases = [base(near, onces, once_groups, group, name) for group, name in zip(base_groups, ("base_a", "base_b"))]
+    bases = [
+        base(sides, near, onces, once_groups, group, name) for group, name in zip(base_groups, ("base_a", "base_b"))
+    ]
     columns = ring_columns(y_table)
 
-    share = sum_over_ring(pieces)
+    beside = ((onces[0], columns), (onces[1],), (onces[2],), tuple(bases))
+    share = sum_over_ring(pieces, beside)
     pencils = across(share).reshape(SIDES * nz, nx)
     hats = gather_over_ring(across(solve(pencils, x_table, z_table, ny, planes)))
 
     v_first, v_last = outer_potential(v_local, columns, hats)
     v_before, v_after = slab_shift(v_last, 1), slab_shift(v_first, -1)
     new_re, new_im, v_kept = inner_update(
-        v_local, columns, v_first, v_last, near, hats, onces, once_groups, bases, base_groups
+        sides, v_local, columns, v_first, v_last, near, hats, onces, once_groups, bases, base_groups
     )
     v_planes = (v_first, v_last, v_before, v_after, v_kept)
-    return tuple(outer_update(new_re, new_im, v_planes, near, edges, onces, once_groups, bases, base_groups))
+    return tuple(outer_update(sides, new_re, new_im, v_planes, near, edges, onces, once_groups, bases, base_groups))
 
 
 def solution(mesh):

time: 169 us -> 137 us (0.81); the launches traced: 166 us -> 136 us
  Pallas kernels: 49 us -> 29.8 us
  local copies, waits for them, and re-layouts: 19.5 us -> 7.95 us
  blocking collectives: 14.9 us -> 24.8 us
  starting transfers between devices: 42.4 us -> 36.8 us
  waiting for transfers between devices: 38.5 us -> 33.1 us
  other arithmetic: 0.27 us -> 2.24 us
    ppermute x8, waiting for transfers between devices: 15.9 us -> 2.42 us  [backward(): return lax.ppermute(value, axis, ring(axis, -1))]
    unnamed x74 -> x44, local copies, waits for them, and re-layouts: 18.2 us -> 7.93 us
    all_to_all x1 -> x2, blocking collectives: 14.9 us -> 24.8 us  [across(): lax.all_to_all(value, ('y', 'slab'), split_axis=0, concat_axis=0, tiled=T...]
    pallas_call x1, Pallas kernels: 13.9 us -> 5.51 us  [inner_update(): pl.pallas_call(functools.partial(inner_kernel, once_groups, base_groups,...]
    ppermute x8, waiting for transfers between devices: 20.3 us -> 27.2 us  [forward(): return lax.ppermute(value, axis, ring(axis, 1))]
    all_to_all x1 -> x0, starting transfers between devices: 6.03 us -> none  [across(): lax.all_to_all(value, ('y', 'slab'), split_axis=0, concat_axis=0, tiled=T...]
    pallas_call x3, Pallas kernels: 9.9 us -> 4.37 us  [once(): pl.pallas_call(functools.partial(once_kernel, planes, wanted, bool(edges)...]
    pallas_call x2, Pallas kernels: 7.02 us -> 3.04 us  [base(): pl.pallas_call(functools.partial(base_kernel, groups, wanted), in_specs=[...]
  transfers between devices with their start and end apart: 21 -> 20, of which waited for: 10 -> 10; matrix products, arithmetic and copies ran while one was open for 1% -> 2% of each run, Pallas kernels for 21% -> 11%
where the time goes in v3:
time: 137 us; the launch traced here: 136 us
  starting transfers between devices  36.8 us (27%)
  waiting for transfers between devices  33.1 us (24%)
  Pallas kernels  29.8 us (22%)
  blocking collectives  24.8 us (18%)
  local copies, waits for them, and re-layouts  7.95 us (6%)
  other arithmetic  2.24 us (2%)
    ppermute x8, starting transfers between devices, backward(): return lax.ppermute(value, axis, ring(axis, -1))  28.4 us
    ppermute x8, waiting for transfers between devices, forward(): return lax.ppermute(value, axis, ring(axis, 1))  27.2 us
    all_to_all x2, blocking collectives, across(): lax.all_to_all(value, ('y', 'slab'), split_axis=0, concat_axis=0, tiled=T...  24.8 us
    pallas_call x1, Pallas kernels, density(): pl.pallas_call(functools.partial(density_kernel, 2.0 / total_orbs), in_sp...  9.9 us
    unnamed x44, local copies, waits for them, and re-layouts  7.93 us
    ppermute x4, starting transfers between devices, slab_shift(): return lax.ppermute(value, 'slab', ring('slab', shift))  5.94 us
    pallas_call x1, Pallas kernels, inner_update(): pl.pallas_call(functools.partial(inner_kernel, once_groups, base_groups,...  5.51 us
    pallas_call x3, Pallas kernels, once(): pl.pallas_call(functools.partial(once_kernel, planes, wanted, bool(edges)...  4.37 us
  transfers between devices with their start and end apart: 20, of which 10 were waited for; matrix products, arithmetic and copies ran while one was open for 2% of the time, Pallas kernels for 11%

profile of v3, /device:TPU:8, one launch (start us, length us, event | category | flops | bytes accessed | tf_op | source)
XLA Modules:
  0.0 135.9 jit_solution(7402568787531813918)
XLA Ops:
  0.6 9.9 %density_y.1 = (f32[32,8,256]{2,1,0:T(8,128)S(1)}, f32[32,8,256]{2,1,0:T(8,128)S(1)}, f32[32,8,256]{2,1,0:T(8,128)S(1)}, f32[32,8,256]{2,1,0:T(8,128)S(1)}, f32[...) custom-call(f32[1,8,256,256]{3,2,1,0:T(8,128)} %psi_re.1, ...), custom_call_target="tpu_custom_call" | custom-call | tf_op jit(solution)/shard_map/density_y/pallas_call | solution.py:110
  10.6 1.3 copy-done
  11.9 0.7 copy-done.7
  12.6 0.7 copy-done.9
  13.3 0.7 copy-done.11
  14.0 0.7 copy-done.13
  14.7 0.7 copy-done.15
  15.4 0.7 copy-done.17
  16.1 0.7 copy-done.19
  16.8 1.9 %collective-permute-start = (f32[16,8,256]{2,1,0:T(8,128)}, f32[16,8,256]{2,1,0:T(8,128)}, u32[]{:S(2)}, u32[]{:S(2)}) collective-permute-start(f32[16,8,256]{2,1,0:T(8,128)} %get-tuple-element.25), channel_id=1, source_target_pairs={{0,16},{16,32},{32,48},{48,64},{64,80},{80,96},{96,112},{112,0},{1... | collective-permute-start | bytes 393224 | tf_op jit(solution)/shard_map/ppermute | solution.py:443
  18.8 5.4 %collective-permute-start.4 = (f32[5,256,256]{2,1,0:T(8,128)}, f32[5,256,256]{2,1,0:T(8,128)}, u32[]{:S(2)}, u32[]{:S(2)}) collective-permute-start(f32[5,256,256]{2,1,0:T(8,128)} %get-tuple-element.32), channel_id=1, source_target_pairs={{0,15},{1,0},{2,1},{3,2},{4,3},{5,4},{6,5},{7,6},{8,7},{9,8},{10,9... | collective-permute-start | bytes 3932168 | tf_op jit(solution)/shard_map/ppermute | solution.py:451
  24.1 4.0 %collective-permute-start.6 = (f32[16,8,256]{2,1,0:T(8,128)}, f32[16,8,256]{2,1,0:T(8,128)}, u32[]{:S(2)}, u32[]{:S(2)}) collective-permute-start(f32[16,8,256]{2,1,0:T(8,128)} %get-tuple-element.37), channel_id=1, source_target_pairs={{0,112},{16,0},{32,16},{48,32},{64,48},{80,64},{96,80},{112,96},{1... | collective-permute-start | bytes 393224 | tf_op jit(solution)/shard_map/ppermute | solution.py:447
  28.1 1.8 %ring_columns.1.columns.refs_2_ = f32[256,256]{1,0:T(8,128)} custom-call(f32[256,256]{1,0:T(8,128)} %constant.6.clone.table.y_table.x_table), custom_call_target="tpu_custom_call" | custom-call | tf_op jit(solution)/shard_map/ring_columns/pallas_call | solution.py:261
  29.9 1.6 %copy-done.1 = f32[8,256,256]{2,1,0:T(8,128)S(1)} copy-done((f32[8,256,256]{2,1,0:T(8,128)S(1)}, f32[8,256,256]{2,1,0:T(8,128)}, u32[]{:S(2)}) %copy-start.1) | copy-done | bytes 2097176
  31.5 0.9 once_a.1.refs_0_.refs_16_.refs_10_
  32.4 1.1 slice_add_fusion.1
  33.6 0.1 collective-permute-start.1
  33.7 0.9 fusion
  34.6 3.3 %collective-permute-start.7 = (f32[32,8,256]{2,1,0:T(8,128)S(1)}, f32[32,8,256]{2,1,0:T(8,128)S(1)}, u32[]{:S(2)}, u32[]{:S(2)}) collective-permute-start(f32[32,8,256]{2,1,0:T(8,128)S(1)} %pad_maximum_fusion.1), channel_id=1, source_target_pairs={{0,112},{16,0},{32,16},{48,32},{64,48},{80,64},{96,80},{112,96},{1... | collective-permute-start | bytes 786440 | tf_op jit(solution)/shard_map/ppermute | solution.py:447
  37.9 0.9 once_b.1.refs_1_.refs_17_.refs_11_
  38.9 3.2 %collective-permute-done.1 = f32[32,8,256]{2,1,0:T(8,128)S(1)} collective-permute-done((f32[32,8,256]{2,1,0:T(8,128)S(1)}, f32[32,8,256]{2,1,0:T(8,128)S(1)}, u32[]{:S(2)}, u32[]{:S(2)}) %collective-permute-start.1) | collective-permute-done | bytes 262176 | tf_op jit(solution)/shard_map/ppermute | solution.py:443
  42.2 0.6 collective-permute-done.7
  42.9 3.9 %collective-permute-start.8 = (f32[32,8,256]{2,1,0:T(8,128)S(1)}, f32[32,8,256]{2,1,0:T(8,128)S(1)}, u32[]{:S(2)}, u32[]{:S(2)}) collective-permute-start(f32[32,8,256]{2,1,0:T(8,128)S(1)} %add.28), channel_id=1, source_target_pairs={{0,112},{16,0},{32,16},{48,32},{64,48},{80,64},{96,80},{112,96},{1... | collective-permute-start | bytes 786440 | tf_op jit(solution)/shard_map/ppermute | solution.py:447
  46.8 2.5 %once_c.1.refs_2_.refs_18_.refs_12_ = f32[2,4,256,256]{3,2,1,0:T(8,128)S(1)} custom-call(bf16[256,256]{1,0:T(8,128)(2,1)S(1)} %copy-done.4, f32[8,256,256]{2,1,0:T(8,128)S(1)} %get-tuple-element.26.refs_0_.re.refs_5_.refs_6_, f32[8,256,256]{2,1,0:T(8,128)S(1)} %copy-done.2, f32[5,256,256]{2,1,0:T(8,128)S(1)} %collective-permute-done.3.refs_2_.refs_8_, ...), custom_call_target="tpu_custom_call" | custom-call | flops 26214400 | bytes 2097152 | tf_op jit(solution)/shard_map/once_c/pallas_call | solution.py:215
  49.3 2.5 %collective-permute-done.2 = f32[32,8,256]{2,1,0:T(8,128)S(1)} collective-permute-done((f32[32,8,256]{2,1,0:T(8,128)S(1)}, f32[32,8,256]{2,1,0:T(8,128)S(1)}, u32[]{:S(2)}, u32[]{:S(2)}) %collective-permute-start.2) | collective-permute-done | bytes 262176 | tf_op jit(solution)/shard_map/ppermute | solution.py:443
  51.9 0.1 collective-permute-start.5
  52.0 1.1 collective-permute-done.8
  53.1 3.8 %collective-permute-start.9 = (f32[32,8,256]{2,1,0:T(8,128)S(1)}, f32[32,8,256]{2,1,0:T(8,128)S(1)}, u32[]{:S(2)}, u32[]{:S(2)}) collective-permute-start(f32[32,8,256]{2,1,0:T(8,128)S(1)} %add.29), channel_id=1, source_target_pairs={{0,112},{16,0},{32,16},{48,32},{64,48},{80,64},{96,80},{112,96},{1... | collective-permute-start | bytes 786440 | tf_op jit(solution)/shard_map/ppermute | solution.py:447
  56.9 1.5 %base_b.1.refs_20_.refs_14_ = f32[2,4,256,256]{3,2,1,0:T(8,128)S(1)} custom-call(bf16[256,256]{1,0:T(8,128)(2,1)S(1)} %copy-done.4, f32[8,256,256]{2,1,0:T(8,128)S(1)} %get-tuple-element.26.refs_0_.re.refs_5_.refs_6_, f32[8,256,256]{2,1,0:T(8,128)S(1)} %copy-done.2, f32[2,3,256,256]{3,2,1,0:T(8,128)S(1)} %once_a.1.refs_0_.refs_16_.refs_10_, ...), custom_call_target="tpu_custom_call" | custom-call | flops 26214400 | bytes 2097152 | tf_op jit(solution)/shard_map/base_b/pallas_call | solution.py:244
  58.5 1.5 %base_a.1.refs_19_.refs_13_ = f32[2,4,256,256]{3,2,1,0:T(8,128)S(1)} custom-call(bf16[256,256]{1,0:T(8,128)(2,1)S(1)} %copy-done.4, f32[8,256,256]{2,1,0:T(8,128)S(1)} %get-tuple-element.26.refs_0_.re.refs_5_.refs_6_, f32[8,256,256]{2,1,0:T(8,128)S(1)} %copy-done.2, f32[2,3,256,256]{3,2,1,0:T(8,128)S(1)} %once_a.1.refs_0_.refs_16_.refs_10_, ...), custom_call_target="tpu_custom_call" | custom-call | flops 26214400 | bytes 2097152 | tf_op jit(solution)/shard_map/base_a/pallas_call | solution.py:244
  60.0 0.8 collective-permute-done.9
  60.9 12.4 %all_to_all.10 = f32[32,8,256]{2,1,0:T(8,128)S(1)} all-to-all(f32[32,8,256]{2,1,0:T(8,128)S(1)} %add_add_fusion), channel_id=1, replica_groups=mesh['y'=2,'z'=8,'slab'=16] {'y','slab'}, dimensions={0} | all-to-all | bytes 524288 | tf_op jit(solution)/shard_map/all_to_all | solution.py:484
  73.3 1.3 solve_xz.1
  74.6 12.3 %all_to_all.11.refs_0_.refs_7_ = f32[32,8,256]{2,1,0:T(8,128)S(1)} all-to-all(f32[32,8,256]{2,1,0:T(8,128)S(1)} %solve_xz.1), channel_id=1, replica_groups=mesh['y'=2,'z'=8,'slab'=16] {'y','slab'}, dimensions={0} | all-to-all | bytes 524288 | tf_op jit(solution)/shard_map/all_to_all | solution.py:484
  86.9 3.7 %collective-permute-start.10 = (f32[32,8,256]{2,1,0:T(8,128)S(1)}, f32[32,8,256]{2,1,0:T(8,128)S(1)}, u32[]{:S(2)}, u32[]{:S(2)}) collective-permute-start(f32[32,8,256]{2,1,0:T(8,128)S(1)} %all_to_all.11.refs_0_.refs_7_), channel_id=1, source_target_pairs={{0,112},{16,0},{32,16},{48,32},{64,48},{80,64},{96,80},{112,96},{1... | collective-permute-start | bytes 786440 | tf_op jit(solution)/shard_map/ppermute | solution.py:447
  90.6 7.1 %collective-permute-done.13.refs_8_.refs_15_ = f32[32,8,256]{2,1,0:T(8,128)S(1)} collective-permute-done((f32[32,8,256]{2,1,0:T(8,128)S(1)}, f32[32,8,256]{2,1,0:T(8,128)S(1)}, u32[]{:S(2)}, u32[]{:S(2)}) %collective-permute-start.13) | collective-permute-done | bytes 262176 | tf_op jit(solution)/shard_map/ppermute | solution.py:443
  97.7 3.2 %collective-permute-start.11 = (f32[32,8,256]{2,1,0:T(8,128)S(1)}, f32[32,8,256]{2,1,0:T(8,128)S(1)}, u32[]{:S(2)}, u32[]{:S(2)}) collective-permute-start(f32[32,8,256]{2,1,0:T(8,128)S(1)} %collective-permute-done.10.refs_1_.refs_8_), channel_id=1, source_target_pairs={{0,112},{16,0},{32,16},{48,32},{64,48},{80,64},{96,80},{112,96},{1... | collective-permute-start | bytes 786440 | tf_op jit(solution)/shard_map/ppermute | solution.py:447
  100.9 6.2 %collective-permute-done.14.refs_7_.refs_14_ = f32[32,8,256]{2,1,0:T(8,128)S(1)} collective-permute-done((f32[32,8,256]{2,1,0:T(8,128)S(1)}, f32[32,8,256]{2,1,0:T(8,128)S(1)}, u32[]{:S(2)}, u32[]{:S(2)}) %collective-permute-start.14) | collective-permute-done | bytes 262176 | tf_op jit(solution)/shard_map/ppermute | solution.py:443
  107.1 3.2 %collective-permute-start.12 = (f32[32,8,256]{2,1,0:T(8,128)S(1)}, f32[32,8,256]{2,1,0:T(8,128)S(1)}, u32[]{:S(2)}, u32[]{:S(2)}) collective-permute-start(f32[32,8,256]{2,1,0:T(8,128)S(1)} %collective-permute-done.11.refs_2_.refs_9_), channel_id=1, source_target_pairs={{0,112},{16,0},{32,16},{48,32},{64,48},{80,64},{96,80},{112,96},{1... | collective-permute-start | bytes 786440 | tf_op jit(solution)/shard_map/ppermute | solution.py:447
  110.4 5.4 %collective-permute-done.15.refs_6_.refs_13_ = f32[32,8,256]{2,1,0:T(8,128)S(1)} collective-permute-done((f32[32,8,256]{2,1,0:T(8,128)S(1)}, f32[32,8,256]{2,1,0:T(8,128)S(1)}, u32[]{:S(2)}, u32[]{:S(2)}) %collective-permute-start.15) | collective-permute-done | bytes 262176 | tf_op jit(solution)/shard_map/ppermute | solution.py:443
  115.7 0.3 collective-permute-start.16
  116.1 3.3 %collective-permute-start.17 = (f32[16,8,256]{2,1,0:T(8,128)S(1)}, f32[16,8,256]{2,1,0:T(8,128)S(1)}, u32[]{:S(2)}, u32[]{:S(2)}) collective-permute-start(f32[16,8,256]{2,1,0:T(8,128)S(1)} %slice.25), channel_id=1, source_target_pairs={{0,112},{16,0},{32,16},{48,32},{64,48},{80,64},{96,80},{112,96},{1... | collective-permute-start | bytes 393224 | tf_op jit(solution)/shard_map/ppermute | solution.py:447
  119.4 2.8 %collective-permute-done.16.refs_4_.refs_11_ = f32[16,8,256]{2,1,0:T(8,128)S(1)} collective-permute-done((f32[16,8,256]{2,1,0:T(8,128)S(1)}, f32[16,8,256]{2,1,0:T(8,128)S(1)}, u32[]{:S(2)}, u32[]{:S(2)}) %collective-permute-start.16) | collective-permute-done | bytes 131104 | tf_op jit(solution)/shard_map/ppermute | solution.py:443
  122.2 0.8 outer_potential.1
  123.1 0.5 collective-permute-start.18
  123.6 5.5 %inner_update.1 = (f32[1,8,256,256]{3,2,1,0:T(8,128)}, f32[1,8,256,256]{3,2,1,0:T(8,128)}, f32[2,256,256]{2,1,0:T(8,128)S(1)}) custom-call(bf16[256,256]{1,0:T(8,128)(2,1)S(1)} %copy-done.4, f32[8,256,256]{2,1,0:T(8,128)S(1)} %copy-done.3, f32[256,256]{1,0:T(8,128)S(1)} %copy-done.5, f32[1,256,256]{2,1,0:T(8,128)S(1)} %get-tuple-element.41.refs_3_.refs_1_, ...), custom_call_target="tpu_custom_call" | custom-call | flops 209715200 | bytes 4194304 | tf_op jit(solution)/shard_map/inner_update/pallas_call | solution.py:354
  129.1 3.5 %collective-permute-done.18.refs_3_ = f32[1,256,256]{2,1,0:T(8,128)S(1)} collective-permute-done((f32[1,256,256]{2,1,0:T(8,128)S(1)}, f32[1,256,256]{2,1,0:T(8,128)S(1)}, u32[]{:S(2)}, u32[]{:S(2)}) %collective-permute-start.18) | collective-permute-done | bytes 262176 | tf_op jit(solution)/shard_map/ppermute | solution.py:451
  132.6 3.1 %outer_update.1 = (f32[1,8,256,256]{3,2,1,0:T(8,128)}, f32[1,8,256,256]{3,2,1,0:T(8,128)}) custom-call(bf16[256,256]{1,0:T(8,128)(2,1)S(1)} %copy-done.4, f32[1,256,256]{2,1,0:T(8,128)S(1)} %get-tuple-element.41.refs_3_.refs_1_, f32[1,256,256]{2,1,0:T(8,128)S(1)} %get-tuple-element.42.refs_4_.refs_2_, ...), custom_call_target="tpu_custom_call", output_to_operand_aliasing={{0}: (15, {}), {1}: (16, {})} | custom-call | tf_op jit(solution)/shard_map/outer_update/pallas_call | solution.py:421
  (60 shorter events, 0.5 us)
Async XLA Ops:
  0.6 29.3 %copy-start.4 = (bf16[256,256]{1,0:T(8,128)(2,1)S(1)}, bf16[256,256]{1,0:T(8,128)(2,1)}, u32[]{:S(2)}) copy-start(bf16[256,256]{1,0:T(8,128)(2,1)} %constant.8.clone.sides.refs_0_) | copy-start | bytes 393220
  10.5 1.3 copy-start
  11.9 0.7 copy-start.7
  12.6 0.7 copy-start.9
  13.3 0.7 copy-start.11
  14.0 0.7 copy-start.13
  14.7 0.7 copy-start.15
  15.4 0.7 copy-start.17
  16.1 0.7 copy-start.19
  16.8 15.6 %collective-permute-start = (f32[16,8,256]{2,1,0:T(8,128)}, f32[16,8,256]{2,1,0:T(8,128)}, u32[]{:S(2)}, u32[]{:S(2)}) collective-permute-start(f32[16,8,256]{2,1,0:T(8,128)} %get-tuple-element.25), channel_id=1, source_target_pairs={{0,16},{16,32},{32,48},{48,64},{64,80},{80,96},{96,112},{112,0},{1... | collective-permute-start | bytes 393224 | tf_op jit(solution)/shard_map/ppermute | solution.py:443
  18.8 28.1 %collective-permute-start.3 = (f32[5,256,256]{2,1,0:T(8,128)}, f32[5,256,256]{2,1,0:T(8,128)S(1)}, u32[]{:S(2)}, u32[]{:S(2)}) collective-permute-start(f32[5,256,256]{2,1,0:T(8,128)} %get-tuple-element.31), channel_id=1, source_target_pairs={{0,1},{1,2},{2,3},{3,4},{4,5},{5,6},{6,7},{7,8},{8,9},{9,10},{10,1... | collective-permute-start | bytes 3932168 | tf_op jit(solution)/shard_map/ppermute | solution.py:451
  18.8 28.1 %collective-permute-start.4 = (f32[5,256,256]{2,1,0:T(8,128)}, f32[5,256,256]{2,1,0:T(8,128)}, u32[]{:S(2)}, u32[]{:S(2)}) collective-permute-start(f32[5,256,256]{2,1,0:T(8,128)} %get-tuple-element.32), channel_id=1, source_target_pairs={{0,15},{1,0},{2,1},{3,2},{4,3},{5,4},{6,5},{7,6},{8,7},{9,8},{10,9... | collective-permute-start | bytes 3932168 | tf_op jit(solution)/shard_map/ppermute | solution.py:451
  24.1 9.5 %collective-permute-start.6 = (f32[16,8,256]{2,1,0:T(8,128)}, f32[16,8,256]{2,1,0:T(8,128)}, u32[]{:S(2)}, u32[]{:S(2)}) collective-permute-start(f32[16,8,256]{2,1,0:T(8,128)} %get-tuple-element.37), channel_id=1, source_target_pairs={{0,112},{16,0},{32,16},{48,32},{64,48},{80,64},{96,80},{112,96},{1... | collective-permute-start | bytes 393224 | tf_op jit(solution)/shard_map/ppermute | solution.py:447
  29.9 1.6 %copy-start.1 = (f32[8,256,256]{2,1,0:T(8,128)S(1)}, f32[8,256,256]{2,1,0:T(8,128)}, u32[]{:S(2)}) copy-start(f32[8,256,256]{2,1,0:T(8,128)} %copy-done) | copy-start | bytes 6291460
  31.5 1.0 copy-start.18
  31.5 2.2 %copy-start.16 = (f32[32,8,256]{2,1,0:T(8,128)S(1)}, f32[32,8,256]{2,1,0:T(8,128)}, u32[]{:S(2)}) copy-start(f32[32,8,256]{2,1,0:T(8,128)} %copy-done.15) | copy-start | bytes 786436
  32.4 5.5 %copy-start.2 = (f32[8,256,256]{2,1,0:T(8,128)S(1)}, f32[8,256,256]{2,1,0:T(8,128)}, u32[]{:S(2)}) copy-start(f32[8,256,256]{2,1,0:T(8,128)} %copy-done) | copy-start | bytes 6291460
  33.6 8.6 %collective-permute-start.1 = (f32[32,8,256]{2,1,0:T(8,128)S(1)}, f32[32,8,256]{2,1,0:T(8,128)S(1)}, u32[]{:S(2)}, u32[]{:S(2)}) collective-permute-start(f32[32,8,256]{2,1,0:T(8,128)S(1)} %pad_maximum_fusion), channel_id=1, source_target_pairs={{0,16},{16,32},{32,48},{48,64},{64,80},{80,96},{96,112},{112,0},{1... | collective-permute-start | bytes 786440 | tf_op jit(solution)/shard_map/ppermute | solution.py:443
  34.6 7.5 %copy-start.14 = (f32[32,8,256]{2,1,0:T(8,128)S(1)}, f32[32,8,256]{2,1,0:T(8,128)}, u32[]{:S(2)}) copy-start(f32[32,8,256]{2,1,0:T(8,128)} %copy-done.13) | copy-start | bytes 786436
  34.6 8.2 %copy-start.12 = (f32[32,8,256]{2,1,0:T(8,128)S(1)}, f32[32,8,256]{2,1,0:T(8,128)}, u32[]{:S(2)}) copy-start(f32[32,8,256]{2,1,0:T(8,128)} %copy-done.11) | copy-start | bytes 786436
  34.6 8.1 %collective-permute-start.7 = (f32[32,8,256]{2,1,0:T(8,128)S(1)}, f32[32,8,256]{2,1,0:T(8,128)S(1)}, u32[]{:S(2)}, u32[]{:S(2)}) collective-permute-start(f32[32,8,256]{2,1,0:T(8,128)S(1)} %pad_maximum_fusion.1), channel_id=1, source_target_pairs={{0,112},{16,0},{32,16},{48,32},{64,48},{80,64},{96,80},{112,96},{1... | collective-permute-start | bytes 786440 | tf_op jit(solution)/shard_map/ppermute | solution.py:447
  42.2 9.7 %collective-permute-start.2 = (f32[32,8,256]{2,1,0:T(8,128)S(1)}, f32[32,8,256]{2,1,0:T(8,128)S(1)}, u32[]{:S(2)}, u32[]{:S(2)}) collective-permute-start(f32[32,8,256]{2,1,0:T(8,128)S(1)} %add.25), channel_id=1, source_target_pairs={{0,16},{16,32},{32,48},{48,64},{64,80},{80,96},{96,112},{112,0},{1... | collective-permute-start | bytes 786440 | tf_op jit(solution)/shard_map/ppermute | solution.py:443
  42.8 9.0 %copy-start.10 = (f32[32,8,256]{2,1,0:T(8,128)S(1)}, f32[32,8,256]{2,1,0:T(8,128)}, u32[]{:S(2)}) copy-start(f32[32,8,256]{2,1,0:T(8,128)} %copy-done.9) | copy-start | bytes 786436
  42.8 10.2 %copy-start.8 = (f32[32,8,256]{2,1,0:T(8,128)S(1)}, f32[32,8,256]{2,1,0:T(8,128)}, u32[]{:S(2)}) copy-start(f32[32,8,256]{2,1,0:T(8,128)} %copy-done.7) | copy-start | bytes 786436
  42.9 10.2 %collective-permute-start.8 = (f32[32,8,256]{2,1,0:T(8,128)S(1)}, f32[32,8,256]{2,1,0:T(8,128)S(1)}, u32[]{:S(2)}, u32[]{:S(2)}) collective-permute-start(f32[32,8,256]{2,1,0:T(8,128)S(1)} %add.28), channel_id=1, source_target_pairs={{0,112},{16,0},{32,16},{48,32},{64,48},{80,64},{96,80},{112,96},{1... | collective-permute-start | bytes 786440 | tf_op jit(solution)/shard_map/ppermute | solution.py:447
  51.9 8.1 %collective-permute-start.5 = (f32[32,8,256]{2,1,0:T(8,128)S(1)}, f32[32,8,256]{2,1,0:T(8,128)S(1)}, u32[]{:S(2)}, u32[]{:S(2)}) collective-permute-start(f32[32,8,256]{2,1,0:T(8,128)S(1)} %add.26), channel_id=1, source_target_pairs={{0,16},{16,32},{32,48},{48,64},{64,80},{80,96},{96,112},{112,0},{1... | collective-permute-start | bytes 786440 | tf_op jit(solution)/shard_map/ppermute | solution.py:443
  53.1 7.7 %collective-permute-start.9 = (f32[32,8,256]{2,1,0:T(8,128)S(1)}, f32[32,8,256]{2,1,0:T(8,128)S(1)}, u32[]{:S(2)}, u32[]{:S(2)}) collective-permute-start(f32[32,8,256]{2,1,0:T(8,128)S(1)} %add.29), channel_id=1, source_target_pairs={{0,112},{16,0},{32,16},{48,32},{64,48},{80,64},{96,80},{112,96},{1... | collective-permute-start | bytes 786440 | tf_op jit(solution)/shard_map/ppermute | solution.py:447
  58.4 2.4 %copy-start.20 = (f32[32,8,256]{2,1,0:T(8,128)S(1)}, f32[32,8,256]{2,1,0:T(8,128)}, u32[]{:S(2)}) copy-start(f32[32,8,256]{2,1,0:T(8,128)} %copy-done.19) | copy-start | bytes 786436
  58.4 14.9 %copy-start.6 = (f32[256,256]{1,0:T(8,128)S(1)}, f32[256,256]{1,0:T(8,128)}, u32[]{:S(2)}) copy-start(f32[256,256]{1,0:T(8,128)} %constant.6.clone.table.y_table.x_table) | copy-start | bytes 786436
  58.5 14.9 %copy-start.21 = (f32[128,128]{1,0:T(8,128)S(1)}, f32[128,128]{1,0:T(8,128)}, u32[]{:S(2)}) copy-start(f32[128,128]{1,0:T(8,128)} %constant.7.clone.z_table) | copy-start | bytes 196612
  60.0 62.2 %copy-start.3 = (f32[8,256,256]{2,1,0:T(8,128)S(1)}, f32[8,256,256]{2,1,0:T(8,128)}, u32[]{:S(2)}) copy-start(f32[8,256,256]{2,1,0:T(8,128)} %refs_1_.1) | copy-start | bytes 6291460
  60.0 62.2 %copy-start.5 = (f32[256,256]{1,0:T(8,128)S(1)}, f32[256,256]{1,0:T(8,128)}, u32[]{:S(2)}) copy-start(f32[256,256]{1,0:T(8,128)} %ring_columns.1.columns.refs_2_) | copy-start | bytes 786436
  86.9 10.8 %collective-permute-start.13 = (f32[32,8,256]{2,1,0:T(8,128)S(1)}, f32[32,8,256]{2,1,0:T(8,128)S(1)}, u32[]{:S(2)}, u32[]{:S(2)}) collective-permute-start(f32[32,8,256]{2,1,0:T(8,128)S(1)} %all_to_all.11.refs_0_.refs_7_), channel_id=1, source_target_pairs={{0,16},{16,32},{32,48},{48,64},{64,80},{80,96},{96,112},{112,0},{1... | collective-permute-start | bytes 786440 | tf_op jit(solution)/shard_map/ppermute | solution.py:443
  86.9 10.8 %collective-permute-start.10 = (f32[32,8,256]{2,1,0:T(8,128)S(1)}, f32[32,8,256]{2,1,0:T(8,128)S(1)}, u32[]{:S(2)}, u32[]{:S(2)}) collective-permute-start(f32[32,8,256]{2,1,0:T(8,128)S(1)} %all_to_all.11.refs_0_.refs_7_), channel_id=1, source_target_pairs={{0,112},{16,0},{32,16},{48,32},{64,48},{80,64},{96,80},{112,96},{1... | collective-permute-start | bytes 786440 | tf_op jit(solution)/shard_map/ppermute | solution.py:447
  97.7 9.4 %collective-permute-start.14 = (f32[32,8,256]{2,1,0:T(8,128)S(1)}, f32[32,8,256]{2,1,0:T(8,128)S(1)}, u32[]{:S(2)}, u32[]{:S(2)}) collective-permute-start(f32[32,8,256]{2,1,0:T(8,128)S(1)} %collective-permute-done.13.refs_8_.refs_15_), channel_id=1, source_target_pairs={{0,16},{16,32},{32,48},{48,64},{64,80},{80,96},{96,112},{112,0},{1... | collective-permute-start | bytes 786440 | tf_op jit(solution)/shard_map/ppermute | solution.py:443
  97.7 9.4 %collective-permute-start.11 = (f32[32,8,256]{2,1,0:T(8,128)S(1)}, f32[32,8,256]{2,1,0:T(8,128)S(1)}, u32[]{:S(2)}, u32[]{:S(2)}) collective-permute-start(f32[32,8,256]{2,1,0:T(8,128)S(1)} %collective-permute-done.10.refs_1_.refs_8_), channel_id=1, source_target_pairs={{0,112},{16,0},{32,16},{48,32},{64,48},{80,64},{96,80},{112,96},{1... | collective-permute-start | bytes 786440 | tf_op jit(solution)/shard_map/ppermute | solution.py:447
  107.1 8.6 %collective-permute-start.15 = (f32[32,8,256]{2,1,0:T(8,128)S(1)}, f32[32,8,256]{2,1,0:T(8,128)S(1)}, u32[]{:S(2)}, u32[]{:S(2)}) collective-permute-start(f32[32,8,256]{2,1,0:T(8,128)S(1)} %collective-permute-done.14.refs_7_.refs_14_), channel_id=1, source_target_pairs={{0,16},{16,32},{32,48},{48,64},{64,80},{80,96},{96,112},{112,0},{1... | collective-permute-start | bytes 786440 | tf_op jit(solution)/shard_map/ppermute | solution.py:443
  107.1 8.9 %collective-permute-start.12 = (f32[32,8,256]{2,1,0:T(8,128)S(1)}, f32[32,8,256]{2,1,0:T(8,128)S(1)}, u32[]{:S(2)}, u32[]{:S(2)}) collective-permute-start(f32[32,8,256]{2,1,0:T(8,128)S(1)} %collective-permute-done.11.refs_2_.refs_9_), channel_id=1, source_target_pairs={{0,112},{16,0},{32,16},{48,32},{64,48},{80,64},{96,80},{112,96},{1... | collective-permute-start | bytes 786440 | tf_op jit(solution)/shard_map/ppermute | solution.py:447
  115.7 6.5 %collective-permute-start.16 = (f32[16,8,256]{2,1,0:T(8,128)S(1)}, f32[16,8,256]{2,1,0:T(8,128)S(1)}, u32[]{:S(2)}, u32[]{:S(2)}) collective-permute-start(f32[16,8,256]{2,1,0:T(8,128)S(1)} %slice.24), channel_id=1, source_target_pairs={{0,16},{16,32},{32,48},{48,64},{64,80},{80,96},{96,112},{112,0},{1... | collective-permute-start | bytes 393224 | tf_op jit(solution)/shard_map/ppermute | solution.py:443
  116.1 6.1 %collective-permute-start.17 = (f32[16,8,256]{2,1,0:T(8,128)S(1)}, f32[16,8,256]{2,1,0:T(8,128)S(1)}, u32[]{:S(2)}, u32[]{:S(2)}) collective-permute-start(f32[16,8,256]{2,1,0:T(8,128)S(1)} %slice.25), channel_id=1, source_target_pairs={{0,112},{16,0},{32,16},{48,32},{64,48},{80,64},{96,80},{112,96},{1... | collective-permute-start | bytes 393224 | tf_op jit(solution)/shard_map/ppermute | solution.py:447
  123.0 6.1 %collective-permute-start.19 = (f32[1,256,256]{2,1,0:T(8,128)S(1)}, f32[1,256,256]{2,1,0:T(8,128)S(1)}, u32[]{:S(2)}, u32[]{:S(2)}) collective-permute-start(f32[1,256,256]{2,1,0:T(8,128)S(1)} %get-tuple-element.41.refs_3_.refs_1_), channel_id=1, source_target_pairs={{0,15},{1,0},{2,1},{3,2},{4,3},{5,4},{6,5},{7,6},{8,7},{9,8},{10,9... | collective-permute-start | bytes 786440 | tf_op jit(solution)/shard_map/ppermute | solution.py:451
  123.1 9.5 %collective-permute-start.18 = (f32[1,256,256]{2,1,0:T(8,128)S(1)}, f32[1,256,256]{2,1,0:T(8,128)S(1)}, u32[]{:S(2)}, u32[]{:S(2)}) collective-permute-start(f32[1,256,256]{2,1,0:T(8,128)S(1)} %get-tuple-element.42.refs_4_.refs_2_), channel_id=1, source_target_pairs={{0,1},{1,2},{2,3},{3,4},{4,5},{5,6},{6,7},{7,8},{8,9},{9,10},{10,1... | collective-permute-start | bytes 786440 | tf_op jit(solution)/shard_map/ppermute | solution.py:451

commit v4 on v3

--- a/solution.py
+++ b/solution.py
@@ -53,50 +53,51 @@
 
 
 def density_kernel(scale, psi_re, psi_im, v_local, ground, y_table, *refs):
-    pieces, (near_re, near_im, to_prev, to_next) = refs[:9], refs[9:13]
-    table, own_ground, rows, rho, plane_sem, edge_sem, small_sem = refs[13:]
-    planes, ny, nx = near_re.shape
-    copies = []
+    pieces, (to_prev, to_next) = refs[:9], refs[9:11]
+    near, table, own_ground, rows, rho, plane_sem, edge_sem, small_sem = refs[11:]
+    planes = near.shape[1]
+    half = planes // 2
     small = [
         pltpu.make_async_copy(y_table, table, small_sem.at[0]),
         pltpu.make_async_copy(ground, own_ground, small_sem.at[1]),
     ]
-    for copy in small:
-        copy.start()
-    for z in range(planes):
-        pair = [
-            pltpu.make_async_copy(psi_re.at[0, z], near_re.at[z], plane_sem.at[0, z]),
-            pltpu.make_async_copy(psi_im.at[0, z], near_im.at[z], plane_sem.at[1, z]),
-        ]
-        for copy in pair:
-            copy.start()
-        copies.append(pair)
+    copies = []
+    for group in range(2):
+        some = pl.ds(group * half, half)
+        copies.append(
+            [
+                pltpu.make_async_copy(psi.at[0, some], near.at[part, some], plane_sem.at[part, group])
+                for part, psi in enumerate((psi_re, psi_im))
+            ]
+        )
     edges = []
     for which, (target, first, v_plane) in enumerate(((to_prev, 0, 0), (to_next, planes - 2, planes - 1))):
+        pair = pl.ds(first, 2)
         edges += [
-            pltpu.make_async_copy(psi_re.at[0, pl.ds(first, 2)], target.at[pl.ds(0, 2)], edge_sem.at[which, 0]),
-            pltpu.make_async_copy(psi_im.at[0, pl.ds(first, 2)], target.at[pl.ds(2, 2)], edge_sem.at[which, 1]),
+            pltpu.make_async_copy(psi_re.at[0, pair], target.at[pl.ds(0, 2)], edge_sem.at[which, 0]),
+            pltpu.make_async_copy(psi_im.at[0, pair], target.at[pl.ds(2, 2)], edge_sem.at[which, 1]),
             pltpu.make_async_copy(v_local.at[pl.ds(v_plane, 1)], target.at[pl.ds(4, 1)], edge_sem.at[which, 2]),
         ]
-    for copy in edges:
+    for copy in copies[0] + small + copies[1] + edges:
         copy.start()
-    for copy in small:
-        copy.wait()
-    fill_rows(rows, table)
     ground_rows = own_ground.shape[1]
     place = lax.axis_index("y") * lax.axis_size("z") + lax.axis_index("z")
     own = pl.ds(pl.multiple_of(place * ground_rows, ground_rows), ground_rows)
-    for z in range(planes):
-        for copy in copies[z]:
+    for group in range(2):
+        for copy in copies[group] + (small if group == 0 else []):
             copy.wait()
-        re, im = near_re[z], near_im[z]
-        rho[...] = scale * (re * re + im * im)
-        rho[own, :] = rho[own, :] - own_ground[z]
-        image = dot(rows[...], rho[...])
-        at = 0
-        for piece in pieces:
-            piece[:, z, :] = image[at : at + piece.shape[0]]
-            at += piece.shape[0]
+        if group == 0:
+            fill_rows(rows, table)
+        for z in range(group * half, (group + 1) * half):
+            re, im = near[0, z], near[1, z]
+            rho[z] = scale * (re * re + im * im)
+            rho[z, own, :] = rho[z, own, :] - own_ground[z]
+        for z in range(group * half, (group + 1) * half):
+            image = dot(rows[...], rho[z])
+            at = 0
+            for piece in pieces:
+                piece[z] = image[at : at + piece.shape[1]]
+                at += piece.shape[1]
     for copy in edges:
         copy.wait()
 
@@ -105,26 +106,44 @@
     planes, ny, nx = v_local.shape
     width = ny // lax.axis_size("z")
     heights = [width] * 4 + [width // 2] * 2 + [width] * 3
-    outs = [shaped(h, planes, nx) for h in heights] + [shaped(planes, ny, nx)] * 2 + [shaped(5, ny, nx)] * 2
+    shapes = [(planes, h, nx) for h in heights] + [(5, ny, nx)] * 2
     far = [pltpu.with_memory_space_constraint(a, pltpu.HBM) for a in (psi_re, psi_im, v_local, n_ground, y_table)]
     result = pl.pallas_call(
         functools.partial(density_kernel, 2.0 / total_orbs),
         in_specs=[ANY] * 5,
-        out_specs=[VMEM] * len(outs),
-        out_shape=outs,
+        out_specs=[VMEM] * len(shapes),
+        out_shape=[pltpu.VMEM(shape, jnp.float32) for shape in shapes],
         scratch_shapes=[
+            plane_scratch(2, planes, ny=ny, nx=nx),
             pltpu.VMEM((ny, ny), jnp.float32),
             pltpu.VMEM(n_ground.shape, jnp.float32),
             pltpu.VMEM((ny, ny), jnp.float32),
-            pltpu.VMEM((ny, nx), jnp.float32),
-            pltpu.SemaphoreType.DMA((2, planes)),
+            plane_scratch(planes, ny=ny, nx=nx),
+            pltpu.SemaphoreType.DMA((2, 2)),
             pltpu.SemaphoreType.DMA((2, 3)),
             pltpu.SemaphoreType.DMA((2,)),
         ],
-        compiler_params=pltpu.CompilerParams(vmem_limit_bytes=6 * MIB),
+        compiler_params=pltpu.CompilerParams(vmem_limit_bytes=10 * MIB),
         name="density_y",
     )(*far)
-    return result[:9], result[9], result[10], result[11], result[12]
+    return result[:9], result[9], result[10]
+
+
+def share_kernel(own, up, down, out):
+    for z in range(own.shape[0]):
+        out[:, z, :] = own[z] + up[z] + down[z]
+
+
+def add_shares(own, up, down):
+    planes, rows, nx = own.shape
+    return pl.pallas_call(
+        share_kernel,
+        in_specs=[VMEM] * 3,
+        out_specs=VMEM,
+        out_shape=shaped(rows, planes, nx),
+        compiler_params=pltpu.CompilerParams(vmem_limit_bytes=4 * MIB),
+        name="add_shares",
+    )(own, up, down)
 
 
 def wave_sq(freq_index, length):
@@ -252,34 +271,24 @@
     )(sides, *near, *onces)
 
 
-def columns_kernel(table, out, rows):
-    fill_rows(rows, table)
-    out[...] = rows[...].T
-
-
-def ring_columns(y_table):
-    return pl.pallas_call(
-        columns_kernel,
-        in_specs=[VMEM],
-        out_specs=VMEM,
-        out_shape=shaped(*y_table.shape),
-        scratch_shapes=[pltpu.VMEM(y_table.shape, jnp.float32)],
-        name="ring_columns",
-    )(y_table)
+def ring_columns(table):
+    ny = table.shape[1]
+    return pltpu.roll(table[...], ny - lax.axis_index("z") * (ny // lax.axis_size("z")), 1)
 
 
 def potential_plane(v_local, columns, hats, z):
     hat = jnp.concatenate([h[:, z, :] for h in hats], axis=0)
-    return v_local[z] + dot(columns[...], hat)
-
-
-def outer_kernel(v_local, columns, *refs):
+    return v_local[z] + dot(columns, hat)
+
+
+def outer_kernel(v_local, table, *refs):
     hats, (first, last) = refs[:-2], refs[-2:]
+    columns = ring_columns(table)
     first[0] = potential_plane(v_local, columns, hats, 0)
     last[0] = potential_plane(v_local, columns, hats, v_local.shape[0] - 1)
 
 
-def outer_potential(v_local, columns, hats):
+def outer_potential(v_local, table, hats):
     planes, ny, nx = v_local.shape
     return pl.pallas_call(
         outer_kernel,
@@ -288,33 +297,48 @@
         out_shape=[shaped(1, ny, nx)] * 2,
         compiler_params=pltpu.CompilerParams(vmem_limit_bytes=6 * MIB),
         name="outer_potential",
-    )(v_local, columns, *hats)
-
-
-def update_plane(at_w, at_once, at_base, local, sides, stage, slot, z):
-    here = whole(local)
-    mid_re, kin_re = kinetic(at_w(0, z - 1), at_w(0, z), at_w(0, z + 1), sides)
-    mid_im, kin_im = kinetic(at_w(1, z - 1), at_w(1, z), at_w(1, z + 1), sides)
-    second_re = kin_re + here * (whole(at_once(0, z)) + mid_re)
-    second_im = kin_im + here * (whole(at_once(1, z)) + mid_im)
-    stage[0, slot] = whole(at_base(0, z)) + TIME_STEP * mid_im - HALF_SQ * second_re
-    stage[1, slot] = whole(at_base(1, z)) - TIME_STEP * mid_re - HALF_SQ * second_im
+    )(v_local, table, *hats)
 
 
 def inner_kernel(once_groups, base_groups, hat_count, *refs):
     refs = list(refs)
-    sides, v_local, columns, v_first, v_last, re, im = [refs.pop(0) for _ in range(7)]
+    sides, v_local, table, v_first, v_last, re, im = [refs.pop(0) for _ in range(7)]
     hats = [refs.pop(0) for _ in range(hat_count)]
     onces = [refs.pop(0) for _ in once_groups]
     bases = [refs.pop(0) for _ in base_groups]
-    out_re, out_im, v_kept, pot, work, stage, sem = refs
-    planes, ny, _ = re.shape
+    out_re, out_im, open_ends, pot, work, stage, sem = refs
+    planes = re.shape[0]
     fields = (re, im)
-
-    def at_w(part, z):
-        return (work, (part, z))
+    columns = ring_columns(table)
+    at_once = functools.partial(once_plane, once_groups, onces)
+    at_base = functools.partial(once_plane, base_groups, bases)
+    work[:, 0] = jnp.zeros_like(work[:, 0])
+    work[:, planes + 1] = jnp.zeros_like(work[:, planes + 1])
+
+    def update_plane(z):
+        here = pot[z]
+        mids, seconds = [], []
+        for part in range(2):
+            mid, kin = kinetic((work, (part, z)), (work, (part, z + 1)), (work, (part, z + 2)), sides)
+            mids.append(mid)
+            seconds.append(kin + here * (whole(at_once(part, z)) + mid))
+        new_re = whole(at_base(0, z)) + TIME_STEP * mids[1] - HALF_SQ * seconds[0]
+        new_im = whole(at_base(1, z)) - TIME_STEP * mids[0] - HALF_SQ * seconds[1]
+        return new_re, new_im
 
     copies = []
+
+    def finish(z):
+        new = update_plane(z)
+        for part, out in enumerate((out_re, out_im)):
+            if z in (0, planes - 1):
+                open_ends[part, 0 if z == 0 else 1] = new[part]
+            else:
+                stage[part, z - 1] = new[part]
+                copy = pltpu.make_async_copy(stage.at[part, z - 1], out.at[0, z], sem.at[part, z - 1])
+                copy.start()
+                copies.append(copy)
+
     for z in range(planes):
         if z == 0:
             here = v_first[0]
@@ -322,43 +346,28 @@
             here = v_last[0]
         else:
             here = potential_plane(v_local, columns, hats, z)
-            pot[z] = here
+        pot[z] = here
         for part in range(2):
-            work[part, z] = here * fields[part][z]
-        if z >= 2:
-            done = z - 1
-            update_plane(
-                at_w,
-                functools.partial(once_plane, once_groups, onces),
-                functools.partial(once_plane, base_groups, bases),
-                (pot, (done,)),
-                sides,
-                stage,
-                done - 1,
-                done,
-            )
-            for part, out in enumerate((out_re, out_im)):
-                copy = pltpu.make_async_copy(stage.at[part, done - 1], out.at[0, done], sem.at[part, done - 1])
-                copy.start()
-                copies.append(copy)
-    v_kept[0] = pot[1]
-    v_kept[1] = pot[planes - 2]
+            work[part, z + 1] = here * fields[part][z]
+        if z >= 1:
+            finish(z - 1)
+    finish(planes - 1)
     for copy in copies:
         copy.wait()
 
 
-def inner_update(sides, v_local, columns, v_first, v_last, near, hats, onces, once_groups, bases, base_groups):
+def inner_update(sides, v_local, table, v_first, v_last, near, hats, onces, once_groups, bases, base_groups):
     planes, ny, nx = v_local.shape
-    operands = [sides, v_local, columns, v_first, v_last, *near, *hats, *onces, *bases]
+    operands = [sides, v_local, table, v_first, v_last, *near, *hats, *onces, *bases]
     full = shaped(1, planes, ny, nx)
     return pl.pallas_call(
         functools.partial(inner_kernel, once_groups, base_groups, len(hats)),
         in_specs=[VMEM] * len(operands),
         out_specs=[ANY, ANY, VMEM],
-        out_shape=[full, full, shaped(2, ny, nx)],
+        out_shape=[full, full, shaped(2, 2, ny, nx)],
         scratch_shapes=[
             plane_scratch(planes, ny=ny, nx=nx),
-            plane_scratch(2, planes, ny=ny, nx=nx),
+            plane_scratch(2, planes + 2, ny=ny, nx=nx),
             plane_scratch(2, planes - 2, ny=ny, nx=nx),
             pltpu.SemaphoreType.DMA((2, planes - 2)),
         ],
@@ -368,46 +377,13 @@
     )(*operands)
 
 
-def outer_kernel_update(once_groups, base_groups, *refs):
-    refs = list(refs)
-    sides, v_first, v_last, v_before, v_after, v_kept, re, im, low, high = [refs.pop(0) for _ in range(10)]
-    onces = [refs.pop(0) for _ in once_groups]
-    bases = [refs.pop(0) for _ in base_groups]
-    _, _, out_re, out_im, work, stage, sem = refs
-    planes = re.shape[0]
-    at_psi = functools.partial(psi_plane, (re, im), low, high, planes)
-    locals_of = {
-        -1: (v_before, (0,)),
-        0: (v_first, (0,)),
-        1: (v_kept, (0,)),
-        planes - 2: (v_kept, (1,)),
-        planes - 1: (v_last, (0,)),
-        planes: (v_after, (0,)),
-    }
-    order = list(locals_of)
-
-    def at_w(part, z):
-        return (work, (part, order.index(z)))
-
+def close_kernel(open_ends, v_before, v_after, low, high, _re, _im, out_re, out_im, stage, sem):
+    planes = out_re.shape[1]
     copies = []
-    for slot, z in enumerate((0, planes - 1)):
-        for near in (z - 1, z, z + 1):
-            ref, lead = locals_of[near]
-            here = ref[lead]
-            for part in range(2):
-                source, where = at_psi(part, near)
-                work[part, order.index(near)] = here * source[where]
-        update_plane(
-            at_w,
-            functools.partial(once_plane, once_groups, onces),
-            functools.partial(once_plane, base_groups, bases),
-            locals_of[z],
-            sides,
-            stage,
-            slot,
-            z,
-        )
+    for slot, (z, v_ref, edge, first) in enumerate(((0, v_before, low, 1), (planes - 1, v_after, high, 0))):
         for part, out in enumerate((out_re, out_im)):
+            beyond = v_ref[0] * edge[2 * part + first]
+            stage[part, slot] = open_ends[part, slot] - (HALF_SQ * KINETIC) * beyond
             copy = pltpu.make_async_copy(stage.at[part, slot], out.at[0, z], sem.at[part, slot])
             copy.start()
             copies.append(copy)
@@ -415,23 +391,18 @@
         copy.wait()
 
 
-def outer_update(sides, new_re, new_im, v_planes, near, edges, onces, once_groups, bases, base_groups):
-    planes, ny, nx = near[0].shape
-    operands = [sides, *v_planes, *near, *edges, *onces, *bases]
-    return pl.pallas_call(
-        functools.partial(outer_kernel_update, once_groups, base_groups),
-        in_specs=[VMEM] * len(operands) + [ANY, ANY],
+def close_ends(new_re, new_im, open_ends, v_before, v_after, edges):
+    _, _, ny, nx = open_ends.shape
+    return pl.pallas_call(
+        close_kernel,
+        in_specs=[VMEM] * 5 + [ANY, ANY],
         out_specs=[ANY, ANY],
         out_shape=[shaped(*new_re.shape)] * 2,
-        input_output_aliases={len(operands): 0, len(operands) + 1: 1},
-        scratch_shapes=[
-            plane_scratch(2, 6, ny=ny, nx=nx),
-            plane_scratch(2, 2, ny=ny, nx=nx),
-            pltpu.SemaphoreType.DMA((2, 2)),
-        ],
-        compiler_params=pltpu.CompilerParams(vmem_limit_bytes=8 * MIB),
-        name="outer_update",
-    )(*operands, new_re, new_im)
+        input_output_aliases={5: 0, 6: 1},
+        scratch_shapes=[plane_scratch(2, 2, ny=ny, nx=nx), pltpu.SemaphoreType.DMA((2, 2))],
+        compiler_params=pltpu.CompilerParams(vmem_limit_bytes=4 * MIB),
+        name="close_ends",
+    )(open_ends, v_before, v_after, *edges, new_re, new_im)
 
 
 def ring(axis, shift):
@@ -457,24 +428,25 @@
 
 def sum_over_ring(pieces, beside):
     s0, s1, s2, s3, s4_first, s4_second, s5, s6, s7 = pieces
-    half = s4_first.shape[0]
+    half = s4_first.shape[1]
     got_up, got_down = forward(s4_first), backward(s4_second)
-    got_up = after(got_up, *beside[0])
-    up = jnp.concatenate([s3[:half] + got_up, s3[half:]], axis=0)
-    down = jnp.concatenate([s5[:half], s5[half:] + got_down], axis=0)
+    up = jnp.concatenate([s3[:, :half] + got_up, s3[:, half:]], axis=1)
+    down = jnp.concatenate([s5[:, :half], s5[:, half:] + got_down], axis=1)
     up, down = forward(up), backward(down)
+    up = after(up, *beside[0])
+    up, down = forward(up + s2), backward(down + s6)
     up = after(up, *beside[1])
-    up, down = forward(up + s2), backward(down + s6)
+    up, down = forward(up + s1), backward(down + s7)
     up = after(up, *beside[2])
-    up, down = forward(up + s1), backward(down + s7)
-    up = after(up, *beside[3])
-    return up + down + s0
-
-
-def gather_over_ring(block):
+    return add_shares(s0, up, down)
+
+
+def gather_over_ring(block, beside):
     half = block.shape[0] // 2
     up1, down1 = forward(block), backward(block)
+    up1 = after(up1, *beside[0])
     up2, down2 = forward(up1), backward(down1)
+    up2 = after(up2, *beside[1])
     up3, down3 = forward(up2), backward(down2)
     up4, down4 = forward(up3[:half]), backward(down3[half:])
     return [block, down1, down2, down3, up4, down4, up3, up2, up1]
@@ -490,8 +462,8 @@
     nz = planes * lax.axis_size("slab")
     y_table, x_table, z_table = cas_table(ny), cas_table(nx), cas_table(nz)
 
-    pieces, near_re, near_im, to_prev, to_next = density(psi_re, psi_im, v_local, n_ground, y_table, total_orbs)
-    near = (near_re, near_im)
+    pieces, to_prev, to_next = density(psi_re, psi_im, v_local, n_ground, y_table, total_orbs)
+    near = (psi_re[0], psi_im[0])
     low, high = slab_shift(to_next, 1), slab_shift(to_prev, -1)
     edges = (low, high)
 
@@ -507,20 +479,16 @@
     bases = [
         base(sides, near, onces, once_groups, group, name) for group, name in zip(base_groups, ("base_a", "base_b"))
     ]
-    columns = ring_columns(y_table)
-
-    beside = ((onces[0], columns), (onces[1],), (onces[2],), tuple(bases))
-    share = sum_over_ring(pieces, beside)
+    share = sum_over_ring(pieces, [[onces[0]], [onces[1]], [onces[2]]])
     pencils = across(share).reshape(SIDES * nz, nx)
-    hats = gather_over_ring(across(solve(pencils, x_table, z_table, ny, planes)))
-
-    v_first, v_last = outer_potential(v_local, columns, hats)
+    hats = gather_over_ring(across(solve(pencils, x_table, z_table, ny, planes)), [[bases[0]], [bases[1]]])
+
+    v_first, v_last = outer_potential(v_local, y_table, hats)
     v_before, v_after = slab_shift(v_last, 1), slab_shift(v_first, -1)
-    new_re, new_im, v_kept = inner_update(
-        sides, v_local, columns, v_first, v_last, near, hats, onces, once_groups, bases, base_groups
+    new_re, new_im, open_ends = inner_update(
+        sides, v_local, y_table, v_first, v_last, near, hats, onces, once_groups, bases, base_groups
     )
-    v_planes = (v_first, v_last, v_before, v_after, v_kept)
-    return tuple(outer_update(sides, new_re, new_im, v_planes, near, edges, onces, once_groups, bases, base_groups))
+    return tuple(close_ends(new_re, new_im, open_ends, v_before, v_after, edges))
 
 
 def solution(mesh):

time: 137 us -> 118 us (0.86)
  Pallas kernels: 29.8 us -> 20.7 us
  local copies, waits for them, and re-layouts: 7.95 us -> 0.06 us
  other arithmetic: 2.24 us -> 0.26 us
  blocking collectives: 24.8 us -> 26.2 us
    ppermute x8, waiting for transfers between devices: 2.42 us -> 10.9 us  [backward(): return lax.ppermute(value, axis, ring(axis, -1))]
    ppermute x8, waiting for transfers between devices: 27.2 us -> 19.1 us  [forward(): return lax.ppermute(value, axis, ring(axis, 1))]
    unnamed x44 -> x12, local copies, waits for them, and re-layouts: 7.93 us -> 0.04 us
    pallas_call x1, Pallas kernels: 9.9 us -> 5.61 us  [density(): pl.pallas_call(functools.partial(density_kernel, 2.0 / total_orbs), in_sp...]
    pallas_call x2, Pallas kernels: 4.92 us -> 1.13 us  [the longest x1 1.04 us: close_ends(): pl.pallas_call(close_kernel, in_specs=[VMEM] * 5 + [ANY, ANY], out_specs=...]
    all_to_all x2, blocking collectives: 24.8 us -> 26.2 us  [across(): lax.all_to_all(value, ('y', 'slab'), split_axis=0, concat_axis=0, tiled=T...]
  transfers between devices with their start and end apart: 20 -> 20, of which waited for: 10 -> 9; matrix products, arithmetic and copies ran while one was open for 2% -> 0% of each run, Pallas kernels for 11% -> 10%
where the time goes in v4:
time: 118 us
  starting transfers between devices  36.7 us (31%)
  waiting for transfers between devices  33.3 us (28%)
  blocking collectives  26.2 us (22%)
  Pallas kernels  20.7 us (18%)
    ppermute x8, starting transfers between devices, backward(): return lax.ppermute(value, axis, ring(axis, -1))  28.2 us
    all_to_all x2, blocking collectives, across(): lax.all_to_all(value, ('y', 'slab'), split_axis=0, concat_axis=0, tiled=T...  26.2 us
    ppermute x8, waiting for transfers between devices, forward(): return lax.ppermute(value, axis, ring(axis, 1))  19.1 us
    ppermute x8, waiting for transfers between devices, backward(): return lax.ppermute(value, axis, ring(axis, -1))  10.9 us
    ppermute x4, starting transfers between devices, slab_shift(): return lax.ppermute(value, 'slab', ring('slab', shift))  5.94 us
    pallas_call x1, Pallas kernels, inner_update(): pl.pallas_call(functools.partial(inner_kernel, once_groups, base_groups,...  5.75 us
    pallas_call x1, Pallas kernels, density(): pl.pallas_call(functools.partial(density_kernel, 2.0 / total_orbs), in_sp...  5.61 us
    ppermute x4, waiting for transfers between devices, slab_shift(): return lax.ppermute(value, 'slab', ring('slab', shift))  3.23 us
  transfers between devices with their start and end apart: 20, of which 9 were waited for; matrix products, arithmetic and copies ran while one was open for 0% of the time, Pallas kernels for 10%

profile of v4, /device:TPU:8, one launch (start us, length us, event | category | flops | bytes accessed | tf_op | source)
XLA Modules:
  0.0 118.2 jit_solution(13603629299644682170)
XLA Ops:
  0.6 5.6 %density_y.1 = (f32[8,32,256]{2,1,0:T(8,128)S(1)}, f32[8,32,256]{2,1,0:T(8,128)S(1)}, f32[8,32,256]{2,1,0:T(8,128)S(1)}, f32[8,32,256]{2,1,0:T(8,128)S(1)}, f32[...) custom-call(f32[1,8,256,256]{3,2,1,0:T(8,128)} %psi_re.1, ...), custom_call_target="tpu_custom_call" | custom-call | tf_op jit(solution)/shard_map/density_y/pallas_call | solution.py:111
  6.3 0.0 copy-start
  6.3 0.0 copy-start.3
  6.3 2.0 %collective-permute-start = (f32[8,16,256]{2,1,0:T(8,128)S(1)}, f32[8,16,256]{2,1,0:T(8,128)S(1)}, u32[]{:S(2)}, u32[]{:S(2)}) collective-permute-start(f32[8,16,256]{2,1,0:T(8,128)S(1)} %get-tuple-element.25), channel_id=1, source_target_pairs={{0,16},{16,32},{32,48},{48,64},{64,80},{80,96},{96,112},{112,0},{1... | collective-permute-start | bytes 393224 | tf_op jit(solution)/shard_map/ppermute | solution.py:414
  8.3 4.0 %collective-permute-start.6 = (f32[8,16,256]{2,1,0:T(8,128)S(1)}, f32[8,16,256]{2,1,0:T(8,128)S(1)}, u32[]{:S(2)}, u32[]{:S(2)}) collective-permute-start(f32[8,16,256]{2,1,0:T(8,128)S(1)} %get-tuple-element.34), channel_id=1, source_target_pairs={{0,112},{16,0},{32,16},{48,32},{64,48},{80,64},{96,80},{112,96},{1... | collective-permute-start | bytes 393224 | tf_op jit(solution)/shard_map/ppermute | solution.py:418
  12.3 5.4 %collective-permute-start.5 = (f32[5,256,256]{2,1,0:T(8,128)S(1)}, f32[5,256,256]{2,1,0:T(8,128)S(1)}, u32[]{:S(2)}, u32[]{:S(2)}) collective-permute-start(f32[5,256,256]{2,1,0:T(8,128)S(1)} %get-tuple-element.31), channel_id=1, source_target_pairs={{0,15},{1,0},{2,1},{3,2},{4,3},{5,4},{6,5},{7,6},{8,7},{9,8},{10,9... | collective-permute-start | bytes 3932168 | tf_op jit(solution)/shard_map/ppermute | solution.py:422
  17.7 0.0 collective-permute-done
  17.7 0.1 collective-permute-start.1
  17.9 3.3 %collective-permute-start.7 = (f32[8,32,256]{2,1,0:T(8,128)S(1)}, f32[8,32,256]{2,1,0:T(8,128)S(1)}, u32[]{:S(2)}, u32[]{:S(2)}) collective-permute-start(f32[8,32,256]{2,1,0:T(8,128)S(1)} %pad_maximum_fusion.1), channel_id=1, source_target_pairs={{0,112},{16,0},{32,16},{48,32},{64,48},{80,64},{96,80},{112,96},{1... | collective-permute-start | bytes 786440 | tf_op jit(solution)/shard_map/ppermute | solution.py:418
  21.2 0.9 once_a.1.refs_0_.refs_16_
  22.1 3.3 %collective-permute-done.1 = f32[8,32,256]{2,1,0:T(8,128)S(1)} collective-permute-done((f32[8,32,256]{2,1,0:T(8,128)S(1)}, f32[8,32,256]{2,1,0:T(8,128)S(1)}, u32[]{:S(2)}, u32[]{:S(2)}) %collective-permute-start.1) | collective-permute-done | bytes 262176 | tf_op jit(solution)/shard_map/ppermute | solution.py:414
  25.4 0.1 collective-permute-start.2
  25.5 0.0 collective-permute-done.7
  25.6 3.3 %collective-permute-start.8 = (f32[8,32,256]{2,1,0:T(8,128)S(1)}, f32[8,32,256]{2,1,0:T(8,128)S(1)}, u32[]{:S(2)}, u32[]{:S(2)}) collective-permute-start(f32[8,32,256]{2,1,0:T(8,128)S(1)} %add.22), channel_id=1, source_target_pairs={{0,112},{16,0},{32,16},{48,32},{64,48},{80,64},{96,80},{112,96},{1... | collective-permute-start | bytes 786440 | tf_op jit(solution)/shard_map/ppermute | solution.py:418
  28.9 0.9 once_b.1.refs_1_.refs_17_
  29.8 3.7 %collective-permute-done.2 = f32[8,32,256]{2,1,0:T(8,128)S(1)} collective-permute-done((f32[8,32,256]{2,1,0:T(8,128)S(1)}, f32[8,32,256]{2,1,0:T(8,128)S(1)}, u32[]{:S(2)}, u32[]{:S(2)}) %collective-permute-start.2) | collective-permute-done | bytes 262176 | tf_op jit(solution)/shard_map/ppermute | solution.py:414
  33.5 0.1 collective-permute-start.3
  33.7 0.0 copy-start.4
  33.7 0.0 copy-start.5
  33.7 3.6 %collective-permute-start.9 = (f32[8,32,256]{2,1,0:T(8,128)S(1)}, f32[8,32,256]{2,1,0:T(8,128)S(1)}, u32[]{:S(2)}, u32[]{:S(2)}) collective-permute-start(f32[8,32,256]{2,1,0:T(8,128)S(1)} %add.23), channel_id=1, source_target_pairs={{0,112},{16,0},{32,16},{48,32},{64,48},{80,64},{96,80},{112,96},{1... | collective-permute-start | bytes 786440 | tf_op jit(solution)/shard_map/ppermute | solution.py:418
  37.3 0.0 collective-permute-done.5.refs_3_.high
  37.3 1.2 %once_c.1.refs_2_.refs_18_ = f32[2,4,256,256]{3,2,1,0:T(8,128)S(1)} custom-call(bf16[256,256]{1,0:T(8,128)(2,1)S(1)} %copy-done.3, f32[8,256,256]{2,1,0:T(8,128)S(1)} %bitcast.5, f32[8,256,256]{2,1,0:T(8,128)S(1)} %bitcast.11, f32[5,256,256]{2,1,0:T(8,128)S(1)} %collective-permute-done.4.refs_2_.low, f32[5,256,256]{2,1,0:T(8,128)S(1)} %collective-permute-done.5.refs_3_.high), custom_call_target="tpu_custom_call" | custom-call | flops 26214400 | bytes 2097152 | tf_op jit(solution)/shard_map/once_c/pallas_call | solution.py:234
  38.5 2.7 %collective-permute-done.3.up = f32[8,32,256]{2,1,0:T(8,128)S(1)} collective-permute-done((f32[8,32,256]{2,1,0:T(8,128)S(1)}, f32[8,32,256]{2,1,0:T(8,128)S(1)}, u32[]{:S(2)}, u32[]{:S(2)}) %collective-permute-start.3) | collective-permute-done | bytes 262176 | tf_op jit(solution)/shard_map/ppermute | solution.py:414
  41.2 0.1 add_shares.1
  41.3 13.9 %all_to_all.10 = f32[32,8,256]{2,1,0:T(8,128)S(1)} all-to-all(f32[32,8,256]{2,1,0:T(8,128)S(1)} %add_shares.1), channel_id=1, replica_groups=mesh['y'=2,'z'=8,'slab'=16] {'y','slab'}, dimensions={0} | all-to-all | bytes 524288 | tf_op jit(solution)/shard_map/all_to_all | solution.py:456
  55.2 1.3 %solve_xz.1 = f32[32,8,256]{2,1,0:T(8,128)S(1)} custom-call(f32[256,256]{1,0:T(8,128)S(1)} %bitcast.15, f32[256,256]{1,0:T(8,128)S(1)} %copy-done.4, f32[128,128]{1,0:T(8,128)S(1)} %copy-done.5), custom_call_target="tpu_custom_call" | custom-call | tf_op jit(solution)/shard_map/solve_xz/pallas_call | solution.py:177
  56.5 12.3 %all_to_all.11.refs_0_.refs_7_ = f32[32,8,256]{2,1,0:T(8,128)S(1)} all-to-all(f32[32,8,256]{2,1,0:T(8,128)S(1)} %solve_xz.1), channel_id=1, replica_groups=mesh['y'=2,'z'=8,'slab'=16] {'y','slab'}, dimensions={0} | all-to-all | bytes 524288 | tf_op jit(solution)/shard_map/all_to_all | solution.py:456
  68.8 3.6 %collective-permute-start.10 = (f32[32,8,256]{2,1,0:T(8,128)S(1)}, f32[32,8,256]{2,1,0:T(8,128)S(1)}, u32[]{:S(2)}, u32[]{:S(2)}) collective-permute-start(f32[32,8,256]{2,1,0:T(8,128)S(1)} %all_to_all.11.refs_0_.refs_7_), channel_id=1, source_target_pairs={{0,112},{16,0},{32,16},{48,32},{64,48},{80,64},{96,80},{112,96},{1... | collective-permute-start | bytes 786440 | tf_op jit(solution)/shard_map/ppermute | solution.py:418
  72.4 1.5 %base_a.1.refs_19_ = f32[2,4,256,256]{3,2,1,0:T(8,128)S(1)} custom-call(bf16[256,256]{1,0:T(8,128)(2,1)S(1)} %copy-done.3, f32[8,256,256]{2,1,0:T(8,128)S(1)} %bitcast.6, f32[8,256,256]{2,1,0:T(8,128)S(1)} %bitcast.12, f32[2,3,256,256]{3,2,1,0:T(8,128)S(1)} %once_a.1.refs_0_.refs_16_, f32[2,3,256,256]{3,2,1,0:T(8,128)S(1)} %once_b.1.refs_1_.refs_17_, ...), custom_call_target="tpu_custom_call" | custom-call | flops 26214400 | bytes 2097152 | tf_op jit(solution)/shard_map/base_a/pallas_call | solution.py:263
  73.9 0.0 copy-start.2
  73.9 5.5 %collective-permute-done.13.refs_8_.refs_15_ = f32[32,8,256]{2,1,0:T(8,128)S(1)} collective-permute-done((f32[32,8,256]{2,1,0:T(8,128)S(1)}, f32[32,8,256]{2,1,0:T(8,128)S(1)}, u32[]{:S(2)}, u32[]{:S(2)}) %collective-permute-start.13) | collective-permute-done | bytes 262176 | tf_op jit(solution)/shard_map/ppermute | solution.py:414
  79.4 0.0 collective-permute-done.10.refs_1_.refs_8_
  79.5 3.0 %collective-permute-start.11 = (f32[32,8,256]{2,1,0:T(8,128)S(1)}, f32[32,8,256]{2,1,0:T(8,128)S(1)}, u32[]{:S(2)}, u32[]{:S(2)}) collective-permute-start(f32[32,8,256]{2,1,0:T(8,128)S(1)} %collective-permute-done.10.refs_1_.refs_8_), channel_id=1, source_target_pairs={{0,112},{16,0},{32,16},{48,32},{64,48},{80,64},{96,80},{112,96},{1... | collective-permute-start | bytes 786440 | tf_op jit(solution)/shard_map/ppermute | solution.py:418
  82.4 1.5 %base_b.1.refs_20_ = f32[2,4,256,256]{3,2,1,0:T(8,128)S(1)} custom-call(bf16[256,256]{1,0:T(8,128)(2,1)S(1)} %copy-done.3, f32[8,256,256]{2,1,0:T(8,128)S(1)} %bitcast.7, f32[8,256,256]{2,1,0:T(8,128)S(1)} %bitcast.13, f32[2,3,256,256]{3,2,1,0:T(8,128)S(1)} %once_a.1.refs_0_.refs_16_, f32[2,3,256,256]{3,2,1,0:T(8,128)S(1)} %once_b.1.refs_1_.refs_17_, ...), custom_call_target="tpu_custom_call" | custom-call | flops 26214400 | bytes 2097152 | tf_op jit(solution)/shard_map/base_b/pallas_call | solution.py:263
  83.9 4.0 %collective-permute-done.11.refs_2_.refs_9_ = f32[32,8,256]{2,1,0:T(8,128)S(1)} collective-permute-done((f32[32,8,256]{2,1,0:T(8,128)S(1)}, f32[32,8,256]{2,1,0:T(8,128)S(1)}, u32[]{:S(2)}, u32[]{:S(2)}) %collective-permute-start.11) | collective-permute-done | bytes 262176 | tf_op jit(solution)/shard_map/ppermute | solution.py:418
  88.0 3.7 %collective-permute-start.12 = (f32[32,8,256]{2,1,0:T(8,128)S(1)}, f32[32,8,256]{2,1,0:T(8,128)S(1)}, u32[]{:S(2)}, u32[]{:S(2)}) collective-permute-start(f32[32,8,256]{2,1,0:T(8,128)S(1)} %collective-permute-done.11.refs_2_.refs_9_), channel_id=1, source_target_pairs={{0,112},{16,0},{32,16},{48,32},{64,48},{80,64},{96,80},{112,96},{1... | collective-permute-start | bytes 786440 | tf_op jit(solution)/shard_map/ppermute | solution.py:418
  91.7 0.0 collective-permute-done.14.refs_7_.refs_14_
  91.7 4.7 %collective-permute-done.12.refs_3_.refs_10_ = f32[32,8,256]{2,1,0:T(8,128)S(1)} collective-permute-done((f32[32,8,256]{2,1,0:T(8,128)S(1)}, f32[32,8,256]{2,1,0:T(8,128)S(1)}, u32[]{:S(2)}, u32[]{:S(2)}) %collective-permute-start.12) | collective-permute-done | bytes 262176 | tf_op jit(solution)/shard_map/ppermute | solution.py:418
  96.3 3.8 %collective-permute-start.17 = (f32[16,8,256]{2,1,0:T(8,128)S(1)}, f32[16,8,256]{2,1,0:T(8,128)S(1)}, u32[]{:S(2)}, u32[]{:S(2)}) collective-permute-start(f32[16,8,256]{2,1,0:T(8,128)S(1)} %slice.25), channel_id=1, source_target_pairs={{0,112},{16,0},{32,16},{48,32},{64,48},{80,64},{96,80},{112,96},{1... | collective-permute-start | bytes 393224 | tf_op jit(solution)/shard_map/ppermute | solution.py:418
  100.1 0.3 collective-permute-start.16
  100.4 2.2 %collective-permute-done.17.refs_5_.refs_12_ = f32[16,8,256]{2,1,0:T(8,128)S(1)} collective-permute-done((f32[16,8,256]{2,1,0:T(8,128)S(1)}, f32[16,8,256]{2,1,0:T(8,128)S(1)}, u32[]{:S(2)}, u32[]{:S(2)}) %collective-permute-start.17) | collective-permute-done | bytes 131104 | tf_op jit(solution)/shard_map/ppermute | solution.py:418
  102.6 4.0 %collective-permute-done.16.refs_4_.refs_11_ = f32[16,8,256]{2,1,0:T(8,128)S(1)} collective-permute-done((f32[16,8,256]{2,1,0:T(8,128)S(1)}, f32[16,8,256]{2,1,0:T(8,128)S(1)}, u32[]{:S(2)}, u32[]{:S(2)}) %collective-permute-start.16) | collective-permute-done | bytes 131104 | tf_op jit(solution)/shard_map/ppermute | solution.py:414
  106.6 0.8 outer_potential.1
  107.4 0.1 collective-permute-start.19
  107.5 0.5 collective-permute-start.18
  108.0 5.7 %inner_update.1 = (f32[1,8,256,256]{3,2,1,0:T(8,128)}, f32[1,8,256,256]{3,2,1,0:T(8,128)}, f32[2,2,256,256]{3,2,1,0:T(8,128)S(1)}) custom-call(bf16[256,256]{1,0:T(8,128)(2,1)S(1)} %copy-done.3, f32[8,256,256]{2,1,0:T(8,128)S(1)} %copy-done.2, f32[256,256]{1,0:T(8,128)S(1)} %copy-done.4, f32[1,256,256]{2,1,0:T(8,128)S(1)} %get-tuple-element.39.refs_3_, ...), custom_call_target="tpu_custom_call" | custom-call | flops 209715200 | bytes 4194304 | tf_op jit(solution)/shard_map/inner_update/pallas_call | solution.py:363
  113.8 3.2 %collective-permute-done.18.v_before = f32[1,256,256]{2,1,0:T(8,128)S(1)} collective-permute-done((f32[1,256,256]{2,1,0:T(8,128)S(1)}, f32[1,256,256]{2,1,0:T(8,128)S(1)}, u32[]{:S(2)}, u32[]{:S(2)}) %collective-permute-start.18) | collective-permute-done | bytes 262176 | tf_op jit(solution)/shard_map/ppermute | solution.py:422
  117.0 1.0 close_ends.1
  (27 shorter events, 0.3 us)
Async XLA Ops:
  0.6 20.6 %copy-start.1 = (f32[1,8,256,256]{3,2,1,0:T(8,128)S(1)}, f32[1,8,256,256]{3,2,1,0:T(8,128)}, u32[]{:S(2)}) copy-start(f32[1,8,256,256]{3,2,1,0:T(8,128)} %psi_im.1) | copy-start | bytes 6291460
  6.3 14.9 %copy-start = (f32[1,8,256,256]{3,2,1,0:T(8,128)S(1)}, f32[1,8,256,256]{3,2,1,0:T(8,128)}, u32[]{:S(2)}) copy-start(f32[1,8,256,256]{3,2,1,0:T(8,128)} %psi_re.1) | copy-start | bytes 6291460
  6.3 14.9 %copy-start.3 = (bf16[256,256]{1,0:T(8,128)(2,1)S(1)}, bf16[256,256]{1,0:T(8,128)(2,1)}, u32[]{:S(2)}) copy-start(bf16[256,256]{1,0:T(8,128)(2,1)} %constant.8.clone.sides.refs_0_) | copy-start | bytes 393220
  6.3 11.4 %collective-permute-start = (f32[8,16,256]{2,1,0:T(8,128)S(1)}, f32[8,16,256]{2,1,0:T(8,128)S(1)}, u32[]{:S(2)}, u32[]{:S(2)}) collective-permute-start(f32[8,16,256]{2,1,0:T(8,128)S(1)} %get-tuple-element.25), channel_id=1, source_target_pairs={{0,16},{16,32},{32,48},{48,64},{64,80},{80,96},{96,112},{112,0},{1... | collective-permute-start | bytes 393224 | tf_op jit(solution)/shard_map/ppermute | solution.py:414
  8.3 9.6 %collective-permute-start.6 = (f32[8,16,256]{2,1,0:T(8,128)S(1)}, f32[8,16,256]{2,1,0:T(8,128)S(1)}, u32[]{:S(2)}, u32[]{:S(2)}) collective-permute-start(f32[8,16,256]{2,1,0:T(8,128)S(1)} %get-tuple-element.34), channel_id=1, source_target_pairs={{0,112},{16,0},{32,16},{48,32},{64,48},{80,64},{96,80},{112,96},{1... | collective-permute-start | bytes 393224 | tf_op jit(solution)/shard_map/ppermute | solution.py:418
  12.3 25.0 %collective-permute-start.4 = (f32[5,256,256]{2,1,0:T(8,128)S(1)}, f32[5,256,256]{2,1,0:T(8,128)S(1)}, u32[]{:S(2)}, u32[]{:S(2)}) collective-permute-start(f32[5,256,256]{2,1,0:T(8,128)S(1)} %get-tuple-element.30), channel_id=1, source_target_pairs={{0,1},{1,2},{2,3},{3,4},{4,5},{5,6},{6,7},{7,8},{8,9},{9,10},{10,1... | collective-permute-start | bytes 3932168 | tf_op jit(solution)/shard_map/ppermute | solution.py:422
  12.3 25.0 %collective-permute-start.5 = (f32[5,256,256]{2,1,0:T(8,128)S(1)}, f32[5,256,256]{2,1,0:T(8,128)S(1)}, u32[]{:S(2)}, u32[]{:S(2)}) collective-permute-start(f32[5,256,256]{2,1,0:T(8,128)S(1)} %get-tuple-element.31), channel_id=1, source_target_pairs={{0,15},{1,0},{2,1},{3,2},{4,3},{5,4},{6,5},{7,6},{8,7},{9,8},{10,9... | collective-permute-start | bytes 3932168 | tf_op jit(solution)/shard_map/ppermute | solution.py:422
  17.7 7.7 %collective-permute-start.1 = (f32[8,32,256]{2,1,0:T(8,128)S(1)}, f32[8,32,256]{2,1,0:T(8,128)S(1)}, u32[]{:S(2)}, u32[]{:S(2)}) collective-permute-start(f32[8,32,256]{2,1,0:T(8,128)S(1)} %pad_maximum_fusion), channel_id=1, source_target_pairs={{0,16},{16,32},{32,48},{48,64},{64,80},{80,96},{96,112},{112,0},{1... | collective-permute-start | bytes 786440 | tf_op jit(solution)/shard_map/ppermute | solution.py:414
  17.9 7.6 %collective-permute-start.7 = (f32[8,32,256]{2,1,0:T(8,128)S(1)}, f32[8,32,256]{2,1,0:T(8,128)S(1)}, u32[]{:S(2)}, u32[]{:S(2)}) collective-permute-start(f32[8,32,256]{2,1,0:T(8,128)S(1)} %pad_maximum_fusion.1), channel_id=1, source_target_pairs={{0,112},{16,0},{32,16},{48,32},{64,48},{80,64},{96,80},{112,96},{1... | collective-permute-start | bytes 786440 | tf_op jit(solution)/shard_map/ppermute | solution.py:418
  25.4 8.1 %collective-permute-start.2 = (f32[8,32,256]{2,1,0:T(8,128)S(1)}, f32[8,32,256]{2,1,0:T(8,128)S(1)}, u32[]{:S(2)}, u32[]{:S(2)}) collective-permute-start(f32[8,32,256]{2,1,0:T(8,128)S(1)} %add.19), channel_id=1, source_target_pairs={{0,16},{16,32},{32,48},{48,64},{64,80},{80,96},{96,112},{112,0},{1... | collective-permute-start | bytes 786440 | tf_op jit(solution)/shard_map/ppermute | solution.py:414
  25.6 8.0 %collective-permute-start.8 = (f32[8,32,256]{2,1,0:T(8,128)S(1)}, f32[8,32,256]{2,1,0:T(8,128)S(1)}, u32[]{:S(2)}, u32[]{:S(2)}) collective-permute-start(f32[8,32,256]{2,1,0:T(8,128)S(1)} %add.22), channel_id=1, source_target_pairs={{0,112},{16,0},{32,16},{48,32},{64,48},{80,64},{96,80},{112,96},{1... | collective-permute-start | bytes 786440 | tf_op jit(solution)/shard_map/ppermute | solution.py:418
  33.5 7.7 %collective-permute-start.3 = (f32[8,32,256]{2,1,0:T(8,128)S(1)}, f32[8,32,256]{2,1,0:T(8,128)S(1)}, u32[]{:S(2)}, u32[]{:S(2)}) collective-permute-start(f32[8,32,256]{2,1,0:T(8,128)S(1)} %add.20), channel_id=1, source_target_pairs={{0,16},{16,32},{32,48},{48,64},{64,80},{80,96},{96,112},{112,0},{1... | collective-permute-start | bytes 786440 | tf_op jit(solution)/shard_map/ppermute | solution.py:414
  33.7 21.5 %copy-start.4 = (f32[256,256]{1,0:T(8,128)S(1)}, f32[256,256]{1,0:T(8,128)}, u32[]{:S(2)}) copy-start(f32[256,256]{1,0:T(8,128)} %constant.6.clone.y_table.x_table.table.refs_2_) | copy-start | bytes 786436
  33.7 21.5 %copy-start.5 = (f32[128,128]{1,0:T(8,128)S(1)}, f32[128,128]{1,0:T(8,128)}, u32[]{:S(2)}) copy-start(f32[128,128]{1,0:T(8,128)} %constant.7.clone.z_table) | copy-start | bytes 196612
  33.7 7.5 %collective-permute-start.9 = (f32[8,32,256]{2,1,0:T(8,128)S(1)}, f32[8,32,256]{2,1,0:T(8,128)S(1)}, u32[]{:S(2)}, u32[]{:S(2)}) collective-permute-start(f32[8,32,256]{2,1,0:T(8,128)S(1)} %add.23), channel_id=1, source_target_pairs={{0,112},{16,0},{32,16},{48,32},{64,48},{80,64},{96,80},{112,96},{1... | collective-permute-start | bytes 786440 | tf_op jit(solution)/shard_map/ppermute | solution.py:418
  68.8 10.6 %collective-permute-start.13 = (f32[32,8,256]{2,1,0:T(8,128)S(1)}, f32[32,8,256]{2,1,0:T(8,128)S(1)}, u32[]{:S(2)}, u32[]{:S(2)}) collective-permute-start(f32[32,8,256]{2,1,0:T(8,128)S(1)} %all_to_all.11.refs_0_.refs_7_), channel_id=1, source_target_pairs={{0,16},{16,32},{32,48},{48,64},{64,80},{80,96},{96,112},{112,0},{1... | collective-permute-start | bytes 786440 | tf_op jit(solution)/shard_map/ppermute | solution.py:414
  68.8 10.6 %collective-permute-start.10 = (f32[32,8,256]{2,1,0:T(8,128)S(1)}, f32[32,8,256]{2,1,0:T(8,128)S(1)}, u32[]{:S(2)}, u32[]{:S(2)}) collective-permute-start(f32[32,8,256]{2,1,0:T(8,128)S(1)} %all_to_all.11.refs_0_.refs_7_), channel_id=1, source_target_pairs={{0,112},{16,0},{32,16},{48,32},{64,48},{80,64},{96,80},{112,96},{1... | collective-permute-start | bytes 786440 | tf_op jit(solution)/shard_map/ppermute | solution.py:418
  73.9 32.7 %copy-start.2 = (f32[8,256,256]{2,1,0:T(8,128)S(1)}, f32[8,256,256]{2,1,0:T(8,128)}, u32[]{:S(2)}) copy-start(f32[8,256,256]{2,1,0:T(8,128)} %refs_1_.1) | copy-start | bytes 6291460
  79.5 8.5 %collective-permute-start.11 = (f32[32,8,256]{2,1,0:T(8,128)S(1)}, f32[32,8,256]{2,1,0:T(8,128)S(1)}, u32[]{:S(2)}, u32[]{:S(2)}) collective-permute-start(f32[32,8,256]{2,1,0:T(8,128)S(1)} %collective-permute-done.10.refs_1_.refs_8_), channel_id=1, source_target_pairs={{0,112},{16,0},{32,16},{48,32},{64,48},{80,64},{96,80},{112,96},{1... | collective-permute-start | bytes 786440 | tf_op jit(solution)/shard_map/ppermute | solution.py:418
  82.4 9.2 %collective-permute-start.14 = (f32[32,8,256]{2,1,0:T(8,128)S(1)}, f32[32,8,256]{2,1,0:T(8,128)S(1)}, u32[]{:S(2)}, u32[]{:S(2)}) collective-permute-start(f32[32,8,256]{2,1,0:T(8,128)S(1)} %collective-permute-done.13.refs_8_.refs_15_), channel_id=1, source_target_pairs={{0,16},{16,32},{32,48},{48,64},{64,80},{80,96},{96,112},{112,0},{1... | collective-permute-start | bytes 786440 | tf_op jit(solution)/shard_map/ppermute | solution.py:414
  88.0 8.4 %collective-permute-start.12 = (f32[32,8,256]{2,1,0:T(8,128)S(1)}, f32[32,8,256]{2,1,0:T(8,128)S(1)}, u32[]{:S(2)}, u32[]{:S(2)}) collective-permute-start(f32[32,8,256]{2,1,0:T(8,128)S(1)} %collective-permute-done.11.refs_2_.refs_9_), channel_id=1, source_target_pairs={{0,112},{16,0},{32,16},{48,32},{64,48},{80,64},{96,80},{112,96},{1... | collective-permute-start | bytes 786440 | tf_op jit(solution)/shard_map/ppermute | solution.py:418
  91.7 8.5 %collective-permute-start.15 = (f32[32,8,256]{2,1,0:T(8,128)S(1)}, f32[32,8,256]{2,1,0:T(8,128)S(1)}, u32[]{:S(2)}, u32[]{:S(2)}) collective-permute-start(f32[32,8,256]{2,1,0:T(8,128)S(1)} %collective-permute-done.14.refs_7_.refs_14_), channel_id=1, source_target_pairs={{0,16},{16,32},{32,48},{48,64},{64,80},{80,96},{96,112},{112,0},{1... | collective-permute-start | bytes 786440 | tf_op jit(solution)/shard_map/ppermute | solution.py:414
  96.3 6.3 %collective-permute-start.17 = (f32[16,8,256]{2,1,0:T(8,128)S(1)}, f32[16,8,256]{2,1,0:T(8,128)S(1)}, u32[]{:S(2)}, u32[]{:S(2)}) collective-permute-start(f32[16,8,256]{2,1,0:T(8,128)S(1)} %slice.25), channel_id=1, source_target_pairs={{0,112},{16,0},{32,16},{48,32},{64,48},{80,64},{96,80},{112,96},{1... | collective-permute-start | bytes 393224 | tf_op jit(solution)/shard_map/ppermute | solution.py:418
  100.1 6.5 %collective-permute-start.16 = (f32[16,8,256]{2,1,0:T(8,128)S(1)}, f32[16,8,256]{2,1,0:T(8,128)S(1)}, u32[]{:S(2)}, u32[]{:S(2)}) collective-permute-start(f32[16,8,256]{2,1,0:T(8,128)S(1)} %slice.24), channel_id=1, source_target_pairs={{0,16},{16,32},{32,48},{48,64},{64,80},{80,96},{96,112},{112,0},{1... | collective-permute-start | bytes 393224 | tf_op jit(solution)/shard_map/ppermute | solution.py:414
  107.4 6.3 %collective-permute-start.19 = (f32[1,256,256]{2,1,0:T(8,128)S(1)}, f32[1,256,256]{2,1,0:T(8,128)S(1)}, u32[]{:S(2)}, u32[]{:S(2)}) collective-permute-start(f32[1,256,256]{2,1,0:T(8,128)S(1)} %get-tuple-element.39.refs_3_), channel_id=1, source_target_pairs={{0,15},{1,0},{2,1},{3,2},{4,3},{5,4},{6,5},{7,6},{8,7},{9,8},{10,9... | collective-permute-start | bytes 786440 | tf_op jit(solution)/shard_map/ppermute | solution.py:422
  107.5 9.5 %collective-permute-start.18 = (f32[1,256,256]{2,1,0:T(8,128)S(1)}, f32[1,256,256]{2,1,0:T(8,128)S(1)}, u32[]{:S(2)}, u32[]{:S(2)}) collective-permute-start(f32[1,256,256]{2,1,0:T(8,128)S(1)} %get-tuple-element.40.refs_4_), channel_id=1, source_target_pairs={{0,1},{1,2},{2,3},{3,4},{4,5},{5,6},{6,7},{7,8},{8,9},{9,10},{10,1... | collective-permute-start | bytes 786440 | tf_op jit(solution)/shard_map/ppermute | solution.py:422

commit v5 on v4

--- a/solution.py
+++ b/solution.py
@@ -39,8 +39,12 @@
     return pltpu.VMEM(lead + (ny, nx), jnp.float32)
 
 
-def cost(planes, weight):
-    return pl.CostEstimate(flops=planes * weight, bytes_accessed=planes * MIB // 2, transcendentals=0)
+def cost(microseconds):
+    return pl.CostEstimate(flops=0, bytes_accessed=int(microseconds * 3.6e6), transcendentals=0)
+
+
+def lower_core():
+    return lax.rem(lax.axis_index("slab"), 2) == 0
 
 
 def fill_rows(rows, table):
@@ -52,81 +56,101 @@
         rows[offset * width : (offset + 1) * width, :] = table[pl.ds(start, width), :]
 
 
-def density_kernel(scale, psi_re, psi_im, v_local, ground, y_table, *refs):
-    pieces, (to_prev, to_next) = refs[:9], refs[9:11]
-    near, table, own_ground, rows, rho, plane_sem, edge_sem, small_sem = refs[11:]
+def density_kernel(scale, psi_re, psi_im, ground, y_table, *refs):
+    rho, rows, first, second, to_mate, to_other = refs[:6]
+    near, table, own_ground, plane_sem, small_sem = refs[6:]
     planes = near.shape[1]
-    half = planes // 2
+    groups = plane_sem.shape[1]
+    part_planes = planes // groups
     small = [
         pltpu.make_async_copy(y_table, table, small_sem.at[0]),
         pltpu.make_async_copy(ground, own_ground, small_sem.at[1]),
     ]
     copies = []
-    for group in range(2):
-        some = pl.ds(group * half, half)
+    for group in range(groups):
+        some = pl.ds(group * part_planes, part_planes)
         copies.append(
             [
                 pltpu.make_async_copy(psi.at[0, some], near.at[part, some], plane_sem.at[part, group])
                 for part, psi in enumerate((psi_re, psi_im))
             ]
         )
-    edges = []
-    for which, (target, first, v_plane) in enumerate(((to_prev, 0, 0), (to_next, planes - 2, planes - 1))):
-        pair = pl.ds(first, 2)
-        edges += [
-            pltpu.make_async_copy(psi_re.at[0, pair], target.at[pl.ds(0, 2)], edge_sem.at[which, 0]),
-            pltpu.make_async_copy(psi_im.at[0, pair], target.at[pl.ds(2, 2)], edge_sem.at[which, 1]),
-            pltpu.make_async_copy(v_local.at[pl.ds(v_plane, 1)], target.at[pl.ds(4, 1)], edge_sem.at[which, 2]),
-        ]
-    for copy in copies[0] + small + copies[1] + edges:
+    for copy in copies[0] + small + sum(copies[1:], []):
         copy.start()
+    for copy in small:
+        copy.wait()
+    fill_rows(rows, table)
     ground_rows = own_ground.shape[1]
     place = lax.axis_index("y") * lax.axis_size("z") + lax.axis_index("z")
     own = pl.ds(pl.multiple_of(place * ground_rows, ground_rows), ground_rows)
-    for group in range(2):
-        for copy in copies[group] + (small if group == 0 else []):
+    width = first.shape[1] + second.shape[1]
+    far = rows[rows.shape[0] // 2 : rows.shape[0] // 2 + width, :]
+    for group in range(groups):
+        for copy in copies[group]:
             copy.wait()
-        if group == 0:
-            fill_rows(rows, table)
-        for z in range(group * half, (group + 1) * half):
+        some = range(group * part_planes, (group + 1) * part_planes)
+        for z in some:
             re, im = near[0, z], near[1, z]
             rho[z] = scale * (re * re + im * im)
             rho[z, own, :] = rho[z, own, :] - own_ground[z]
-        for z in range(group * half, (group + 1) * half):
-            image = dot(rows[...], rho[z])
-            at = 0
-            for piece in pieces:
-                piece[z] = image[at : at + piece.shape[1]]
-                at += piece.shape[1]
-    for copy in edges:
-        copy.wait()
-
-
-def density(psi_re, psi_im, v_local, n_ground, y_table, total_orbs):
-    planes, ny, nx = v_local.shape
-    width = ny // lax.axis_size("z")
-    heights = [width] * 4 + [width // 2] * 2 + [width] * 3
-    shapes = [(planes, h, nx) for h in heights] + [(5, ny, nx)] * 2
-    far = [pltpu.with_memory_space_constraint(a, pltpu.HBM) for a in (psi_re, psi_im, v_local, n_ground, y_table)]
-    result = pl.pallas_call(
+        for z in some:
+            image = dot(far, rho[z])
+            first[z] = image[: first.shape[1]]
+            second[z] = image[first.shape[1] :]
+    lower = lower_core()
+
+    def fill_edges(low_target, high_target):
+        for part in range(2):
+            for which in range(2):
+                low_target[2 * part + which] = near[part, which]
+                high_target[2 * part + which] = near[part, planes - 2 + which]
+
+    pl.when(lower)(functools.partial(fill_edges, to_other, to_mate))
+    pl.when(jnp.logical_not(lower))(functools.partial(fill_edges, to_mate, to_other))
+
+
+def density(psi_re, psi_im, n_ground, y_table, total_orbs):
+    _, planes, ny, nx = psi_re.shape
+    half = ny // lax.axis_size("z") // 2
+    shapes = [(planes, ny, nx), (ny, ny), (planes, half, nx), (planes, half, nx)] + [(4, ny, nx)] * 2
+    far = [pltpu.with_memory_space_constraint(a, pltpu.HBM) for a in (psi_re, psi_im, n_ground, y_table)]
+    return pl.pallas_call(
         functools.partial(density_kernel, 2.0 / total_orbs),
-        in_specs=[ANY] * 5,
+        in_specs=[ANY] * 4,
         out_specs=[VMEM] * len(shapes),
         out_shape=[pltpu.VMEM(shape, jnp.float32) for shape in shapes],
         scratch_shapes=[
             plane_scratch(2, planes, ny=ny, nx=nx),
             pltpu.VMEM((ny, ny), jnp.float32),
             pltpu.VMEM(n_ground.shape, jnp.float32),
-            pltpu.VMEM((ny, ny), jnp.float32),
-            plane_scratch(planes, ny=ny, nx=nx),
             pltpu.SemaphoreType.DMA((2, 2)),
-            pltpu.SemaphoreType.DMA((2, 3)),
             pltpu.SemaphoreType.DMA((2,)),
         ],
-        compiler_params=pltpu.CompilerParams(vmem_limit_bytes=10 * MIB),
-        name="density_y",
+        compiler_params=pltpu.CompilerParams(vmem_limit_bytes=8 * MIB),
+        name="density",
     )(*far)
-    return result[:9], result[9], result[10]
+
+
+def shares_kernel(rho, rows, *pieces):
+    width = pieces[0].shape[1]
+    for z in range(rho.shape[0]):
+        image = dot(rows[...], rho[z])
+        for offset, piece in zip((0, 1, 2, 3, 5, 6, 7), pieces):
+            piece[z] = image[offset * width : (offset + 1) * width]
+
+
+def shares(rho, rows):
+    planes, ny, nx = rho.shape
+    width = ny // lax.axis_size("z")
+    return pl.pallas_call(
+        shares_kernel,
+        in_specs=[VMEM] * 2,
+        out_specs=[VMEM] * 7,
+        out_shape=[pltpu.VMEM((planes, width, nx), jnp.float32)] * 7,
+        compiler_params=pltpu.CompilerParams(vmem_limit_bytes=4 * MIB),
+        cost_estimate=cost(2.0),
+        name="shares",
+    )(rho, rows)
 
 
 def share_kernel(own, up, down, out):
@@ -209,6 +233,13 @@
     return mid, along_x + (KINETIC * (along_y + along_z) - (6.0 * KINETIC) * mid)
 
 
+def by_side(edges, run):
+    mate, other = edges
+    lower = lower_core()
+    pl.when(lower)(functools.partial(run, other, mate))
+    pl.when(jnp.logical_not(lower))(functools.partial(run, mate, other))
+
+
 def psi_plane(fields, low, high, planes, part, z):
     if z < 0:
         return (low, (2 * part + z + 2,))
@@ -218,15 +249,19 @@
 
 
 def once_kernel(planes, wanted, with_edges, sides, *refs):
-    refs = list(refs)
-    fields = [refs.pop(0), refs.pop(0)]
-    low, high = (refs.pop(0), refs.pop(0)) if with_edges else (None, None)
-    out = refs.pop(0)
-    at = functools.partial(psi_plane, fields, low, high, planes)
-    for slot, z in enumerate(wanted):
-        for part in range(2):
-            _, value = kinetic(at(part, z - 1), at(part, z), at(part, z + 1), sides)
-            out[part, slot] = value
+    fields, edges, out = refs[:2], refs[2:-1], refs[-1]
+
+    def run(low, high):
+        at = functools.partial(psi_plane, fields, low, high, planes)
+        for slot, z in enumerate(wanted):
+            for part in range(2):
+                _, value = kinetic(at(part, z - 1), at(part, z), at(part, z + 1), sides)
+                out[part, slot] = value
+
+    if with_edges:
+        by_side(edges, run)
+    else:
+        run(None, None)
 
 
 def once(sides, near, edges, wanted, name):
@@ -237,7 +272,7 @@
         out_specs=VMEM,
         out_shape=shaped(2, len(wanted), ny, nx),
         compiler_params=pltpu.CompilerParams(vmem_limit_bytes=6 * MIB),
-        cost_estimate=cost(len(wanted), 100 * ny * nx),
+        cost_estimate=cost(0.3 * len(wanted)),
         name=name,
     )(sides, *near, *edges)
 
@@ -266,7 +301,7 @@
         out_specs=VMEM,
         out_shape=shaped(2, len(wanted), ny, nx),
         compiler_params=pltpu.CompilerParams(vmem_limit_bytes=6 * MIB),
-        cost_estimate=cost(len(wanted), 100 * ny * nx),
+        cost_estimate=cost(0.4 * len(wanted)),
         name=name,
     )(sides, *near, *onces)
 
@@ -276,40 +311,79 @@
     return pltpu.roll(table[...], ny - lax.axis_index("z") * (ny // lax.axis_size("z")), 1)
 
 
-def potential_plane(v_local, columns, hats, z):
-    hat = jnp.concatenate([h[:, z, :] for h in hats], axis=0)
-    return v_local[z] + dot(columns, hat)
-
-
-def outer_kernel(v_local, table, *refs):
-    hats, (first, last) = refs[:-2], refs[-2:]
+def terms(value, count):
+    found = []
+    for _ in range(count):
+        found.append(value.astype(jnp.bfloat16))
+        value = value - found[-1].astype(jnp.float32)
+    return found
+
+
+LEFT_TERMS = (0, 0, 1, 1, 0, 2)
+RIGHT_TERMS = (0, 1, 0, 1, 2, 0)
+
+
+def early_kernel(v_local, table, *refs):
+    hats, (pot, tail) = refs[:-2], refs[-2:]
     columns = ring_columns(table)
-    first[0] = potential_plane(v_local, columns, hats, 0)
-    last[0] = potential_plane(v_local, columns, hats, v_local.shape[0] - 1)
-
-
-def outer_potential(v_local, table, hats):
+    width = hats[0].shape[0]
+    first = columns.shape[1] // 2
+    left = terms(columns[:, first : first + width], 3)
+    tail[...] = jnp.concatenate([left[i] for i in LEFT_TERMS], axis=1)
+    for z in range(v_local.shape[0]):
+        rows = [hat[:, z, :] for hat in hats]
+        rows.insert(len(hats) // 2 + 1, jnp.zeros_like(rows[0]))
+        pot[z] = v_local[z] + dot(columns, jnp.concatenate(rows, axis=0))
+
+
+def early_potential(v_local, table, hats):
     planes, ny, nx = v_local.shape
-    return pl.pallas_call(
-        outer_kernel,
+    width = ny // lax.axis_size("z")
+    return pl.pallas_call(
+        early_kernel,
         in_specs=[VMEM] * (2 + len(hats)),
         out_specs=[VMEM] * 2,
+        out_shape=[shaped(planes, ny, nx), jax.ShapeDtypeStruct((ny, len(LEFT_TERMS) * width), jnp.bfloat16)],
+        compiler_params=pltpu.CompilerParams(vmem_limit_bytes=6 * MIB),
+        cost_estimate=cost(2.3),
+        name="early_potential",
+    )(v_local, table, *hats)
+
+
+def potential_plane(early, tail, late, z):
+    right = terms(jnp.concatenate([hat[:, z, :] for hat in late], axis=0), 3)
+    stacked = jnp.concatenate([right[i] for i in RIGHT_TERMS], axis=0)
+    return early[z] + jnp.dot(tail[...], stacked, preferred_element_type=jnp.float32)
+
+
+def outer_kernel(early, tail, up, down, to_mate, to_other):
+    first = potential_plane(early, tail, (up, down), 0)
+    last = potential_plane(early, tail, (up, down), early.shape[0] - 1)
+    lower = lower_core()
+    to_mate[0] = jnp.where(lower, last, first)
+    to_other[0] = jnp.where(lower, first, last)
+
+
+def outer_potential(early, tail, late):
+    planes, ny, nx = early.shape
+    return pl.pallas_call(
+        outer_kernel,
+        in_specs=[VMEM] * (2 + len(late)),
+        out_specs=[VMEM] * 2,
         out_shape=[shaped(1, ny, nx)] * 2,
-        compiler_params=pltpu.CompilerParams(vmem_limit_bytes=6 * MIB),
+        compiler_params=pltpu.CompilerParams(vmem_limit_bytes=4 * MIB),
         name="outer_potential",
-    )(v_local, table, *hats)
-
-
-def inner_kernel(once_groups, base_groups, hat_count, *refs):
+    )(early, tail, *late)
+
+
+def inner_kernel(once_groups, base_groups, *refs):
     refs = list(refs)
-    sides, v_local, table, v_first, v_last, re, im = [refs.pop(0) for _ in range(7)]
-    hats = [refs.pop(0) for _ in range(hat_count)]
+    sides, early, tail, late_up, late_down, re, im = [refs.pop(0) for _ in range(7)]
     onces = [refs.pop(0) for _ in once_groups]
     bases = [refs.pop(0) for _ in base_groups]
     out_re, out_im, open_ends, pot, work, stage, sem = refs
     planes = re.shape[0]
     fields = (re, im)
-    columns = ring_columns(table)
     at_once = functools.partial(once_plane, once_groups, onces)
     at_base = functools.partial(once_plane, base_groups, bases)
     work[:, 0] = jnp.zeros_like(work[:, 0])
@@ -340,12 +414,7 @@
                 copies.append(copy)
 
     for z in range(planes):
-        if z == 0:
-            here = v_first[0]
-        elif z == planes - 1:
-            here = v_last[0]
-        else:
-            here = potential_plane(v_local, columns, hats, z)
+        here = potential_plane(early, tail, (late_up, late_down), z)
         pot[z] = here
         for part in range(2):
             work[part, z + 1] = here * fields[part][z]
@@ -356,12 +425,12 @@
         copy.wait()
 
 
-def inner_update(sides, v_local, table, v_first, v_last, near, hats, onces, once_groups, bases, base_groups):
-    planes, ny, nx = v_local.shape
-    operands = [sides, v_local, table, v_first, v_last, *near, *hats, *onces, *bases]
+def inner_update(sides, early, tail, late, near, onces, once_groups, bases, base_groups):
+    planes, ny, nx = early.shape
+    operands = [sides, early, tail, *late, *near, *onces, *bases]
     full = shaped(1, planes, ny, nx)
     return pl.pallas_call(
-        functools.partial(inner_kernel, once_groups, base_groups, len(hats)),
+        functools.partial(inner_kernel, once_groups, base_groups),
         in_specs=[VMEM] * len(operands),
         out_specs=[ANY, ANY, VMEM],
         out_shape=[full, full, shaped(2, 2, ny, nx)],
@@ -372,18 +441,24 @@
             pltpu.SemaphoreType.DMA((2, planes - 2)),
         ],
         compiler_params=pltpu.CompilerParams(vmem_limit_bytes=14 * MIB),
-        cost_estimate=cost(planes, 400 * ny * nx),
+        cost_estimate=cost(4.3),
         name="inner_update",
     )(*operands)
 
 
-def close_kernel(open_ends, v_before, v_after, low, high, _re, _im, out_re, out_im, stage, sem):
+def close_kernel(open_ends, v_mate, v_other, mate, other, _re, _im, out_re, out_im, stage, sem):
     planes = out_re.shape[1]
+
+    def run(below, above):
+        for slot, ((v_ref, edge), first) in enumerate(((below, 1), (above, 0))):
+            for part in range(2):
+                beyond = v_ref[0] * edge[2 * part + first]
+                stage[part, slot] = open_ends[part, slot] - (HALF_SQ * KINETIC) * beyond
+
+    by_side(((v_mate, mate), (v_other, other)), run)
     copies = []
-    for slot, (z, v_ref, edge, first) in enumerate(((0, v_before, low, 1), (planes - 1, v_after, high, 0))):
+    for slot, z in enumerate((0, planes - 1)):
         for part, out in enumerate((out_re, out_im)):
-            beyond = v_ref[0] * edge[2 * part + first]
-            stage[part, slot] = open_ends[part, slot] - (HALF_SQ * KINETIC) * beyond
             copy = pltpu.make_async_copy(stage.at[part, slot], out.at[0, z], sem.at[part, slot])
             copy.start()
             copies.append(copy)
@@ -391,7 +466,7 @@
         copy.wait()
 
 
-def close_ends(new_re, new_im, open_ends, v_before, v_after, edges):
+def close_ends(new_re, new_im, open_ends, v_planes, edges):
     _, _, ny, nx = open_ends.shape
     return pl.pallas_call(
         close_kernel,
@@ -402,7 +477,7 @@
         scratch_shapes=[plane_scratch(2, 2, ny=ny, nx=nx), pltpu.SemaphoreType.DMA((2, 2))],
         compiler_params=pltpu.CompilerParams(vmem_limit_bytes=4 * MIB),
         name="close_ends",
-    )(open_ends, v_before, v_after, *edges, new_re, new_im)
+    )(open_ends, *v_planes, *edges, new_re, new_im)
 
 
 def ring(axis, shift):
@@ -418,18 +493,22 @@
     return lax.ppermute(value, axis, ring(axis, -1))
 
 
-def slab_shift(value, shift):
-    return lax.ppermute(value, "slab", ring("slab", shift))
+def swap_edges(to_mate, to_other):
+    count = lax.axis_size("slab")
+    others = [(i, (i - 1) % count if i % 2 == 0 else (i + 1) % count) for i in range(count)]
+    from_other = lax.ppermute(to_other, "slab", others)
+    from_mate = lax.ppermute(to_mate, "slab", [(i, i ^ 1) for i in range(count)])
+    return from_mate, from_other
 
 
 def after(value, *others):
     return lax.optimization_barrier((value,) + others)[0]
 
 
-def sum_over_ring(pieces, beside):
-    s0, s1, s2, s3, s4_first, s4_second, s5, s6, s7 = pieces
-    half = s4_first.shape[1]
-    got_up, got_down = forward(s4_first), backward(s4_second)
+def sum_over_ring(first, second, pieces, beside):
+    s0, s1, s2, s3, s5, s6, s7 = pieces
+    half = first.shape[1]
+    got_up, got_down = forward(first), backward(second)
     up = jnp.concatenate([s3[:, :half] + got_up, s3[:, half:]], axis=1)
     down = jnp.concatenate([s5[:, :half], s5[:, half:] + got_down], axis=1)
     up, down = forward(up), backward(down)
@@ -441,7 +520,7 @@
     return add_shares(s0, up, down)
 
 
-def gather_over_ring(block, beside):
+def gather_over_ring(block, beside, early):
     half = block.shape[0] // 2
     up1, down1 = forward(block), backward(block)
     up1 = after(up1, *beside[0])
@@ -449,7 +528,8 @@
     up2 = after(up2, *beside[1])
     up3, down3 = forward(up2), backward(down2)
     up4, down4 = forward(up3[:half]), backward(down3[half:])
-    return [block, down1, down2, down3, up4, down4, up3, up2, up1]
+    made = early([block, down1, down2, down3, up3, up2, up1])
+    return made, (after(up4, *made), down4)
 
 
 def across(value):
@@ -462,10 +542,10 @@
     nz = planes * lax.axis_size("slab")
     y_table, x_table, z_table = cas_table(ny), cas_table(nx), cas_table(nz)
 
-    pieces, to_prev, to_next = density(psi_re, psi_im, v_local, n_ground, y_table, total_orbs)
+    rho, rows, first, second, to_mate, to_other = density(psi_re, psi_im, n_ground, y_table, total_orbs)
+    pieces = shares(rho, rows)
     near = (psi_re[0], psi_im[0])
-    low, high = slab_shift(to_next, 1), slab_shift(to_prev, -1)
-    edges = (low, high)
+    edges = swap_edges(to_mate, to_other)
 
     middle = planes // 2
     once_groups = [list(range(1, middle)), list(range(middle, planes - 1)), [-1, 0, planes - 1, planes]]
@@ -479,16 +559,18 @@
     bases = [
         base(sides, near, onces, once_groups, group, name) for group, name in zip(base_groups, ("base_a", "base_b"))
     ]
-    share = sum_over_ring(pieces, [[onces[0]], [onces[1]], [onces[2]]])
+    share = sum_over_ring(first, second, pieces, [[onces[0]], [onces[1]], [onces[2]]])
     pencils = across(share).reshape(SIDES * nz, nx)
-    hats = gather_over_ring(across(solve(pencils, x_table, z_table, ny, planes)), [[bases[0]], [bases[1]]])
-
-    v_first, v_last = outer_potential(v_local, y_table, hats)
-    v_before, v_after = slab_shift(v_last, 1), slab_shift(v_first, -1)
+    (early, tail), late = gather_over_ring(
+        across(solve(pencils, x_table, z_table, ny, planes)),
+        [[bases[0]], [bases[1]]],
+        functools.partial(early_potential, v_local, y_table),
+    )
+    v_planes = swap_edges(*outer_potential(early, tail, late))
     new_re, new_im, open_ends = inner_update(
-        sides, v_local, y_table, v_first, v_last, near, hats, onces, once_groups, bases, base_groups
+        sides, early, tail, late, near, onces, once_groups, bases, base_groups
     )
-    return tuple(close_ends(new_re, new_im, open_ends, v_before, v_after, edges))
+    return tuple(close_ends(new_re, new_im, open_ends, v_planes, edges))
 
 
 def solution(mesh):

time: 118 us -> 117 us (level); the launches traced: 118 us -> 115 us
  waiting for transfers between devices: 33.3 us -> 29 us
    ppermute x8, waiting for transfers between devices: 10.9 us -> 0.38 us  [backward(): return lax.ppermute(value, axis, ring(axis, -1))]
    ppermute x8, waiting for transfers between devices: 19.1 us -> 25.6 us  [forward(): return lax.ppermute(value, axis, ring(axis, 1))]
    pallas_call x2 -> x4, Pallas kernels: 6.54 us -> 8.94 us  [the longest x1 4.5 us: inner_update(): pl.pallas_call(functools.partial(inner_kernel, once_groups, base_groups),...]
    pallas_call x1, Pallas kernels: 5.61 us -> 3.85 us  [density(): pl.pallas_call(functools.partial(density_kernel, 2.0 / total_orbs), in_sp...]
    ppermute x8, starting transfers between devices: 28.2 us -> 26.9 us  [backward(): return lax.ppermute(value, axis, ring(axis, -1))]
  transfers between devices with their start and end apart: 20 -> 20, of which waited for: 9 -> 10; matrix products, arithmetic and copies ran while one was open for 0% -> 0% of each run, Pallas kernels for 10% -> 13%
where the time goes in v5:
time: 117 us; the launch traced here: 115 us
  starting transfers between devices  36.8 us (31%)
  waiting for transfers between devices  29 us (25%)
  blocking collectives  26.6 us (23%)
  Pallas kernels  21.4 us (18%)
    ppermute x8, starting transfers between devices, backward(): return lax.ppermute(value, axis, ring(axis, -1))  26.9 us
    all_to_all x2, blocking collectives, across(): lax.all_to_all(value, ('y', 'slab'), split_axis=0, concat_axis=0, tiled=T...  26.6 us
    ppermute x8, waiting for transfers between devices, forward(): return lax.ppermute(value, axis, ring(axis, 1))  25.6 us
    ppermute x2, starting transfers between devices, swap_edges(): from_other = lax.ppermute(to_other, 'slab', others)  6.61 us
    pallas_call x1, Pallas kernels, inner_update(): pl.pallas_call(functools.partial(inner_kernel, once_groups, base_groups),...  4.5 us
    pallas_call x1, Pallas kernels, density(): pl.pallas_call(functools.partial(density_kernel, 2.0 / total_orbs), in_sp...  3.85 us
    ppermute x8, starting transfers between devices, forward(): return lax.ppermute(value, axis, ring(axis, 1))  3.26 us
    pallas_call x3, Pallas kernels, once(): pl.pallas_call(functools.partial(once_kernel, planes, wanted, bool(edges)...  3.07 us
  transfers between devices with their start and end apart: 20, of which 10 were waited for; matrix products, arithmetic and copies ran while one was open for 0% of the time, Pallas kernels for 13%

profile of v5, /device:TPU:8, one launch (start us, length us, event | category | flops | bytes accessed | tf_op | source)
XLA Modules:
  0.0 115.2 jit_solution(3806657609377896884)
XLA Ops:
  0.6 3.8 %density.1 = (f32[8,256,256]{2,1,0:T(8,128)S(1)}, f32[256,256]{1,0:T(8,128)S(1)}, f32[8,16,256]{2,1,0:T(8,128)S(1)}, f32[8,16,256]{2,1,0:T(8,128)S(1)}, f32[4,25...) custom-call(f32[1,8,256,256]{3,2,1,0:T(8,128)} %psi_re.1, f32[1,8,256,256]{3,2,1,0:T(8,128)} %psi_im.1, ...), custom_call_target="tpu_custom_call" | custom-call | tf_op jit(solution)/shard_map/density/pallas_call | solution.py:117
  4.5 2.0 %collective-permute-start = (f32[8,16,256]{2,1,0:T(8,128)S(1)}, f32[8,16,256]{2,1,0:T(8,128)S(1)}, u32[]{:S(2)}, u32[]{:S(2)}) collective-permute-start(f32[8,16,256]{2,1,0:T(8,128)S(1)} %get-tuple-element.32), channel_id=1, source_target_pairs={{0,16},{16,32},{32,48},{48,64},{64,80},{80,96},{96,112},{112,0},{1... | collective-permute-start | bytes 393224 | tf_op jit(solution)/shard_map/ppermute | solution.py:489
  6.5 4.0 %collective-permute-start.6 = (f32[8,16,256]{2,1,0:T(8,128)S(1)}, f32[8,16,256]{2,1,0:T(8,128)S(1)}, u32[]{:S(2)}, u32[]{:S(2)}) collective-permute-start(f32[8,16,256]{2,1,0:T(8,128)S(1)} %get-tuple-element.41), channel_id=1, source_target_pairs={{0,112},{16,0},{32,16},{48,32},{64,48},{80,64},{96,80},{112,96},{1... | collective-permute-start | bytes 393224 | tf_op jit(solution)/shard_map/ppermute | solution.py:493
  10.5 4.6 %collective-permute-start.5 = (f32[4,256,256]{2,1,0:T(8,128)S(1)}, f32[4,256,256]{2,1,0:T(8,128)S(1)}, u32[]{:S(2)}, u32[]{:S(2)}) collective-permute-start(f32[4,256,256]{2,1,0:T(8,128)S(1)} %get-tuple-element.38), channel_id=1, source_target_pairs={{0,15},{1,2},{2,1},{3,4},{4,3},{5,6},{6,5},{7,8},{8,7},{9,10},{10,... | collective-permute-start | bytes 3145736 | tf_op jit(solution)/shard_map/ppermute | solution.py:499
  15.1 1.9 %shares.1 = (f32[8,32,256]{2,1,0:T(8,128)S(1)}, f32[8,32,256]{2,1,0:T(8,128)S(1)}, f32[8,32,256]{2,1,0:T(8,128)S(1)}, f32[8,32,256]{2,1,0:T(8,128)S(1)}, f32[8,3...) custom-call(f32[8,256,256]{2,1,0:T(8,128)S(1)} %get-tuple-element.28.rho, ...), custom_call_target="tpu_custom_call" | custom-call | bytes 7200000 | tf_op jit(solution)/shard_map/shares/pallas_call | solution.py:145
  17.1 0.1 collective-permute-start.1
  17.2 0.0 collective-permute-done.6
  17.3 3.3 %collective-permute-start.7 = (f32[8,32,256]{2,1,0:T(8,128)S(1)}, f32[8,32,256]{2,1,0:T(8,128)S(1)}, u32[]{:S(2)}, u32[]{:S(2)}) collective-permute-start(f32[8,32,256]{2,1,0:T(8,128)S(1)} %pad_maximum_fusion.1), channel_id=1, source_target_pairs={{0,112},{16,0},{32,16},{48,32},{64,48},{80,64},{96,80},{112,96},{1... | collective-permute-start | bytes 786440 | tf_op jit(solution)/shard_map/ppermute | solution.py:493
  20.6 0.9 once_a.1.refs_0_.refs_7_
  21.5 3.3 %collective-permute-done.1 = f32[8,32,256]{2,1,0:T(8,128)S(1)} collective-permute-done((f32[8,32,256]{2,1,0:T(8,128)S(1)}, f32[8,32,256]{2,1,0:T(8,128)S(1)}, u32[]{:S(2)}, u32[]{:S(2)}) %collective-permute-start.1) | collective-permute-done | bytes 262176 | tf_op jit(solution)/shard_map/ppermute | solution.py:489
  24.8 0.1 collective-permute-start.2
  24.9 0.0 collective-permute-done.7
  25.0 3.4 %collective-permute-start.8 = (f32[8,32,256]{2,1,0:T(8,128)S(1)}, f32[8,32,256]{2,1,0:T(8,128)S(1)}, u32[]{:S(2)}, u32[]{:S(2)}) collective-permute-start(f32[8,32,256]{2,1,0:T(8,128)S(1)} %add.22), channel_id=1, source_target_pairs={{0,112},{16,0},{32,16},{48,32},{64,48},{80,64},{96,80},{112,96},{1... | collective-permute-start | bytes 786440 | tf_op jit(solution)/shard_map/ppermute | solution.py:493
  28.4 0.9 once_b.1.refs_1_.refs_8_
  29.3 3.9 %collective-permute-done.2 = f32[8,32,256]{2,1,0:T(8,128)S(1)} collective-permute-done((f32[8,32,256]{2,1,0:T(8,128)S(1)}, f32[8,32,256]{2,1,0:T(8,128)S(1)}, u32[]{:S(2)}, u32[]{:S(2)}) %collective-permute-start.2) | collective-permute-done | bytes 262176 | tf_op jit(solution)/shard_map/ppermute | solution.py:489
  33.2 0.1 collective-permute-start.3
  33.4 0.0 copy-start.3
  33.4 0.0 copy-start.5
  33.4 3.9 %collective-permute-start.9 = (f32[8,32,256]{2,1,0:T(8,128)S(1)}, f32[8,32,256]{2,1,0:T(8,128)S(1)}, u32[]{:S(2)}, u32[]{:S(2)}) collective-permute-start(f32[8,32,256]{2,1,0:T(8,128)S(1)} %add.23), channel_id=1, source_target_pairs={{0,112},{16,0},{32,16},{48,32},{64,48},{80,64},{96,80},{112,96},{1... | collective-permute-start | bytes 786440 | tf_op jit(solution)/shard_map/ppermute | solution.py:493
  37.3 0.0 collective-permute-done.4.refs_2_.mate
  37.3 1.2 %once_c.1.refs_2_.refs_9_ = f32[2,4,256,256]{3,2,1,0:T(8,128)S(1)} custom-call(bf16[256,256]{1,0:T(8,128)(2,1)S(1)} %copy-done.2, f32[8,256,256]{2,1,0:T(8,128)S(1)} %bitcast.5, f32[8,256,256]{2,1,0:T(8,128)S(1)} %bitcast.11, f32[4,256,256]{2,1,0:T(8,128)S(1)} %collective-permute-done.4.refs_2_.mate, f32[4,256,256]{2,1,0:T(8,128)S(1)} %collective-permute-done.5.refs_3_.other), custom_call_target="tpu_custom_call" | custom-call | bytes 4320000 | tf_op jit(solution)/shard_map/once_c/pallas_call | solution.py:269
  38.5 2.4 %collective-permute-done.3.up = f32[8,32,256]{2,1,0:T(8,128)S(1)} collective-permute-done((f32[8,32,256]{2,1,0:T(8,128)S(1)}, f32[8,32,256]{2,1,0:T(8,128)S(1)}, u32[]{:S(2)}, u32[]{:S(2)}) %collective-permute-start.3) | collective-permute-done | bytes 262176 | tf_op jit(solution)/shard_map/ppermute | solution.py:489
  40.9 0.3 collective-permute-done.9.down
  41.2 0.1 add_shares.1
  41.3 14.2 %all_to_all.10 = f32[32,8,256]{2,1,0:T(8,128)S(1)} all-to-all(f32[32,8,256]{2,1,0:T(8,128)S(1)} %add_shares.1), channel_id=1, replica_groups=mesh['y'=2,'z'=8,'slab'=16] {'y','slab'}, dimensions={0} | all-to-all | bytes 524288 | tf_op jit(solution)/shard_map/all_to_all | solution.py:536
  55.5 1.3 %solve_xz.1 = f32[32,8,256]{2,1,0:T(8,128)S(1)} custom-call(f32[256,256]{1,0:T(8,128)S(1)} %bitcast.15, f32[256,256]{1,0:T(8,128)S(1)} %copy-done.3, f32[128,128]{1,0:T(8,128)S(1)} %copy-done.5), custom_call_target="tpu_custom_call" | custom-call | tf_op jit(solution)/shard_map/solve_xz/pallas_call | solution.py:201
  56.8 12.3 %all_to_all.11.refs_0_ = f32[32,8,256]{2,1,0:T(8,128)S(1)} all-to-all(f32[32,8,256]{2,1,0:T(8,128)S(1)} %solve_xz.1), channel_id=1, replica_groups=mesh['y'=2,'z'=8,'slab'=16] {'y','slab'}, dimensions={0} | all-to-all | bytes 524288 | tf_op jit(solution)/shard_map/all_to_all | solution.py:536
  69.1 0.7 collective-permute-start.13
  69.8 2.6 %collective-permute-start.10 = (f32[32,8,256]{2,1,0:T(8,128)S(1)}, f32[32,8,256]{2,1,0:T(8,128)S(1)}, u32[]{:S(2)}, u32[]{:S(2)}) collective-permute-start(f32[32,8,256]{2,1,0:T(8,128)S(1)} %all_to_all.11.refs_0_), channel_id=1, source_target_pairs={{0,112},{16,0},{32,16},{48,32},{64,48},{80,64},{96,80},{112,96},{1... | collective-permute-start | bytes 786440 | tf_op jit(solution)/shard_map/ppermute | solution.py:493
  72.4 1.5 %base_a.1.refs_10_ = f32[2,4,256,256]{3,2,1,0:T(8,128)S(1)} custom-call(bf16[256,256]{1,0:T(8,128)(2,1)S(1)} %copy-done.2, f32[8,256,256]{2,1,0:T(8,128)S(1)} %bitcast.6, f32[8,256,256]{2,1,0:T(8,128)S(1)} %bitcast.12, f32[2,3,256,256]{3,2,1,0:T(8,128)S(1)} %once_a.1.refs_0_.refs_7_, f32[2,3,256,256]{3,2,1,0:T(8,128)S(1)} %once_b.1.refs_1_.refs_8_, ...), custom_call_target="tpu_custom_call" | custom-call | bytes 5760000 | tf_op jit(solution)/shard_map/base_a/pallas_call | solution.py:298
  73.9 0.0 copy-start.4
  73.9 5.5 %collective-permute-done.13.refs_6_ = f32[32,8,256]{2,1,0:T(8,128)S(1)} collective-permute-done((f32[32,8,256]{2,1,0:T(8,128)S(1)}, f32[32,8,256]{2,1,0:T(8,128)S(1)}, u32[]{:S(2)}, u32[]{:S(2)}) %collective-permute-start.13) | collective-permute-done | bytes 262176 | tf_op jit(solution)/shard_map/ppermute | solution.py:489
  79.5 0.1 collective-permute-done.10.refs_1_
  79.6 3.1 %collective-permute-start.11 = (f32[32,8,256]{2,1,0:T(8,128)S(1)}, f32[32,8,256]{2,1,0:T(8,128)S(1)}, u32[]{:S(2)}, u32[]{:S(2)}) collective-permute-start(f32[32,8,256]{2,1,0:T(8,128)S(1)} %collective-permute-done.10.refs_1_), channel_id=1, source_target_pairs={{0,112},{16,0},{32,16},{48,32},{64,48},{80,64},{96,80},{112,96},{1... | collective-permute-start | bytes 786440 | tf_op jit(solution)/shard_map/ppermute | solution.py:493
  82.7 1.5 %base_b.1.refs_11_ = f32[2,4,256,256]{3,2,1,0:T(8,128)S(1)} custom-call(bf16[256,256]{1,0:T(8,128)(2,1)S(1)} %copy-done.2, f32[8,256,256]{2,1,0:T(8,128)S(1)} %bitcast.7, f32[8,256,256]{2,1,0:T(8,128)S(1)} %bitcast.13, f32[2,3,256,256]{3,2,1,0:T(8,128)S(1)} %once_a.1.refs_0_.refs_7_, f32[2,3,256,256]{3,2,1,0:T(8,128)S(1)} %once_b.1.refs_1_.refs_8_, ...), custom_call_target="tpu_custom_call" | custom-call | bytes 5760000 | tf_op jit(solution)/shard_map/base_b/pallas_call | solution.py:298
  84.2 4.7 %collective-permute-done.14.refs_5_ = f32[32,8,256]{2,1,0:T(8,128)S(1)} collective-permute-done((f32[32,8,256]{2,1,0:T(8,128)S(1)}, f32[32,8,256]{2,1,0:T(8,128)S(1)}, u32[]{:S(2)}, u32[]{:S(2)}) %collective-permute-start.14) | collective-permute-done | bytes 262176 | tf_op jit(solution)/shard_map/ppermute | solution.py:489
  88.9 3.2 %collective-permute-start.12 = (f32[32,8,256]{2,1,0:T(8,128)S(1)}, f32[32,8,256]{2,1,0:T(8,128)S(1)}, u32[]{:S(2)}, u32[]{:S(2)}) collective-permute-start(f32[32,8,256]{2,1,0:T(8,128)S(1)} %collective-permute-done.11.refs_2_), channel_id=1, source_target_pairs={{0,112},{16,0},{32,16},{48,32},{64,48},{80,64},{96,80},{112,96},{1... | collective-permute-start | bytes 786440 | tf_op jit(solution)/shard_map/ppermute | solution.py:493
  92.1 5.4 %collective-permute-done.15.refs_4_ = f32[32,8,256]{2,1,0:T(8,128)S(1)} collective-permute-done((f32[32,8,256]{2,1,0:T(8,128)S(1)}, f32[32,8,256]{2,1,0:T(8,128)S(1)}, u32[]{:S(2)}, u32[]{:S(2)}) %collective-permute-start.15) | collective-permute-done | bytes 262176 | tf_op jit(solution)/shard_map/ppermute | solution.py:489
  97.5 0.3 collective-permute-start.16
  97.8 3.3 %collective-permute-start.17 = (f32[16,8,256]{2,1,0:T(8,128)S(1)}, f32[16,8,256]{2,1,0:T(8,128)S(1)}, u32[]{:S(2)}, u32[]{:S(2)}) collective-permute-start(f32[16,8,256]{2,1,0:T(8,128)S(1)} %slice.25), channel_id=1, source_target_pairs={{0,112},{16,0},{32,16},{48,32},{64,48},{80,64},{96,80},{112,96},{1... | collective-permute-start | bytes 393224 | tf_op jit(solution)/shard_map/ppermute | solution.py:493
  101.1 2.3 %early_potential.1 = (f32[8,256,256]{2,1,0:T(8,128)S(1)}, bf16[256,192]{1,0:T(8,128)(2,1)S(1)}) custom-call(f32[8,256,256]{2,1,0:T(8,128)S(1)} %copy-done.4, f32[256,256]{1,0:T(8,128)S(1)} %copy-done.3, f32[32,8,256]{2,1,0:T(8,128)S(1)} %all_to_all.11.refs_0_, f32[32,8,256]{2,1,0:T(8,128)S(1)} %collective-permute-done.10.refs_1_, ...), custom_call_target="tpu_custom_call" | custom-call | bytes 8279999 | tf_op jit(solution)/shard_map/early_potential/pallas_call | solution.py:342
  103.4 0.5 collective-permute-done.16.refs_3_.up
  104.0 0.2 outer_potential.1
  104.2 0.1 collective-permute-start.18
  104.3 2.0 %collective-permute-start.19 = (f32[1,256,256]{2,1,0:T(8,128)S(1)}, f32[1,256,256]{2,1,0:T(8,128)S(1)}, u32[]{:S(2)}, u32[]{:S(2)}) collective-permute-start(f32[1,256,256]{2,1,0:T(8,128)S(1)} %get-tuple-element.51), channel_id=1, source_target_pairs={{0,15},{1,2},{2,1},{3,4},{4,3},{5,6},{6,5},{7,8},{8,7},{9,10},{10,... | collective-permute-start | bytes 786440 | tf_op jit(solution)/shard_map/ppermute | solution.py:499
  106.3 4.5 %inner_update.1 = (f32[1,8,256,256]{3,2,1,0:T(8,128)}, f32[1,8,256,256]{3,2,1,0:T(8,128)}, f32[2,2,256,256]{3,2,1,0:T(8,128)S(1)}) custom-call(bf16[256,256]{1,0:T(8,128)(2,1)S(1)} %copy-done.2, f32[8,256,256]{2,1,0:T(8,128)S(1)} %get-tuple-element.46.refs_1_.early, bf16[256,192]{1,0:T(8,128)(2,1)S(1)} %get-tuple-element.47.refs_2_.tail, ...), custom_call_target="tpu_custom_call" | custom-call | bytes 15480000 | tf_op jit(solution)/shard_map/inner_update/pallas_call | solution.py:432
  110.9 3.0 %collective-permute-done.19.v_other = f32[1,256,256]{2,1,0:T(8,128)S(1)} collective-permute-done((f32[1,256,256]{2,1,0:T(8,128)S(1)}, f32[1,256,256]{2,1,0:T(8,128)S(1)}, u32[]{:S(2)}, u32[]{:S(2)}) %collective-permute-start.19) | collective-permute-done | bytes 262176 | tf_op jit(solution)/shard_map/ppermute | solution.py:499
  113.8 1.1 close_ends.1
  (29 shorter events, 0.3 us)
Async XLA Ops:
  4.5 12.6 %collective-permute-start = (f32[8,16,256]{2,1,0:T(8,128)S(1)}, f32[8,16,256]{2,1,0:T(8,128)S(1)}, u32[]{:S(2)}, u32[]{:S(2)}) collective-permute-start(f32[8,16,256]{2,1,0:T(8,128)S(1)} %get-tuple-element.32), channel_id=1, source_target_pairs={{0,16},{16,32},{32,48},{48,64},{64,80},{80,96},{96,112},{112,0},{1... | collective-permute-start | bytes 393224 | tf_op jit(solution)/shard_map/ppermute | solution.py:489
  6.5 10.7 %collective-permute-start.6 = (f32[8,16,256]{2,1,0:T(8,128)S(1)}, f32[8,16,256]{2,1,0:T(8,128)S(1)}, u32[]{:S(2)}, u32[]{:S(2)}) collective-permute-start(f32[8,16,256]{2,1,0:T(8,128)S(1)} %get-tuple-element.41), channel_id=1, source_target_pairs={{0,112},{16,0},{32,16},{48,32},{64,48},{80,64},{96,80},{112,96},{1... | collective-permute-start | bytes 393224 | tf_op jit(solution)/shard_map/ppermute | solution.py:493
  10.5 26.8 %collective-permute-start.4 = (f32[4,256,256]{2,1,0:T(8,128)S(1)}, f32[4,256,256]{2,1,0:T(8,128)S(1)}, u32[]{:S(2)}, u32[]{:S(2)}) collective-permute-start(f32[4,256,256]{2,1,0:T(8,128)S(1)} %get-tuple-element.37), channel_id=1, source_target_pairs={{0,1},{1,0},{2,3},{3,2},{4,5},{5,4},{6,7},{7,6},{8,9},{9,8},{10,11... | collective-permute-start | bytes 3145736 | tf_op jit(solution)/shard_map/ppermute | solution.py:500
  10.5 26.8 %collective-permute-start.5 = (f32[4,256,256]{2,1,0:T(8,128)S(1)}, f32[4,256,256]{2,1,0:T(8,128)S(1)}, u32[]{:S(2)}, u32[]{:S(2)}) collective-permute-start(f32[4,256,256]{2,1,0:T(8,128)S(1)} %get-tuple-element.38), channel_id=1, source_target_pairs={{0,15},{1,2},{2,1},{3,4},{4,3},{5,6},{6,5},{7,8},{8,7},{9,10},{10,... | collective-permute-start | bytes 3145736 | tf_op jit(solution)/shard_map/ppermute | solution.py:499
  15.1 5.4 %copy-start = (f32[1,8,256,256]{3,2,1,0:T(8,128)S(1)}, f32[1,8,256,256]{3,2,1,0:T(8,128)}, u32[]{:S(2)}) copy-start(f32[1,8,256,256]{3,2,1,0:T(8,128)} %psi_re.1) | copy-start | bytes 6291460
  15.1 5.4 %copy-start.1 = (f32[1,8,256,256]{3,2,1,0:T(8,128)S(1)}, f32[1,8,256,256]{3,2,1,0:T(8,128)}, u32[]{:S(2)}) copy-start(f32[1,8,256,256]{3,2,1,0:T(8,128)} %psi_im.1) | copy-start | bytes 6291460
  15.1 5.4 %copy-start.2 = (bf16[256,256]{1,0:T(8,128)(2,1)S(1)}, bf16[256,256]{1,0:T(8,128)(2,1)}, u32[]{:S(2)}) copy-start(bf16[256,256]{1,0:T(8,128)(2,1)} %constant.8.clone.sides.refs_0_) | copy-start | bytes 393220
  17.1 7.7 %collective-permute-start.1 = (f32[8,32,256]{2,1,0:T(8,128)S(1)}, f32[8,32,256]{2,1,0:T(8,128)S(1)}, u32[]{:S(2)}, u32[]{:S(2)}) collective-permute-start(f32[8,32,256]{2,1,0:T(8,128)S(1)} %pad_maximum_fusion), channel_id=1, source_target_pairs={{0,16},{16,32},{32,48},{48,64},{64,80},{80,96},{96,112},{112,0},{1... | collective-permute-start | bytes 786440 | tf_op jit(solution)/shard_map/ppermute | solution.py:489
  17.3 7.6 %collective-permute-start.7 = (f32[8,32,256]{2,1,0:T(8,128)S(1)}, f32[8,32,256]{2,1,0:T(8,128)S(1)}, u32[]{:S(2)}, u32[]{:S(2)}) collective-permute-start(f32[8,32,256]{2,1,0:T(8,128)S(1)} %pad_maximum_fusion.1), channel_id=1, source_target_pairs={{0,112},{16,0},{32,16},{48,32},{64,48},{80,64},{96,80},{112,96},{1... | collective-permute-start | bytes 786440 | tf_op jit(solution)/shard_map/ppermute | solution.py:493
  24.8 8.4 %collective-permute-start.2 = (f32[8,32,256]{2,1,0:T(8,128)S(1)}, f32[8,32,256]{2,1,0:T(8,128)S(1)}, u32[]{:S(2)}, u32[]{:S(2)}) collective-permute-start(f32[8,32,256]{2,1,0:T(8,128)S(1)} %add.19), channel_id=1, source_target_pairs={{0,16},{16,32},{32,48},{48,64},{64,80},{80,96},{96,112},{112,0},{1... | collective-permute-start | bytes 786440 | tf_op jit(solution)/shard_map/ppermute | solution.py:489
  25.0 8.4 %collective-permute-start.8 = (f32[8,32,256]{2,1,0:T(8,128)S(1)}, f32[8,32,256]{2,1,0:T(8,128)S(1)}, u32[]{:S(2)}, u32[]{:S(2)}) collective-permute-start(f32[8,32,256]{2,1,0:T(8,128)S(1)} %add.22), channel_id=1, source_target_pairs={{0,112},{16,0},{32,16},{48,32},{64,48},{80,64},{96,80},{112,96},{1... | collective-permute-start | bytes 786440 | tf_op jit(solution)/shard_map/ppermute | solution.py:493
  33.2 7.7 %collective-permute-start.3 = (f32[8,32,256]{2,1,0:T(8,128)S(1)}, f32[8,32,256]{2,1,0:T(8,128)S(1)}, u32[]{:S(2)}, u32[]{:S(2)}) collective-permute-start(f32[8,32,256]{2,1,0:T(8,128)S(1)} %add.20), channel_id=1, source_target_pairs={{0,16},{16,32},{32,48},{48,64},{64,80},{80,96},{96,112},{112,0},{1... | collective-permute-start | bytes 786440 | tf_op jit(solution)/shard_map/ppermute | solution.py:489
  33.4 22.1 %copy-start.3 = (f32[256,256]{1,0:T(8,128)S(1)}, f32[256,256]{1,0:T(8,128)}, u32[]{:S(2)}) copy-start(f32[256,256]{1,0:T(8,128)} %constant.6.clone.y_table.x_table.table) | copy-start | bytes 786436
  33.4 22.1 %copy-start.5 = (f32[128,128]{1,0:T(8,128)S(1)}, f32[128,128]{1,0:T(8,128)}, u32[]{:S(2)}) copy-start(f32[128,128]{1,0:T(8,128)} %constant.7.clone.z_table) | copy-start | bytes 196612
  33.4 7.8 %collective-permute-start.9 = (f32[8,32,256]{2,1,0:T(8,128)S(1)}, f32[8,32,256]{2,1,0:T(8,128)S(1)}, u32[]{:S(2)}, u32[]{:S(2)}) collective-permute-start(f32[8,32,256]{2,1,0:T(8,128)S(1)} %add.23), channel_id=1, source_target_pairs={{0,112},{16,0},{32,16},{48,32},{64,48},{80,64},{96,80},{112,96},{1... | collective-permute-start | bytes 786440 | tf_op jit(solution)/shard_map/ppermute | solution.py:493
  69.1 10.3 %collective-permute-start.13 = (f32[32,8,256]{2,1,0:T(8,128)S(1)}, f32[32,8,256]{2,1,0:T(8,128)S(1)}, u32[]{:S(2)}, u32[]{:S(2)}) collective-permute-start(f32[32,8,256]{2,1,0:T(8,128)S(1)} %all_to_all.11.refs_0_), channel_id=1, source_target_pairs={{0,16},{16,32},{32,48},{48,64},{64,80},{80,96},{96,112},{112,0},{1... | collective-permute-start | bytes 786440 | tf_op jit(solution)/shard_map/ppermute | solution.py:489
  69.8 9.7 %collective-permute-start.10 = (f32[32,8,256]{2,1,0:T(8,128)S(1)}, f32[32,8,256]{2,1,0:T(8,128)S(1)}, u32[]{:S(2)}, u32[]{:S(2)}) collective-permute-start(f32[32,8,256]{2,1,0:T(8,128)S(1)} %all_to_all.11.refs_0_), channel_id=1, source_target_pairs={{0,112},{16,0},{32,16},{48,32},{64,48},{80,64},{96,80},{112,96},{1... | collective-permute-start | bytes 786440 | tf_op jit(solution)/shard_map/ppermute | solution.py:493
  73.9 27.2 %copy-start.4 = (f32[8,256,256]{2,1,0:T(8,128)S(1)}, f32[8,256,256]{2,1,0:T(8,128)}, u32[]{:S(2)}) copy-start(f32[8,256,256]{2,1,0:T(8,128)} %v_local.1) | copy-start | bytes 6291460
  79.5 9.4 %collective-permute-start.14 = (f32[32,8,256]{2,1,0:T(8,128)S(1)}, f32[32,8,256]{2,1,0:T(8,128)S(1)}, u32[]{:S(2)}, u32[]{:S(2)}) collective-permute-start(f32[32,8,256]{2,1,0:T(8,128)S(1)} %collective-permute-done.13.refs_6_), channel_id=1, source_target_pairs={{0,16},{16,32},{32,48},{48,64},{64,80},{80,96},{96,112},{112,0},{1... | collective-permute-start | bytes 786440 | tf_op jit(solution)/shard_map/ppermute | solution.py:489
  79.6 9.3 %collective-permute-start.11 = (f32[32,8,256]{2,1,0:T(8,128)S(1)}, f32[32,8,256]{2,1,0:T(8,128)S(1)}, u32[]{:S(2)}, u32[]{:S(2)}) collective-permute-start(f32[32,8,256]{2,1,0:T(8,128)S(1)} %collective-permute-done.10.refs_1_), channel_id=1, source_target_pairs={{0,112},{16,0},{32,16},{48,32},{64,48},{80,64},{96,80},{112,96},{1... | collective-permute-start | bytes 786440 | tf_op jit(solution)/shard_map/ppermute | solution.py:493
  88.9 8.6 %collective-permute-start.15 = (f32[32,8,256]{2,1,0:T(8,128)S(1)}, f32[32,8,256]{2,1,0:T(8,128)S(1)}, u32[]{:S(2)}, u32[]{:S(2)}) collective-permute-start(f32[32,8,256]{2,1,0:T(8,128)S(1)} %collective-permute-done.14.refs_5_), channel_id=1, source_target_pairs={{0,16},{16,32},{32,48},{48,64},{64,80},{80,96},{96,112},{112,0},{1... | collective-permute-start | bytes 786440 | tf_op jit(solution)/shard_map/ppermute | solution.py:489
  88.9 8.9 %collective-permute-start.12 = (f32[32,8,256]{2,1,0:T(8,128)S(1)}, f32[32,8,256]{2,1,0:T(8,128)S(1)}, u32[]{:S(2)}, u32[]{:S(2)}) collective-permute-start(f32[32,8,256]{2,1,0:T(8,128)S(1)} %collective-permute-done.11.refs_2_), channel_id=1, source_target_pairs={{0,112},{16,0},{32,16},{48,32},{64,48},{80,64},{96,80},{112,96},{1... | collective-permute-start | bytes 786440 | tf_op jit(solution)/shard_map/ppermute | solution.py:493
  97.5 6.5 %collective-permute-start.16 = (f32[16,8,256]{2,1,0:T(8,128)S(1)}, f32[16,8,256]{2,1,0:T(8,128)S(1)}, u32[]{:S(2)}, u32[]{:S(2)}) collective-permute-start(f32[16,8,256]{2,1,0:T(8,128)S(1)} %slice.24), channel_id=1, source_target_pairs={{0,16},{16,32},{32,48},{48,64},{64,80},{80,96},{96,112},{112,0},{1... | collective-permute-start | bytes 393224 | tf_op jit(solution)/shard_map/ppermute | solution.py:489
  97.8 6.1 %collective-permute-start.17 = (f32[16,8,256]{2,1,0:T(8,128)S(1)}, f32[16,8,256]{2,1,0:T(8,128)S(1)}, u32[]{:S(2)}, u32[]{:S(2)}) collective-permute-start(f32[16,8,256]{2,1,0:T(8,128)S(1)} %slice.25), channel_id=1, source_target_pairs={{0,112},{16,0},{32,16},{48,32},{64,48},{80,64},{96,80},{112,96},{1... | collective-permute-start | bytes 393224 | tf_op jit(solution)/shard_map/ppermute | solution.py:493
  104.2 6.6 %collective-permute-start.18 = (f32[1,256,256]{2,1,0:T(8,128)S(1)}, f32[1,256,256]{2,1,0:T(8,128)S(1)}, u32[]{:S(2)}, u32[]{:S(2)}) collective-permute-start(f32[1,256,256]{2,1,0:T(8,128)S(1)} %get-tuple-element.50), channel_id=1, source_target_pairs={{0,1},{1,0},{2,3},{3,2},{4,5},{5,4},{6,7},{7,6},{8,9},{9,8},{10,11... | collective-permute-start | bytes 786440 | tf_op jit(solution)/shard_map/ppermute | solution.py:500
  104.3 9.5 %collective-permute-start.19 = (f32[1,256,256]{2,1,0:T(8,128)S(1)}, f32[1,256,256]{2,1,0:T(8,128)S(1)}, u32[]{:S(2)}, u32[]{:S(2)}) collective-permute-start(f32[1,256,256]{2,1,0:T(8,128)S(1)} %get-tuple-element.51), channel_id=1, source_target_pairs={{0,15},{1,2},{2,1},{3,4},{4,3},{5,6},{6,5},{7,8},{8,7},{9,10},{10,... | collective-permute-start | bytes 786440 | tf_op jit(solution)/shard_map/ppermute | solution.py:499

commit v6 on v5

--- a/solution.py
+++ b/solution.py
@@ -31,6 +31,23 @@
     return jnp.dot(left, right, precision=HIGHEST, preferred_element_type=jnp.float32)
 
 
+def terms(value, count):
+    found = []
+    for _ in range(count):
+        found.append(value.astype(jnp.bfloat16))
+        value = value - found[-1].astype(jnp.float32)
+    return found
+
+
+def dot_three(left, right):
+    (a, b), (c, d) = terms(left, 2), terms(right, 2)
+
+    def one(x, y):
+        return jnp.dot(x, y, preferred_element_type=jnp.float32)
+
+    return one(a, c) + (one(a, d) + one(b, c))
+
+
 def shaped(*shape):
     return jax.ShapeDtypeStruct(shape, jnp.float32)
 
@@ -51,8 +68,9 @@
     ring = lax.axis_size("z")
     width = rows.shape[0] // ring
     z = lax.axis_index("z")
+    step = 1 + lax.rem(z, 2) * (ring - 2)
     for offset in range(ring):
-        start = pl.multiple_of(lax.rem(z + offset, ring) * width, width)
+        start = pl.multiple_of(lax.rem(z + offset * step, ring) * width, width)
         rows[offset * width : (offset + 1) * width, :] = table[pl.ds(start, width), :]
 
 
@@ -190,7 +208,7 @@
     greens = jnp.where(anchor, jnp.float32(0.0), (4.0 * math.pi) / safe) * (1.0 / (nz * y_len * nx))
     rho = field[0:nz] + field[nz : 2 * nz]
     spectrum = dot(z_table[...], dot(rho, x_table[...]))
-    solved = dot(dot(z_table[...], spectrum * greens), x_table[...])
+    solved = dot_three(dot_three(z_table[...], spectrum * greens), x_table[...])
     solved = solved.reshape((half,) + out.shape[1:])
     out[0:half] = solved
     out[half:] = solved
@@ -311,14 +329,6 @@
     return pltpu.roll(table[...], ny - lax.axis_index("z") * (ny // lax.axis_size("z")), 1)
 
 
-def terms(value, count):
-    found = []
-    for _ in range(count):
-        found.append(value.astype(jnp.bfloat16))
-        value = value - found[-1].astype(jnp.float32)
-    return found
-
-
 LEFT_TERMS = (0, 0, 1, 1, 0, 2)
 RIGHT_TERMS = (0, 1, 0, 1, 2, 0)
 
@@ -330,10 +340,17 @@
     first = columns.shape[1] // 2
     left = terms(columns[:, first : first + width], 3)
     tail[...] = jnp.concatenate([left[i] for i in LEFT_TERMS], axis=1)
-    for z in range(v_local.shape[0]):
-        rows = [hat[:, z, :] for hat in hats]
-        rows.insert(len(hats) // 2 + 1, jnp.zeros_like(rows[0]))
-        pot[z] = v_local[z] + dot(columns, jnp.concatenate(rows, axis=0))
+    hats = list(hats)
+    hats.insert(len(hats) // 2 + 1, None)
+    even = lax.rem(lax.axis_index("z"), 2) == 0
+
+    def fill(order):
+        for z in range(v_local.shape[0]):
+            rows = [jnp.zeros((width, columns.shape[1]), jnp.float32) if h is None else h[:, z, :] for h in order]
+            pot[z] = v_local[z] + dot(columns, jnp.concatenate(rows, axis=0))
+
+    pl.when(even)(functools.partial(fill, hats))
+    pl.when(jnp.logical_not(even))(functools.partial(fill, hats[:1] + hats[:0:-1]))
 
 
 def early_potential(v_local, table, hats):
@@ -480,23 +497,25 @@
     )(open_ends, *v_planes, *edges, new_re, new_im)
 
 
-def ring(axis, shift):
-    count = lax.axis_size(axis)
-    return [(i, (i + shift) % count) for i in range(count)]
-
-
-def forward(value, axis="z"):
-    return lax.ppermute(value, axis, ring(axis, 1))
-
-
-def backward(value, axis="z"):
-    return lax.ppermute(value, axis, ring(axis, -1))
-
-
-def swap_edges(to_mate, to_other):
+def swap_near(value):
+    return lax.ppermute(value, "z", [(i, i ^ 1) for i in range(lax.axis_size("z"))])
+
+
+def swap_far(value):
+    count = lax.axis_size("z")
+    return lax.ppermute(value, "z", [(i, (i - 1) % count if i % 2 == 0 else (i + 1) % count) for i in range(count)])
+
+
+def swap_edges(to_mate, to_other, same_on_orb=False):
     count = lax.axis_size("slab")
-    others = [(i, (i - 1) % count if i % 2 == 0 else (i + 1) % count) for i in range(count)]
-    from_other = lax.ppermute(to_other, "slab", others)
+    pairs = []
+    for y in range(SIDES):
+        for slab in range(count):
+            other = (slab - 1) % count if slab % 2 == 0 else (slab + 1) % count
+            crossing = slab * 2 // count != other * 2 // count
+            side = (y + 1) % SIDES if crossing and same_on_orb else y
+            pairs.append((y * count + slab, side * count + other))
+    from_other = lax.ppermute(to_other, ("y", "slab"), pairs)
     from_mate = lax.ppermute(to_mate, "slab", [(i, i ^ 1) for i in range(count)])
     return from_mate, from_other
 
@@ -508,28 +527,28 @@
 def sum_over_ring(first, second, pieces, beside):
     s0, s1, s2, s3, s5, s6, s7 = pieces
     half = first.shape[1]
-    got_up, got_down = forward(first), backward(second)
-    up = jnp.concatenate([s3[:, :half] + got_up, s3[:, half:]], axis=1)
-    down = jnp.concatenate([s5[:, :half], s5[:, half:] + got_down], axis=1)
-    up, down = forward(up), backward(down)
-    up = after(up, *beside[0])
-    up, down = forward(up + s2), backward(down + s6)
-    up = after(up, *beside[1])
-    up, down = forward(up + s1), backward(down + s7)
-    up = after(up, *beside[2])
-    return add_shares(s0, up, down)
+    near, far = swap_near(first), swap_far(second)
+    near = jnp.concatenate([s5[:, :half] + near, s5[:, half:]], axis=1)
+    far = jnp.concatenate([s3[:, :half], s3[:, half:] + far], axis=1)
+    near, far = swap_far(near), swap_near(far)
+    near, far = after(near, *beside[0]), after(far, *beside[0])
+    near, far = swap_near(near + s2), swap_far(far + s6)
+    near, far = after(near, *beside[1]), after(far, *beside[1])
+    near, far = swap_far(near + s7), swap_near(far + s1)
+    near, far = after(near, *beside[2]), after(far, *beside[2])
+    return add_shares(s0, near, far)
 
 
 def gather_over_ring(block, beside, early):
     half = block.shape[0] // 2
-    up1, down1 = forward(block), backward(block)
-    up1 = after(up1, *beside[0])
-    up2, down2 = forward(up1), backward(down1)
-    up2 = after(up2, *beside[1])
-    up3, down3 = forward(up2), backward(down2)
-    up4, down4 = forward(up3[:half]), backward(down3[half:])
-    made = early([block, down1, down2, down3, up3, up2, up1])
-    return made, (after(up4, *made), down4)
+    near1, far1 = swap_near(block), swap_far(block)
+    near1, far1 = after(near1, *beside[0]), after(far1, *beside[0])
+    near2, far2 = swap_near(far1), swap_far(near1)
+    near2, far2 = after(near2, *beside[1]), after(far2, *beside[1])
+    near3, far3 = swap_near(far2), swap_far(near2)
+    near4, far4 = swap_near(far3[:half]), swap_far(near3[half:])
+    made = early([block, near1, near2, near3, far3, far2, far1])
+    return made, (after(near4, *made), far4)
 
 
 def across(value):
@@ -566,7 +585,7 @@
         [[bases[0]], [bases[1]]],
         functools.partial(early_potential, v_local, y_table),
     )
-    v_planes = swap_edges(*outer_potential(early, tail, late))
+    v_planes = swap_edges(*outer_potential(early, tail, late), same_on_orb=True)
     new_re, new_im, open_ends = inner_update(
         sides, early, tail, late, near, onces, once_groups, bases, base_groups
     )

time: 117 us -> 113 us (0.966)
  waiting for transfers between devices: 29 us -> 42.5 us
  starting transfers between devices: 36.8 us -> 23.6 us
  blocking collectives: 26.6 us -> 23.2 us
    ppermute x18, waiting for transfers between devices: 29 us -> 42.5 us  [the longest x8 25.9 us: swap_far(): lax.ppermute(value, 'z', [(i, (i - 1) % count if i % 2 == 0 else (i + 1)...]
    ppermute x18, starting transfers between devices: 36.7 us -> 23.5 us  [the longest x8 14.5 us: swap_far(): lax.ppermute(value, 'z', [(i, (i - 1) % count if i % 2 == 0 else (i + 1)...]
    all_to_all x2, blocking collectives: 26.6 us -> 23.2 us  [across(): lax.all_to_all(value, ('y', 'slab'), split_axis=0, concat_axis=0, tiled=T...]
  transfers between devices with their start and end apart: 20 -> 20, of which waited for: 10 -> 13; matrix products, arithmetic and copies ran while one was open for 0% -> 0% of each run, Pallas kernels for 13% -> 14%
where the time goes in v6:
time: 113 us; the launch traced here: 112 us
  waiting for transfers between devices  42.5 us (38%)
  starting transfers between devices  23.6 us (21%)
  blocking collectives  23.2 us (21%)
  Pallas kernels  21.7 us (19%)
    ppermute x8, waiting for transfers between devices, swap_far(): lax.ppermute(value, 'z', [(i, (i - 1) % count if i % 2 == 0 else (i + 1)...  25.9 us
    all_to_all x2, blocking collectives, across(): lax.all_to_all(value, ('y', 'slab'), split_axis=0, concat_axis=0, tiled=T...  23.2 us
    ppermute x8, starting transfers between devices, swap_far(): lax.ppermute(value, 'z', [(i, (i - 1) % count if i % 2 == 0 else (i + 1)...  14.5 us
    ppermute x8, waiting for transfers between devices, swap_near(): lax.ppermute(value, 'z', [(i, i ^ 1) for i in range(lax.axis_size('z'))])  14.3 us
    ppermute x2, starting transfers between devices, swap_edges(): from_other = lax.ppermute(to_other, ('y', 'slab'), pairs)  5.82 us
    pallas_call x1, Pallas kernels, inner_update(): pl.pallas_call(functools.partial(inner_kernel, once_groups, base_groups),...  4.5 us
    pallas_call x1, Pallas kernels, density(): pl.pallas_call(functools.partial(density_kernel, 2.0 / total_orbs), in_sp...  3.85 us
    ppermute x8, starting transfers between devices, swap_near(): lax.ppermute(value, 'z', [(i, i ^ 1) for i in range(lax.axis_size('z'))])  3.21 us
  transfers between devices with their start and end apart: 20, of which 13 were waited for; matrix products, arithmetic and copies ran while one was open for 0% of the time, Pallas kernels for 14%

profile of v6, /device:TPU:8, one launch (start us, length us, event | category | flops | bytes accessed | tf_op | source)
XLA Modules:
  0.0 112.3 jit_solution(2471248705567070145)
XLA Ops:
  0.6 3.8 %density.1 = (f32[8,256,256]{2,1,0:T(8,128)S(1)}, f32[256,256]{1,0:T(8,128)S(1)}, f32[8,16,256]{2,1,0:T(8,128)S(1)}, f32[8,16,256]{2,1,0:T(8,128)S(1)}, f32[4,25...) custom-call(f32[1,8,256,256]{3,2,1,0:T(8,128)} %psi_re.1, f32[1,8,256,256]{3,2,1,0:T(8,128)} %psi_im.1, ...), custom_call_target="tpu_custom_call" | custom-call | tf_op jit(solution)/shard_map/density/pallas_call | solution.py:135
  4.5 6.0 %collective-permute-start.6 = (f32[8,16,256]{2,1,0:T(8,128)S(1)}, f32[8,16,256]{2,1,0:T(8,128)S(1)}, u32[]{:S(2)}, u32[]{:S(2)}) collective-permute-start(f32[8,16,256]{2,1,0:T(8,128)S(1)} %get-tuple-element.46), channel_id=1, source_target_pairs={{0,112},{16,32},{32,16},{48,64},{64,48},{80,96},{96,80},{112,0},{1... | collective-permute-start | bytes 393224 | tf_op jit(solution)/shard_map/ppermute | solution.py:506
  10.4 0.0 collective-permute-start
  10.4 4.6 %collective-permute-start.5 = (f32[4,256,256]{2,1,0:T(8,128)S(1)}, f32[4,256,256]{2,1,0:T(8,128)S(1)}, u32[]{:S(2)}, u32[]{:S(2)}) collective-permute-start(f32[4,256,256]{2,1,0:T(8,128)S(1)} %get-tuple-element.43), channel_id=1, source_target_pairs={{0,15},{1,2},{2,1},{3,4},{4,3},{5,6},{6,5},{7,8},{8,7},{9,10},{10,... | collective-permute-start | bytes 3145736 | tf_op jit(solution)/shard_map/ppermute | solution.py:518
  15.1 1.9 %shares.1 = (f32[8,32,256]{2,1,0:T(8,128)S(1)}, f32[8,32,256]{2,1,0:T(8,128)S(1)}, f32[8,32,256]{2,1,0:T(8,128)S(1)}, f32[8,32,256]{2,1,0:T(8,128)S(1)}, f32[8,3...) custom-call(f32[8,256,256]{2,1,0:T(8,128)S(1)} %get-tuple-element.33.rho, ...), custom_call_target="tpu_custom_call" | custom-call | bytes 7200000 | tf_op jit(solution)/shard_map/shares/pallas_call | solution.py:163
  17.0 2.1 %collective-permute-start.7 = (f32[8,32,256]{2,1,0:T(8,128)S(1)}, f32[8,32,256]{2,1,0:T(8,128)S(1)}, u32[]{:S(2)}, u32[]{:S(2)}) collective-permute-start(f32[8,32,256]{2,1,0:T(8,128)S(1)} %pad_maximum_fusion.1), channel_id=1, source_target_pairs={{0,16},{16,0},{32,48},{48,32},{64,80},{80,64},{96,112},{112,96},{1... | collective-permute-start | bytes 786440 | tf_op jit(solution)/shard_map/ppermute | solution.py:501
  19.2 0.2 collective-permute-start.1
  19.4 0.9 once_a.1.refs_0_.refs_7_
  20.3 3.2 %collective-permute-done.7 = f32[8,32,256]{2,1,0:T(8,128)S(1)} collective-permute-done((f32[8,32,256]{2,1,0:T(8,128)S(1)}, f32[8,32,256]{2,1,0:T(8,128)S(1)}, u32[]{:S(2)}, u32[]{:S(2)}) %collective-permute-start.7) | collective-permute-done | bytes 262176 | tf_op jit(solution)/shard_map/ppermute | solution.py:501
  23.5 2.1 %collective-permute-start.8 = (f32[8,32,256]{2,1,0:T(8,128)S(1)}, f32[8,32,256]{2,1,0:T(8,128)S(1)}, u32[]{:S(2)}, u32[]{:S(2)}) collective-permute-start(f32[8,32,256]{2,1,0:T(8,128)S(1)} %add.22), channel_id=1, source_target_pairs={{0,112},{16,32},{32,16},{48,64},{64,48},{80,96},{96,80},{112,0},{1... | collective-permute-start | bytes 786440 | tf_op jit(solution)/shard_map/ppermute | solution.py:506
  25.6 3.9 %collective-permute-done.1 = f32[8,32,256]{2,1,0:T(8,128)S(1)} collective-permute-done((f32[8,32,256]{2,1,0:T(8,128)S(1)}, f32[8,32,256]{2,1,0:T(8,128)S(1)}, u32[]{:S(2)}, u32[]{:S(2)}) %collective-permute-start.1) | collective-permute-done | bytes 262176 | tf_op jit(solution)/shard_map/ppermute | solution.py:506
  29.5 0.1 collective-permute-start.2
  29.6 0.9 once_b.1.refs_1_.refs_8_
  30.5 1.7 %collective-permute-done.8 = f32[8,32,256]{2,1,0:T(8,128)S(1)} collective-permute-done((f32[8,32,256]{2,1,0:T(8,128)S(1)}, f32[8,32,256]{2,1,0:T(8,128)S(1)}, u32[]{:S(2)}, u32[]{:S(2)}) %collective-permute-start.8) | collective-permute-done | bytes 262176 | tf_op jit(solution)/shard_map/ppermute | solution.py:506
  32.3 0.4 collective-permute-start.9
  32.7 5.0 %collective-permute-done.2 = f32[8,32,256]{2,1,0:T(8,128)S(1)} collective-permute-done((f32[8,32,256]{2,1,0:T(8,128)S(1)}, f32[8,32,256]{2,1,0:T(8,128)S(1)}, u32[]{:S(2)}, u32[]{:S(2)}) %collective-permute-start.2) | collective-permute-done | bytes 262176 | tf_op jit(solution)/shard_map/ppermute | solution.py:501
  37.8 0.0 copy-start.3
  37.8 0.0 copy-start.5
  37.8 0.6 collective-permute-start.3
  38.4 1.2 %once_c.1.refs_2_.refs_9_ = f32[2,4,256,256]{3,2,1,0:T(8,128)S(1)} custom-call(bf16[256,256]{1,0:T(8,128)(2,1)S(1)} %copy-done.2, f32[8,256,256]{2,1,0:T(8,128)S(1)} %bitcast.5, f32[8,256,256]{2,1,0:T(8,128)S(1)} %bitcast.11, f32[4,256,256]{2,1,0:T(8,128)S(1)} %collective-permute-done.4.refs_2_.mate, f32[4,256,256]{2,1,0:T(8,128)S(1)} %collective-permute-done.5.refs_3_.other), custom_call_target="tpu_custom_call" | custom-call | bytes 4320000 | tf_op jit(solution)/shard_map/once_c/pallas_call | solution.py:287
  39.6 0.9 collective-permute-done.9.down
  40.5 4.9 %collective-permute-done.3.up = f32[8,32,256]{2,1,0:T(8,128)S(1)} collective-permute-done((f32[8,32,256]{2,1,0:T(8,128)S(1)}, f32[8,32,256]{2,1,0:T(8,128)S(1)}, u32[]{:S(2)}, u32[]{:S(2)}) %collective-permute-start.3) | collective-permute-done | bytes 262176 | tf_op jit(solution)/shard_map/ppermute | solution.py:506
  45.5 0.1 add_shares.1
  45.6 10.8 %all_to_all.10 = f32[32,8,256]{2,1,0:T(8,128)S(1)} all-to-all(f32[32,8,256]{2,1,0:T(8,128)S(1)} %add_shares.1), channel_id=1, replica_groups=mesh['y'=2,'z'=8,'slab'=16] {'y','slab'}, dimensions={0} | all-to-all | bytes 524288 | tf_op jit(solution)/shard_map/all_to_all | solution.py:555
  56.4 1.1 solve_xz.1
  57.5 12.3 %all_to_all.11.refs_0_ = f32[32,8,256]{2,1,0:T(8,128)S(1)} all-to-all(f32[32,8,256]{2,1,0:T(8,128)S(1)} %solve_xz.1), channel_id=1, replica_groups=mesh['y'=2,'z'=8,'slab'=16] {'y','slab'}, dimensions={0} | all-to-all | bytes 524288 | tf_op jit(solution)/shard_map/all_to_all | solution.py:555
  69.8 1.1 collective-permute-start.11
  70.9 1.5 %base_a.1.refs_10_ = f32[2,4,256,256]{3,2,1,0:T(8,128)S(1)} custom-call(bf16[256,256]{1,0:T(8,128)(2,1)S(1)} %copy-done.2, f32[8,256,256]{2,1,0:T(8,128)S(1)} %bitcast.6, f32[8,256,256]{2,1,0:T(8,128)S(1)} %bitcast.12, f32[2,3,256,256]{3,2,1,0:T(8,128)S(1)} %once_a.1.refs_0_.refs_7_, f32[2,3,256,256]{3,2,1,0:T(8,128)S(1)} %once_b.1.refs_1_.refs_8_, ...), custom_call_target="tpu_custom_call" | custom-call | bytes 5760000 | tf_op jit(solution)/shard_map/base_a/pallas_call | solution.py:316
  72.5 0.0 copy-start.4
  72.5 7.3 %collective-permute-done.11.refs_6_ = f32[32,8,256]{2,1,0:T(8,128)S(1)} collective-permute-done((f32[32,8,256]{2,1,0:T(8,128)S(1)}, f32[32,8,256]{2,1,0:T(8,128)S(1)}, u32[]{:S(2)}, u32[]{:S(2)}) %collective-permute-start.11) | collective-permute-done | bytes 262176 | tf_op jit(solution)/shard_map/ppermute | solution.py:506
  79.8 1.7 %collective-permute-start.13 = (f32[32,8,256]{2,1,0:T(8,128)S(1)}, f32[32,8,256]{2,1,0:T(8,128)S(1)}, u32[]{:S(2)}, u32[]{:S(2)}) collective-permute-start(f32[32,8,256]{2,1,0:T(8,128)S(1)} %collective-permute-done.10.refs_1_), channel_id=1, source_target_pairs={{0,112},{16,32},{32,16},{48,64},{64,48},{80,96},{96,80},{112,0},{1... | collective-permute-start | bytes 786440 | tf_op jit(solution)/shard_map/ppermute | solution.py:506
  81.6 1.5 %base_b.1.refs_11_ = f32[2,4,256,256]{3,2,1,0:T(8,128)S(1)} custom-call(bf16[256,256]{1,0:T(8,128)(2,1)S(1)} %copy-done.2, f32[8,256,256]{2,1,0:T(8,128)S(1)} %bitcast.7, f32[8,256,256]{2,1,0:T(8,128)S(1)} %bitcast.13, f32[2,3,256,256]{3,2,1,0:T(8,128)S(1)} %once_a.1.refs_0_.refs_7_, f32[2,3,256,256]{3,2,1,0:T(8,128)S(1)} %once_b.1.refs_1_.refs_8_, ...), custom_call_target="tpu_custom_call" | custom-call | bytes 5760000 | tf_op jit(solution)/shard_map/base_b/pallas_call | solution.py:316
  83.1 4.8 %collective-permute-done.12.refs_2_ = f32[32,8,256]{2,1,0:T(8,128)S(1)} collective-permute-done((f32[32,8,256]{2,1,0:T(8,128)S(1)}, f32[32,8,256]{2,1,0:T(8,128)S(1)}, u32[]{:S(2)}, u32[]{:S(2)}) %collective-permute-start.12) | collective-permute-done | bytes 262176 | tf_op jit(solution)/shard_map/ppermute | solution.py:501
  87.9 1.1 collective-permute-start.15
  89.0 0.1 collective-permute-done.13.refs_5_
  89.1 0.5 collective-permute-start.14
  89.6 6.6 %collective-permute-done.15.refs_4_ = f32[32,8,256]{2,1,0:T(8,128)S(1)} collective-permute-done((f32[32,8,256]{2,1,0:T(8,128)S(1)}, f32[32,8,256]{2,1,0:T(8,128)S(1)}, u32[]{:S(2)}, u32[]{:S(2)}) %collective-permute-start.15) | collective-permute-done | bytes 262176 | tf_op jit(solution)/shard_map/ppermute | solution.py:506
  96.3 0.1 collective-permute-start.16
  96.4 1.7 %collective-permute-start.17 = (f32[16,8,256]{2,1,0:T(8,128)S(1)}, f32[16,8,256]{2,1,0:T(8,128)S(1)}, u32[]{:S(2)}, u32[]{:S(2)}) collective-permute-start(f32[16,8,256]{2,1,0:T(8,128)S(1)} %slice.25), channel_id=1, source_target_pairs={{0,112},{16,32},{32,16},{48,64},{64,48},{80,96},{96,80},{112,0},{1... | collective-permute-start | bytes 393224 | tf_op jit(solution)/shard_map/ppermute | solution.py:506
  98.1 2.8 %early_potential.1 = (f32[8,256,256]{2,1,0:T(8,128)S(1)}, bf16[256,192]{1,0:T(8,128)(2,1)S(1)}) custom-call(f32[8,256,256]{2,1,0:T(8,128)S(1)} %copy-done.4, f32[256,256]{1,0:T(8,128)S(1)} %copy-done.3, f32[32,8,256]{2,1,0:T(8,128)S(1)} %all_to_all.11.refs_0_, f32[32,8,256]{2,1,0:T(8,128)S(1)} %collective-permute-done.10.refs_1_, ...), custom_call_target="tpu_custom_call" | custom-call | bytes 8279999 | tf_op jit(solution)/shard_map/early_potential/pallas_call | solution.py:359
  100.9 0.4 collective-permute-done.16.refs_3_.up
  101.3 1.3 %collective-permute-done.17.refs_4_.down = f32[16,8,256]{2,1,0:T(8,128)S(1)} collective-permute-done((f32[16,8,256]{2,1,0:T(8,128)S(1)}, f32[16,8,256]{2,1,0:T(8,128)S(1)}, u32[]{:S(2)}, u32[]{:S(2)}) %collective-permute-start.17) | collective-permute-done | bytes 131104 | tf_op jit(solution)/shard_map/ppermute | solution.py:506
  102.7 0.2 outer_potential.1
  102.9 0.1 collective-permute-start.18
  103.0 1.2 %collective-permute-start.19 = (f32[1,256,256]{2,1,0:T(8,128)S(1)}, f32[1,256,256]{2,1,0:T(8,128)S(1)}, u32[]{:S(2)}, u32[]{:S(2)}) collective-permute-start(f32[1,256,256]{2,1,0:T(8,128)S(1)} %get-tuple-element.61), channel_id=1, source_target_pairs={{0,143},{1,2},{2,1},{3,4},{4,3},{5,6},{6,5},{7,136},{8,135},{9,10}... | collective-permute-start | bytes 786440 | tf_op jit(solution)/shard_map/ppermute | solution.py:518
  104.2 4.5 %inner_update.1 = (f32[1,8,256,256]{3,2,1,0:T(8,128)}, f32[1,8,256,256]{3,2,1,0:T(8,128)}, f32[2,2,256,256]{3,2,1,0:T(8,128)S(1)}) custom-call(bf16[256,256]{1,0:T(8,128)(2,1)S(1)} %copy-done.2, f32[8,256,256]{2,1,0:T(8,128)S(1)} %get-tuple-element.56.refs_1_.early, bf16[256,192]{1,0:T(8,128)(2,1)S(1)} %get-tuple-element.57.refs_2_.tail, ...), custom_call_target="tpu_custom_call" | custom-call | bytes 15480000 | tf_op jit(solution)/shard_map/inner_update/pallas_call | solution.py:449
  108.7 2.3 %collective-permute-done.19.v_other = f32[1,256,256]{2,1,0:T(8,128)S(1)} collective-permute-done((f32[1,256,256]{2,1,0:T(8,128)S(1)}, f32[1,256,256]{2,1,0:T(8,128)S(1)}, u32[]{:S(2)}, u32[]{:S(2)}) %collective-permute-start.19) | collective-permute-done | bytes 262176 | tf_op jit(solution)/shard_map/ppermute | solution.py:518
  111.0 1.1 %close_ends.1 = (f32[1,8,256,256]{3,2,1,0:T(8,128)}, f32[1,8,256,256]{3,2,1,0:T(8,128)}) custom-call(f32[2,2,256,256]{3,2,1,0:T(8,128)S(1)} %get-tuple-element.59.open_ends, f32[1,256,256]{2,1,0:T(8,128)S(1)} %collective-permute-done.18.v_mate, f32[1,256,256]{2,1,0:T(8,128)S(1)} %collective-permute-done.19.v_other, ...), custom_call_target="tpu_custom_call", output_to_operand_aliasing={{0}: (5, {}), {1}: (6, {})} | custom-call | tf_op jit(solution)/shard_map/close_ends/pallas_call | solution.py:488
  (29 shorter events, 0.3 us)
Async XLA Ops:
  4.5 12.5 %collective-permute-start.6 = (f32[8,16,256]{2,1,0:T(8,128)S(1)}, f32[8,16,256]{2,1,0:T(8,128)S(1)}, u32[]{:S(2)}, u32[]{:S(2)}) collective-permute-start(f32[8,16,256]{2,1,0:T(8,128)S(1)} %get-tuple-element.46), channel_id=1, source_target_pairs={{0,112},{16,32},{32,16},{48,64},{64,48},{80,96},{96,80},{112,0},{1... | collective-permute-start | bytes 393224 | tf_op jit(solution)/shard_map/ppermute | solution.py:506
  10.4 8.7 %collective-permute-start = (f32[8,16,256]{2,1,0:T(8,128)S(1)}, f32[8,16,256]{2,1,0:T(8,128)S(1)}, u32[]{:S(2)}, u32[]{:S(2)}) collective-permute-start(f32[8,16,256]{2,1,0:T(8,128)S(1)} %get-tuple-element.37), channel_id=1, source_target_pairs={{0,16},{16,0},{32,48},{48,32},{64,80},{80,64},{96,112},{112,96},{1... | collective-permute-start | bytes 393224 | tf_op jit(solution)/shard_map/ppermute | solution.py:501
  10.4 28.0 %collective-permute-start.4 = (f32[4,256,256]{2,1,0:T(8,128)S(1)}, f32[4,256,256]{2,1,0:T(8,128)S(1)}, u32[]{:S(2)}, u32[]{:S(2)}) collective-permute-start(f32[4,256,256]{2,1,0:T(8,128)S(1)} %get-tuple-element.42), channel_id=1, source_target_pairs={{0,1},{1,0},{2,3},{3,2},{4,5},{5,4},{6,7},{7,6},{8,9},{9,8},{10,11... | collective-permute-start | bytes 3145736 | tf_op jit(solution)/shard_map/ppermute | solution.py:519
  10.4 28.0 %collective-permute-start.5 = (f32[4,256,256]{2,1,0:T(8,128)S(1)}, f32[4,256,256]{2,1,0:T(8,128)S(1)}, u32[]{:S(2)}, u32[]{:S(2)}) collective-permute-start(f32[4,256,256]{2,1,0:T(8,128)S(1)} %get-tuple-element.43), channel_id=1, source_target_pairs={{0,15},{1,2},{2,1},{3,4},{4,3},{5,6},{6,5},{7,8},{8,7},{9,10},{10,... | collective-permute-start | bytes 3145736 | tf_op jit(solution)/shard_map/ppermute | solution.py:518
  15.0 4.4 %copy-start = (f32[1,8,256,256]{3,2,1,0:T(8,128)S(1)}, f32[1,8,256,256]{3,2,1,0:T(8,128)}, u32[]{:S(2)}) copy-start(f32[1,8,256,256]{3,2,1,0:T(8,128)} %psi_re.1) | copy-start | bytes 6291460
  15.0 4.4 %copy-start.1 = (f32[1,8,256,256]{3,2,1,0:T(8,128)S(1)}, f32[1,8,256,256]{3,2,1,0:T(8,128)}, u32[]{:S(2)}) copy-start(f32[1,8,256,256]{3,2,1,0:T(8,128)} %psi_im.1) | copy-start | bytes 6291460
  15.1 4.4 %copy-start.2 = (bf16[256,256]{1,0:T(8,128)(2,1)S(1)}, bf16[256,256]{1,0:T(8,128)(2,1)}, u32[]{:S(2)}) copy-start(bf16[256,256]{1,0:T(8,128)(2,1)} %constant.8.clone.sides.refs_0_) | copy-start | bytes 393220
  17.0 6.5 %collective-permute-start.7 = (f32[8,32,256]{2,1,0:T(8,128)S(1)}, f32[8,32,256]{2,1,0:T(8,128)S(1)}, u32[]{:S(2)}, u32[]{:S(2)}) collective-permute-start(f32[8,32,256]{2,1,0:T(8,128)S(1)} %pad_maximum_fusion.1), channel_id=1, source_target_pairs={{0,16},{16,0},{32,48},{48,32},{64,80},{80,64},{96,112},{112,96},{1... | collective-permute-start | bytes 786440 | tf_op jit(solution)/shard_map/ppermute | solution.py:501
  19.2 10.3 %collective-permute-start.1 = (f32[8,32,256]{2,1,0:T(8,128)S(1)}, f32[8,32,256]{2,1,0:T(8,128)S(1)}, u32[]{:S(2)}, u32[]{:S(2)}) collective-permute-start(f32[8,32,256]{2,1,0:T(8,128)S(1)} %pad_maximum_fusion), channel_id=1, source_target_pairs={{0,112},{16,32},{32,16},{48,64},{64,48},{80,96},{96,80},{112,0},{1... | collective-permute-start | bytes 786440 | tf_op jit(solution)/shard_map/ppermute | solution.py:506
  23.5 8.8 %collective-permute-start.8 = (f32[8,32,256]{2,1,0:T(8,128)S(1)}, f32[8,32,256]{2,1,0:T(8,128)S(1)}, u32[]{:S(2)}, u32[]{:S(2)}) collective-permute-start(f32[8,32,256]{2,1,0:T(8,128)S(1)} %add.22), channel_id=1, source_target_pairs={{0,112},{16,32},{32,16},{48,64},{64,48},{80,96},{96,80},{112,0},{1... | collective-permute-start | bytes 786440 | tf_op jit(solution)/shard_map/ppermute | solution.py:506
  29.5 8.2 %collective-permute-start.2 = (f32[8,32,256]{2,1,0:T(8,128)S(1)}, f32[8,32,256]{2,1,0:T(8,128)S(1)}, u32[]{:S(2)}, u32[]{:S(2)}) collective-permute-start(f32[8,32,256]{2,1,0:T(8,128)S(1)} %add.19), channel_id=1, source_target_pairs={{0,16},{16,0},{32,48},{48,32},{64,80},{80,64},{96,112},{112,96},{1... | collective-permute-start | bytes 786440 | tf_op jit(solution)/shard_map/ppermute | solution.py:501
  32.3 8.2 %collective-permute-start.9 = (f32[8,32,256]{2,1,0:T(8,128)S(1)}, f32[8,32,256]{2,1,0:T(8,128)S(1)}, u32[]{:S(2)}, u32[]{:S(2)}) collective-permute-start(f32[8,32,256]{2,1,0:T(8,128)S(1)} %add.23), channel_id=1, source_target_pairs={{0,16},{16,0},{32,48},{48,32},{64,80},{80,64},{96,112},{112,96},{1... | collective-permute-start | bytes 786440 | tf_op jit(solution)/shard_map/ppermute | solution.py:501
  37.8 18.6 %copy-start.3 = (f32[256,256]{1,0:T(8,128)S(1)}, f32[256,256]{1,0:T(8,128)}, u32[]{:S(2)}) copy-start(f32[256,256]{1,0:T(8,128)} %constant.6.clone.y_table.x_table.table) | copy-start | bytes 786436
  37.8 18.6 %copy-start.5 = (f32[128,128]{1,0:T(8,128)S(1)}, f32[128,128]{1,0:T(8,128)}, u32[]{:S(2)}) copy-start(f32[128,128]{1,0:T(8,128)} %constant.7.clone.z_table) | copy-start | bytes 196612
  37.8 7.7 %collective-permute-start.3 = (f32[8,32,256]{2,1,0:T(8,128)S(1)}, f32[8,32,256]{2,1,0:T(8,128)S(1)}, u32[]{:S(2)}, u32[]{:S(2)}) collective-permute-start(f32[8,32,256]{2,1,0:T(8,128)S(1)} %add.20), channel_id=1, source_target_pairs={{0,112},{16,32},{32,16},{48,64},{64,48},{80,96},{96,80},{112,0},{1... | collective-permute-start | bytes 786440 | tf_op jit(solution)/shard_map/ppermute | solution.py:506
  69.8 10.0 %collective-permute-start.11 = (f32[32,8,256]{2,1,0:T(8,128)S(1)}, f32[32,8,256]{2,1,0:T(8,128)S(1)}, u32[]{:S(2)}, u32[]{:S(2)}) collective-permute-start(f32[32,8,256]{2,1,0:T(8,128)S(1)} %all_to_all.11.refs_0_), channel_id=1, source_target_pairs={{0,112},{16,32},{32,16},{48,64},{64,48},{80,96},{96,80},{112,0},{1... | collective-permute-start | bytes 786440 | tf_op jit(solution)/shard_map/ppermute | solution.py:506
  70.9 8.9 %collective-permute-start.10 = (f32[32,8,256]{2,1,0:T(8,128)S(1)}, f32[32,8,256]{2,1,0:T(8,128)S(1)}, u32[]{:S(2)}, u32[]{:S(2)}) collective-permute-start(f32[32,8,256]{2,1,0:T(8,128)S(1)} %all_to_all.11.refs_0_), channel_id=1, source_target_pairs={{0,16},{16,0},{32,48},{48,32},{64,80},{80,64},{96,112},{112,96},{1... | collective-permute-start | bytes 786440 | tf_op jit(solution)/shard_map/ppermute | solution.py:501
  72.5 25.6 %copy-start.4 = (f32[8,256,256]{2,1,0:T(8,128)S(1)}, f32[8,256,256]{2,1,0:T(8,128)}, u32[]{:S(2)}) copy-start(f32[8,256,256]{2,1,0:T(8,128)} %v_local.1) | copy-start | bytes 6291460
  79.8 8.0 %collective-permute-start.12 = (f32[32,8,256]{2,1,0:T(8,128)S(1)}, f32[32,8,256]{2,1,0:T(8,128)S(1)}, u32[]{:S(2)}, u32[]{:S(2)}) collective-permute-start(f32[32,8,256]{2,1,0:T(8,128)S(1)} %collective-permute-done.11.refs_6_), channel_id=1, source_target_pairs={{0,16},{16,0},{32,48},{48,32},{64,80},{80,64},{96,112},{112,96},{1... | collective-permute-start | bytes 786440 | tf_op jit(solution)/shard_map/ppermute | solution.py:501
  79.8 9.2 %collective-permute-start.13 = (f32[32,8,256]{2,1,0:T(8,128)S(1)}, f32[32,8,256]{2,1,0:T(8,128)S(1)}, u32[]{:S(2)}, u32[]{:S(2)}) collective-permute-start(f32[32,8,256]{2,1,0:T(8,128)S(1)} %collective-permute-done.10.refs_1_), channel_id=1, source_target_pairs={{0,112},{16,32},{32,16},{48,64},{64,48},{80,96},{96,80},{112,0},{1... | collective-permute-start | bytes 786440 | tf_op jit(solution)/shard_map/ppermute | solution.py:506
  87.9 8.4 %collective-permute-start.15 = (f32[32,8,256]{2,1,0:T(8,128)S(1)}, f32[32,8,256]{2,1,0:T(8,128)S(1)}, u32[]{:S(2)}, u32[]{:S(2)}) collective-permute-start(f32[32,8,256]{2,1,0:T(8,128)S(1)} %collective-permute-done.12.refs_2_), channel_id=1, source_target_pairs={{0,112},{16,32},{32,16},{48,64},{64,48},{80,96},{96,80},{112,0},{1... | collective-permute-start | bytes 786440 | tf_op jit(solution)/shard_map/ppermute | solution.py:506
  89.1 7.3 %collective-permute-start.14 = (f32[32,8,256]{2,1,0:T(8,128)S(1)}, f32[32,8,256]{2,1,0:T(8,128)S(1)}, u32[]{:S(2)}, u32[]{:S(2)}) collective-permute-start(f32[32,8,256]{2,1,0:T(8,128)S(1)} %collective-permute-done.13.refs_5_), channel_id=1, source_target_pairs={{0,16},{16,0},{32,48},{48,32},{64,80},{80,64},{96,112},{112,96},{1... | collective-permute-start | bytes 786440 | tf_op jit(solution)/shard_map/ppermute | solution.py:501
  96.3 5.1 %collective-permute-start.16 = (f32[16,8,256]{2,1,0:T(8,128)S(1)}, f32[16,8,256]{2,1,0:T(8,128)S(1)}, u32[]{:S(2)}, u32[]{:S(2)}) collective-permute-start(f32[16,8,256]{2,1,0:T(8,128)S(1)} %slice.24), channel_id=1, source_target_pairs={{0,16},{16,0},{32,48},{48,32},{64,80},{80,64},{96,112},{112,96},{1... | collective-permute-start | bytes 393224 | tf_op jit(solution)/shard_map/ppermute | solution.py:501
  96.4 6.3 %collective-permute-start.17 = (f32[16,8,256]{2,1,0:T(8,128)S(1)}, f32[16,8,256]{2,1,0:T(8,128)S(1)}, u32[]{:S(2)}, u32[]{:S(2)}) collective-permute-start(f32[16,8,256]{2,1,0:T(8,128)S(1)} %slice.25), channel_id=1, source_target_pairs={{0,112},{16,32},{32,16},{48,64},{64,48},{80,96},{96,80},{112,0},{1... | collective-permute-start | bytes 393224 | tf_op jit(solution)/shard_map/ppermute | solution.py:506
  102.9 5.8 %collective-permute-start.18 = (f32[1,256,256]{2,1,0:T(8,128)S(1)}, f32[1,256,256]{2,1,0:T(8,128)S(1)}, u32[]{:S(2)}, u32[]{:S(2)}) collective-permute-start(f32[1,256,256]{2,1,0:T(8,128)S(1)} %get-tuple-element.60), channel_id=1, source_target_pairs={{0,1},{1,0},{2,3},{3,2},{4,5},{5,4},{6,7},{7,6},{8,9},{9,8},{10,11... | collective-permute-start | bytes 786440 | tf_op jit(solution)/shard_map/ppermute | solution.py:519
  103.0 8.0 %collective-permute-start.19 = (f32[1,256,256]{2,1,0:T(8,128)S(1)}, f32[1,256,256]{2,1,0:T(8,128)S(1)}, u32[]{:S(2)}, u32[]{:S(2)}) collective-permute-start(f32[1,256,256]{2,1,0:T(8,128)S(1)} %get-tuple-element.61), channel_id=1, source_target_pairs={{0,143},{1,2},{2,1},{3,4},{4,3},{5,6},{6,5},{7,136},{8,135},{9,10}... | collective-permute-start | bytes 786440 | tf_op jit(solution)/shard_map/ppermute | solution.py:518

commit v7 on v6

--- a/solution.py
+++ b/solution.py
@@ -149,25 +149,26 @@
     )(*far)
 
 
-def shares_kernel(rho, rows, *pieces):
+def shares_kernel(offsets, rho, rows, *pieces):
     width = pieces[0].shape[1]
+    wanted = jnp.concatenate([rows[offset * width : (offset + 1) * width, :] for offset in offsets], axis=0)
     for z in range(rho.shape[0]):
-        image = dot(rows[...], rho[z])
-        for offset, piece in zip((0, 1, 2, 3, 5, 6, 7), pieces):
-            piece[z] = image[offset * width : (offset + 1) * width]
-
-
-def shares(rho, rows):
+        image = dot(wanted, rho[z])
+        for index, piece in enumerate(pieces):
+            piece[z] = image[index * width : (index + 1) * width]
+
+
+def shares(offsets, rho, rows, name):
     planes, ny, nx = rho.shape
     width = ny // lax.axis_size("z")
     return pl.pallas_call(
-        shares_kernel,
+        functools.partial(shares_kernel, offsets),
         in_specs=[VMEM] * 2,
-        out_specs=[VMEM] * 7,
-        out_shape=[pltpu.VMEM((planes, width, nx), jnp.float32)] * 7,
+        out_specs=[VMEM] * len(offsets),
+        out_shape=[pltpu.VMEM((planes, width, nx), jnp.float32)] * len(offsets),
         compiler_params=pltpu.CompilerParams(vmem_limit_bytes=4 * MIB),
-        cost_estimate=cost(2.0),
-        name="shares",
+        cost_estimate=cost(0.3 * len(offsets)),
+        name=name,
     )(rho, rows)
 
 
@@ -373,7 +374,7 @@
     return early[z] + jnp.dot(tail[...], stacked, preferred_element_type=jnp.float32)
 
 
-def outer_kernel(early, tail, up, down, to_mate, to_other):
+def outer_kernel(early, tail, up, down, to_other, to_mate):
     first = potential_plane(early, tail, (up, down), 0)
     last = potential_plane(early, tail, (up, down), early.shape[0] - 1)
     lower = lower_core()
@@ -463,7 +464,7 @@
     )(*operands)
 
 
-def close_kernel(open_ends, v_mate, v_other, mate, other, _re, _im, out_re, out_im, stage, sem):
+def close_kernel(open_ends, v_other, v_mate, mate, other, _re, _im, out_re, out_im, stage, sem):
     planes = out_re.shape[1]
 
     def run(below, above):
@@ -484,6 +485,7 @@
 
 
 def close_ends(new_re, new_im, open_ends, v_planes, edges):
+    v_planes = v_planes[::-1]
     _, _, ny, nx = open_ends.shape
     return pl.pallas_call(
         close_kernel,
@@ -515,8 +517,8 @@
             crossing = slab * 2 // count != other * 2 // count
             side = (y + 1) % SIDES if crossing and same_on_orb else y
             pairs.append((y * count + slab, side * count + other))
+    from_mate = lax.ppermute(to_mate, "slab", [(i, i ^ 1) for i in range(count)])
     from_other = lax.ppermute(to_other, ("y", "slab"), pairs)
-    from_mate = lax.ppermute(to_mate, "slab", [(i, i ^ 1) for i in range(count)])
     return from_mate, from_other
 
 
@@ -562,7 +564,9 @@
     y_table, x_table, z_table = cas_table(ny), cas_table(nx), cas_table(nz)
 
     rho, rows, first, second, to_mate, to_other = density(psi_re, psi_im, n_ground, y_table, total_orbs)
-    pieces = shares(rho, rows)
+    s3, s5 = shares((3, 5), rho, rows, "shares_a")
+    s0, s1, s2, s6, s7 = shares((0, 1, 2, 6, 7), rho, rows, "shares_b")
+    pieces = (s0, s1, s2, s3, s5, s6, s7)
     near = (psi_re[0], psi_im[0])
     edges = swap_edges(to_mate, to_other)
 
@@ -585,7 +589,8 @@
         [[bases[0]], [bases[1]]],
         functools.partial(early_potential, v_local, y_table),
     )
-    v_planes = swap_edges(*outer_potential(early, tail, late), same_on_orb=True)
+    v_other, v_mate = outer_potential(early, tail, late)
+    v_planes = swap_edges(v_mate, v_other, same_on_orb=True)
     new_re, new_im, open_ends = inner_update(
         sides, early, tail, late, near, onces, once_groups, bases, base_groups
     )

time: 113 us -> 113 us (level)
  waiting for transfers between devices: 42.5 us -> 38 us
  blocking collectives: 23.2 us -> 25 us
  starting transfers between devices: 23.6 us -> 24.9 us
    ppermute x8, waiting for transfers between devices: 25.9 us -> 22.6 us  [swap_far(): lax.ppermute(value, 'z', [(i, (i - 1) % count if i % 2 == 0 else (i + 1)...]
    all_to_all x2, blocking collectives: 23.2 us -> 25 us  [across(): lax.all_to_all(value, ('y', 'slab'), split_axis=0, concat_axis=0, tiled=T...]
    ppermute x8, waiting for transfers between devices: 14.3 us -> 12.7 us  [swap_near(): lax.ppermute(value, 'z', [(i, i ^ 1) for i in range(lax.axis_size('z'))])]
    ppermute x8, starting transfers between devices: 3.21 us -> 4.69 us  [swap_near(): lax.ppermute(value, 'z', [(i, i ^ 1) for i in range(lax.axis_size('z'))])]
    pallas_call x1 -> x2, Pallas kernels: 1.9 us -> 2.69 us  [shares(): pl.pallas_call(functools.partial(shares_kernel, offsets), in_specs=[VMEM]...]
  transfers between devices with their start and end apart: 20 -> 20, of which waited for: 13 -> 14; matrix products, arithmetic and copies ran while one was open for 0% -> 0% of each run, Pallas kernels for 14% -> 15%
where the time goes in v7:
time: 113 us; the launch traced here: 112 us
  waiting for transfers between devices  38 us (34%)
  blocking collectives  25 us (22%)
  starting transfers between devices  24.9 us (22%)
  Pallas kernels  22.7 us (20%)
    all_to_all x2, blocking collectives, across(): lax.all_to_all(value, ('y', 'slab'), split_axis=0, concat_axis=0, tiled=T...  25 us
    ppermute x8, waiting for transfers between devices, swap_far(): lax.ppermute(value, 'z', [(i, (i - 1) % count if i % 2 == 0 else (i + 1)...  22.6 us
    ppermute x8, starting transfers between devices, swap_far(): lax.ppermute(value, 'z', [(i, (i - 1) % count if i % 2 == 0 else (i + 1)...  14.7 us
    ppermute x8, waiting for transfers between devices, swap_near(): lax.ppermute(value, 'z', [(i, i ^ 1) for i in range(lax.axis_size('z'))])  12.7 us
    ppermute x2, starting transfers between devices, swap_edges(): from_other = lax.ppermute(to_other, ('y', 'slab'), pairs)  4.69 us
    ppermute x8, starting transfers between devices, swap_near(): lax.ppermute(value, 'z', [(i, i ^ 1) for i in range(lax.axis_size('z'))])  4.69 us
    pallas_call x1, Pallas kernels, inner_update(): pl.pallas_call(functools.partial(inner_kernel, once_groups, base_groups),...  4.5 us
    pallas_call x1, Pallas kernels, density(): pl.pallas_call(functools.partial(density_kernel, 2.0 / total_orbs), in_sp...  3.85 us
  transfers between devices with their start and end apart: 20, of which 14 were waited for; matrix products, arithmetic and copies ran while one was open for 0% of the time, Pallas kernels for 15%

profile of v7, /device:TPU:8, one launch (start us, length us, event | category | flops | bytes accessed | tf_op | source)
XLA Modules:
  0.0 111.9 jit_solution(1514604185128386681)
XLA Ops:
  0.6 3.8 %density.1 = (f32[8,256,256]{2,1,0:T(8,128)S(1)}, f32[256,256]{1,0:T(8,128)S(1)}, f32[8,16,256]{2,1,0:T(8,128)S(1)}, f32[8,16,256]{2,1,0:T(8,128)S(1)}, f32[4,25...) custom-call(f32[1,8,256,256]{3,2,1,0:T(8,128)} %psi_re.1, f32[1,8,256,256]{3,2,1,0:T(8,128)} %psi_im.1, ...), custom_call_target="tpu_custom_call" | custom-call | tf_op jit(solution)/shard_map/density/pallas_call | solution.py:135
  4.5 2.0 %collective-permute-start = (f32[8,16,256]{2,1,0:T(8,128)S(1)}, f32[8,16,256]{2,1,0:T(8,128)S(1)}, u32[]{:S(2)}, u32[]{:S(2)}) collective-permute-start(f32[8,16,256]{2,1,0:T(8,128)S(1)} %get-tuple-element.37), channel_id=1, source_target_pairs={{0,16},{16,0},{32,48},{48,32},{64,80},{80,64},{96,112},{112,96},{1... | collective-permute-start | bytes 393224 | tf_op jit(solution)/shard_map/ppermute | solution.py:503
  6.5 5.0 %collective-permute-start.6 = (f32[8,16,256]{2,1,0:T(8,128)S(1)}, f32[8,16,256]{2,1,0:T(8,128)S(1)}, u32[]{:S(2)}, u32[]{:S(2)}) collective-permute-start(f32[8,16,256]{2,1,0:T(8,128)S(1)} %get-tuple-element.46), channel_id=1, source_target_pairs={{0,112},{16,32},{32,16},{48,64},{64,48},{80,96},{96,80},{112,0},{1... | collective-permute-start | bytes 393224 | tf_op jit(solution)/shard_map/ppermute | solution.py:508
  11.4 4.6 %collective-permute-start.5 = (f32[4,256,256]{2,1,0:T(8,128)S(1)}, f32[4,256,256]{2,1,0:T(8,128)S(1)}, u32[]{:S(2)}, u32[]{:S(2)}) collective-permute-start(f32[4,256,256]{2,1,0:T(8,128)S(1)} %get-tuple-element.43), channel_id=1, source_target_pairs={{0,15},{1,2},{2,1},{3,4},{4,3},{5,6},{6,5},{7,8},{8,7},{9,10},{10,... | collective-permute-start | bytes 3145736 | tf_op jit(solution)/shard_map/ppermute | solution.py:521
  16.0 1.3 %shares_a.1 = (f32[8,32,256]{2,1,0:T(8,128)S(1)}, f32[8,32,256]{2,1,0:T(8,128)S(1)}) custom-call(f32[8,256,256]{2,1,0:T(8,128)S(1)} %get-tuple-element.33.rho, f32[256,256]{1,0:T(8,128)S(1)} %get-tuple-element.34.rows), custom_call_target="tpu_custom_call" | custom-call | bytes 2160000 | tf_op jit(solution)/shard_map/shares_a/pallas_call | solution.py:164
  17.4 0.1 slice_add_fusion.1
  17.5 0.1 collective-permute-start.7
  17.6 2.1 %collective-permute-start.1 = (f32[8,32,256]{2,1,0:T(8,128)S(1)}, f32[8,32,256]{2,1,0:T(8,128)S(1)}, u32[]{:S(2)}, u32[]{:S(2)}) collective-permute-start(f32[8,32,256]{2,1,0:T(8,128)S(1)} %pad_maximum_fusion), channel_id=1, source_target_pairs={{0,112},{16,32},{32,16},{48,64},{64,48},{80,96},{96,80},{112,0},{1... | collective-permute-start | bytes 786440 | tf_op jit(solution)/shard_map/ppermute | solution.py:508
  19.7 1.4 %shares_b.1 = (f32[8,32,256]{2,1,0:T(8,128)S(1)}, f32[8,32,256]{2,1,0:T(8,128)S(1)}, f32[8,32,256]{2,1,0:T(8,128)S(1)}, f32[8,32,256]{2,1,0:T(8,128)S(1)}, f32[8,32,256]{2,1,0:T(8,128)S(1)}) custom-call(f32[8,256,256]{2,1,0:T(8,128)S(1)} %get-tuple-element.33.rho, f32[256,256]{1,0:T(8,128)S(1)} %get-tuple-element.34.rows), custom_call_target="tpu_custom_call" | custom-call | bytes 5400000 | tf_op jit(solution)/shard_map/shares_b/pallas_call | solution.py:164
  21.1 0.9 once_a.1.refs_0_.refs_7_
  22.1 1.9 %collective-permute-done.7 = f32[8,32,256]{2,1,0:T(8,128)S(1)} collective-permute-done((f32[8,32,256]{2,1,0:T(8,128)S(1)}, f32[8,32,256]{2,1,0:T(8,128)S(1)}, u32[]{:S(2)}, u32[]{:S(2)}) %collective-permute-start.7) | collective-permute-done | bytes 262176 | tf_op jit(solution)/shard_map/ppermute | solution.py:503
  24.0 1.0 collective-permute-start.8
  25.0 1.5 %collective-permute-done.1 = f32[8,32,256]{2,1,0:T(8,128)S(1)} collective-permute-done((f32[8,32,256]{2,1,0:T(8,128)S(1)}, f32[8,32,256]{2,1,0:T(8,128)S(1)}, u32[]{:S(2)}, u32[]{:S(2)}) %collective-permute-start.1) | collective-permute-done | bytes 262176 | tf_op jit(solution)/shard_map/ppermute | solution.py:508
  26.5 2.3 %collective-permute-start.2 = (f32[8,32,256]{2,1,0:T(8,128)S(1)}, f32[8,32,256]{2,1,0:T(8,128)S(1)}, u32[]{:S(2)}, u32[]{:S(2)}) collective-permute-start(f32[8,32,256]{2,1,0:T(8,128)S(1)} %add.19), channel_id=1, source_target_pairs={{0,16},{16,0},{32,48},{48,32},{64,80},{80,64},{96,112},{112,96},{1... | collective-permute-start | bytes 786440 | tf_op jit(solution)/shard_map/ppermute | solution.py:503
  28.8 0.9 once_b.1.refs_1_.refs_8_
  29.8 1.9 %collective-permute-done.8 = f32[8,32,256]{2,1,0:T(8,128)S(1)} collective-permute-done((f32[8,32,256]{2,1,0:T(8,128)S(1)}, f32[8,32,256]{2,1,0:T(8,128)S(1)}, u32[]{:S(2)}, u32[]{:S(2)}) %collective-permute-start.8) | collective-permute-done | bytes 262176 | tf_op jit(solution)/shard_map/ppermute | solution.py:508
  31.7 0.1 collective-permute-start.9
  31.8 3.7 %collective-permute-done.2 = f32[8,32,256]{2,1,0:T(8,128)S(1)} collective-permute-done((f32[8,32,256]{2,1,0:T(8,128)S(1)}, f32[8,32,256]{2,1,0:T(8,128)S(1)}, u32[]{:S(2)}, u32[]{:S(2)}) %collective-permute-start.2) | collective-permute-done | bytes 262176 | tf_op jit(solution)/shard_map/ppermute | solution.py:503
  35.6 0.1 collective-permute-start.3
  35.7 1.4 %once_c.1.refs_2_.refs_9_ = f32[2,4,256,256]{3,2,1,0:T(8,128)S(1)} custom-call(bf16[256,256]{1,0:T(8,128)(2,1)S(1)} %copy-done.2, f32[8,256,256]{2,1,0:T(8,128)S(1)} %bitcast.5, f32[8,256,256]{2,1,0:T(8,128)S(1)} %bitcast.11, f32[4,256,256]{2,1,0:T(8,128)S(1)} %collective-permute-done.4.refs_2_.mate, f32[4,256,256]{2,1,0:T(8,128)S(1)} %collective-permute-done.5.refs_3_.other), custom_call_target="tpu_custom_call" | custom-call | bytes 4320000 | tf_op jit(solution)/shard_map/once_c/pallas_call | solution.py:288
  37.1 1.7 %collective-permute-done.9.down = f32[8,32,256]{2,1,0:T(8,128)S(1)} collective-permute-done((f32[8,32,256]{2,1,0:T(8,128)S(1)}, f32[8,32,256]{2,1,0:T(8,128)S(1)}, u32[]{:S(2)}, u32[]{:S(2)}) %collective-permute-start.9) | collective-permute-done | bytes 262176 | tf_op jit(solution)/shard_map/ppermute | solution.py:503
  38.8 4.4 %collective-permute-done.3.up = f32[8,32,256]{2,1,0:T(8,128)S(1)} collective-permute-done((f32[8,32,256]{2,1,0:T(8,128)S(1)}, f32[8,32,256]{2,1,0:T(8,128)S(1)}, u32[]{:S(2)}, u32[]{:S(2)}) %collective-permute-start.3) | collective-permute-done | bytes 262176 | tf_op jit(solution)/shard_map/ppermute | solution.py:508
  43.3 0.1 add_shares.1
  43.4 12.7 %all_to_all.10 = f32[32,8,256]{2,1,0:T(8,128)S(1)} all-to-all(f32[32,8,256]{2,1,0:T(8,128)S(1)} %add_shares.1), channel_id=1, replica_groups=mesh['y'=2,'z'=8,'slab'=16] {'y','slab'}, dimensions={0} | all-to-all | bytes 524288 | tf_op jit(solution)/shard_map/all_to_all | solution.py:557
  56.1 1.1 solve_xz.1
  57.1 12.3 %all_to_all.11.refs_0_ = f32[32,8,256]{2,1,0:T(8,128)S(1)} all-to-all(f32[32,8,256]{2,1,0:T(8,128)S(1)} %solve_xz.1), channel_id=1, replica_groups=mesh['y'=2,'z'=8,'slab'=16] {'y','slab'}, dimensions={0} | all-to-all | bytes 524288 | tf_op jit(solution)/shard_map/all_to_all | solution.py:557
  69.5 1.7 %collective-permute-start.11 = (f32[32,8,256]{2,1,0:T(8,128)S(1)}, f32[32,8,256]{2,1,0:T(8,128)S(1)}, u32[]{:S(2)}, u32[]{:S(2)}) collective-permute-start(f32[32,8,256]{2,1,0:T(8,128)S(1)} %all_to_all.11.refs_0_), channel_id=1, source_target_pairs={{0,112},{16,32},{32,16},{48,64},{64,48},{80,96},{96,80},{112,0},{1... | collective-permute-start | bytes 786440 | tf_op jit(solution)/shard_map/ppermute | solution.py:508
  71.1 1.5 %base_a.1.refs_10_ = f32[2,4,256,256]{3,2,1,0:T(8,128)S(1)} custom-call(bf16[256,256]{1,0:T(8,128)(2,1)S(1)} %copy-done.2, f32[8,256,256]{2,1,0:T(8,128)S(1)} %bitcast.6, f32[8,256,256]{2,1,0:T(8,128)S(1)} %bitcast.12, f32[2,3,256,256]{3,2,1,0:T(8,128)S(1)} %once_a.1.refs_0_.refs_7_, f32[2,3,256,256]{3,2,1,0:T(8,128)S(1)} %once_b.1.refs_1_.refs_8_, ...), custom_call_target="tpu_custom_call" | custom-call | bytes 5760000 | tf_op jit(solution)/shard_map/base_a/pallas_call | solution.py:317
  72.7 6.8 %collective-permute-done.11.refs_6_ = f32[32,8,256]{2,1,0:T(8,128)S(1)} collective-permute-done((f32[32,8,256]{2,1,0:T(8,128)S(1)}, f32[32,8,256]{2,1,0:T(8,128)S(1)}, u32[]{:S(2)}, u32[]{:S(2)}) %collective-permute-start.11) | collective-permute-done | bytes 262176 | tf_op jit(solution)/shard_map/ppermute | solution.py:508
  79.5 0.2 collective-permute-done.10.refs_1_
  79.7 1.6 %collective-permute-start.13 = (f32[32,8,256]{2,1,0:T(8,128)S(1)}, f32[32,8,256]{2,1,0:T(8,128)S(1)}, u32[]{:S(2)}, u32[]{:S(2)}) collective-permute-start(f32[32,8,256]{2,1,0:T(8,128)S(1)} %collective-permute-done.10.refs_1_), channel_id=1, source_target_pairs={{0,112},{16,32},{32,16},{48,64},{64,48},{80,96},{96,80},{112,0},{1... | collective-permute-start | bytes 786440 | tf_op jit(solution)/shard_map/ppermute | solution.py:508
  81.2 1.5 %base_b.1.refs_11_ = f32[2,4,256,256]{3,2,1,0:T(8,128)S(1)} custom-call(bf16[256,256]{1,0:T(8,128)(2,1)S(1)} %copy-done.2, f32[8,256,256]{2,1,0:T(8,128)S(1)} %bitcast.7, f32[8,256,256]{2,1,0:T(8,128)S(1)} %bitcast.13, f32[2,3,256,256]{3,2,1,0:T(8,128)S(1)} %once_a.1.refs_0_.refs_7_, f32[2,3,256,256]{3,2,1,0:T(8,128)S(1)} %once_b.1.refs_1_.refs_8_, ...), custom_call_target="tpu_custom_call" | custom-call | bytes 5760000 | tf_op jit(solution)/shard_map/base_b/pallas_call | solution.py:317
  82.7 4.8 %collective-permute-done.12.refs_2_ = f32[32,8,256]{2,1,0:T(8,128)S(1)} collective-permute-done((f32[32,8,256]{2,1,0:T(8,128)S(1)}, f32[32,8,256]{2,1,0:T(8,128)S(1)}, u32[]{:S(2)}, u32[]{:S(2)}) %collective-permute-start.12) | collective-permute-done | bytes 262176 | tf_op jit(solution)/shard_map/ppermute | solution.py:503
  87.5 1.7 %collective-permute-start.15 = (f32[32,8,256]{2,1,0:T(8,128)S(1)}, f32[32,8,256]{2,1,0:T(8,128)S(1)}, u32[]{:S(2)}, u32[]{:S(2)}) collective-permute-start(f32[32,8,256]{2,1,0:T(8,128)S(1)} %collective-permute-done.12.refs_2_), channel_id=1, source_target_pairs={{0,112},{16,32},{32,16},{48,64},{64,48},{80,96},{96,80},{112,0},{1... | collective-permute-start | bytes 786440 | tf_op jit(solution)/shard_map/ppermute | solution.py:508
  89.2 0.1 collective-permute-start.14
  89.3 6.6 %collective-permute-done.15.refs_4_ = f32[32,8,256]{2,1,0:T(8,128)S(1)} collective-permute-done((f32[32,8,256]{2,1,0:T(8,128)S(1)}, f32[32,8,256]{2,1,0:T(8,128)S(1)}, u32[]{:S(2)}, u32[]{:S(2)}) %collective-permute-start.15) | collective-permute-done | bytes 262176 | tf_op jit(solution)/shard_map/ppermute | solution.py:508
  95.9 0.1 collective-permute-start.16
  96.0 0.1 collective-permute-done.14.refs_3_
  96.1 1.7 %collective-permute-start.17 = (f32[16,8,256]{2,1,0:T(8,128)S(1)}, f32[16,8,256]{2,1,0:T(8,128)S(1)}, u32[]{:S(2)}, u32[]{:S(2)}) collective-permute-start(f32[16,8,256]{2,1,0:T(8,128)S(1)} %slice.25), channel_id=1, source_target_pairs={{0,112},{16,32},{32,16},{48,64},{64,48},{80,96},{96,80},{112,0},{1... | collective-permute-start | bytes 393224 | tf_op jit(solution)/shard_map/ppermute | solution.py:508
  97.8 2.8 %early_potential.1 = (f32[8,256,256]{2,1,0:T(8,128)S(1)}, bf16[256,192]{1,0:T(8,128)(2,1)S(1)}) custom-call(f32[8,256,256]{2,1,0:T(8,128)S(1)} %copy-done.4, f32[256,256]{1,0:T(8,128)S(1)} %copy-done.3, f32[32,8,256]{2,1,0:T(8,128)S(1)} %all_to_all.11.refs_0_, f32[32,8,256]{2,1,0:T(8,128)S(1)} %collective-permute-done.10.refs_1_, ...), custom_call_target="tpu_custom_call" | custom-call | bytes 8279999 | tf_op jit(solution)/shard_map/early_potential/pallas_call | solution.py:360
  100.6 0.4 collective-permute-done.16.refs_3_.up
  101.0 1.4 %collective-permute-done.17.refs_4_.down = f32[16,8,256]{2,1,0:T(8,128)S(1)} collective-permute-done((f32[16,8,256]{2,1,0:T(8,128)S(1)}, f32[16,8,256]{2,1,0:T(8,128)S(1)}, u32[]{:S(2)}, u32[]{:S(2)}) %collective-permute-start.17) | collective-permute-done | bytes 131104 | tf_op jit(solution)/shard_map/ppermute | solution.py:508
  102.4 0.2 outer_potential.1
  102.6 0.1 collective-permute-start.18
  102.7 0.7 collective-permute-start.19
  103.4 4.5 %inner_update.1 = (f32[1,8,256,256]{3,2,1,0:T(8,128)}, f32[1,8,256,256]{3,2,1,0:T(8,128)}, f32[2,2,256,256]{3,2,1,0:T(8,128)S(1)}) custom-call(bf16[256,256]{1,0:T(8,128)(2,1)S(1)} %copy-done.2, f32[8,256,256]{2,1,0:T(8,128)S(1)} %get-tuple-element.56.refs_1_.early, bf16[256,192]{1,0:T(8,128)(2,1)S(1)} %get-tuple-element.57.refs_2_.tail, ...), custom_call_target="tpu_custom_call" | custom-call | bytes 15480000 | tf_op jit(solution)/shard_map/inner_update/pallas_call | solution.py:450
  107.9 2.7 %collective-permute-done.18.v_other = f32[1,256,256]{2,1,0:T(8,128)S(1)} collective-permute-done((f32[1,256,256]{2,1,0:T(8,128)S(1)}, f32[1,256,256]{2,1,0:T(8,128)S(1)}, u32[]{:S(2)}, u32[]{:S(2)}) %collective-permute-start.18) | collective-permute-done | bytes 262176 | tf_op jit(solution)/shard_map/ppermute | solution.py:521
  110.6 1.1 %close_ends.1 = (f32[1,8,256,256]{3,2,1,0:T(8,128)}, f32[1,8,256,256]{3,2,1,0:T(8,128)}) custom-call(f32[2,2,256,256]{3,2,1,0:T(8,128)S(1)} %get-tuple-element.59.open_ends, f32[1,256,256]{2,1,0:T(8,128)S(1)} %collective-permute-done.18.v_other, f32[1,256,256]{2,1,0:T(8,128)S(1)} %collective-permute-done.19.v_mate, ...), custom_call_target="tpu_custom_call", output_to_operand_aliasing={{0}: (5, {}), {1}: (6, {})} | custom-call | tf_op jit(solution)/shard_map/close_ends/pallas_call | solution.py:490
  (29 shorter events, 0.3 us)
Async XLA Ops:
  4.5 12.9 %collective-permute-start = (f32[8,16,256]{2,1,0:T(8,128)S(1)}, f32[8,16,256]{2,1,0:T(8,128)S(1)}, u32[]{:S(2)}, u32[]{:S(2)}) collective-permute-start(f32[8,16,256]{2,1,0:T(8,128)S(1)} %get-tuple-element.37), channel_id=1, source_target_pairs={{0,16},{16,0},{32,48},{48,32},{64,80},{80,64},{96,112},{112,96},{1... | collective-permute-start | bytes 393224 | tf_op jit(solution)/shard_map/ppermute | solution.py:503
  6.5 10.9 %collective-permute-start.6 = (f32[8,16,256]{2,1,0:T(8,128)S(1)}, f32[8,16,256]{2,1,0:T(8,128)S(1)}, u32[]{:S(2)}, u32[]{:S(2)}) collective-permute-start(f32[8,16,256]{2,1,0:T(8,128)S(1)} %get-tuple-element.46), channel_id=1, source_target_pairs={{0,112},{16,32},{32,16},{48,64},{64,48},{80,96},{96,80},{112,0},{1... | collective-permute-start | bytes 393224 | tf_op jit(solution)/shard_map/ppermute | solution.py:508
  11.4 24.2 %collective-permute-start.4 = (f32[4,256,256]{2,1,0:T(8,128)S(1)}, f32[4,256,256]{2,1,0:T(8,128)S(1)}, u32[]{:S(2)}, u32[]{:S(2)}) collective-permute-start(f32[4,256,256]{2,1,0:T(8,128)S(1)} %get-tuple-element.42), channel_id=1, source_target_pairs={{0,1},{1,0},{2,3},{3,2},{4,5},{5,4},{6,7},{7,6},{8,9},{9,8},{10,11... | collective-permute-start | bytes 3145736 | tf_op jit(solution)/shard_map/ppermute | solution.py:520
  11.4 24.3 %collective-permute-start.5 = (f32[4,256,256]{2,1,0:T(8,128)S(1)}, f32[4,256,256]{2,1,0:T(8,128)S(1)}, u32[]{:S(2)}, u32[]{:S(2)}) collective-permute-start(f32[4,256,256]{2,1,0:T(8,128)S(1)} %get-tuple-element.43), channel_id=1, source_target_pairs={{0,15},{1,2},{2,1},{3,4},{4,3},{5,6},{6,5},{7,8},{8,7},{9,10},{10,... | collective-permute-start | bytes 3145736 | tf_op jit(solution)/shard_map/ppermute | solution.py:521
  17.4 3.7 %copy-start = (f32[1,8,256,256]{3,2,1,0:T(8,128)S(1)}, f32[1,8,256,256]{3,2,1,0:T(8,128)}, u32[]{:S(2)}) copy-start(f32[1,8,256,256]{3,2,1,0:T(8,128)} %psi_re.1) | copy-start | bytes 6291460
  17.4 3.7 %copy-start.1 = (f32[1,8,256,256]{3,2,1,0:T(8,128)S(1)}, f32[1,8,256,256]{3,2,1,0:T(8,128)}, u32[]{:S(2)}) copy-start(f32[1,8,256,256]{3,2,1,0:T(8,128)} %psi_im.1) | copy-start | bytes 6291460
  17.4 3.7 %copy-start.2 = (bf16[256,256]{1,0:T(8,128)(2,1)S(1)}, bf16[256,256]{1,0:T(8,128)(2,1)}, u32[]{:S(2)}) copy-start(bf16[256,256]{1,0:T(8,128)(2,1)} %constant.8.clone.sides.refs_0_) | copy-start | bytes 393220
  17.5 6.5 %collective-permute-start.7 = (f32[8,32,256]{2,1,0:T(8,128)S(1)}, f32[8,32,256]{2,1,0:T(8,128)S(1)}, u32[]{:S(2)}, u32[]{:S(2)}) collective-permute-start(f32[8,32,256]{2,1,0:T(8,128)S(1)} %pad_maximum_fusion.1), channel_id=1, source_target_pairs={{0,16},{16,0},{32,48},{48,32},{64,80},{80,64},{96,112},{112,96},{1... | collective-permute-start | bytes 786440 | tf_op jit(solution)/shard_map/ppermute | solution.py:503
  17.6 8.9 %collective-permute-start.1 = (f32[8,32,256]{2,1,0:T(8,128)S(1)}, f32[8,32,256]{2,1,0:T(8,128)S(1)}, u32[]{:S(2)}, u32[]{:S(2)}) collective-permute-start(f32[8,32,256]{2,1,0:T(8,128)S(1)} %pad_maximum_fusion), channel_id=1, source_target_pairs={{0,112},{16,32},{32,16},{48,64},{64,48},{80,96},{96,80},{112,0},{1... | collective-permute-start | bytes 786440 | tf_op jit(solution)/shard_map/ppermute | solution.py:508
  24.0 7.7 %collective-permute-start.8 = (f32[8,32,256]{2,1,0:T(8,128)S(1)}, f32[8,32,256]{2,1,0:T(8,128)S(1)}, u32[]{:S(2)}, u32[]{:S(2)}) collective-permute-start(f32[8,32,256]{2,1,0:T(8,128)S(1)} %add.22), channel_id=1, source_target_pairs={{0,112},{16,32},{32,16},{48,64},{64,48},{80,96},{96,80},{112,0},{1... | collective-permute-start | bytes 786440 | tf_op jit(solution)/shard_map/ppermute | solution.py:508
  26.5 9.0 %collective-permute-start.2 = (f32[8,32,256]{2,1,0:T(8,128)S(1)}, f32[8,32,256]{2,1,0:T(8,128)S(1)}, u32[]{:S(2)}, u32[]{:S(2)}) collective-permute-start(f32[8,32,256]{2,1,0:T(8,128)S(1)} %add.19), channel_id=1, source_target_pairs={{0,16},{16,0},{32,48},{48,32},{64,80},{80,64},{96,112},{112,96},{1... | collective-permute-start | bytes 786440 | tf_op jit(solution)/shard_map/ppermute | solution.py:503
  31.7 7.1 %collective-permute-start.9 = (f32[8,32,256]{2,1,0:T(8,128)S(1)}, f32[8,32,256]{2,1,0:T(8,128)S(1)}, u32[]{:S(2)}, u32[]{:S(2)}) collective-permute-start(f32[8,32,256]{2,1,0:T(8,128)S(1)} %add.23), channel_id=1, source_target_pairs={{0,16},{16,0},{32,48},{48,32},{64,80},{80,64},{96,112},{112,96},{1... | collective-permute-start | bytes 786440 | tf_op jit(solution)/shard_map/ppermute | solution.py:503
  35.6 20.5 %copy-start.3 = (f32[256,256]{1,0:T(8,128)S(1)}, f32[256,256]{1,0:T(8,128)}, u32[]{:S(2)}) copy-start(f32[256,256]{1,0:T(8,128)} %constant.6.clone.y_table.x_table.table) | copy-start | bytes 786436
  35.6 20.5 %copy-start.5 = (f32[128,128]{1,0:T(8,128)S(1)}, f32[128,128]{1,0:T(8,128)}, u32[]{:S(2)}) copy-start(f32[128,128]{1,0:T(8,128)} %constant.7.clone.z_table) | copy-start | bytes 196612
  35.6 7.7 %collective-permute-start.3 = (f32[8,32,256]{2,1,0:T(8,128)S(1)}, f32[8,32,256]{2,1,0:T(8,128)S(1)}, u32[]{:S(2)}, u32[]{:S(2)}) collective-permute-start(f32[8,32,256]{2,1,0:T(8,128)S(1)} %add.20), channel_id=1, source_target_pairs={{0,112},{16,32},{32,16},{48,64},{64,48},{80,96},{96,80},{112,0},{1... | collective-permute-start | bytes 786440 | tf_op jit(solution)/shard_map/ppermute | solution.py:508
  69.5 10.0 %collective-permute-start.11 = (f32[32,8,256]{2,1,0:T(8,128)S(1)}, f32[32,8,256]{2,1,0:T(8,128)S(1)}, u32[]{:S(2)}, u32[]{:S(2)}) collective-permute-start(f32[32,8,256]{2,1,0:T(8,128)S(1)} %all_to_all.11.refs_0_), channel_id=1, source_target_pairs={{0,112},{16,32},{32,16},{48,64},{64,48},{80,96},{96,80},{112,0},{1... | collective-permute-start | bytes 786440 | tf_op jit(solution)/shard_map/ppermute | solution.py:508
  71.1 8.5 %collective-permute-start.10 = (f32[32,8,256]{2,1,0:T(8,128)S(1)}, f32[32,8,256]{2,1,0:T(8,128)S(1)}, u32[]{:S(2)}, u32[]{:S(2)}) collective-permute-start(f32[32,8,256]{2,1,0:T(8,128)S(1)} %all_to_all.11.refs_0_), channel_id=1, source_target_pairs={{0,16},{16,0},{32,48},{48,32},{64,80},{80,64},{96,112},{112,96},{1... | collective-permute-start | bytes 786440 | tf_op jit(solution)/shard_map/ppermute | solution.py:503
  72.7 25.1 %copy-start.4 = (f32[8,256,256]{2,1,0:T(8,128)S(1)}, f32[8,256,256]{2,1,0:T(8,128)}, u32[]{:S(2)}) copy-start(f32[8,256,256]{2,1,0:T(8,128)} %v_local.1) | copy-start | bytes 6291460
  79.5 8.0 %collective-permute-start.12 = (f32[32,8,256]{2,1,0:T(8,128)S(1)}, f32[32,8,256]{2,1,0:T(8,128)S(1)}, u32[]{:S(2)}, u32[]{:S(2)}) collective-permute-start(f32[32,8,256]{2,1,0:T(8,128)S(1)} %collective-permute-done.11.refs_6_), channel_id=1, source_target_pairs={{0,16},{16,0},{32,48},{48,32},{64,80},{80,64},{96,112},{112,96},{1... | collective-permute-start | bytes 786440 | tf_op jit(solution)/shard_map/ppermute | solution.py:503
  79.7 9.5 %collective-permute-start.13 = (f32[32,8,256]{2,1,0:T(8,128)S(1)}, f32[32,8,256]{2,1,0:T(8,128)S(1)}, u32[]{:S(2)}, u32[]{:S(2)}) collective-permute-start(f32[32,8,256]{2,1,0:T(8,128)S(1)} %collective-permute-done.10.refs_1_), channel_id=1, source_target_pairs={{0,112},{16,32},{32,16},{48,64},{64,48},{80,96},{96,80},{112,0},{1... | collective-permute-start | bytes 786440 | tf_op jit(solution)/shard_map/ppermute | solution.py:508
  87.5 8.4 %collective-permute-start.15 = (f32[32,8,256]{2,1,0:T(8,128)S(1)}, f32[32,8,256]{2,1,0:T(8,128)S(1)}, u32[]{:S(2)}, u32[]{:S(2)}) collective-permute-start(f32[32,8,256]{2,1,0:T(8,128)S(1)} %collective-permute-done.12.refs_2_), channel_id=1, source_target_pairs={{0,112},{16,32},{32,16},{48,64},{64,48},{80,96},{96,80},{112,0},{1... | collective-permute-start | bytes 786440 | tf_op jit(solution)/shard_map/ppermute | solution.py:508
  89.2 6.9 %collective-permute-start.14 = (f32[32,8,256]{2,1,0:T(8,128)S(1)}, f32[32,8,256]{2,1,0:T(8,128)S(1)}, u32[]{:S(2)}, u32[]{:S(2)}) collective-permute-start(f32[32,8,256]{2,1,0:T(8,128)S(1)} %collective-permute-done.13.refs_5_), channel_id=1, source_target_pairs={{0,16},{16,0},{32,48},{48,32},{64,80},{80,64},{96,112},{112,96},{1... | collective-permute-start | bytes 786440 | tf_op jit(solution)/shard_map/ppermute | solution.py:503
  95.9 5.1 %collective-permute-start.16 = (f32[16,8,256]{2,1,0:T(8,128)S(1)}, f32[16,8,256]{2,1,0:T(8,128)S(1)}, u32[]{:S(2)}, u32[]{:S(2)}) collective-permute-start(f32[16,8,256]{2,1,0:T(8,128)S(1)} %slice.24), channel_id=1, source_target_pairs={{0,16},{16,0},{32,48},{48,32},{64,80},{80,64},{96,112},{112,96},{1... | collective-permute-start | bytes 393224 | tf_op jit(solution)/shard_map/ppermute | solution.py:503
  96.1 6.3 %collective-permute-start.17 = (f32[16,8,256]{2,1,0:T(8,128)S(1)}, f32[16,8,256]{2,1,0:T(8,128)S(1)}, u32[]{:S(2)}, u32[]{:S(2)}) collective-permute-start(f32[16,8,256]{2,1,0:T(8,128)S(1)} %slice.25), channel_id=1, source_target_pairs={{0,112},{16,32},{32,16},{48,64},{64,48},{80,96},{96,80},{112,0},{1... | collective-permute-start | bytes 393224 | tf_op jit(solution)/shard_map/ppermute | solution.py:508
  102.6 8.0 %collective-permute-start.18 = (f32[1,256,256]{2,1,0:T(8,128)S(1)}, f32[1,256,256]{2,1,0:T(8,128)S(1)}, u32[]{:S(2)}, u32[]{:S(2)}) collective-permute-start(f32[1,256,256]{2,1,0:T(8,128)S(1)} %get-tuple-element.60), channel_id=1, source_target_pairs={{0,143},{1,2},{2,1},{3,4},{4,3},{5,6},{6,5},{7,136},{8,135},{9,10}... | collective-permute-start | bytes 786440 | tf_op jit(solution)/shard_map/ppermute | solution.py:521
  102.7 7.9 %collective-permute-start.19 = (f32[1,256,256]{2,1,0:T(8,128)S(1)}, f32[1,256,256]{2,1,0:T(8,128)S(1)}, u32[]{:S(2)}, u32[]{:S(2)}) collective-permute-start(f32[1,256,256]{2,1,0:T(8,128)S(1)} %get-tuple-element.61), channel_id=1, source_target_pairs={{0,1},{1,0},{2,3},{3,2},{4,5},{5,4},{6,7},{7,6},{8,9},{9,8},{10,11... | collective-permute-start | bytes 786440 | tf_op jit(solution)/shard_map/ppermute | solution.py:520

commit v8 on v7

--- a/solution.py
+++ b/solution.py
@@ -537,7 +537,6 @@
     near, far = swap_near(near + s2), swap_far(far + s6)
     near, far = after(near, *beside[1]), after(far, *beside[1])
     near, far = swap_far(near + s7), swap_near(far + s1)
-    near, far = after(near, *beside[2]), after(far, *beside[2])
     return add_shares(s0, near, far)
 
 
@@ -548,6 +547,7 @@
     near2, far2 = swap_near(far1), swap_far(near1)
     near2, far2 = after(near2, *beside[1]), after(far2, *beside[1])
     near3, far3 = swap_near(far2), swap_far(near2)
+    near3, far3 = after(near3, *beside[2]), after(far3, *beside[2])
     near4, far4 = swap_near(far3[:half]), swap_far(near3[half:])
     made = early([block, near1, near2, near3, far3, far2, far1])
     return made, (after(near4, *made), far4)
@@ -582,11 +582,11 @@
     bases = [
         base(sides, near, onces, once_groups, group, name) for group, name in zip(base_groups, ("base_a", "base_b"))
     ]
-    share = sum_over_ring(first, second, pieces, [[onces[0]], [onces[1]], [onces[2]]])
+    share = sum_over_ring(first, second, pieces, [[onces[0]], [onces[1]]])
     pencils = across(share).reshape(SIDES * nz, nx)
     (early, tail), late = gather_over_ring(
         across(solve(pencils, x_table, z_table, ny, planes)),
-        [[bases[0]], [bases[1]]],
+        [[onces[2]], [bases[0]], [bases[1]]],
         functools.partial(early_potential, v_local, y_table),
     )
     v_other, v_mate = outer_potential(early, tail, late)

time: 113 us -> 112 us (level)
  waiting for transfers between devices: 38 us -> 33.9 us
  blocking collectives: 25 us -> 27.4 us
  starting transfers between devices: 24.9 us -> 26.5 us
    ppermute x8, waiting for transfers between devices: 12.7 us -> 9.95 us  [swap_near(): lax.ppermute(value, 'z', [(i, i ^ 1) for i in range(lax.axis_size('z'))])]
    all_to_all x2, blocking collectives: 25 us -> 27.4 us  [across(): lax.all_to_all(value, ('y', 'slab'), split_axis=0, concat_axis=0, tiled=T...]
    ppermute x8, waiting for transfers between devices: 22.6 us -> 21.2 us  [swap_far(): lax.ppermute(value, 'z', [(i, (i - 1) % count if i % 2 == 0 else (i + 1)...]
    ppermute x8, starting transfers between devices: 14.7 us -> 16.1 us  [swap_far(): lax.ppermute(value, 'z', [(i, (i - 1) % count if i % 2 == 0 else (i + 1)...]
  transfers between devices with their start and end apart: 20 -> 20, of which waited for: 14 -> 11; matrix products, arithmetic and copies ran while one was open for 0% -> 0% of each run, Pallas kernels for 15% -> 15%
where the time goes in v8:
time: 112 us
  waiting for transfers between devices  33.9 us (30%)
  blocking collectives  27.4 us (24%)
  starting transfers between devices  26.5 us (24%)
  Pallas kernels  22.5 us (20%)
    all_to_all x2, blocking collectives, across(): lax.all_to_all(value, ('y', 'slab'), split_axis=0, concat_axis=0, tiled=T...  27.4 us
    ppermute x8, waiting for transfers between devices, swap_far(): lax.ppermute(value, 'z', [(i, (i - 1) % count if i % 2 == 0 else (i + 1)...  21.2 us
    ppermute x8, starting transfers between devices, swap_far(): lax.ppermute(value, 'z', [(i, (i - 1) % count if i % 2 == 0 else (i + 1)...  16.1 us
    ppermute x8, waiting for transfers between devices, swap_near(): lax.ppermute(value, 'z', [(i, i ^ 1) for i in range(lax.axis_size('z'))])  9.95 us
    ppermute x8, starting transfers between devices, swap_near(): lax.ppermute(value, 'z', [(i, i ^ 1) for i in range(lax.axis_size('z'))])  4.83 us
    ppermute x2, starting transfers between devices, swap_edges(): from_other = lax.ppermute(to_other, ('y', 'slab'), pairs)  4.69 us
    pallas_call x1, Pallas kernels, inner_update(): pl.pallas_call(functools.partial(inner_kernel, once_groups, base_groups),...  4.5 us
    pallas_call x1, Pallas kernels, density(): pl.pallas_call(functools.partial(density_kernel, 2.0 / total_orbs), in_sp...  3.85 us
  transfers between devices with their start and end apart: 20, of which 11 were waited for; matrix products, arithmetic and copies ran while one was open for 0% of the time, Pallas kernels for 15%

profile of v8, /device:TPU:8, one launch (start us, length us, event | category | flops | bytes accessed | tf_op | source)
XLA Modules:
  0.0 111.6 jit_solution(9438810570126283016)
XLA Ops:
  0.6 3.8 %density.1 = (f32[8,256,256]{2,1,0:T(8,128)S(1)}, f32[256,256]{1,0:T(8,128)S(1)}, f32[8,16,256]{2,1,0:T(8,128)S(1)}, f32[8,16,256]{2,1,0:T(8,128)S(1)}, f32[4,25...) custom-call(f32[1,8,256,256]{3,2,1,0:T(8,128)} %psi_re.1, f32[1,8,256,256]{3,2,1,0:T(8,128)} %psi_im.1, ...), custom_call_target="tpu_custom_call" | custom-call | tf_op jit(solution)/shard_map/density/pallas_call | solution.py:135
  4.5 2.0 %collective-permute-start = (f32[8,16,256]{2,1,0:T(8,128)S(1)}, f32[8,16,256]{2,1,0:T(8,128)S(1)}, u32[]{:S(2)}, u32[]{:S(2)}) collective-permute-start(f32[8,16,256]{2,1,0:T(8,128)S(1)} %get-tuple-element.37), channel_id=1, source_target_pairs={{0,16},{16,0},{32,48},{48,32},{64,80},{80,64},{96,112},{112,96},{1... | collective-permute-start | bytes 393224 | tf_op jit(solution)/shard_map/ppermute | solution.py:503
  6.5 5.0 %collective-permute-start.4 = (f32[8,16,256]{2,1,0:T(8,128)S(1)}, f32[8,16,256]{2,1,0:T(8,128)S(1)}, u32[]{:S(2)}, u32[]{:S(2)}) collective-permute-start(f32[8,16,256]{2,1,0:T(8,128)S(1)} %get-tuple-element.43), channel_id=1, source_target_pairs={{0,112},{16,32},{32,16},{48,64},{64,48},{80,96},{96,80},{112,0},{1... | collective-permute-start | bytes 393224 | tf_op jit(solution)/shard_map/ppermute | solution.py:508
  11.4 1.3 %shares_a.1 = (f32[8,32,256]{2,1,0:T(8,128)S(1)}, f32[8,32,256]{2,1,0:T(8,128)S(1)}) custom-call(f32[8,256,256]{2,1,0:T(8,128)S(1)} %get-tuple-element.33.rho, f32[256,256]{1,0:T(8,128)S(1)} %get-tuple-element.34.rows), custom_call_target="tpu_custom_call" | custom-call | bytes 2160000 | tf_op jit(solution)/shard_map/shares_a/pallas_call | solution.py:164
  12.7 2.0 %collective-permute-done.4 = f32[8,16,256]{2,1,0:T(8,128)S(1)} collective-permute-done((f32[8,16,256]{2,1,0:T(8,128)S(1)}, f32[8,16,256]{2,1,0:T(8,128)S(1)}, u32[]{:S(2)}, u32[]{:S(2)}) %collective-permute-start.4) | collective-permute-done | bytes 131104 | tf_op jit(solution)/shard_map/ppermute | solution.py:508
  14.8 0.1 slice_add_fusion.1
  14.9 0.1 collective-permute-start.5
  15.0 3.0 %collective-permute-start.1 = (f32[8,32,256]{2,1,0:T(8,128)S(1)}, f32[8,32,256]{2,1,0:T(8,128)S(1)}, u32[]{:S(2)}, u32[]{:S(2)}) collective-permute-start(f32[8,32,256]{2,1,0:T(8,128)S(1)} %pad_maximum_fusion), channel_id=1, source_target_pairs={{0,112},{16,32},{32,16},{48,64},{64,48},{80,96},{96,80},{112,0},{1... | collective-permute-start | bytes 786440 | tf_op jit(solution)/shard_map/ppermute | solution.py:508
  18.0 1.4 %shares_b.1 = (f32[8,32,256]{2,1,0:T(8,128)S(1)}, f32[8,32,256]{2,1,0:T(8,128)S(1)}, f32[8,32,256]{2,1,0:T(8,128)S(1)}, f32[8,32,256]{2,1,0:T(8,128)S(1)}, f32[8,32,256]{2,1,0:T(8,128)S(1)}) custom-call(f32[8,256,256]{2,1,0:T(8,128)S(1)} %get-tuple-element.33.rho, f32[256,256]{1,0:T(8,128)S(1)} %get-tuple-element.34.rows), custom_call_target="tpu_custom_call" | custom-call | bytes 5400000 | tf_op jit(solution)/shard_map/shares_b/pallas_call | solution.py:164
  19.5 0.9 once_a.1.refs_0_.refs_7_
  20.4 1.8 %collective-permute-done.5 = f32[8,32,256]{2,1,0:T(8,128)S(1)} collective-permute-done((f32[8,32,256]{2,1,0:T(8,128)S(1)}, f32[8,32,256]{2,1,0:T(8,128)S(1)}, u32[]{:S(2)}, u32[]{:S(2)}) %collective-permute-start.5) | collective-permute-done | bytes 262176 | tf_op jit(solution)/shard_map/ppermute | solution.py:503
  22.3 2.7 %collective-permute-start.6 = (f32[8,32,256]{2,1,0:T(8,128)S(1)}, f32[8,32,256]{2,1,0:T(8,128)S(1)}, u32[]{:S(2)}, u32[]{:S(2)}) collective-permute-start(f32[8,32,256]{2,1,0:T(8,128)S(1)} %add.22), channel_id=1, source_target_pairs={{0,112},{16,32},{32,16},{48,64},{64,48},{80,96},{96,80},{112,0},{1... | collective-permute-start | bytes 786440 | tf_op jit(solution)/shard_map/ppermute | solution.py:508
  25.0 0.1 collective-permute-start.2
  25.1 0.1 collective-permute-start.9
  25.2 4.6 %collective-permute-start.10 = (f32[4,256,256]{2,1,0:T(8,128)S(1)}, f32[4,256,256]{2,1,0:T(8,128)S(1)}, u32[]{:S(2)}, u32[]{:S(2)}) collective-permute-start(f32[4,256,256]{2,1,0:T(8,128)S(1)} %get-tuple-element.49), channel_id=1, source_target_pairs={{0,15},{1,2},{2,1},{3,4},{4,3},{5,6},{6,5},{7,8},{8,7},{9,10},{10,... | collective-permute-start | bytes 3145736 | tf_op jit(solution)/shard_map/ppermute | solution.py:521
  29.8 0.9 once_b.1.refs_1_.refs_8_
  30.8 0.0 copy-start.3
  30.8 0.0 copy-start.5
  30.8 2.0 %collective-permute-start.7 = (f32[8,32,256]{2,1,0:T(8,128)S(1)}, f32[8,32,256]{2,1,0:T(8,128)S(1)}, u32[]{:S(2)}, u32[]{:S(2)}) collective-permute-start(f32[8,32,256]{2,1,0:T(8,128)S(1)} %add.23), channel_id=1, source_target_pairs={{0,16},{16,0},{32,48},{48,32},{64,80},{80,64},{96,112},{112,96},{1... | collective-permute-start | bytes 786440 | tf_op jit(solution)/shard_map/ppermute | solution.py:503
  32.9 1.3 %collective-permute-start.3 = (f32[8,32,256]{2,1,0:T(8,128)S(1)}, f32[8,32,256]{2,1,0:T(8,128)S(1)}, u32[]{:S(2)}, u32[]{:S(2)}) collective-permute-start(f32[8,32,256]{2,1,0:T(8,128)S(1)} %add.20), channel_id=1, source_target_pairs={{0,112},{16,32},{32,16},{48,64},{64,48},{80,96},{96,80},{112,0},{1... | collective-permute-start | bytes 786440 | tf_op jit(solution)/shard_map/ppermute | solution.py:508
  34.2 3.1 %collective-permute-done.7.down = f32[8,32,256]{2,1,0:T(8,128)S(1)} collective-permute-done((f32[8,32,256]{2,1,0:T(8,128)S(1)}, f32[8,32,256]{2,1,0:T(8,128)S(1)}, u32[]{:S(2)}, u32[]{:S(2)}) %collective-permute-start.7) | collective-permute-done | bytes 262176 | tf_op jit(solution)/shard_map/ppermute | solution.py:503
  37.3 3.3 %collective-permute-done.3.up = f32[8,32,256]{2,1,0:T(8,128)S(1)} collective-permute-done((f32[8,32,256]{2,1,0:T(8,128)S(1)}, f32[8,32,256]{2,1,0:T(8,128)S(1)}, u32[]{:S(2)}, u32[]{:S(2)}) %collective-permute-start.3) | collective-permute-done | bytes 262176 | tf_op jit(solution)/shard_map/ppermute | solution.py:508
  40.6 0.1 add_shares.1
  40.7 15.1 %all_to_all.10 = f32[32,8,256]{2,1,0:T(8,128)S(1)} all-to-all(f32[32,8,256]{2,1,0:T(8,128)S(1)} %add_shares.1), channel_id=1, replica_groups=mesh['y'=2,'z'=8,'slab'=16] {'y','slab'}, dimensions={0} | all-to-all | bytes 524288 | tf_op jit(solution)/shard_map/all_to_all | solution.py:557
  55.8 1.1 solve_xz.1
  56.9 12.3 %all_to_all.11.refs_0_ = f32[32,8,256]{2,1,0:T(8,128)S(1)} all-to-all(f32[32,8,256]{2,1,0:T(8,128)S(1)} %solve_xz.1), channel_id=1, replica_groups=mesh['y'=2,'z'=8,'slab'=16] {'y','slab'}, dimensions={0} | all-to-all | bytes 524288 | tf_op jit(solution)/shard_map/all_to_all | solution.py:557
  69.2 0.0 collective-permute-start.11
  69.2 1.2 %once_c.1.refs_2_.refs_9_ = f32[2,4,256,256]{3,2,1,0:T(8,128)S(1)} custom-call(bf16[256,256]{1,0:T(8,128)(2,1)S(1)} %copy-done.2, f32[8,256,256]{2,1,0:T(8,128)S(1)} %bitcast.5, f32[8,256,256]{2,1,0:T(8,128)S(1)} %bitcast.11, f32[4,256,256]{2,1,0:T(8,128)S(1)} %collective-permute-done.9.refs_2_.mate, f32[4,256,256]{2,1,0:T(8,128)S(1)} %collective-permute-done.10.refs_3_.other), custom_call_target="tpu_custom_call" | custom-call | bytes 4320000 | tf_op jit(solution)/shard_map/once_c/pallas_call | solution.py:288
  70.5 8.7 %collective-permute-done.11.refs_6_ = f32[32,8,256]{2,1,0:T(8,128)S(1)} collective-permute-done((f32[32,8,256]{2,1,0:T(8,128)S(1)}, f32[32,8,256]{2,1,0:T(8,128)S(1)}, u32[]{:S(2)}, u32[]{:S(2)}) %collective-permute-start.11) | collective-permute-done | bytes 262176 | tf_op jit(solution)/shard_map/ppermute | solution.py:508
  79.2 1.7 %collective-permute-start.13 = (f32[32,8,256]{2,1,0:T(8,128)S(1)}, f32[32,8,256]{2,1,0:T(8,128)S(1)}, u32[]{:S(2)}, u32[]{:S(2)}) collective-permute-start(f32[32,8,256]{2,1,0:T(8,128)S(1)} %collective-permute-done.8.refs_1_), channel_id=1, source_target_pairs={{0,112},{16,32},{32,16},{48,64},{64,48},{80,96},{96,80},{112,0},{1... | collective-permute-start | bytes 786440 | tf_op jit(solution)/shard_map/ppermute | solution.py:508
  80.9 1.5 %base_a.1.refs_10_ = f32[2,4,256,256]{3,2,1,0:T(8,128)S(1)} custom-call(bf16[256,256]{1,0:T(8,128)(2,1)S(1)} %copy-done.2, f32[8,256,256]{2,1,0:T(8,128)S(1)} %bitcast.6, f32[8,256,256]{2,1,0:T(8,128)S(1)} %bitcast.12, f32[2,3,256,256]{3,2,1,0:T(8,128)S(1)} %once_a.1.refs_0_.refs_7_, f32[2,3,256,256]{3,2,1,0:T(8,128)S(1)} %once_b.1.refs_1_.refs_8_, ...), custom_call_target="tpu_custom_call" | custom-call | bytes 5760000 | tf_op jit(solution)/shard_map/base_a/pallas_call | solution.py:317
  82.5 4.8 %collective-permute-done.12.refs_2_ = f32[32,8,256]{2,1,0:T(8,128)S(1)} collective-permute-done((f32[32,8,256]{2,1,0:T(8,128)S(1)}, f32[32,8,256]{2,1,0:T(8,128)S(1)}, u32[]{:S(2)}, u32[]{:S(2)}) %collective-permute-start.12) | collective-permute-done | bytes 262176 | tf_op jit(solution)/shard_map/ppermute | solution.py:503
  87.2 0.4 collective-permute-start.15
  87.7 0.8 collective-permute-done.13.refs_5_
  88.5 0.5 collective-permute-start.14
  89.0 1.5 %base_b.1.refs_11_ = f32[2,4,256,256]{3,2,1,0:T(8,128)S(1)} custom-call(bf16[256,256]{1,0:T(8,128)(2,1)S(1)} %copy-done.2, f32[8,256,256]{2,1,0:T(8,128)S(1)} %bitcast.7, f32[8,256,256]{2,1,0:T(8,128)S(1)} %bitcast.13, f32[2,3,256,256]{3,2,1,0:T(8,128)S(1)} %once_a.1.refs_0_.refs_7_, f32[2,3,256,256]{3,2,1,0:T(8,128)S(1)} %once_b.1.refs_1_.refs_8_, ...), custom_call_target="tpu_custom_call" | custom-call | bytes 5760000 | tf_op jit(solution)/shard_map/base_b/pallas_call | solution.py:317
  90.5 5.1 %collective-permute-done.15.refs_4_ = f32[32,8,256]{2,1,0:T(8,128)S(1)} collective-permute-done((f32[32,8,256]{2,1,0:T(8,128)S(1)}, f32[32,8,256]{2,1,0:T(8,128)S(1)}, u32[]{:S(2)}, u32[]{:S(2)}) %collective-permute-start.15) | collective-permute-done | bytes 262176 | tf_op jit(solution)/shard_map/ppermute | solution.py:508
  95.6 0.1 collective-permute-start.16
  95.7 1.9 %collective-permute-start.17 = (f32[16,8,256]{2,1,0:T(8,128)S(1)}, f32[16,8,256]{2,1,0:T(8,128)S(1)}, u32[]{:S(2)}, u32[]{:S(2)}) collective-permute-start(f32[16,8,256]{2,1,0:T(8,128)S(1)} %slice.23), channel_id=1, source_target_pairs={{0,112},{16,32},{32,16},{48,64},{64,48},{80,96},{96,80},{112,0},{1... | collective-permute-start | bytes 393224 | tf_op jit(solution)/shard_map/ppermute | solution.py:508
  97.7 2.8 %early_potential.1 = (f32[8,256,256]{2,1,0:T(8,128)S(1)}, bf16[256,192]{1,0:T(8,128)(2,1)S(1)}) custom-call(f32[8,256,256]{2,1,0:T(8,128)S(1)} %copy-done.4, f32[256,256]{1,0:T(8,128)S(1)} %copy-done.3, f32[32,8,256]{2,1,0:T(8,128)S(1)} %all_to_all.11.refs_0_, f32[32,8,256]{2,1,0:T(8,128)S(1)} %collective-permute-done.8.refs_1_, ...), custom_call_target="tpu_custom_call" | custom-call | bytes 8279999 | tf_op jit(solution)/shard_map/early_potential/pallas_call | solution.py:360
  100.4 0.2 collective-permute-done.16.refs_3_.up
  100.7 1.3 %collective-permute-done.17.refs_4_.down = f32[16,8,256]{2,1,0:T(8,128)S(1)} collective-permute-done((f32[16,8,256]{2,1,0:T(8,128)S(1)}, f32[16,8,256]{2,1,0:T(8,128)S(1)}, u32[]{:S(2)}, u32[]{:S(2)}) %collective-permute-start.17) | collective-permute-done | bytes 131104 | tf_op jit(solution)/shard_map/ppermute | solution.py:508
  102.0 0.2 outer_potential.1
  102.3 0.1 collective-permute-start.18
  102.4 0.7 collective-permute-start.19
  103.1 4.5 %inner_update.1 = (f32[1,8,256,256]{3,2,1,0:T(8,128)}, f32[1,8,256,256]{3,2,1,0:T(8,128)}, f32[2,2,256,256]{3,2,1,0:T(8,128)S(1)}) custom-call(bf16[256,256]{1,0:T(8,128)(2,1)S(1)} %copy-done.2, f32[8,256,256]{2,1,0:T(8,128)S(1)} %get-tuple-element.56.refs_1_.early, bf16[256,192]{1,0:T(8,128)(2,1)S(1)} %get-tuple-element.57.refs_2_.tail, ...), custom_call_target="tpu_custom_call" | custom-call | bytes 15480000 | tf_op jit(solution)/shard_map/inner_update/pallas_call | solution.py:450
  107.6 2.7 %collective-permute-done.18.v_other = f32[1,256,256]{2,1,0:T(8,128)S(1)} collective-permute-done((f32[1,256,256]{2,1,0:T(8,128)S(1)}, f32[1,256,256]{2,1,0:T(8,128)S(1)}, u32[]{:S(2)}, u32[]{:S(2)}) %collective-permute-start.18) | collective-permute-done | bytes 262176 | tf_op jit(solution)/shard_map/ppermute | solution.py:521
  110.3 1.1 %close_ends.1 = (f32[1,8,256,256]{3,2,1,0:T(8,128)}, f32[1,8,256,256]{3,2,1,0:T(8,128)}) custom-call(f32[2,2,256,256]{3,2,1,0:T(8,128)S(1)} %get-tuple-element.59.open_ends, f32[1,256,256]{2,1,0:T(8,128)S(1)} %collective-permute-done.18.v_other, f32[1,256,256]{2,1,0:T(8,128)S(1)} %collective-permute-done.19.v_mate, ...), custom_call_target="tpu_custom_call", output_to_operand_aliasing={{0}: (5, {}), {1}: (6, {})} | custom-call | tf_op jit(solution)/shard_map/close_ends/pallas_call | solution.py:490
  (29 shorter events, 0.3 us)
Async XLA Ops:
  4.5 8.2 %collective-permute-start = (f32[8,16,256]{2,1,0:T(8,128)S(1)}, f32[8,16,256]{2,1,0:T(8,128)S(1)}, u32[]{:S(2)}, u32[]{:S(2)}) collective-permute-start(f32[8,16,256]{2,1,0:T(8,128)S(1)} %get-tuple-element.37), channel_id=1, source_target_pairs={{0,16},{16,0},{32,48},{48,32},{64,80},{80,64},{96,112},{112,96},{1... | collective-permute-start | bytes 393224 | tf_op jit(solution)/shard_map/ppermute | solution.py:503
  6.5 8.3 %collective-permute-start.4 = (f32[8,16,256]{2,1,0:T(8,128)S(1)}, f32[8,16,256]{2,1,0:T(8,128)S(1)}, u32[]{:S(2)}, u32[]{:S(2)}) collective-permute-start(f32[8,16,256]{2,1,0:T(8,128)S(1)} %get-tuple-element.43), channel_id=1, source_target_pairs={{0,112},{16,32},{32,16},{48,64},{64,48},{80,96},{96,80},{112,0},{1... | collective-permute-start | bytes 393224 | tf_op jit(solution)/shard_map/ppermute | solution.py:508
  14.8 4.7 %copy-start = (f32[1,8,256,256]{3,2,1,0:T(8,128)S(1)}, f32[1,8,256,256]{3,2,1,0:T(8,128)}, u32[]{:S(2)}) copy-start(f32[1,8,256,256]{3,2,1,0:T(8,128)} %psi_re.1) | copy-start | bytes 6291460
  14.8 4.7 %copy-start.1 = (f32[1,8,256,256]{3,2,1,0:T(8,128)S(1)}, f32[1,8,256,256]{3,2,1,0:T(8,128)}, u32[]{:S(2)}) copy-start(f32[1,8,256,256]{3,2,1,0:T(8,128)} %psi_im.1) | copy-start | bytes 6291460
  14.8 4.7 %copy-start.2 = (bf16[256,256]{1,0:T(8,128)(2,1)S(1)}, bf16[256,256]{1,0:T(8,128)(2,1)}, u32[]{:S(2)}) copy-start(bf16[256,256]{1,0:T(8,128)(2,1)} %constant.8.clone.sides.refs_0_) | copy-start | bytes 393220
  14.9 7.4 %collective-permute-start.5 = (f32[8,32,256]{2,1,0:T(8,128)S(1)}, f32[8,32,256]{2,1,0:T(8,128)S(1)}, u32[]{:S(2)}, u32[]{:S(2)}) collective-permute-start(f32[8,32,256]{2,1,0:T(8,128)S(1)} %pad_maximum_fusion.1), channel_id=1, source_target_pairs={{0,16},{16,0},{32,48},{48,32},{64,80},{80,64},{96,112},{112,96},{1... | collective-permute-start | bytes 786440 | tf_op jit(solution)/shard_map/ppermute | solution.py:503
  15.0 10.0 %collective-permute-start.1 = (f32[8,32,256]{2,1,0:T(8,128)S(1)}, f32[8,32,256]{2,1,0:T(8,128)S(1)}, u32[]{:S(2)}, u32[]{:S(2)}) collective-permute-start(f32[8,32,256]{2,1,0:T(8,128)S(1)} %pad_maximum_fusion), channel_id=1, source_target_pairs={{0,112},{16,32},{32,16},{48,64},{64,48},{80,96},{96,80},{112,0},{1... | collective-permute-start | bytes 786440 | tf_op jit(solution)/shard_map/ppermute | solution.py:508
  22.3 8.5 %collective-permute-start.6 = (f32[8,32,256]{2,1,0:T(8,128)S(1)}, f32[8,32,256]{2,1,0:T(8,128)S(1)}, u32[]{:S(2)}, u32[]{:S(2)}) collective-permute-start(f32[8,32,256]{2,1,0:T(8,128)S(1)} %add.22), channel_id=1, source_target_pairs={{0,112},{16,32},{32,16},{48,64},{64,48},{80,96},{96,80},{112,0},{1... | collective-permute-start | bytes 786440 | tf_op jit(solution)/shard_map/ppermute | solution.py:508
  25.0 7.8 %collective-permute-start.2 = (f32[8,32,256]{2,1,0:T(8,128)S(1)}, f32[8,32,256]{2,1,0:T(8,128)S(1)}, u32[]{:S(2)}, u32[]{:S(2)}) collective-permute-start(f32[8,32,256]{2,1,0:T(8,128)S(1)} %add.19), channel_id=1, source_target_pairs={{0,16},{16,0},{32,48},{48,32},{64,80},{80,64},{96,112},{112,96},{1... | collective-permute-start | bytes 786440 | tf_op jit(solution)/shard_map/ppermute | solution.py:503
  25.1 44.1 %collective-permute-start.9 = (f32[4,256,256]{2,1,0:T(8,128)S(1)}, f32[4,256,256]{2,1,0:T(8,128)S(1)}, u32[]{:S(2)}, u32[]{:S(2)}) collective-permute-start(f32[4,256,256]{2,1,0:T(8,128)S(1)} %get-tuple-element.48), channel_id=1, source_target_pairs={{0,1},{1,0},{2,3},{3,2},{4,5},{5,4},{6,7},{7,6},{8,9},{9,8},{10,11... | collective-permute-start | bytes 3145736 | tf_op jit(solution)/shard_map/ppermute | solution.py:520
  25.2 44.0 %collective-permute-start.10 = (f32[4,256,256]{2,1,0:T(8,128)S(1)}, f32[4,256,256]{2,1,0:T(8,128)S(1)}, u32[]{:S(2)}, u32[]{:S(2)}) collective-permute-start(f32[4,256,256]{2,1,0:T(8,128)S(1)} %get-tuple-element.49), channel_id=1, source_target_pairs={{0,15},{1,2},{2,1},{3,4},{4,3},{5,6},{6,5},{7,8},{8,7},{9,10},{10,... | collective-permute-start | bytes 3145736 | tf_op jit(solution)/shard_map/ppermute | solution.py:521
  30.8 25.0 %copy-start.3 = (f32[256,256]{1,0:T(8,128)S(1)}, f32[256,256]{1,0:T(8,128)}, u32[]{:S(2)}) copy-start(f32[256,256]{1,0:T(8,128)} %constant.6.clone.y_table.x_table.table) | copy-start | bytes 786436
  30.8 25.0 %copy-start.5 = (f32[128,128]{1,0:T(8,128)S(1)}, f32[128,128]{1,0:T(8,128)}, u32[]{:S(2)}) copy-start(f32[128,128]{1,0:T(8,128)} %constant.7.clone.z_table) | copy-start | bytes 196612
  30.8 6.5 %collective-permute-start.7 = (f32[8,32,256]{2,1,0:T(8,128)S(1)}, f32[8,32,256]{2,1,0:T(8,128)S(1)}, u32[]{:S(2)}, u32[]{:S(2)}) collective-permute-start(f32[8,32,256]{2,1,0:T(8,128)S(1)} %add.23), channel_id=1, source_target_pairs={{0,16},{16,0},{32,48},{48,32},{64,80},{80,64},{96,112},{112,96},{1... | collective-permute-start | bytes 786440 | tf_op jit(solution)/shard_map/ppermute | solution.py:503
  32.9 7.7 %collective-permute-start.3 = (f32[8,32,256]{2,1,0:T(8,128)S(1)}, f32[8,32,256]{2,1,0:T(8,128)S(1)}, u32[]{:S(2)}, u32[]{:S(2)}) collective-permute-start(f32[8,32,256]{2,1,0:T(8,128)S(1)} %add.20), channel_id=1, source_target_pairs={{0,112},{16,32},{32,16},{48,64},{64,48},{80,96},{96,80},{112,0},{1... | collective-permute-start | bytes 786440 | tf_op jit(solution)/shard_map/ppermute | solution.py:508
  69.2 10.0 %collective-permute-start.11 = (f32[32,8,256]{2,1,0:T(8,128)S(1)}, f32[32,8,256]{2,1,0:T(8,128)S(1)}, u32[]{:S(2)}, u32[]{:S(2)}) collective-permute-start(f32[32,8,256]{2,1,0:T(8,128)S(1)} %all_to_all.11.refs_0_), channel_id=1, source_target_pairs={{0,112},{16,32},{32,16},{48,64},{64,48},{80,96},{96,80},{112,0},{1... | collective-permute-start | bytes 786440 | tf_op jit(solution)/shard_map/ppermute | solution.py:508
  69.2 10.0 %collective-permute-start.8 = (f32[32,8,256]{2,1,0:T(8,128)S(1)}, f32[32,8,256]{2,1,0:T(8,128)S(1)}, u32[]{:S(2)}, u32[]{:S(2)}) collective-permute-start(f32[32,8,256]{2,1,0:T(8,128)S(1)} %all_to_all.11.refs_0_), channel_id=1, source_target_pairs={{0,16},{16,0},{32,48},{48,32},{64,80},{80,64},{96,112},{112,96},{1... | collective-permute-start | bytes 786440 | tf_op jit(solution)/shard_map/ppermute | solution.py:503
  79.2 8.0 %collective-permute-start.12 = (f32[32,8,256]{2,1,0:T(8,128)S(1)}, f32[32,8,256]{2,1,0:T(8,128)S(1)}, u32[]{:S(2)}, u32[]{:S(2)}) collective-permute-start(f32[32,8,256]{2,1,0:T(8,128)S(1)} %collective-permute-done.11.refs_6_), channel_id=1, source_target_pairs={{0,16},{16,0},{32,48},{48,32},{64,80},{80,64},{96,112},{112,96},{1... | collective-permute-start | bytes 786440 | tf_op jit(solution)/shard_map/ppermute | solution.py:503
  79.2 9.2 %collective-permute-start.13 = (f32[32,8,256]{2,1,0:T(8,128)S(1)}, f32[32,8,256]{2,1,0:T(8,128)S(1)}, u32[]{:S(2)}, u32[]{:S(2)}) collective-permute-start(f32[32,8,256]{2,1,0:T(8,128)S(1)} %collective-permute-done.8.refs_1_), channel_id=1, source_target_pairs={{0,112},{16,32},{32,16},{48,64},{64,48},{80,96},{96,80},{112,0},{1... | collective-permute-start | bytes 786440 | tf_op jit(solution)/shard_map/ppermute | solution.py:508
  82.5 15.2 %copy-start.4 = (f32[8,256,256]{2,1,0:T(8,128)S(1)}, f32[8,256,256]{2,1,0:T(8,128)}, u32[]{:S(2)}) copy-start(f32[8,256,256]{2,1,0:T(8,128)} %v_local.1) | copy-start | bytes 6291460
  87.2 8.4 %collective-permute-start.15 = (f32[32,8,256]{2,1,0:T(8,128)S(1)}, f32[32,8,256]{2,1,0:T(8,128)S(1)}, u32[]{:S(2)}, u32[]{:S(2)}) collective-permute-start(f32[32,8,256]{2,1,0:T(8,128)S(1)} %collective-permute-done.12.refs_2_), channel_id=1, source_target_pairs={{0,112},{16,32},{32,16},{48,64},{64,48},{80,96},{96,80},{112,0},{1... | collective-permute-start | bytes 786440 | tf_op jit(solution)/shard_map/ppermute | solution.py:508
  88.5 7.3 %collective-permute-start.14 = (f32[32,8,256]{2,1,0:T(8,128)S(1)}, f32[32,8,256]{2,1,0:T(8,128)S(1)}, u32[]{:S(2)}, u32[]{:S(2)}) collective-permute-start(f32[32,8,256]{2,1,0:T(8,128)S(1)} %collective-permute-done.13.refs_5_), channel_id=1, source_target_pairs={{0,16},{16,0},{32,48},{48,32},{64,80},{80,64},{96,112},{112,96},{1... | collective-permute-start | bytes 786440 | tf_op jit(solution)/shard_map/ppermute | solution.py:503
  95.6 5.1 %collective-permute-start.16 = (f32[16,8,256]{2,1,0:T(8,128)S(1)}, f32[16,8,256]{2,1,0:T(8,128)S(1)}, u32[]{:S(2)}, u32[]{:S(2)}) collective-permute-start(f32[16,8,256]{2,1,0:T(8,128)S(1)} %slice.22), channel_id=1, source_target_pairs={{0,16},{16,0},{32,48},{48,32},{64,80},{80,64},{96,112},{112,96},{1... | collective-permute-start | bytes 393224 | tf_op jit(solution)/shard_map/ppermute | solution.py:503
  95.7 6.3 %collective-permute-start.17 = (f32[16,8,256]{2,1,0:T(8,128)S(1)}, f32[16,8,256]{2,1,0:T(8,128)S(1)}, u32[]{:S(2)}, u32[]{:S(2)}) collective-permute-start(f32[16,8,256]{2,1,0:T(8,128)S(1)} %slice.23), channel_id=1, source_target_pairs={{0,112},{16,32},{32,16},{48,64},{64,48},{80,96},{96,80},{112,0},{1... | collective-permute-start | bytes 393224 | tf_op jit(solution)/shard_map/ppermute | solution.py:508
  102.3 8.0 %collective-permute-start.18 = (f32[1,256,256]{2,1,0:T(8,128)S(1)}, f32[1,256,256]{2,1,0:T(8,128)S(1)}, u32[]{:S(2)}, u32[]{:S(2)}) collective-permute-start(f32[1,256,256]{2,1,0:T(8,128)S(1)} %get-tuple-element.60), channel_id=1, source_target_pairs={{0,143},{1,2},{2,1},{3,4},{4,3},{5,6},{6,5},{7,136},{8,135},{9,10}... | collective-permute-start | bytes 786440 | tf_op jit(solution)/shard_map/ppermute | solution.py:521
  102.4 7.9 %collective-permute-start.19 = (f32[1,256,256]{2,1,0:T(8,128)S(1)}, f32[1,256,256]{2,1,0:T(8,128)S(1)}, u32[]{:S(2)}, u32[]{:S(2)}) collective-permute-start(f32[1,256,256]{2,1,0:T(8,128)S(1)} %get-tuple-element.61), channel_id=1, source_target_pairs={{0,1},{1,0},{2,3},{3,2},{4,5},{5,4},{6,7},{7,6},{8,9},{9,8},{10,11... | collective-permute-start | bytes 786440 | tf_op jit(solution)/shard_map/ppermute | solution.py:520

commit v9 on v8

--- a/solution.py
+++ b/solution.py
@@ -199,7 +199,7 @@
     nz, nx = z_table.shape[0], x_table.shape[0]
     half = out.shape[0] // SIDES
     width = y_len // lax.axis_size("z")
-    ky = lax.axis_index("z") * width + lax.axis_index("y") * lax.axis_size("slab") + lax.axis_index("slab")
+    ky = lax.axis_index("z") * width + lax.axis_index("slab") * SIDES + lax.axis_index("y")
     z_index = lax.broadcasted_iota(jnp.int32, (nz, nx), 0)
     x_index = lax.broadcasted_iota(jnp.int32, (nz, nx), 1)
     y_index = jnp.full((nz, nx), ky, jnp.int32)
@@ -207,12 +207,15 @@
     anchor = (z_index == 0) & (y_index == 0) & (x_index == 0)
     safe = jnp.where(anchor, jnp.float32(1.0), total)
     greens = jnp.where(anchor, jnp.float32(0.0), (4.0 * math.pi) / safe) * (1.0 / (nz * y_len * nx))
-    rho = field[0:nz] + field[nz : 2 * nz]
+    planes = out.shape[1]
+    pairs = field[...].reshape(half, SIDES * planes, nx)
+    rho = (pairs[:, :planes] + pairs[:, planes:]).reshape(nz, nx)
     spectrum = dot(z_table[...], dot(rho, x_table[...]))
     solved = dot_three(dot_three(z_table[...], spectrum * greens), x_table[...])
     solved = solved.reshape((half,) + out.shape[1:])
-    out[0:half] = solved
-    out[half:] = solved
+    for slab in range(half):
+        for side in range(SIDES):
+            out[SIDES * slab + side] = solved[slab]
 
 
 def solve(field, x_table, z_table, y_len, planes):
@@ -554,7 +557,7 @@
 
 
 def across(value):
-    return lax.all_to_all(value, ("y", "slab"), split_axis=0, concat_axis=0, tiled=True)
+    return lax.all_to_all(value, ("slab", "y"), split_axis=0, concat_axis=0, tiled=True)
 
 
 def on_device(psi_re, psi_im, v_local, n_ground):

time: 112 us -> 111 us (level)
  waiting for transfers between devices: 33.9 us -> 29.1 us
  starting transfers between devices: 26.5 us -> 28.7 us
    ppermute x8, waiting for transfers between devices: 21.2 us -> 17.5 us  [swap_far(): lax.ppermute(value, 'z', [(i, (i - 1) % count if i % 2 == 0 else (i + 1)...]
  transfers between devices with their start and end apart: 20 -> 20, of which waited for: 11 -> 11; matrix products, arithmetic and copies ran while one was open for 0% -> 0% of each run, Pallas kernels for 15% -> 16%
where the time goes in v9:
time: 111 us; the launch traced here: 110 us
  waiting for transfers between devices  29.1 us (26%)
  starting transfers between devices  28.7 us (26%)
  blocking collectives  28.3 us (25%)
  Pallas kernels  22.5 us (20%)
    all_to_all x2, blocking collectives, across(): lax.all_to_all(value, ('slab', 'y'), split_axis=0, concat_axis=0, tiled=T...  28.3 us
    ppermute x8, waiting for transfers between devices, swap_far(): lax.ppermute(value, 'z', [(i, (i - 1) % count if i % 2 == 0 else (i + 1)...  17.5 us
    ppermute x8, starting transfers between devices, swap_far(): lax.ppermute(value, 'z', [(i, (i - 1) % count if i % 2 == 0 else (i + 1)...  17.2 us
    ppermute x8, waiting for transfers between devices, swap_near(): lax.ppermute(value, 'z', [(i, i ^ 1) for i in range(lax.axis_size('z'))])  9.05 us
    ppermute x8, starting transfers between devices, swap_near(): lax.ppermute(value, 'z', [(i, i ^ 1) for i in range(lax.axis_size('z'))])  5.78 us
    ppermute x2, starting transfers between devices, swap_edges(): from_other = lax.ppermute(to_other, ('y', 'slab'), pairs)  4.69 us
    pallas_call x1, Pallas kernels, inner_update(): pl.pallas_call(functools.partial(inner_kernel, once_groups, base_groups),...  4.5 us
    pallas_call x1, Pallas kernels, density(): pl.pallas_call(functools.partial(density_kernel, 2.0 / total_orbs), in_sp...  3.85 us
  transfers between devices with their start and end apart: 20, of which 11 were waited for; matrix products, arithmetic and copies ran while one was open for 0% of the time, Pallas kernels for 16%

profile of v9, /device:TPU:8, one launch (start us, length us, event | category | flops | bytes accessed | tf_op | source)
XLA Modules:
  0.0 109.9 jit_solution(11386883811432000592)
XLA Ops:
  0.6 3.8 %density.1 = (f32[8,256,256]{2,1,0:T(8,128)S(1)}, f32[256,256]{1,0:T(8,128)S(1)}, f32[8,16,256]{2,1,0:T(8,128)S(1)}, f32[8,16,256]{2,1,0:T(8,128)S(1)}, f32[4,25...) custom-call(f32[1,8,256,256]{3,2,1,0:T(8,128)} %psi_re.1, f32[1,8,256,256]{3,2,1,0:T(8,128)} %psi_im.1, ...), custom_call_target="tpu_custom_call" | custom-call | tf_op jit(solution)/shard_map/density/pallas_call | solution.py:135
  4.5 2.0 %collective-permute-start = (f32[8,16,256]{2,1,0:T(8,128)S(1)}, f32[8,16,256]{2,1,0:T(8,128)S(1)}, u32[]{:S(2)}, u32[]{:S(2)}) collective-permute-start(f32[8,16,256]{2,1,0:T(8,128)S(1)} %get-tuple-element.37), channel_id=1, source_target_pairs={{0,16},{16,0},{32,48},{48,32},{64,80},{80,64},{96,112},{112,96},{1... | collective-permute-start | bytes 393224 | tf_op jit(solution)/shard_map/ppermute | solution.py:506
  6.5 5.0 %collective-permute-start.4 = (f32[8,16,256]{2,1,0:T(8,128)S(1)}, f32[8,16,256]{2,1,0:T(8,128)S(1)}, u32[]{:S(2)}, u32[]{:S(2)}) collective-permute-start(f32[8,16,256]{2,1,0:T(8,128)S(1)} %get-tuple-element.43), channel_id=1, source_target_pairs={{0,112},{16,32},{32,16},{48,64},{64,48},{80,96},{96,80},{112,0},{1... | collective-permute-start | bytes 393224 | tf_op jit(solution)/shard_map/ppermute | solution.py:511
  11.4 1.3 %shares_a.1 = (f32[8,32,256]{2,1,0:T(8,128)S(1)}, f32[8,32,256]{2,1,0:T(8,128)S(1)}) custom-call(f32[8,256,256]{2,1,0:T(8,128)S(1)} %get-tuple-element.33.rho, f32[256,256]{1,0:T(8,128)S(1)} %get-tuple-element.34.rows), custom_call_target="tpu_custom_call" | custom-call | bytes 2160000 | tf_op jit(solution)/shard_map/shares_a/pallas_call | solution.py:164
  12.7 2.0 %collective-permute-done.4 = f32[8,16,256]{2,1,0:T(8,128)S(1)} collective-permute-done((f32[8,16,256]{2,1,0:T(8,128)S(1)}, f32[8,16,256]{2,1,0:T(8,128)S(1)}, u32[]{:S(2)}, u32[]{:S(2)}) %collective-permute-start.4) | collective-permute-done | bytes 131104 | tf_op jit(solution)/shard_map/ppermute | solution.py:511
  14.8 0.1 slice_add_fusion.1
  14.9 0.1 collective-permute-start.5
  15.0 3.0 %collective-permute-start.1 = (f32[8,32,256]{2,1,0:T(8,128)S(1)}, f32[8,32,256]{2,1,0:T(8,128)S(1)}, u32[]{:S(2)}, u32[]{:S(2)}) collective-permute-start(f32[8,32,256]{2,1,0:T(8,128)S(1)} %pad_maximum_fusion), channel_id=1, source_target_pairs={{0,112},{16,32},{32,16},{48,64},{64,48},{80,96},{96,80},{112,0},{1... | collective-permute-start | bytes 786440 | tf_op jit(solution)/shard_map/ppermute | solution.py:511
  18.0 1.4 %shares_b.1 = (f32[8,32,256]{2,1,0:T(8,128)S(1)}, f32[8,32,256]{2,1,0:T(8,128)S(1)}, f32[8,32,256]{2,1,0:T(8,128)S(1)}, f32[8,32,256]{2,1,0:T(8,128)S(1)}, f32[8,32,256]{2,1,0:T(8,128)S(1)}) custom-call(f32[8,256,256]{2,1,0:T(8,128)S(1)} %get-tuple-element.33.rho, f32[256,256]{1,0:T(8,128)S(1)} %get-tuple-element.34.rows), custom_call_target="tpu_custom_call" | custom-call | bytes 5400000 | tf_op jit(solution)/shard_map/shares_b/pallas_call | solution.py:164
  19.5 0.9 once_a.1.refs_0_.refs_7_
  20.4 1.8 %collective-permute-done.5 = f32[8,32,256]{2,1,0:T(8,128)S(1)} collective-permute-done((f32[8,32,256]{2,1,0:T(8,128)S(1)}, f32[8,32,256]{2,1,0:T(8,128)S(1)}, u32[]{:S(2)}, u32[]{:S(2)}) %collective-permute-start.5) | collective-permute-done | bytes 262176 | tf_op jit(solution)/shard_map/ppermute | solution.py:506
  22.3 2.7 %collective-permute-start.6 = (f32[8,32,256]{2,1,0:T(8,128)S(1)}, f32[8,32,256]{2,1,0:T(8,128)S(1)}, u32[]{:S(2)}, u32[]{:S(2)}) collective-permute-start(f32[8,32,256]{2,1,0:T(8,128)S(1)} %add.22), channel_id=1, source_target_pairs={{0,112},{16,32},{32,16},{48,64},{64,48},{80,96},{96,80},{112,0},{1... | collective-permute-start | bytes 786440 | tf_op jit(solution)/shard_map/ppermute | solution.py:511
  25.0 0.1 collective-permute-start.2
  25.1 0.1 collective-permute-start.9
  25.2 4.6 %collective-permute-start.10 = (f32[4,256,256]{2,1,0:T(8,128)S(1)}, f32[4,256,256]{2,1,0:T(8,128)S(1)}, u32[]{:S(2)}, u32[]{:S(2)}) collective-permute-start(f32[4,256,256]{2,1,0:T(8,128)S(1)} %get-tuple-element.49), channel_id=1, source_target_pairs={{0,15},{1,2},{2,1},{3,4},{4,3},{5,6},{6,5},{7,8},{8,7},{9,10},{10,... | collective-permute-start | bytes 3145736 | tf_op jit(solution)/shard_map/ppermute | solution.py:524
  29.8 0.9 once_b.1.refs_1_.refs_8_
  30.8 0.0 copy-start.3
  30.8 0.0 copy-start.5
  30.8 2.0 %collective-permute-start.7 = (f32[8,32,256]{2,1,0:T(8,128)S(1)}, f32[8,32,256]{2,1,0:T(8,128)S(1)}, u32[]{:S(2)}, u32[]{:S(2)}) collective-permute-start(f32[8,32,256]{2,1,0:T(8,128)S(1)} %add.23), channel_id=1, source_target_pairs={{0,16},{16,0},{32,48},{48,32},{64,80},{80,64},{96,112},{112,96},{1... | collective-permute-start | bytes 786440 | tf_op jit(solution)/shard_map/ppermute | solution.py:506
  32.9 1.3 %collective-permute-start.3 = (f32[8,32,256]{2,1,0:T(8,128)S(1)}, f32[8,32,256]{2,1,0:T(8,128)S(1)}, u32[]{:S(2)}, u32[]{:S(2)}) collective-permute-start(f32[8,32,256]{2,1,0:T(8,128)S(1)} %add.20), channel_id=1, source_target_pairs={{0,112},{16,32},{32,16},{48,64},{64,48},{80,96},{96,80},{112,0},{1... | collective-permute-start | bytes 786440 | tf_op jit(solution)/shard_map/ppermute | solution.py:511
  34.2 3.1 %collective-permute-done.7.down = f32[8,32,256]{2,1,0:T(8,128)S(1)} collective-permute-done((f32[8,32,256]{2,1,0:T(8,128)S(1)}, f32[8,32,256]{2,1,0:T(8,128)S(1)}, u32[]{:S(2)}, u32[]{:S(2)}) %collective-permute-start.7) | collective-permute-done | bytes 262176 | tf_op jit(solution)/shard_map/ppermute | solution.py:506
  37.3 3.3 %collective-permute-done.3.up = f32[8,32,256]{2,1,0:T(8,128)S(1)} collective-permute-done((f32[8,32,256]{2,1,0:T(8,128)S(1)}, f32[8,32,256]{2,1,0:T(8,128)S(1)}, u32[]{:S(2)}, u32[]{:S(2)}) %collective-permute-start.3) | collective-permute-done | bytes 262176 | tf_op jit(solution)/shard_map/ppermute | solution.py:511
  40.6 0.1 add_shares.1
  40.7 15.8 %all_to_all.10 = f32[32,8,256]{2,1,0:T(8,128)S(1)} all-to-all(f32[32,8,256]{2,1,0:T(8,128)S(1)} %add_shares.1), channel_id=1, replica_groups=mesh['y'=2,'z'=8,'slab'=16] {'slab','y'}, dimensions={0} | all-to-all | bytes 524288 | tf_op jit(solution)/shard_map/all_to_all | solution.py:560
  56.4 1.1 solve_xz.1
  57.5 12.5 %all_to_all.11.refs_0_ = f32[32,8,256]{2,1,0:T(8,128)S(1)} all-to-all(f32[32,8,256]{2,1,0:T(8,128)S(1)} %solve_xz.1), channel_id=1, replica_groups=mesh['y'=2,'z'=8,'slab'=16] {'slab','y'}, dimensions={0} | all-to-all | bytes 524288 | tf_op jit(solution)/shard_map/all_to_all | solution.py:560
  70.1 0.0 collective-permute-start.11
  70.1 1.2 %once_c.1.refs_2_.refs_9_ = f32[2,4,256,256]{3,2,1,0:T(8,128)S(1)} custom-call(bf16[256,256]{1,0:T(8,128)(2,1)S(1)} %copy-done.2, f32[8,256,256]{2,1,0:T(8,128)S(1)} %bitcast.5, f32[8,256,256]{2,1,0:T(8,128)S(1)} %bitcast.11, f32[4,256,256]{2,1,0:T(8,128)S(1)} %collective-permute-done.9.refs_2_.mate, f32[4,256,256]{2,1,0:T(8,128)S(1)} %collective-permute-done.10.refs_3_.other), custom_call_target="tpu_custom_call" | custom-call | bytes 4320000 | tf_op jit(solution)/shard_map/once_c/pallas_call | solution.py:291
  71.4 7.5 %collective-permute-done.11.refs_6_ = f32[32,8,256]{2,1,0:T(8,128)S(1)} collective-permute-done((f32[32,8,256]{2,1,0:T(8,128)S(1)}, f32[32,8,256]{2,1,0:T(8,128)S(1)}, u32[]{:S(2)}, u32[]{:S(2)}) %collective-permute-start.11) | collective-permute-done | bytes 262176 | tf_op jit(solution)/shard_map/ppermute | solution.py:511
  78.9 1.8 %collective-permute-start.13 = (f32[32,8,256]{2,1,0:T(8,128)S(1)}, f32[32,8,256]{2,1,0:T(8,128)S(1)}, u32[]{:S(2)}, u32[]{:S(2)}) collective-permute-start(f32[32,8,256]{2,1,0:T(8,128)S(1)} %collective-permute-done.8.refs_1_), channel_id=1, source_target_pairs={{0,112},{16,32},{32,16},{48,64},{64,48},{80,96},{96,80},{112,0},{1... | collective-permute-start | bytes 786440 | tf_op jit(solution)/shard_map/ppermute | solution.py:511
  80.7 1.5 %base_a.1.refs_10_ = f32[2,4,256,256]{3,2,1,0:T(8,128)S(1)} custom-call(bf16[256,256]{1,0:T(8,128)(2,1)S(1)} %copy-done.2, f32[8,256,256]{2,1,0:T(8,128)S(1)} %bitcast.6, f32[8,256,256]{2,1,0:T(8,128)S(1)} %bitcast.12, f32[2,3,256,256]{3,2,1,0:T(8,128)S(1)} %once_a.1.refs_0_.refs_7_, f32[2,3,256,256]{3,2,1,0:T(8,128)S(1)} %once_b.1.refs_1_.refs_8_, ...), custom_call_target="tpu_custom_call" | custom-call | bytes 5760000 | tf_op jit(solution)/shard_map/base_a/pallas_call | solution.py:320
  82.2 3.4 %collective-permute-done.12.refs_2_ = f32[32,8,256]{2,1,0:T(8,128)S(1)} collective-permute-done((f32[32,8,256]{2,1,0:T(8,128)S(1)}, f32[32,8,256]{2,1,0:T(8,128)S(1)}, u32[]{:S(2)}, u32[]{:S(2)}) %collective-permute-start.12) | collective-permute-done | bytes 262176 | tf_op jit(solution)/shard_map/ppermute | solution.py:506
  85.6 0.7 collective-permute-start.15
  86.3 0.6 collective-permute-done.13.refs_5_
  86.8 1.5 %collective-permute-start.14 = (f32[32,8,256]{2,1,0:T(8,128)S(1)}, f32[32,8,256]{2,1,0:T(8,128)S(1)}, u32[]{:S(2)}, u32[]{:S(2)}) collective-permute-start(f32[32,8,256]{2,1,0:T(8,128)S(1)} %collective-permute-done.13.refs_5_), channel_id=1, source_target_pairs={{0,16},{16,0},{32,48},{48,32},{64,80},{80,64},{96,112},{112,96},{1... | collective-permute-start | bytes 786440 | tf_op jit(solution)/shard_map/ppermute | solution.py:506
  88.3 1.5 %base_b.1.refs_11_ = f32[2,4,256,256]{3,2,1,0:T(8,128)S(1)} custom-call(bf16[256,256]{1,0:T(8,128)(2,1)S(1)} %copy-done.2, f32[8,256,256]{2,1,0:T(8,128)S(1)} %bitcast.7, f32[8,256,256]{2,1,0:T(8,128)S(1)} %bitcast.13, f32[2,3,256,256]{3,2,1,0:T(8,128)S(1)} %once_a.1.refs_0_.refs_7_, f32[2,3,256,256]{3,2,1,0:T(8,128)S(1)} %once_b.1.refs_1_.refs_8_, ...), custom_call_target="tpu_custom_call" | custom-call | bytes 5760000 | tf_op jit(solution)/shard_map/base_b/pallas_call | solution.py:320
  89.8 3.4 %collective-permute-done.15.refs_4_ = f32[32,8,256]{2,1,0:T(8,128)S(1)} collective-permute-done((f32[32,8,256]{2,1,0:T(8,128)S(1)}, f32[32,8,256]{2,1,0:T(8,128)S(1)}, u32[]{:S(2)}, u32[]{:S(2)}) %collective-permute-start.15) | collective-permute-done | bytes 262176 | tf_op jit(solution)/shard_map/ppermute | solution.py:511
  93.2 0.1 collective-permute-start.16
  93.3 0.7 collective-permute-done.14.refs_3_
  94.0 2.7 %collective-permute-start.17 = (f32[16,8,256]{2,1,0:T(8,128)S(1)}, f32[16,8,256]{2,1,0:T(8,128)S(1)}, u32[]{:S(2)}, u32[]{:S(2)}) collective-permute-start(f32[16,8,256]{2,1,0:T(8,128)S(1)} %slice.23), channel_id=1, source_target_pairs={{0,112},{16,32},{32,16},{48,64},{64,48},{80,96},{96,80},{112,0},{1... | collective-permute-start | bytes 393224 | tf_op jit(solution)/shard_map/ppermute | solution.py:511
  96.7 2.8 %early_potential.1 = (f32[8,256,256]{2,1,0:T(8,128)S(1)}, bf16[256,192]{1,0:T(8,128)(2,1)S(1)}) custom-call(f32[8,256,256]{2,1,0:T(8,128)S(1)} %copy-done.4, f32[256,256]{1,0:T(8,128)S(1)} %copy-done.3, f32[32,8,256]{2,1,0:T(8,128)S(1)} %all_to_all.11.refs_0_, f32[32,8,256]{2,1,0:T(8,128)S(1)} %collective-permute-done.8.refs_1_, ...), custom_call_target="tpu_custom_call" | custom-call | bytes 8279999 | tf_op jit(solution)/shard_map/early_potential/pallas_call | solution.py:363
  99.5 0.8 collective-permute-done.17.refs_4_.down
  100.3 0.2 outer_potential.1
  100.5 0.1 collective-permute-start.18
  100.6 0.9 collective-permute-start.19
  101.6 4.5 %inner_update.1 = (f32[1,8,256,256]{3,2,1,0:T(8,128)}, f32[1,8,256,256]{3,2,1,0:T(8,128)}, f32[2,2,256,256]{3,2,1,0:T(8,128)S(1)}) custom-call(bf16[256,256]{1,0:T(8,128)(2,1)S(1)} %copy-done.2, f32[8,256,256]{2,1,0:T(8,128)S(1)} %get-tuple-element.56.refs_1_.early, bf16[256,192]{1,0:T(8,128)(2,1)S(1)} %get-tuple-element.57.refs_2_.tail, ...), custom_call_target="tpu_custom_call" | custom-call | bytes 15480000 | tf_op jit(solution)/shard_map/inner_update/pallas_call | solution.py:453
  106.1 2.5 %collective-permute-done.18.v_other = f32[1,256,256]{2,1,0:T(8,128)S(1)} collective-permute-done((f32[1,256,256]{2,1,0:T(8,128)S(1)}, f32[1,256,256]{2,1,0:T(8,128)S(1)}, u32[]{:S(2)}, u32[]{:S(2)}) %collective-permute-start.18) | collective-permute-done | bytes 262176 | tf_op jit(solution)/shard_map/ppermute | solution.py:524
  108.5 1.1 %close_ends.1 = (f32[1,8,256,256]{3,2,1,0:T(8,128)}, f32[1,8,256,256]{3,2,1,0:T(8,128)}) custom-call(f32[2,2,256,256]{3,2,1,0:T(8,128)S(1)} %get-tuple-element.59.open_ends, f32[1,256,256]{2,1,0:T(8,128)S(1)} %collective-permute-done.18.v_other, f32[1,256,256]{2,1,0:T(8,128)S(1)} %collective-permute-done.19.v_mate, ...), custom_call_target="tpu_custom_call", output_to_operand_aliasing={{0}: (5, {}), {1}: (6, {})} | custom-call | tf_op jit(solution)/shard_map/close_ends/pallas_call | solution.py:493
  (29 shorter events, 0.3 us)
Async XLA Ops:
  4.5 8.2 %collective-permute-start = (f32[8,16,256]{2,1,0:T(8,128)S(1)}, f32[8,16,256]{2,1,0:T(8,128)S(1)}, u32[]{:S(2)}, u32[]{:S(2)}) collective-permute-start(f32[8,16,256]{2,1,0:T(8,128)S(1)} %get-tuple-element.37), channel_id=1, source_target_pairs={{0,16},{16,0},{32,48},{48,32},{64,80},{80,64},{96,112},{112,96},{1... | collective-permute-start | bytes 393224 | tf_op jit(solution)/shard_map/ppermute | solution.py:506
  6.5 8.3 %collective-permute-start.4 = (f32[8,16,256]{2,1,0:T(8,128)S(1)}, f32[8,16,256]{2,1,0:T(8,128)S(1)}, u32[]{:S(2)}, u32[]{:S(2)}) collective-permute-start(f32[8,16,256]{2,1,0:T(8,128)S(1)} %get-tuple-element.43), channel_id=1, source_target_pairs={{0,112},{16,32},{32,16},{48,64},{64,48},{80,96},{96,80},{112,0},{1... | collective-permute-start | bytes 393224 | tf_op jit(solution)/shard_map/ppermute | solution.py:511
  14.8 4.7 %copy-start = (f32[1,8,256,256]{3,2,1,0:T(8,128)S(1)}, f32[1,8,256,256]{3,2,1,0:T(8,128)}, u32[]{:S(2)}) copy-start(f32[1,8,256,256]{3,2,1,0:T(8,128)} %psi_re.1) | copy-start | bytes 6291460
  14.8 4.7 %copy-start.1 = (f32[1,8,256,256]{3,2,1,0:T(8,128)S(1)}, f32[1,8,256,256]{3,2,1,0:T(8,128)}, u32[]{:S(2)}) copy-start(f32[1,8,256,256]{3,2,1,0:T(8,128)} %psi_im.1) | copy-start | bytes 6291460
  14.8 4.7 %copy-start.2 = (bf16[256,256]{1,0:T(8,128)(2,1)S(1)}, bf16[256,256]{1,0:T(8,128)(2,1)}, u32[]{:S(2)}) copy-start(bf16[256,256]{1,0:T(8,128)(2,1)} %constant.8.clone.sides.refs_0_) | copy-start | bytes 393220
  14.9 7.4 %collective-permute-start.5 = (f32[8,32,256]{2,1,0:T(8,128)S(1)}, f32[8,32,256]{2,1,0:T(8,128)S(1)}, u32[]{:S(2)}, u32[]{:S(2)}) collective-permute-start(f32[8,32,256]{2,1,0:T(8,128)S(1)} %pad_maximum_fusion.1), channel_id=1, source_target_pairs={{0,16},{16,0},{32,48},{48,32},{64,80},{80,64},{96,112},{112,96},{1... | collective-permute-start | bytes 786440 | tf_op jit(solution)/shard_map/ppermute | solution.py:506
  15.0 10.0 %collective-permute-start.1 = (f32[8,32,256]{2,1,0:T(8,128)S(1)}, f32[8,32,256]{2,1,0:T(8,128)S(1)}, u32[]{:S(2)}, u32[]{:S(2)}) collective-permute-start(f32[8,32,256]{2,1,0:T(8,128)S(1)} %pad_maximum_fusion), channel_id=1, source_target_pairs={{0,112},{16,32},{32,16},{48,64},{64,48},{80,96},{96,80},{112,0},{1... | collective-permute-start | bytes 786440 | tf_op jit(solution)/shard_map/ppermute | solution.py:511
  22.3 8.5 %collective-permute-start.6 = (f32[8,32,256]{2,1,0:T(8,128)S(1)}, f32[8,32,256]{2,1,0:T(8,128)S(1)}, u32[]{:S(2)}, u32[]{:S(2)}) collective-permute-start(f32[8,32,256]{2,1,0:T(8,128)S(1)} %add.22), channel_id=1, source_target_pairs={{0,112},{16,32},{32,16},{48,64},{64,48},{80,96},{96,80},{112,0},{1... | collective-permute-start | bytes 786440 | tf_op jit(solution)/shard_map/ppermute | solution.py:511
  25.0 7.8 %collective-permute-start.2 = (f32[8,32,256]{2,1,0:T(8,128)S(1)}, f32[8,32,256]{2,1,0:T(8,128)S(1)}, u32[]{:S(2)}, u32[]{:S(2)}) collective-permute-start(f32[8,32,256]{2,1,0:T(8,128)S(1)} %add.19), channel_id=1, source_target_pairs={{0,16},{16,0},{32,48},{48,32},{64,80},{80,64},{96,112},{112,96},{1... | collective-permute-start | bytes 786440 | tf_op jit(solution)/shard_map/ppermute | solution.py:506
  25.1 45.0 %collective-permute-start.9 = (f32[4,256,256]{2,1,0:T(8,128)S(1)}, f32[4,256,256]{2,1,0:T(8,128)S(1)}, u32[]{:S(2)}, u32[]{:S(2)}) collective-permute-start(f32[4,256,256]{2,1,0:T(8,128)S(1)} %get-tuple-element.48), channel_id=1, source_target_pairs={{0,1},{1,0},{2,3},{3,2},{4,5},{5,4},{6,7},{7,6},{8,9},{9,8},{10,11... | collective-permute-start | bytes 3145736 | tf_op jit(solution)/shard_map/ppermute | solution.py:523
  25.2 44.9 %collective-permute-start.10 = (f32[4,256,256]{2,1,0:T(8,128)S(1)}, f32[4,256,256]{2,1,0:T(8,128)S(1)}, u32[]{:S(2)}, u32[]{:S(2)}) collective-permute-start(f32[4,256,256]{2,1,0:T(8,128)S(1)} %get-tuple-element.49), channel_id=1, source_target_pairs={{0,15},{1,2},{2,1},{3,4},{4,3},{5,6},{6,5},{7,8},{8,7},{9,10},{10,... | collective-permute-start | bytes 3145736 | tf_op jit(solution)/shard_map/ppermute | solution.py:524
  30.8 25.7 %copy-start.3 = (f32[256,256]{1,0:T(8,128)S(1)}, f32[256,256]{1,0:T(8,128)}, u32[]{:S(2)}) copy-start(f32[256,256]{1,0:T(8,128)} %constant.6.clone.y_table.x_table.table) | copy-start | bytes 786436
  30.8 25.7 %copy-start.5 = (f32[128,128]{1,0:T(8,128)S(1)}, f32[128,128]{1,0:T(8,128)}, u32[]{:S(2)}) copy-start(f32[128,128]{1,0:T(8,128)} %constant.7.clone.z_table) | copy-start | bytes 196612
  30.8 6.5 %collective-permute-start.7 = (f32[8,32,256]{2,1,0:T(8,128)S(1)}, f32[8,32,256]{2,1,0:T(8,128)S(1)}, u32[]{:S(2)}, u32[]{:S(2)}) collective-permute-start(f32[8,32,256]{2,1,0:T(8,128)S(1)} %add.23), channel_id=1, source_target_pairs={{0,16},{16,0},{32,48},{48,32},{64,80},{80,64},{96,112},{112,96},{1... | collective-permute-start | bytes 786440 | tf_op jit(solution)/shard_map/ppermute | solution.py:506
  32.9 7.7 %collective-permute-start.3 = (f32[8,32,256]{2,1,0:T(8,128)S(1)}, f32[8,32,256]{2,1,0:T(8,128)S(1)}, u32[]{:S(2)}, u32[]{:S(2)}) collective-permute-start(f32[8,32,256]{2,1,0:T(8,128)S(1)} %add.20), channel_id=1, source_target_pairs={{0,112},{16,32},{32,16},{48,64},{64,48},{80,96},{96,80},{112,0},{1... | collective-permute-start | bytes 786440 | tf_op jit(solution)/shard_map/ppermute | solution.py:511
  70.1 8.8 %collective-permute-start.11 = (f32[32,8,256]{2,1,0:T(8,128)S(1)}, f32[32,8,256]{2,1,0:T(8,128)S(1)}, u32[]{:S(2)}, u32[]{:S(2)}) collective-permute-start(f32[32,8,256]{2,1,0:T(8,128)S(1)} %all_to_all.11.refs_0_), channel_id=1, source_target_pairs={{0,112},{16,32},{32,16},{48,64},{64,48},{80,96},{96,80},{112,0},{1... | collective-permute-start | bytes 786440 | tf_op jit(solution)/shard_map/ppermute | solution.py:511
  70.1 8.8 %collective-permute-start.8 = (f32[32,8,256]{2,1,0:T(8,128)S(1)}, f32[32,8,256]{2,1,0:T(8,128)S(1)}, u32[]{:S(2)}, u32[]{:S(2)}) collective-permute-start(f32[32,8,256]{2,1,0:T(8,128)S(1)} %all_to_all.11.refs_0_), channel_id=1, source_target_pairs={{0,16},{16,0},{32,48},{48,32},{64,80},{80,64},{96,112},{112,96},{1... | collective-permute-start | bytes 786440 | tf_op jit(solution)/shard_map/ppermute | solution.py:506
  78.9 6.7 %collective-permute-start.12 = (f32[32,8,256]{2,1,0:T(8,128)S(1)}, f32[32,8,256]{2,1,0:T(8,128)S(1)}, u32[]{:S(2)}, u32[]{:S(2)}) collective-permute-start(f32[32,8,256]{2,1,0:T(8,128)S(1)} %collective-permute-done.11.refs_6_), channel_id=1, source_target_pairs={{0,16},{16,0},{32,48},{48,32},{64,80},{80,64},{96,112},{112,96},{1... | collective-permute-start | bytes 786440 | tf_op jit(solution)/shard_map/ppermute | solution.py:506
  78.9 7.9 %collective-permute-start.13 = (f32[32,8,256]{2,1,0:T(8,128)S(1)}, f32[32,8,256]{2,1,0:T(8,128)S(1)}, u32[]{:S(2)}, u32[]{:S(2)}) collective-permute-start(f32[32,8,256]{2,1,0:T(8,128)S(1)} %collective-permute-done.8.refs_1_), channel_id=1, source_target_pairs={{0,112},{16,32},{32,16},{48,64},{64,48},{80,96},{96,80},{112,0},{1... | collective-permute-start | bytes 786440 | tf_op jit(solution)/shard_map/ppermute | solution.py:511
  82.2 14.5 %copy-start.4 = (f32[8,256,256]{2,1,0:T(8,128)S(1)}, f32[8,256,256]{2,1,0:T(8,128)}, u32[]{:S(2)}) copy-start(f32[8,256,256]{2,1,0:T(8,128)} %v_local.1) | copy-start | bytes 6291460
  85.6 7.6 %collective-permute-start.15 = (f32[32,8,256]{2,1,0:T(8,128)S(1)}, f32[32,8,256]{2,1,0:T(8,128)S(1)}, u32[]{:S(2)}, u32[]{:S(2)}) collective-permute-start(f32[32,8,256]{2,1,0:T(8,128)S(1)} %collective-permute-done.12.refs_2_), channel_id=1, source_target_pairs={{0,112},{16,32},{32,16},{48,64},{64,48},{80,96},{96,80},{112,0},{1... | collective-permute-start | bytes 786440 | tf_op jit(solution)/shard_map/ppermute | solution.py:511
  86.8 7.2 %collective-permute-start.14 = (f32[32,8,256]{2,1,0:T(8,128)S(1)}, f32[32,8,256]{2,1,0:T(8,128)S(1)}, u32[]{:S(2)}, u32[]{:S(2)}) collective-permute-start(f32[32,8,256]{2,1,0:T(8,128)S(1)} %collective-permute-done.13.refs_5_), channel_id=1, source_target_pairs={{0,16},{16,0},{32,48},{48,32},{64,80},{80,64},{96,112},{112,96},{1... | collective-permute-start | bytes 786440 | tf_op jit(solution)/shard_map/ppermute | solution.py:506
  93.2 6.3 %collective-permute-start.16 = (f32[16,8,256]{2,1,0:T(8,128)S(1)}, f32[16,8,256]{2,1,0:T(8,128)S(1)}, u32[]{:S(2)}, u32[]{:S(2)}) collective-permute-start(f32[16,8,256]{2,1,0:T(8,128)S(1)} %slice.22), channel_id=1, source_target_pairs={{0,16},{16,0},{32,48},{48,32},{64,80},{80,64},{96,112},{112,96},{1... | collective-permute-start | bytes 393224 | tf_op jit(solution)/shard_map/ppermute | solution.py:506
  94.0 6.3 %collective-permute-start.17 = (f32[16,8,256]{2,1,0:T(8,128)S(1)}, f32[16,8,256]{2,1,0:T(8,128)S(1)}, u32[]{:S(2)}, u32[]{:S(2)}) collective-permute-start(f32[16,8,256]{2,1,0:T(8,128)S(1)} %slice.23), channel_id=1, source_target_pairs={{0,112},{16,32},{32,16},{48,64},{64,48},{80,96},{96,80},{112,0},{1... | collective-permute-start | bytes 393224 | tf_op jit(solution)/shard_map/ppermute | solution.py:511
  100.5 8.0 %collective-permute-start.18 = (f32[1,256,256]{2,1,0:T(8,128)S(1)}, f32[1,256,256]{2,1,0:T(8,128)S(1)}, u32[]{:S(2)}, u32[]{:S(2)}) collective-permute-start(f32[1,256,256]{2,1,0:T(8,128)S(1)} %get-tuple-element.60), channel_id=1, source_target_pairs={{0,143},{1,2},{2,1},{3,4},{4,3},{5,6},{6,5},{7,136},{8,135},{9,10}... | collective-permute-start | bytes 786440 | tf_op jit(solution)/shard_map/ppermute | solution.py:524
  100.6 7.9 %collective-permute-start.19 = (f32[1,256,256]{2,1,0:T(8,128)S(1)}, f32[1,256,256]{2,1,0:T(8,128)S(1)}, u32[]{:S(2)}, u32[]{:S(2)}) collective-permute-start(f32[1,256,256]{2,1,0:T(8,128)S(1)} %get-tuple-element.61), channel_id=1, source_target_pairs={{0,1},{1,0},{2,3},{3,2},{4,5},{5,4},{6,7},{7,6},{8,9},{9,8},{10,11... | collective-permute-start | bytes 786440 | tf_op jit(solution)/shard_map/ppermute | solution.py:523

commit v10 on v9

--- a/solution.py
+++ b/solution.py
@@ -348,10 +348,16 @@
     hats.insert(len(hats) // 2 + 1, None)
     even = lax.rem(lax.axis_index("z"), 2) == 0
 
+    high, low = terms(columns, 2)
+
+    def one(left, right):
+        return jnp.dot(left, right, preferred_element_type=jnp.float32)
+
     def fill(order):
         for z in range(v_local.shape[0]):
             rows = [jnp.zeros((width, columns.shape[1]), jnp.float32) if h is None else h[:, z, :] for h in order]
-            pot[z] = v_local[z] + dot(columns, jnp.concatenate(rows, axis=0))
+            upper, lower = terms(jnp.concatenate(rows, axis=0), 2)
+            pot[z] = v_local[z] + (one(high, upper) + (one(high, lower) + one(low, upper)))
 
     pl.when(even)(functools.partial(fill, hats))
     pl.when(jnp.logical_not(even))(functools.partial(fill, hats[:1] + hats[:0:-1]))

time: 111 us -> 111 us (level)
  transfers between devices with their start and end apart: 20 -> 20, of which waited for: 11 -> 11; matrix products, arithmetic and copies ran while one was open for 0% -> 0% of each run, Pallas kernels for 16% -> 15%
where the time goes in v10:
time: 111 us; the launch traced here: 110 us
  waiting for transfers between devices  30 us (27%)
  starting transfers between devices  28.7 us (26%)
  blocking collectives  28.3 us (25%)
  Pallas kernels  21.5 us (19%)
    all_to_all x2, blocking collectives, across(): lax.all_to_all(value, ('slab', 'y'), split_axis=0, concat_axis=0, tiled=T...  28.3 us
    ppermute x8, waiting for transfers between devices, swap_far(): lax.ppermute(value, 'z', [(i, (i - 1) % count if i % 2 == 0 else (i + 1)...  18.5 us
    ppermute x8, starting transfers between devices, swap_far(): lax.ppermute(value, 'z', [(i, (i - 1) % count if i % 2 == 0 else (i + 1)...  17.2 us
    ppermute x8, waiting for transfers between devices, swap_near(): lax.ppermute(value, 'z', [(i, i ^ 1) for i in range(lax.axis_size('z'))])  9.05 us
    ppermute x8, starting transfers between devices, swap_near(): lax.ppermute(value, 'z', [(i, i ^ 1) for i in range(lax.axis_size('z'))])  5.78 us
    ppermute x2, starting transfers between devices, swap_edges(): from_other = lax.ppermute(to_other, ('y', 'slab'), pairs)  4.69 us
    pallas_call x1, Pallas kernels, inner_update(): pl.pallas_call(functools.partial(inner_kernel, once_groups, base_groups),...  4.5 us
    pallas_call x1, Pallas kernels, density(): pl.pallas_call(functools.partial(density_kernel, 2.0 / total_orbs), in_sp...  3.85 us
  transfers between devices with their start and end apart: 20, of which 11 were waited for; matrix products, arithmetic and copies ran while one was open for 0% of the time, Pallas kernels for 15%

profile of v10, /device:TPU:8, one launch (start us, length us, event | category | flops | bytes accessed | tf_op | source)
XLA Modules:
  0.0 109.9 jit_solution(12622217636195927309)
XLA Ops:
  0.6 3.8 %density.1 = (f32[8,256,256]{2,1,0:T(8,128)S(1)}, f32[256,256]{1,0:T(8,128)S(1)}, f32[8,16,256]{2,1,0:T(8,128)S(1)}, f32[8,16,256]{2,1,0:T(8,128)S(1)}, f32[4,25...) custom-call(f32[1,8,256,256]{3,2,1,0:T(8,128)} %psi_re.1, f32[1,8,256,256]{3,2,1,0:T(8,128)} %psi_im.1, ...), custom_call_target="tpu_custom_call" | custom-call | tf_op jit(solution)/shard_map/density/pallas_call | solution.py:135
  4.5 2.0 %collective-permute-start = (f32[8,16,256]{2,1,0:T(8,128)S(1)}, f32[8,16,256]{2,1,0:T(8,128)S(1)}, u32[]{:S(2)}, u32[]{:S(2)}) collective-permute-start(f32[8,16,256]{2,1,0:T(8,128)S(1)} %get-tuple-element.37), channel_id=1, source_target_pairs={{0,16},{16,0},{32,48},{48,32},{64,80},{80,64},{96,112},{112,96},{1... | collective-permute-start | bytes 393224 | tf_op jit(solution)/shard_map/ppermute | solution.py:512
  6.5 5.0 %collective-permute-start.4 = (f32[8,16,256]{2,1,0:T(8,128)S(1)}, f32[8,16,256]{2,1,0:T(8,128)S(1)}, u32[]{:S(2)}, u32[]{:S(2)}) collective-permute-start(f32[8,16,256]{2,1,0:T(8,128)S(1)} %get-tuple-element.43), channel_id=1, source_target_pairs={{0,112},{16,32},{32,16},{48,64},{64,48},{80,96},{96,80},{112,0},{1... | collective-permute-start | bytes 393224 | tf_op jit(solution)/shard_map/ppermute | solution.py:517
  11.4 1.3 %shares_a.1 = (f32[8,32,256]{2,1,0:T(8,128)S(1)}, f32[8,32,256]{2,1,0:T(8,128)S(1)}) custom-call(f32[8,256,256]{2,1,0:T(8,128)S(1)} %get-tuple-element.33.rho, f32[256,256]{1,0:T(8,128)S(1)} %get-tuple-element.34.rows), custom_call_target="tpu_custom_call" | custom-call | bytes 2160000 | tf_op jit(solution)/shard_map/shares_a/pallas_call | solution.py:164
  12.7 2.0 %collective-permute-done.4 = f32[8,16,256]{2,1,0:T(8,128)S(1)} collective-permute-done((f32[8,16,256]{2,1,0:T(8,128)S(1)}, f32[8,16,256]{2,1,0:T(8,128)S(1)}, u32[]{:S(2)}, u32[]{:S(2)}) %collective-permute-start.4) | collective-permute-done | bytes 131104 | tf_op jit(solution)/shard_map/ppermute | solution.py:517
  14.8 0.1 slice_add_fusion.1
  14.9 0.1 collective-permute-start.5
  15.0 3.0 %collective-permute-start.1 = (f32[8,32,256]{2,1,0:T(8,128)S(1)}, f32[8,32,256]{2,1,0:T(8,128)S(1)}, u32[]{:S(2)}, u32[]{:S(2)}) collective-permute-start(f32[8,32,256]{2,1,0:T(8,128)S(1)} %pad_maximum_fusion), channel_id=1, source_target_pairs={{0,112},{16,32},{32,16},{48,64},{64,48},{80,96},{96,80},{112,0},{1... | collective-permute-start | bytes 786440 | tf_op jit(solution)/shard_map/ppermute | solution.py:517
  18.0 1.4 %shares_b.1 = (f32[8,32,256]{2,1,0:T(8,128)S(1)}, f32[8,32,256]{2,1,0:T(8,128)S(1)}, f32[8,32,256]{2,1,0:T(8,128)S(1)}, f32[8,32,256]{2,1,0:T(8,128)S(1)}, f32[8,32,256]{2,1,0:T(8,128)S(1)}) custom-call(f32[8,256,256]{2,1,0:T(8,128)S(1)} %get-tuple-element.33.rho, f32[256,256]{1,0:T(8,128)S(1)} %get-tuple-element.34.rows), custom_call_target="tpu_custom_call" | custom-call | bytes 5400000 | tf_op jit(solution)/shard_map/shares_b/pallas_call | solution.py:164
  19.5 0.9 once_a.1.refs_0_.refs_7_
  20.4 1.8 %collective-permute-done.5 = f32[8,32,256]{2,1,0:T(8,128)S(1)} collective-permute-done((f32[8,32,256]{2,1,0:T(8,128)S(1)}, f32[8,32,256]{2,1,0:T(8,128)S(1)}, u32[]{:S(2)}, u32[]{:S(2)}) %collective-permute-start.5) | collective-permute-done | bytes 262176 | tf_op jit(solution)/shard_map/ppermute | solution.py:512
  22.3 2.7 %collective-permute-start.6 = (f32[8,32,256]{2,1,0:T(8,128)S(1)}, f32[8,32,256]{2,1,0:T(8,128)S(1)}, u32[]{:S(2)}, u32[]{:S(2)}) collective-permute-start(f32[8,32,256]{2,1,0:T(8,128)S(1)} %add.22), channel_id=1, source_target_pairs={{0,112},{16,32},{32,16},{48,64},{64,48},{80,96},{96,80},{112,0},{1... | collective-permute-start | bytes 786440 | tf_op jit(solution)/shard_map/ppermute | solution.py:517
  25.0 0.1 collective-permute-start.2
  25.1 0.1 collective-permute-start.9
  25.2 4.6 %collective-permute-start.10 = (f32[4,256,256]{2,1,0:T(8,128)S(1)}, f32[4,256,256]{2,1,0:T(8,128)S(1)}, u32[]{:S(2)}, u32[]{:S(2)}) collective-permute-start(f32[4,256,256]{2,1,0:T(8,128)S(1)} %get-tuple-element.49), channel_id=1, source_target_pairs={{0,15},{1,2},{2,1},{3,4},{4,3},{5,6},{6,5},{7,8},{8,7},{9,10},{10,... | collective-permute-start | bytes 3145736 | tf_op jit(solution)/shard_map/ppermute | solution.py:530
  29.8 0.9 once_b.1.refs_1_.refs_8_
  30.8 0.0 copy-start.3
  30.8 0.0 copy-start.5
  30.8 2.0 %collective-permute-start.7 = (f32[8,32,256]{2,1,0:T(8,128)S(1)}, f32[8,32,256]{2,1,0:T(8,128)S(1)}, u32[]{:S(2)}, u32[]{:S(2)}) collective-permute-start(f32[8,32,256]{2,1,0:T(8,128)S(1)} %add.23), channel_id=1, source_target_pairs={{0,16},{16,0},{32,48},{48,32},{64,80},{80,64},{96,112},{112,96},{1... | collective-permute-start | bytes 786440 | tf_op jit(solution)/shard_map/ppermute | solution.py:512
  32.9 1.3 %collective-permute-start.3 = (f32[8,32,256]{2,1,0:T(8,128)S(1)}, f32[8,32,256]{2,1,0:T(8,128)S(1)}, u32[]{:S(2)}, u32[]{:S(2)}) collective-permute-start(f32[8,32,256]{2,1,0:T(8,128)S(1)} %add.20), channel_id=1, source_target_pairs={{0,112},{16,32},{32,16},{48,64},{64,48},{80,96},{96,80},{112,0},{1... | collective-permute-start | bytes 786440 | tf_op jit(solution)/shard_map/ppermute | solution.py:517
  34.2 3.1 %collective-permute-done.7.down = f32[8,32,256]{2,1,0:T(8,128)S(1)} collective-permute-done((f32[8,32,256]{2,1,0:T(8,128)S(1)}, f32[8,32,256]{2,1,0:T(8,128)S(1)}, u32[]{:S(2)}, u32[]{:S(2)}) %collective-permute-start.7) | collective-permute-done | bytes 262176 | tf_op jit(solution)/shard_map/ppermute | solution.py:512
  37.3 3.3 %collective-permute-done.3.up = f32[8,32,256]{2,1,0:T(8,128)S(1)} collective-permute-done((f32[8,32,256]{2,1,0:T(8,128)S(1)}, f32[8,32,256]{2,1,0:T(8,128)S(1)}, u32[]{:S(2)}, u32[]{:S(2)}) %collective-permute-start.3) | collective-permute-done | bytes 262176 | tf_op jit(solution)/shard_map/ppermute | solution.py:517
  40.6 0.1 add_shares.1
  40.7 15.8 %all_to_all.10 = f32[32,8,256]{2,1,0:T(8,128)S(1)} all-to-all(f32[32,8,256]{2,1,0:T(8,128)S(1)} %add_shares.1), channel_id=1, replica_groups=mesh['y'=2,'z'=8,'slab'=16] {'slab','y'}, dimensions={0} | all-to-all | bytes 524288 | tf_op jit(solution)/shard_map/all_to_all | solution.py:566
  56.4 1.1 solve_xz.1
  57.5 12.5 %all_to_all.11.refs_0_ = f32[32,8,256]{2,1,0:T(8,128)S(1)} all-to-all(f32[32,8,256]{2,1,0:T(8,128)S(1)} %solve_xz.1), channel_id=1, replica_groups=mesh['y'=2,'z'=8,'slab'=16] {'slab','y'}, dimensions={0} | all-to-all | bytes 524288 | tf_op jit(solution)/shard_map/all_to_all | solution.py:566
  70.1 0.0 collective-permute-start.11
  70.1 1.2 %once_c.1.refs_2_.refs_9_ = f32[2,4,256,256]{3,2,1,0:T(8,128)S(1)} custom-call(bf16[256,256]{1,0:T(8,128)(2,1)S(1)} %copy-done.2, f32[8,256,256]{2,1,0:T(8,128)S(1)} %bitcast.5, f32[8,256,256]{2,1,0:T(8,128)S(1)} %bitcast.11, f32[4,256,256]{2,1,0:T(8,128)S(1)} %collective-permute-done.9.refs_2_.mate, f32[4,256,256]{2,1,0:T(8,128)S(1)} %collective-permute-done.10.refs_3_.other), custom_call_target="tpu_custom_call" | custom-call | bytes 4320000 | tf_op jit(solution)/shard_map/once_c/pallas_call | solution.py:291
  71.4 7.5 %collective-permute-done.11.refs_6_ = f32[32,8,256]{2,1,0:T(8,128)S(1)} collective-permute-done((f32[32,8,256]{2,1,0:T(8,128)S(1)}, f32[32,8,256]{2,1,0:T(8,128)S(1)}, u32[]{:S(2)}, u32[]{:S(2)}) %collective-permute-start.11) | collective-permute-done | bytes 262176 | tf_op jit(solution)/shard_map/ppermute | solution.py:517
  78.9 1.8 %collective-permute-start.13 = (f32[32,8,256]{2,1,0:T(8,128)S(1)}, f32[32,8,256]{2,1,0:T(8,128)S(1)}, u32[]{:S(2)}, u32[]{:S(2)}) collective-permute-start(f32[32,8,256]{2,1,0:T(8,128)S(1)} %collective-permute-done.8.refs_1_), channel_id=1, source_target_pairs={{0,112},{16,32},{32,16},{48,64},{64,48},{80,96},{96,80},{112,0},{1... | collective-permute-start | bytes 786440 | tf_op jit(solution)/shard_map/ppermute | solution.py:517
  80.7 1.5 %base_a.1.refs_10_ = f32[2,4,256,256]{3,2,1,0:T(8,128)S(1)} custom-call(bf16[256,256]{1,0:T(8,128)(2,1)S(1)} %copy-done.2, f32[8,256,256]{2,1,0:T(8,128)S(1)} %bitcast.6, f32[8,256,256]{2,1,0:T(8,128)S(1)} %bitcast.12, f32[2,3,256,256]{3,2,1,0:T(8,128)S(1)} %once_a.1.refs_0_.refs_7_, f32[2,3,256,256]{3,2,1,0:T(8,128)S(1)} %once_b.1.refs_1_.refs_8_, ...), custom_call_target="tpu_custom_call" | custom-call | bytes 5760000 | tf_op jit(solution)/shard_map/base_a/pallas_call | solution.py:320
  82.2 3.4 %collective-permute-done.12.refs_2_ = f32[32,8,256]{2,1,0:T(8,128)S(1)} collective-permute-done((f32[32,8,256]{2,1,0:T(8,128)S(1)}, f32[32,8,256]{2,1,0:T(8,128)S(1)}, u32[]{:S(2)}, u32[]{:S(2)}) %collective-permute-start.12) | collective-permute-done | bytes 262176 | tf_op jit(solution)/shard_map/ppermute | solution.py:512
  85.6 0.7 collective-permute-start.15
  86.3 0.6 collective-permute-done.13.refs_5_
  86.8 1.5 %collective-permute-start.14 = (f32[32,8,256]{2,1,0:T(8,128)S(1)}, f32[32,8,256]{2,1,0:T(8,128)S(1)}, u32[]{:S(2)}, u32[]{:S(2)}) collective-permute-start(f32[32,8,256]{2,1,0:T(8,128)S(1)} %collective-permute-done.13.refs_5_), channel_id=1, source_target_pairs={{0,16},{16,0},{32,48},{48,32},{64,80},{80,64},{96,112},{112,96},{1... | collective-permute-start | bytes 786440 | tf_op jit(solution)/shard_map/ppermute | solution.py:512
  88.3 1.5 %base_b.1.refs_11_ = f32[2,4,256,256]{3,2,1,0:T(8,128)S(1)} custom-call(bf16[256,256]{1,0:T(8,128)(2,1)S(1)} %copy-done.2, f32[8,256,256]{2,1,0:T(8,128)S(1)} %bitcast.7, f32[8,256,256]{2,1,0:T(8,128)S(1)} %bitcast.13, f32[2,3,256,256]{3,2,1,0:T(8,128)S(1)} %once_a.1.refs_0_.refs_7_, f32[2,3,256,256]{3,2,1,0:T(8,128)S(1)} %once_b.1.refs_1_.refs_8_, ...), custom_call_target="tpu_custom_call" | custom-call | bytes 5760000 | tf_op jit(solution)/shard_map/base_b/pallas_call | solution.py:320
  89.8 3.4 %collective-permute-done.15.refs_4_ = f32[32,8,256]{2,1,0:T(8,128)S(1)} collective-permute-done((f32[32,8,256]{2,1,0:T(8,128)S(1)}, f32[32,8,256]{2,1,0:T(8,128)S(1)}, u32[]{:S(2)}, u32[]{:S(2)}) %collective-permute-start.15) | collective-permute-done | bytes 262176 | tf_op jit(solution)/shard_map/ppermute | solution.py:517
  93.2 0.1 collective-permute-start.16
  93.3 0.7 collective-permute-done.14.refs_3_
  94.0 2.7 %collective-permute-start.17 = (f32[16,8,256]{2,1,0:T(8,128)S(1)}, f32[16,8,256]{2,1,0:T(8,128)S(1)}, u32[]{:S(2)}, u32[]{:S(2)}) collective-permute-start(f32[16,8,256]{2,1,0:T(8,128)S(1)} %slice.23), channel_id=1, source_target_pairs={{0,112},{16,32},{32,16},{48,64},{64,48},{80,96},{96,80},{112,0},{1... | collective-permute-start | bytes 393224 | tf_op jit(solution)/shard_map/ppermute | solution.py:517
  96.7 1.8 %early_potential.1 = (f32[8,256,256]{2,1,0:T(8,128)S(1)}, bf16[256,192]{1,0:T(8,128)(2,1)S(1)}) custom-call(f32[8,256,256]{2,1,0:T(8,128)S(1)} %copy-done.4, f32[256,256]{1,0:T(8,128)S(1)} %copy-done.3, f32[32,8,256]{2,1,0:T(8,128)S(1)} %all_to_all.11.refs_0_, f32[32,8,256]{2,1,0:T(8,128)S(1)} %collective-permute-done.8.refs_1_, ...), custom_call_target="tpu_custom_call" | custom-call | bytes 8279999 | tf_op jit(solution)/shard_map/early_potential/pallas_call | solution.py:369
  98.5 1.8 %collective-permute-done.17.refs_4_.down = f32[16,8,256]{2,1,0:T(8,128)S(1)} collective-permute-done((f32[16,8,256]{2,1,0:T(8,128)S(1)}, f32[16,8,256]{2,1,0:T(8,128)S(1)}, u32[]{:S(2)}, u32[]{:S(2)}) %collective-permute-start.17) | collective-permute-done | bytes 131104 | tf_op jit(solution)/shard_map/ppermute | solution.py:517
  100.3 0.2 outer_potential.1
  100.5 0.1 collective-permute-start.18
  100.6 0.9 collective-permute-start.19
  101.6 4.5 %inner_update.1 = (f32[1,8,256,256]{3,2,1,0:T(8,128)}, f32[1,8,256,256]{3,2,1,0:T(8,128)}, f32[2,2,256,256]{3,2,1,0:T(8,128)S(1)}) custom-call(bf16[256,256]{1,0:T(8,128)(2,1)S(1)} %copy-done.2, f32[8,256,256]{2,1,0:T(8,128)S(1)} %get-tuple-element.56.refs_1_.early, bf16[256,192]{1,0:T(8,128)(2,1)S(1)} %get-tuple-element.57.refs_2_.tail, ...), custom_call_target="tpu_custom_call" | custom-call | bytes 15480000 | tf_op jit(solution)/shard_map/inner_update/pallas_call | solution.py:459
  106.1 2.5 %collective-permute-done.18.v_other = f32[1,256,256]{2,1,0:T(8,128)S(1)} collective-permute-done((f32[1,256,256]{2,1,0:T(8,128)S(1)}, f32[1,256,256]{2,1,0:T(8,128)S(1)}, u32[]{:S(2)}, u32[]{:S(2)}) %collective-permute-start.18) | collective-permute-done | bytes 262176 | tf_op jit(solution)/shard_map/ppermute | solution.py:530
  108.5 1.1 %close_ends.1 = (f32[1,8,256,256]{3,2,1,0:T(8,128)}, f32[1,8,256,256]{3,2,1,0:T(8,128)}) custom-call(f32[2,2,256,256]{3,2,1,0:T(8,128)S(1)} %get-tuple-element.59.open_ends, f32[1,256,256]{2,1,0:T(8,128)S(1)} %collective-permute-done.18.v_other, f32[1,256,256]{2,1,0:T(8,128)S(1)} %collective-permute-done.19.v_mate, ...), custom_call_target="tpu_custom_call", output_to_operand_aliasing={{0}: (5, {}), {1}: (6, {})} | custom-call | tf_op jit(solution)/shard_map/close_ends/pallas_call | solution.py:499
  (29 shorter events, 0.3 us)
Async XLA Ops:
  4.5 8.2 %collective-permute-start = (f32[8,16,256]{2,1,0:T(8,128)S(1)}, f32[8,16,256]{2,1,0:T(8,128)S(1)}, u32[]{:S(2)}, u32[]{:S(2)}) collective-permute-start(f32[8,16,256]{2,1,0:T(8,128)S(1)} %get-tuple-element.37), channel_id=1, source_target_pairs={{0,16},{16,0},{32,48},{48,32},{64,80},{80,64},{96,112},{112,96},{1... | collective-permute-start | bytes 393224 | tf_op jit(solution)/shard_map/ppermute | solution.py:512
  6.5 8.3 %collective-permute-start.4 = (f32[8,16,256]{2,1,0:T(8,128)S(1)}, f32[8,16,256]{2,1,0:T(8,128)S(1)}, u32[]{:S(2)}, u32[]{:S(2)}) collective-permute-start(f32[8,16,256]{2,1,0:T(8,128)S(1)} %get-tuple-element.43), channel_id=1, source_target_pairs={{0,112},{16,32},{32,16},{48,64},{64,48},{80,96},{96,80},{112,0},{1... | collective-permute-start | bytes 393224 | tf_op jit(solution)/shard_map/ppermute | solution.py:517
  14.8 4.7 %copy-start = (f32[1,8,256,256]{3,2,1,0:T(8,128)S(1)}, f32[1,8,256,256]{3,2,1,0:T(8,128)}, u32[]{:S(2)}) copy-start(f32[1,8,256,256]{3,2,1,0:T(8,128)} %psi_re.1) | copy-start | bytes 6291460
  14.8 4.7 %copy-start.1 = (f32[1,8,256,256]{3,2,1,0:T(8,128)S(1)}, f32[1,8,256,256]{3,2,1,0:T(8,128)}, u32[]{:S(2)}) copy-start(f32[1,8,256,256]{3,2,1,0:T(8,128)} %psi_im.1) | copy-start | bytes 6291460
  14.8 4.7 %copy-start.2 = (bf16[256,256]{1,0:T(8,128)(2,1)S(1)}, bf16[256,256]{1,0:T(8,128)(2,1)}, u32[]{:S(2)}) copy-start(bf16[256,256]{1,0:T(8,128)(2,1)} %constant.8.clone.sides.refs_0_) | copy-start | bytes 393220
  14.9 7.4 %collective-permute-start.5 = (f32[8,32,256]{2,1,0:T(8,128)S(1)}, f32[8,32,256]{2,1,0:T(8,128)S(1)}, u32[]{:S(2)}, u32[]{:S(2)}) collective-permute-start(f32[8,32,256]{2,1,0:T(8,128)S(1)} %pad_maximum_fusion.1), channel_id=1, source_target_pairs={{0,16},{16,0},{32,48},{48,32},{64,80},{80,64},{96,112},{112,96},{1... | collective-permute-start | bytes 786440 | tf_op jit(solution)/shard_map/ppermute | solution.py:512
  15.0 10.0 %collective-permute-start.1 = (f32[8,32,256]{2,1,0:T(8,128)S(1)}, f32[8,32,256]{2,1,0:T(8,128)S(1)}, u32[]{:S(2)}, u32[]{:S(2)}) collective-permute-start(f32[8,32,256]{2,1,0:T(8,128)S(1)} %pad_maximum_fusion), channel_id=1, source_target_pairs={{0,112},{16,32},{32,16},{48,64},{64,48},{80,96},{96,80},{112,0},{1... | collective-permute-start | bytes 786440 | tf_op jit(solution)/shard_map/ppermute | solution.py:517
  22.3 8.5 %collective-permute-start.6 = (f32[8,32,256]{2,1,0:T(8,128)S(1)}, f32[8,32,256]{2,1,0:T(8,128)S(1)}, u32[]{:S(2)}, u32[]{:S(2)}) collective-permute-start(f32[8,32,256]{2,1,0:T(8,128)S(1)} %add.22), channel_id=1, source_target_pairs={{0,112},{16,32},{32,16},{48,64},{64,48},{80,96},{96,80},{112,0},{1... | collective-permute-start | bytes 786440 | tf_op jit(solution)/shard_map/ppermute | solution.py:517
  25.0 7.8 %collective-permute-start.2 = (f32[8,32,256]{2,1,0:T(8,128)S(1)}, f32[8,32,256]{2,1,0:T(8,128)S(1)}, u32[]{:S(2)}, u32[]{:S(2)}) collective-permute-start(f32[8,32,256]{2,1,0:T(8,128)S(1)} %add.19), channel_id=1, source_target_pairs={{0,16},{16,0},{32,48},{48,32},{64,80},{80,64},{96,112},{112,96},{1... | collective-permute-start | bytes 786440 | tf_op jit(solution)/shard_map/ppermute | solution.py:512
  25.1 45.0 %collective-permute-start.9 = (f32[4,256,256]{2,1,0:T(8,128)S(1)}, f32[4,256,256]{2,1,0:T(8,128)S(1)}, u32[]{:S(2)}, u32[]{:S(2)}) collective-permute-start(f32[4,256,256]{2,1,0:T(8,128)S(1)} %get-tuple-element.48), channel_id=1, source_target_pairs={{0,1},{1,0},{2,3},{3,2},{4,5},{5,4},{6,7},{7,6},{8,9},{9,8},{10,11... | collective-permute-start | bytes 3145736 | tf_op jit(solution)/shard_map/ppermute | solution.py:529
  25.2 44.9 %collective-permute-start.10 = (f32[4,256,256]{2,1,0:T(8,128)S(1)}, f32[4,256,256]{2,1,0:T(8,128)S(1)}, u32[]{:S(2)}, u32[]{:S(2)}) collective-permute-start(f32[4,256,256]{2,1,0:T(8,128)S(1)} %get-tuple-element.49), channel_id=1, source_target_pairs={{0,15},{1,2},{2,1},{3,4},{4,3},{5,6},{6,5},{7,8},{8,7},{9,10},{10,... | collective-permute-start | bytes 3145736 | tf_op jit(solution)/shard_map/ppermute | solution.py:530
  30.8 25.7 %copy-start.3 = (f32[256,256]{1,0:T(8,128)S(1)}, f32[256,256]{1,0:T(8,128)}, u32[]{:S(2)}) copy-start(f32[256,256]{1,0:T(8,128)} %constant.6.clone.y_table.x_table.table) | copy-start | bytes 786436
  30.8 25.7 %copy-start.5 = (f32[128,128]{1,0:T(8,128)S(1)}, f32[128,128]{1,0:T(8,128)}, u32[]{:S(2)}) copy-start(f32[128,128]{1,0:T(8,128)} %constant.7.clone.z_table) | copy-start | bytes 196612
  30.8 6.5 %collective-permute-start.7 = (f32[8,32,256]{2,1,0:T(8,128)S(1)}, f32[8,32,256]{2,1,0:T(8,128)S(1)}, u32[]{:S(2)}, u32[]{:S(2)}) collective-permute-start(f32[8,32,256]{2,1,0:T(8,128)S(1)} %add.23), channel_id=1, source_target_pairs={{0,16},{16,0},{32,48},{48,32},{64,80},{80,64},{96,112},{112,96},{1... | collective-permute-start | bytes 786440 | tf_op jit(solution)/shard_map/ppermute | solution.py:512
  32.9 7.7 %collective-permute-start.3 = (f32[8,32,256]{2,1,0:T(8,128)S(1)}, f32[8,32,256]{2,1,0:T(8,128)S(1)}, u32[]{:S(2)}, u32[]{:S(2)}) collective-permute-start(f32[8,32,256]{2,1,0:T(8,128)S(1)} %add.20), channel_id=1, source_target_pairs={{0,112},{16,32},{32,16},{48,64},{64,48},{80,96},{96,80},{112,0},{1... | collective-permute-start | bytes 786440 | tf_op jit(solution)/shard_map/ppermute | solution.py:517
  70.1 8.8 %collective-permute-start.11 = (f32[32,8,256]{2,1,0:T(8,128)S(1)}, f32[32,8,256]{2,1,0:T(8,128)S(1)}, u32[]{:S(2)}, u32[]{:S(2)}) collective-permute-start(f32[32,8,256]{2,1,0:T(8,128)S(1)} %all_to_all.11.refs_0_), channel_id=1, source_target_pairs={{0,112},{16,32},{32,16},{48,64},{64,48},{80,96},{96,80},{112,0},{1... | collective-permute-start | bytes 786440 | tf_op jit(solution)/shard_map/ppermute | solution.py:517
  70.1 8.8 %collective-permute-start.8 = (f32[32,8,256]{2,1,0:T(8,128)S(1)}, f32[32,8,256]{2,1,0:T(8,128)S(1)}, u32[]{:S(2)}, u32[]{:S(2)}) collective-permute-start(f32[32,8,256]{2,1,0:T(8,128)S(1)} %all_to_all.11.refs_0_), channel_id=1, source_target_pairs={{0,16},{16,0},{32,48},{48,32},{64,80},{80,64},{96,112},{112,96},{1... | collective-permute-start | bytes 786440 | tf_op jit(solution)/shard_map/ppermute | solution.py:512
  78.9 6.7 %collective-permute-start.12 = (f32[32,8,256]{2,1,0:T(8,128)S(1)}, f32[32,8,256]{2,1,0:T(8,128)S(1)}, u32[]{:S(2)}, u32[]{:S(2)}) collective-permute-start(f32[32,8,256]{2,1,0:T(8,128)S(1)} %collective-permute-done.11.refs_6_), channel_id=1, source_target_pairs={{0,16},{16,0},{32,48},{48,32},{64,80},{80,64},{96,112},{112,96},{1... | collective-permute-start | bytes 786440 | tf_op jit(solution)/shard_map/ppermute | solution.py:512
  78.9 7.9 %collective-permute-start.13 = (f32[32,8,256]{2,1,0:T(8,128)S(1)}, f32[32,8,256]{2,1,0:T(8,128)S(1)}, u32[]{:S(2)}, u32[]{:S(2)}) collective-permute-start(f32[32,8,256]{2,1,0:T(8,128)S(1)} %collective-permute-done.8.refs_1_), channel_id=1, source_target_pairs={{0,112},{16,32},{32,16},{48,64},{64,48},{80,96},{96,80},{112,0},{1... | collective-permute-start | bytes 786440 | tf_op jit(solution)/shard_map/ppermute | solution.py:517
  82.2 14.5 %copy-start.4 = (f32[8,256,256]{2,1,0:T(8,128)S(1)}, f32[8,256,256]{2,1,0:T(8,128)}, u32[]{:S(2)}) copy-start(f32[8,256,256]{2,1,0:T(8,128)} %v_local.1) | copy-start | bytes 6291460
  85.6 7.6 %collective-permute-start.15 = (f32[32,8,256]{2,1,0:T(8,128)S(1)}, f32[32,8,256]{2,1,0:T(8,128)S(1)}, u32[]{:S(2)}, u32[]{:S(2)}) collective-permute-start(f32[32,8,256]{2,1,0:T(8,128)S(1)} %collective-permute-done.12.refs_2_), channel_id=1, source_target_pairs={{0,112},{16,32},{32,16},{48,64},{64,48},{80,96},{96,80},{112,0},{1... | collective-permute-start | bytes 786440 | tf_op jit(solution)/shard_map/ppermute | solution.py:517
  86.8 7.2 %collective-permute-start.14 = (f32[32,8,256]{2,1,0:T(8,128)S(1)}, f32[32,8,256]{2,1,0:T(8,128)S(1)}, u32[]{:S(2)}, u32[]{:S(2)}) collective-permute-start(f32[32,8,256]{2,1,0:T(8,128)S(1)} %collective-permute-done.13.refs_5_), channel_id=1, source_target_pairs={{0,16},{16,0},{32,48},{48,32},{64,80},{80,64},{96,112},{112,96},{1... | collective-permute-start | bytes 786440 | tf_op jit(solution)/shard_map/ppermute | solution.py:512
  93.2 5.3 %collective-permute-start.16 = (f32[16,8,256]{2,1,0:T(8,128)S(1)}, f32[16,8,256]{2,1,0:T(8,128)S(1)}, u32[]{:S(2)}, u32[]{:S(2)}) collective-permute-start(f32[16,8,256]{2,1,0:T(8,128)S(1)} %slice.22), channel_id=1, source_target_pairs={{0,16},{16,0},{32,48},{48,32},{64,80},{80,64},{96,112},{112,96},{1... | collective-permute-start | bytes 393224 | tf_op jit(solution)/shard_map/ppermute | solution.py:512
  94.0 6.3 %collective-permute-start.17 = (f32[16,8,256]{2,1,0:T(8,128)S(1)}, f32[16,8,256]{2,1,0:T(8,128)S(1)}, u32[]{:S(2)}, u32[]{:S(2)}) collective-permute-start(f32[16,8,256]{2,1,0:T(8,128)S(1)} %slice.23), channel_id=1, source_target_pairs={{0,112},{16,32},{32,16},{48,64},{64,48},{80,96},{96,80},{112,0},{1... | collective-permute-start | bytes 393224 | tf_op jit(solution)/shard_map/ppermute | solution.py:517
  100.5 8.0 %collective-permute-start.18 = (f32[1,256,256]{2,1,0:T(8,128)S(1)}, f32[1,256,256]{2,1,0:T(8,128)S(1)}, u32[]{:S(2)}, u32[]{:S(2)}) collective-permute-start(f32[1,256,256]{2,1,0:T(8,128)S(1)} %get-tuple-element.60), channel_id=1, source_target_pairs={{0,143},{1,2},{2,1},{3,4},{4,3},{5,6},{6,5},{7,136},{8,135},{9,10}... | collective-permute-start | bytes 786440 | tf_op jit(solution)/shard_map/ppermute | solution.py:530
  100.6 7.9 %collective-permute-start.19 = (f32[1,256,256]{2,1,0:T(8,128)S(1)}, f32[1,256,256]{2,1,0:T(8,128)S(1)}, u32[]{:S(2)}, u32[]{:S(2)}) collective-permute-start(f32[1,256,256]{2,1,0:T(8,128)S(1)} %get-tuple-element.61), channel_id=1, source_target_pairs={{0,1},{1,0},{2,3},{3,2},{4,5},{5,4},{6,7},{7,6},{8,9},{9,8},{10,11... | collective-permute-start | bytes 786440 | tf_op jit(solution)/shard_map/ppermute | solution.py:529
